TPU v7x, 32 devices: a whole 2x2x4 slice. The times are simulated.
32 devices in a mesh: seq: 8 (over y, x, core), row: 4 (over z).
Axes of the slice: x: 2, y: 2, z: 4, core: 2. Of those that a mesh axis runs over, the one named last changes fastest.
Arguments:
- hidden: bfloat16 [4, 1024, 768], P('row', 'seq'), may hold values from -6 to 6
- segments: int32 [4, 1024], P('row', 'seq'), may hold values from 0 to 2, as said below
- rel_embed: bfloat16 [512, 768], replicated, may hold values from -6 to 6
- query_weight: bfloat16 [768, 768], replicated, may hold values from -0.3125 to 0.3125
- key_weight: bfloat16 [768, 768], replicated, may hold values from -0.3125 to 0.3125
- value_weight: bfloat16 [768, 768], replicated, may hold values from -0.21875 to 0.21875
- output_weight: bfloat16 [768, 768], replicated, may hold values from -1.75 to 1.75
- up_weight: bfloat16 [768, 3072], replicated, may hold values from -0.21875 to 0.21875
- down_weight: bfloat16 [3072, 768], replicated, may hold values from -0.109375 to 0.109375
- norm1_gain: float32 [768], replicated, may hold values from 0.5 to 1.5
- norm1_bias: float32 [768], replicated, may hold values from -1 to 1
- norm2_gain: float32 [768], replicated, may hold values from 0.5 to 1.5
- norm2_bias: float32 [768], replicated, may hold values from -1 to 1
- cotangent: bfloat16 [4, 1024, 768], P('row', 'seq'), may hold values from -6 to 6
Outputs:
- output: bfloat16 [4, 1024, 768], P('row', 'seq')
- grad_input: bfloat16 [4, 1024, 768], P('row', 'seq')
- grad_query_weight: float32 [768, 768], P('row')
- grad_key_weight: float32 [768, 768], P('row')
- grad_value_weight: float32 [768, 768], P('row')
- grad_output_weight: float32 [768, 768], P('row')
- grad_up_weight: float32 [768, 3072], P('row')
- grad_down_weight: float32 [3072, 768], P('row')
- grad_norm1_gain: float32 [768], P('row')
- grad_norm1_bias: float32 [768], P('row')
- grad_norm2_gain: float32 [768], P('row')
- grad_norm2_bias: float32 [768], P('row')
- grad_relative: float32 [512, 768], replicated
Inputs may be any that keep to these rules, and one draw needn't show every extreme that they name: `segments`: along each row of 1024 slots the ids never fall and take the values 0, 1 and 2; document 1 begins within the row's first 128 slots and ends within its last 128 slots.
All inputs are finite; a program needn't handle non-finite values.
Results may differ from a plain program's by a relative error of at most 0.024.
Values may be sent and summed in bfloat16 or wider, within the bound.
No kernel may reach another device: no remote copies, remote signals or barrier semaphores. Data moves between devices by JAX's collectives and lax.ppermute only.
A program may use at most 256 MiB of HBM per device.

v0:
```python
import math

import jax
import jax.numpy as jnp
from jax import lax
from jax.sharding import PartitionSpec as P

HEADS = 12


epsilon = 1e-07
masked_value = -1e30


def gelu_exact(value):
    return jax.nn.gelu(value, approximate=False)


def norm_forward(value, gain, shift):
    center = value - jnp.mean(value, axis=-1, keepdims=True)
    scaled = lax.rsqrt(jnp.mean(center * center, axis=-1, keepdims=True) + epsilon)
    normed = center * scaled
    return (normed * gain + shift, normed, scaled)


def norm_backward(grad_out, normed, scaled, gain):
    grad_normed = grad_out * gain
    inner = grad_normed - jnp.mean(grad_normed, axis=-1, keepdims=True)
    inner = inner - normed * jnp.mean(grad_normed * normed, axis=-1, keepdims=True)
    return (scaled * inner, jnp.sum(grad_out * normed, axis=0), jnp.sum(grad_out, axis=0))


def split_dot(form, wide, narrow):
    upper = wide.astype(jnp.bfloat16)
    rest = (wide - upper.astype(jnp.float32)).astype(jnp.bfloat16)
    first_part = jnp.einsum(form, upper, narrow, preferred_element_type=jnp.float32)
    return first_part + jnp.einsum(form, rest, narrow, preferred_element_type=jnp.float32)


def pick_band(table, shift, cols):
    heads, lines, places = table.shape
    span = places // 2
    diag = lines + cols - 1
    raw = shift + jnp.arange(diag, dtype=jnp.int32) - (cols - 1)
    column_ids = jnp.clip(raw, -span, span - 1) + span
    wide = jnp.take(table, column_ids, axis=2)
    flat = wide.reshape(heads, lines * diag)
    flat = jnp.pad(flat, ((0, 0), (0, lines)))
    skewed = flat.reshape(heads, lines, diag + 1)[:, :, :cols]
    return jnp.flip(skewed, axis=2)


def spread_band(grad, shift, places):
    heads, lines, cols = grad.shape
    span = places // 2
    diag = lines + cols - 1
    flipped = jnp.flip(grad, axis=2)
    padded = jnp.pad(flipped, ((0, 0), (0, 0), (0, lines)))
    flat = padded.reshape(heads, lines * (diag + 1))[:, : lines * diag]
    wide = flat.reshape(heads, lines, diag)
    raw = shift + jnp.arange(diag, dtype=jnp.int32) - (cols - 1)
    low_sum = jnp.sum(jnp.where((raw <= -span)[None, None], wide, 0.0), axis=2)
    high_sum = jnp.sum(jnp.where((raw >= span - 1)[None, None], wide, 0.0), axis=2)
    band_ids = jnp.arange(places, dtype=jnp.int32)
    source = band_ids - span - shift + (cols - 1)
    inside = (source >= 0) & (source < diag) & (band_ids > 0) & (band_ids < places - 1)
    source = jnp.where(inside, source, diag)
    extended = jnp.pad(wide, ((0, 0), (0, 0), (0, 1)))
    middle = jnp.take(extended, source, axis=2)
    middle = jnp.where((band_ids == 0)[None, None], low_sum[:, :, None], middle)
    return jnp.where((band_ids == places - 1)[None, None], high_sum[:, :, None], middle)


def pair_scores(queries, keys, c2p_table, query_rel, first_q, first_k, scale):
    direct = jnp.einsum("ihe,jhe->hij", queries, keys, preferred_element_type=jnp.float32)
    p2c_table = jnp.einsum("jhe,phe->hjp", keys, query_rel, preferred_element_type=jnp.float32)
    reverse = jnp.transpose(pick_band(p2c_table, first_k - first_q, queries.shape[0]), (0, 2, 1))
    return (direct + pick_band(c2p_table, first_q - first_k, keys.shape[0]) + reverse) * scale


def pair_grads(
    queries,
    keys,
    values,
    c2p_table,
    query_rel,
    first_q,
    first_k,
    seg_q,
    seg_k,
    log_total,
    row_dot,
    grad_ctx,
    scale,
):
    logits = pair_scores(queries, keys, c2p_table, query_rel, first_q, first_k, scale)
    allowed = (seg_q[:, None] == seg_k[None, :])[None]
    probs = jnp.where(allowed, jnp.exp(logits - log_total[:, :, None]), 0.0)
    grad_probs = jnp.einsum("ihe,jhe->hij", grad_ctx, values, preferred_element_type=jnp.float32)
    grad_logits = (probs * (grad_probs - row_dot[:, :, None])).astype(jnp.bfloat16)
    return (probs.astype(jnp.bfloat16), grad_logits)


def split_blocks(count):
    block = math.gcd(count, 512)
    return (block, count // block)


def on_device(
    hidden,
    segments,
    rel_embed,
    query_weight,
    key_weight,
    value_weight,
    output_weight,
    up_weight,
    down_weight,
    norm1_gain,
    norm1_bias,
    norm2_gain,
    norm2_bias,
    cotangent,
):
    tokens = hidden.shape[1]
    width = hidden.shape[2]
    heads = HEADS
    head_dim = width // heads
    span = rel_embed.shape[0] // 2
    scale = 1.0 / math.sqrt(3.0 * head_dim)
    inputs = hidden[0]
    first = lax.axis_index("seq") * tokens
    row_segs = lax.all_gather(segments, "seq", axis=1, tiled=True)[0]
    seg_q = lax.dynamic_slice_in_dim(row_segs, first, tokens)

    def project(left, right):
        return jnp.dot(left, right, preferred_element_type=jnp.float32).astype(jnp.bfloat16)

    query_flat = project(inputs, query_weight)
    key_flat = project(inputs, key_weight)
    value_flat = project(inputs, value_weight)
    queries = query_flat.reshape(tokens, heads, head_dim)
    query_rel = project(rel_embed, query_weight).reshape(2 * span, heads, head_dim)
    key_rel = project(rel_embed, key_weight).reshape(2 * span, heads, head_dim)
    c2p_local = jnp.einsum("ihe,phe->hip", queries, key_rel, preferred_element_type=jnp.float32)
    start_state = (
        jnp.full((heads, tokens), masked_value, jnp.float32),
        jnp.zeros((heads, tokens), jnp.float32),
        jnp.zeros((tokens, heads, head_dim), jnp.float32),
    )
    carry = start_state
    keys_in = lax.all_gather(key_flat, "seq", axis=0, tiled=True)
    values_in = lax.all_gather(value_flat, "seq", axis=0, tiled=True)
    block, step_count = split_blocks(keys_in.shape[0])

    def forward_inner_step(state, item):
        best, total, accum = state
        key_blk, value_blk, offset = item
        key_heads = key_blk.reshape(block, heads, head_dim)
        value_heads = value_blk.reshape(block, heads, head_dim)
        seg_k = lax.dynamic_slice_in_dim(row_segs, offset, block)
        logits = pair_scores(queries, key_heads, c2p_local, query_rel, first, offset, scale)
        allowed = (seg_q[:, None] == seg_k[None, :])[None]
        logits = jnp.where(allowed, logits, masked_value)
        new_best = jnp.maximum(best, jnp.max(logits, axis=2))
        factor = jnp.exp(best - new_best)
        weights = jnp.where(allowed, jnp.exp(logits - new_best[:, :, None]), 0.0)
        total = total * factor + jnp.sum(weights, axis=2)
        update = jnp.einsum(
            "hij,jhe->ihe",
            weights.astype(jnp.bfloat16),
            value_heads,
            preferred_element_type=jnp.float32,
        )
        accum = accum * jnp.transpose(factor)[:, :, None] + update
        return ((new_best, total, accum), None)

    offsets = block * jnp.arange(step_count, dtype=jnp.int32)
    carry, _ = lax.scan(
        forward_inner_step,
        carry,
        (
            keys_in.reshape(step_count, block, width),
            values_in.reshape(step_count, block, width),
            offsets,
        ),
    )
    best, total, accum = carry
    context_heads = accum / jnp.transpose(total)[:, :, None]
    log_total = best + jnp.log(total)
    context_bf = context_heads.reshape(tokens, width).astype(jnp.bfloat16)
    attn_out = jnp.dot(context_bf, output_weight, preferred_element_type=jnp.float32)
    normed_one, unit_one, scaled_one = norm_forward(
        inputs.astype(jnp.float32) + attn_out, norm1_gain, norm1_bias
    )
    normed_one_bf = normed_one.astype(jnp.bfloat16)
    inner = jnp.dot(normed_one_bf, up_weight, preferred_element_type=jnp.float32)
    active, gelu_back = jax.vjp(gelu_exact, inner)
    active_bf = active.astype(jnp.bfloat16)
    branch = jnp.dot(active_bf, down_weight, preferred_element_type=jnp.float32)
    result, unit_two, scaled_two = norm_forward(normed_one + branch, norm2_gain, norm2_bias)
    output = result.astype(jnp.bfloat16)[None]
    grad_result = cotangent[0].astype(jnp.float32)
    grad_sum_two, grad_gain_two, grad_bias_two = norm_backward(
        grad_result, unit_two, scaled_two, norm2_gain
    )
    grad_branch = grad_sum_two.astype(jnp.bfloat16)
    grad_down = jnp.einsum("tf,td->fd", active_bf, grad_branch, preferred_element_type=jnp.float32)
    grad_active = jnp.einsum(
        "td,fd->tf", grad_branch, down_weight, preferred_element_type=jnp.float32
    )
    grad_inner = gelu_back(grad_active)[0].astype(jnp.bfloat16)
    grad_up = jnp.einsum("td,tf->df", normed_one_bf, grad_inner, preferred_element_type=jnp.float32)
    grad_normed_one = grad_sum_two + jnp.einsum(
        "tf,df->td", grad_inner, up_weight, preferred_element_type=jnp.float32
    )
    grad_sum_one, grad_gain_one, grad_bias_one = norm_backward(
        grad_normed_one, unit_one, scaled_one, norm1_gain
    )
    grad_attn = grad_sum_one.astype(jnp.bfloat16)
    grad_output = jnp.einsum("tc,td->cd", context_bf, grad_attn, preferred_element_type=jnp.float32)
    grad_ctx = jnp.einsum(
        "td,cd->tc", grad_attn, output_weight, preferred_element_type=jnp.float32
    ).astype(jnp.bfloat16)
    grad_ctx_heads = grad_ctx.reshape(tokens, heads, head_dim)
    row_dot = jnp.transpose(jnp.sum(grad_ctx_heads.astype(jnp.float32) * context_heads, axis=2))
    full_rows = lax.axis_size("seq") * tokens
    key_state = (
        jnp.zeros((tokens, heads, head_dim), jnp.float32),
        jnp.zeros((heads, tokens, 2 * span), jnp.float32),
        jnp.zeros((2 * span, heads, head_dim), jnp.float32),
        jnp.zeros((full_rows, width), jnp.float32),
        jnp.zeros((full_rows, width), jnp.float32),
    )
    carry = key_state
    keys_in = lax.all_gather(key_flat, "seq", axis=0, tiled=True)
    values_in = lax.all_gather(value_flat, "seq", axis=0, tiled=True)
    key_block, step_count = split_blocks(keys_in.shape[0])

    def key_inner_step(state, item):
        grad_q, grad_c2p, grad_qrel, grad_keys, grad_values = state
        key_blk, value_blk, offset = item
        key_heads = key_blk.reshape(key_block, heads, head_dim)
        value_heads = value_blk.reshape(key_block, heads, head_dim)
        seg_k = lax.dynamic_slice_in_dim(row_segs, offset, key_block)
        probs_bf, grad_logits = pair_grads(
            queries,
            key_heads,
            value_heads,
            c2p_local,
            query_rel,
            first,
            offset,
            seg_q,
            seg_k,
            log_total,
            row_dot,
            grad_ctx_heads,
            scale,
        )
        scaled_grad = grad_logits.astype(jnp.float32) * scale
        grad_q = grad_q + scale * jnp.einsum(
            "hij,jhe->ihe", grad_logits, key_heads, preferred_element_type=jnp.float32
        )
        grad_c2p = grad_c2p + spread_band(scaled_grad, first - offset, 2 * span)
        band_grad = spread_band(jnp.transpose(scaled_grad, (0, 2, 1)), offset - first, 2 * span)
        key_part = scale * jnp.einsum(
            "hij,ihe->jhe", grad_logits, queries, preferred_element_type=jnp.float32
        )
        key_part = key_part + split_dot("hjp,phe->jhe", band_grad, query_rel)
        value_part = jnp.einsum(
            "hij,ihe->jhe", probs_bf, grad_ctx_heads, preferred_element_type=jnp.float32
        )
        grad_qrel = grad_qrel + split_dot("hjp,jhe->phe", band_grad, key_heads)
        grad_keys = lax.dynamic_update_slice_in_dim(
            grad_keys, key_part.reshape(key_block, width), offset, 0
        )
        grad_values = lax.dynamic_update_slice_in_dim(
            grad_values, value_part.reshape(key_block, width), offset, 0
        )
        return ((grad_q, grad_c2p, grad_qrel, grad_keys, grad_values), None)

    offsets = key_block * jnp.arange(step_count, dtype=jnp.int32)
    carry, _ = lax.scan(
        key_inner_step,
        carry,
        (
            keys_in.reshape(step_count, key_block, width),
            values_in.reshape(step_count, key_block, width),
            offsets,
        ),
    )
    grad_q, grad_c2p, grad_qrel, grad_keys, grad_values = carry
    grad_q = grad_q + split_dot("hip,phe->ihe", grad_c2p, key_rel)
    grad_krel = split_dot("hip,ihe->phe", grad_c2p, queries)
    key_sum, value_sum = (
        lax.psum_scatter(
            grad_keys.astype(jnp.bfloat16), "seq", scatter_dimension=0, tiled=True
        ).astype(jnp.float32),
        lax.psum_scatter(
            grad_values.astype(jnp.bfloat16), "seq", scatter_dimension=0, tiled=True
        ).astype(jnp.float32),
    )
    grad_q_bf = grad_q.reshape(tokens, width).astype(jnp.bfloat16)
    grad_k_bf = key_sum.astype(jnp.bfloat16)
    grad_v_bf = value_sum.astype(jnp.bfloat16)
    rel_q_sum, rel_k_sum = lax.psum(
        (grad_qrel.reshape(2 * span, width), grad_krel.reshape(2 * span, width)), ("seq", "row")
    )
    rel_q_bf = rel_q_sum.astype(jnp.bfloat16)
    rel_k_bf = rel_k_sum.astype(jnp.bfloat16)
    grad_rel = jnp.einsum("pd,cd->pc", rel_q_bf, query_weight, preferred_element_type=jnp.float32)
    grad_rel = grad_rel + jnp.einsum(
        "pd,cd->pc", rel_k_bf, key_weight, preferred_element_type=jnp.float32
    )
    grad_query = jnp.einsum("tc,td->cd", inputs, grad_q_bf, preferred_element_type=jnp.float32)
    grad_key = jnp.einsum("tc,td->cd", inputs, grad_k_bf, preferred_element_type=jnp.float32)
    grad_value = jnp.einsum("tc,td->cd", inputs, grad_v_bf, preferred_element_type=jnp.float32)
    shares = (
        lax.psum_scatter(
            grad_query.astype(jnp.bfloat16), "row", scatter_dimension=0, tiled=True
        ).astype(jnp.float32),
        lax.psum_scatter(
            grad_key.astype(jnp.bfloat16), "row", scatter_dimension=0, tiled=True
        ).astype(jnp.float32),
        lax.psum_scatter(
            grad_value.astype(jnp.bfloat16), "row", scatter_dimension=0, tiled=True
        ).astype(jnp.float32),
        lax.psum_scatter(
            grad_output.astype(jnp.bfloat16), "row", scatter_dimension=0, tiled=True
        ).astype(jnp.float32),
        lax.psum_scatter(
            grad_up.astype(jnp.bfloat16), "row", scatter_dimension=0, tiled=True
        ).astype(jnp.float32),
        lax.psum_scatter(
            grad_down.astype(jnp.bfloat16), "row", scatter_dimension=0, tiled=True
        ).astype(jnp.float32),
        lax.psum_scatter(
            grad_gain_one.astype(jnp.bfloat16), "row", scatter_dimension=0, tiled=True
        ).astype(jnp.float32),
        lax.psum_scatter(
            grad_bias_one.astype(jnp.bfloat16), "row", scatter_dimension=0, tiled=True
        ).astype(jnp.float32),
        lax.psum_scatter(
            grad_gain_two.astype(jnp.bfloat16), "row", scatter_dimension=0, tiled=True
        ).astype(jnp.float32),
        lax.psum_scatter(
            grad_bias_two.astype(jnp.bfloat16), "row", scatter_dimension=0, tiled=True
        ).astype(jnp.float32),
    )
    shares = (
        lax.psum(shares[0].astype(jnp.bfloat16), "seq").astype(jnp.float32),
        lax.psum(shares[1].astype(jnp.bfloat16), "seq").astype(jnp.float32),
        lax.psum(shares[2].astype(jnp.bfloat16), "seq").astype(jnp.float32),
        lax.psum(shares[3].astype(jnp.bfloat16), "seq").astype(jnp.float32),
        lax.psum(shares[4].astype(jnp.bfloat16), "seq").astype(jnp.float32),
        lax.psum(shares[5].astype(jnp.bfloat16), "seq").astype(jnp.float32),
        lax.psum(shares[6].astype(jnp.bfloat16), "seq").astype(jnp.float32),
        lax.psum(shares[7].astype(jnp.bfloat16), "seq").astype(jnp.float32),
        lax.psum(shares[8].astype(jnp.bfloat16), "seq").astype(jnp.float32),
        lax.psum(shares[9].astype(jnp.bfloat16), "seq").astype(jnp.float32),
    )
    share_rows = width // lax.axis_size("row")
    row_first = lax.axis_index("row") * share_rows
    rel_cols = lax.dynamic_slice_in_dim(rel_embed, row_first, share_rows, 1)
    query_share = shares[0] + jnp.einsum(
        "pc,pd->cd", rel_cols, rel_q_bf, preferred_element_type=jnp.float32
    )
    key_share = shares[1] + jnp.einsum(
        "pc,pd->cd", rel_cols, rel_k_bf, preferred_element_type=jnp.float32
    )
    grad_input = grad_sum_one + jnp.einsum(
        "td,cd->tc", grad_q_bf, query_weight, preferred_element_type=jnp.float32
    )
    grad_input = grad_input + jnp.einsum(
        "td,cd->tc", grad_k_bf, key_weight, preferred_element_type=jnp.float32
    )
    grad_input = grad_input + jnp.einsum(
        "td,cd->tc", grad_v_bf, value_weight, preferred_element_type=jnp.float32
    )
    return (
        output,
        grad_input.astype(jnp.bfloat16)[None],
        query_share,
        key_share,
        shares[2],
        shares[3],
        shares[4],
        shares[5],
        shares[6],
        shares[7],
        shares[8],
        shares[9],
        grad_rel,
    )


def solution(mesh):
    placed = (
        P("row", "seq", None),
        P("row", "seq"),
        P(),
        P(),
        P(),
        P(),
        P(),
        P(),
        P(),
        P(),
        P(),
        P(),
        P(),
        P("row", "seq", None),
    )
    return jax.shard_map(
        on_device,
        mesh=mesh,
        in_specs=placed,
        out_specs=(
            P("row", "seq", None),
            P("row", "seq", None),
            P("row", None),
            P("row", None),
            P("row", None),
            P("row", None),
            P("row", None),
            P("row", None),
            P("row"),
            P("row"),
            P("row"),
            P("row"),
            P(),
        ),
        check_vma=False,
    )
```

profile of v0, /device:TPU:0, one launch (start us, length us, event | category | flops | bytes accessed | tf_op | source)
XLA Modules:
  0.0 2165.2 jit_solution(3405345029249767750)
XLA Ops:
  26.6 10.9 all_gather.11
  41.9 25.2 %all-gather.3.cloned.1.call-done = bf16[1024,768]{1,0:T(8,128)(2,1)} async-done(((bf16[128,768]{1,0:T(8,128)(2,1)}), bf16[1024,768]{1,0:T(8,128)(2,1)}) %all-gather.3.cloned.1.call-update) | async-done | bytes 1572880 | tf_op jit(solution)/shard_map/all_gather | solution.py:152
  69.7 483.2 %while.38 = (s32[]{:T(128)}, f32[12,128]{1,0:T(8,128)S(1)}, f32[12,128]{1,0:T(8,128)S(1)}, f32[128,12,64]{0,2,1:T(8,128)}, s32[128]{0:T(128)}, /*index=5*/s32[2]...) while((s32[]{:T(128)}, f32[12,128]{1,0:T(8,128)S(1)}, ...), condition=%wide.region_3.6_spmd.clone, body=%wide.region_0.5_spmd.clone.sunk | while | flops 617931520 | bytes 344770848 | solution.py:179
  130.1 24.4 %rev.49 = f32[12,128,512]{1,2,0:T(8,128)} reverse(f32[12,128,512]{1,2,0:T(8,128)} %copy.243), dimensions={2} | reverse | bytes 6291456 | tf_op jit(solution)/shard_map/while/body/eval_jaxpr/jit(_flip)/rev | solution.py:50
  160.9 18.3 copy.238
  179.2 23.8 %gather_fusion = f32[639,12,512]{2,1,0:T(8,128)} fusion(f32[12,512,512]{1,0,2:T(8,128)} %copy.238, s32[1024]{0:T(1024)} %pad_clamp_fusion.12), kind=kCustom, calls=%fused_computation.1.clone.clone.1 | custom fusion | bytes 31410684 | tf_op jit(solution)/shard_map/while/body/eval_jaxpr/jit(_take)/gather | solution.py:46
  203.1 16.1 select_bitcast_fusion.8
  219.2 21.7 %copy.239 = f32[12,512,639]{2,1,0:T(8,128)} copy(f32[12,512,639]{1,0,2:T(8,128)} %select_bitcast_fusion.8) | data formatting | bytes 31408128 | tf_op jit(solution)/shard_map/while/body/eval_jaxpr/jit(_take)/select_n | solution.py:46
  240.9 25.2 %reshape.540 = f32[12,327168]{1,0:T(8,128)} reshape(f32[12,512,639]{2,1,0:T(8,128)} %copy.239) | data formatting | bytes 31408128 | tf_op jit(solution)/shard_map/while/body/eval_jaxpr/reshape | solution.py:47
  274.0 8.8 copy.240
  286.5 25.7 %rev.48 = f32[12,512,128]{2,1,0:T(8,128)} reverse(f32[12,512,128]{2,1,0:T(8,128)} %slice.82), dimensions={2} | reverse | bytes 6291456 | tf_op jit(solution)/shard_map/while/body/eval_jaxpr/jit(_flip)/rev | solution.py:50
  362.4 24.4 %rev.49 = f32[12,128,512]{1,2,0:T(8,128)} reverse(f32[12,128,512]{1,2,0:T(8,128)} %copy.243), dimensions={2} | reverse | bytes 6291456 | tf_op jit(solution)/shard_map/while/body/eval_jaxpr/jit(_flip)/rev | solution.py:50
  393.2 18.3 copy.238
  411.5 26.2 %gather_fusion = f32[639,12,512]{2,1,0:T(8,128)} fusion(f32[12,512,512]{1,0,2:T(8,128)} %copy.238, s32[1024]{0:T(1024)} %pad_clamp_fusion.12), kind=kCustom, calls=%fused_computation.1.clone.clone.1 | custom fusion | bytes 31410684 | tf_op jit(solution)/shard_map/while/body/eval_jaxpr/jit(_take)/gather | solution.py:46
  437.7 16.1 select_bitcast_fusion.8
  453.9 21.7 %copy.239 = f32[12,512,639]{2,1,0:T(8,128)} copy(f32[12,512,639]{1,0,2:T(8,128)} %select_bitcast_fusion.8) | data formatting | bytes 31408128 | tf_op jit(solution)/shard_map/while/body/eval_jaxpr/jit(_take)/select_n | solution.py:46
  475.6 25.2 %reshape.540 = f32[12,327168]{1,0:T(8,128)} reshape(f32[12,512,639]{2,1,0:T(8,128)} %copy.239) | data formatting | bytes 31408128 | tf_op jit(solution)/shard_map/while/body/eval_jaxpr/reshape | solution.py:47
  508.7 8.8 copy.240
  521.1 25.7 %rev.48 = f32[12,512,128]{2,1,0:T(8,128)} reverse(f32[12,512,128]{2,1,0:T(8,128)} %slice.82), dimensions={2} | reverse | bytes 6291456 | tf_op jit(solution)/shard_map/while/body/eval_jaxpr/jit(_flip)/rev | solution.py:50
  576.2 1060.3 %while.39 = (s32[]{:T(128)}, f32[128,12,64]{0,2,1:T(8,128)S(1)}, f32[12,128,512]{1,0,2:T(8,128)}, f32[512,12,64]{0,2,1:T(8,128)}, bf16[1024,768]{1,0:T(8,128)(2,...) while((s32[]{:T(128)}, f32[128,12,64]{0,2,1:T(8,128)S(1)}, ...), condition=%wide.region_18.21_spmd.clone, body=%wide.region_13.20_spmd.clone.sunk | while | flops 2620565248 | bytes 898613184 | solution.py:284
  621.2 24.4 %rev.52 = f32[12,128,512]{1,2,0:T(8,128)} reverse(f32[12,128,512]{1,2,0:T(8,128)} %copy.249), dimensions={2} | reverse | bytes 6291456 | tf_op jit(solution)/shard_map/while/body/eval_jaxpr/jit(_flip)/rev | solution.py:50
  652.0 18.3 copy.244
  670.3 23.9 %gather_fusion.2 = f32[639,12,512]{2,1,0:T(8,128)} fusion(f32[12,512,512]{1,0,2:T(8,128)} %copy.244, s32[1024]{0:T(1024)S(1)} %pad_clamp_fusion.14), kind=kCustom, calls=%fused_computation.3.clone.clone.1 | custom fusion | bytes 31410684 | tf_op jit(solution)/shard_map/while/body/eval_jaxpr/jit(_take)/gather | solution.py:46
  694.2 16.2 select_bitcast_fusion.10
  710.4 21.7 %copy.245 = f32[12,512,639]{2,1,0:T(8,128)} copy(f32[12,512,639]{1,0,2:T(8,128)} %select_bitcast_fusion.10) | data formatting | bytes 31408128 | tf_op jit(solution)/shard_map/while/body/eval_jaxpr/jit(_take)/select_n | solution.py:46
  732.2 25.2 %reshape.550 = f32[12,327168]{1,0:T(8,128)} reshape(f32[12,512,639]{2,1,0:T(8,128)} %copy.245) | data formatting | bytes 31408128 | tf_op jit(solution)/shard_map/while/body/eval_jaxpr/reshape | solution.py:47
  765.6 8.8 copy.246
  778.1 25.7 %rev.51 = f32[12,512,128]{2,1,0:T(8,128)} reverse(f32[12,512,128]{2,1,0:T(8,128)} %slice.88), dimensions={2} | reverse | bytes 6291456 | tf_op jit(solution)/shard_map/while/body/eval_jaxpr/jit(_flip)/rev | solution.py:50
  823.0 25.7 %rev.53 = f32[12,512,128]{2,1,0:T(8,128)} reverse(f32[12,512,128]{2,1,0:T(8,128)} %multiply_bitcast_fusion.2), dimensions={2} | reverse | bytes 6291456 | tf_op jit(solution)/shard_map/while/body/eval_jaxpr/jit(_flip)/rev | solution.py:57
  848.6 15.2 reverse.8
  919.0 14.3 copy.253
  933.4 15.6 slice.91
  949.0 32.3 %reshape.553 = f32[12,512,639]{2,1,0:T(8,128)} reshape(f32[12,327168]{1,0:T(8,128)} %slice.91) | data formatting | bytes 31408128 | tf_op jit(solution)/shard_map/while/body/eval_jaxpr/reshape | solution.py:60
  989.1 20.0 copy.254
  1009.2 17.2 pad.105
  1026.4 19.5 gather_fusion.5
  1045.9 17.7 copy.255
  1145.4 24.4 %rev.52 = f32[12,128,512]{1,2,0:T(8,128)} reverse(f32[12,128,512]{1,2,0:T(8,128)} %copy.249), dimensions={2} | reverse | bytes 6291456 | tf_op jit(solution)/shard_map/while/body/eval_jaxpr/jit(_flip)/rev | solution.py:50
  1176.1 18.3 copy.244
  1194.5 26.5 %gather_fusion.2 = f32[639,12,512]{2,1,0:T(8,128)} fusion(f32[12,512,512]{1,0,2:T(8,128)} %copy.244, s32[1024]{0:T(1024)S(1)} %pad_clamp_fusion.14), kind=kCustom, calls=%fused_computation.3.clone.clone.1 | custom fusion | bytes 31410684 | tf_op jit(solution)/shard_map/while/body/eval_jaxpr/jit(_take)/gather | solution.py:46
  1221.0 16.2 select_bitcast_fusion.10
  1237.2 21.7 %copy.245 = f32[12,512,639]{2,1,0:T(8,128)} copy(f32[12,512,639]{1,0,2:T(8,128)} %select_bitcast_fusion.10) | data formatting | bytes 31408128 | tf_op jit(solution)/shard_map/while/body/eval_jaxpr/jit(_take)/select_n | solution.py:46
  1258.9 25.2 %reshape.550 = f32[12,327168]{1,0:T(8,128)} reshape(f32[12,512,639]{2,1,0:T(8,128)} %copy.245) | data formatting | bytes 31408128 | tf_op jit(solution)/shard_map/while/body/eval_jaxpr/reshape | solution.py:47
  1304.6 25.7 %rev.51 = f32[12,512,128]{2,1,0:T(8,128)} reverse(f32[12,512,128]{2,1,0:T(8,128)} %slice.88), dimensions={2} | reverse | bytes 6291456 | tf_op jit(solution)/shard_map/while/body/eval_jaxpr/jit(_flip)/rev | solution.py:50
  1349.4 25.7 %rev.53 = f32[12,512,128]{2,1,0:T(8,128)} reverse(f32[12,512,128]{2,1,0:T(8,128)} %multiply_bitcast_fusion.2), dimensions={2} | reverse | bytes 6291456 | tf_op jit(solution)/shard_map/while/body/eval_jaxpr/jit(_flip)/rev | solution.py:57
  1375.1 15.2 reverse.8
  1446.6 14.3 copy.253
  1460.9 15.6 slice.91
  1476.5 32.3 %reshape.553 = f32[12,512,639]{2,1,0:T(8,128)} reshape(f32[12,327168]{1,0:T(8,128)} %slice.91) | data formatting | bytes 31408128 | tf_op jit(solution)/shard_map/while/body/eval_jaxpr/reshape | solution.py:60
  1516.7 20.0 copy.254
  1536.8 17.2 pad.105
  1554.0 21.2 gather_fusion.5
  1575.1 17.7 copy.255
  1637.2 52.6 %reduce-scatter.27.cloned.1.call-done = bf16[128,768]{1,0:T(8,128)(2,1)} async-done(((bf16[1024,768]{1,0:T(8,128)(2,1)}), bf16[128,768]{1,0:T(8,128)(2,1)}) %reduce-scatter.27.cloned.1.call-update) | async-done | bytes 196624
  1715.3 16.2 reduce-scatter.25.cloned.1.call-done
  1753.3 9.5 reduce-scatter.33.cloned.1.call-done
  1764.7 28.2 %reduce-scatter.19.cloned.1.call-done = bf16[192,768]{1,0:T(8,128)(2,1)} async-done(((bf16[768,768]{1,0:T(8,128)(2,1)}), bf16[192,768]{1,0:T(8,128)(2,1)}) %reduce-scatter.19.cloned.1.call-update) | async-done | bytes 294928 | tf_op jit(solution)/shard_map/reduce_scatter | solution.py:329
  1792.9 30.8 %reduce-scatter.29.cloned.1.call-done = bf16[192,768]{1,0:T(8,128)(2,1)} async-done(((bf16[768,768]{1,0:T(8,128)(2,1)}), bf16[192,768]{1,0:T(8,128)(2,1)}) %reduce-scatter.29.cloned.1.call-update) | async-done | bytes 294928 | tf_op jit(solution)/shard_map/reduce_scatter | solution.py:320
  1823.7 30.2 %reduce-scatter.31.cloned.1.call-done = bf16[192,768]{1,0:T(8,128)(2,1)} async-done(((bf16[768,768]{1,0:T(8,128)(2,1)}), bf16[192,768]{1,0:T(8,128)(2,1)}) %reduce-scatter.31.cloned.1.call-update) | async-done | bytes 294928 | tf_op jit(solution)/shard_map/reduce_scatter | solution.py:323
  1854.0 86.3 %reduce-scatter.23.cloned.1.call-done = bf16[768,768]{1,0:T(8,128)(2,1)} async-done(((bf16[3072,768]{1,0:T(8,128)(2,1)}), bf16[768,768]{1,0:T(8,128)(2,1)}) %reduce-scatter.23.cloned.1.call-update) | async-done | bytes 1179664 | tf_op jit(solution)/shard_map/reduce_scatter | solution.py:335
  1940.3 88.0 %reduce-scatter.21.cloned.1.call-done = bf16[192,3072]{1,0:T(8,128)(2,1)} async-done(((bf16[768,3072]{1,0:T(8,128)(2,1)}), bf16[192,3072]{1,0:T(8,128)(2,1)}) %reduce-scatter.21.cloned.1.call-update) | async-done | bytes 1179664 | tf_op jit(solution)/shard_map/reduce_scatter | solution.py:332
  2029.6 11.1 all-reduce.15
  2040.9 12.6 all-reduce.13
  2055.8 84.8 %all-reduce.20 = (bf16[512,768]{0,1:T(8,128)(2,1)}, bf16[512,768]{0,1:T(8,128)(2,1)S(1)}) all-reduce(f32[512,768]{0,1:T(8,128)} %bitcast.380, f32[512,768]{0,1:T(8,128)S(1)} %bitcast.371), channel_id=1, replica_groups=mesh['seq'=8,'row'=4] {'seq','row'}, use_global_device_ids=true, to_apply=%region_23.26 | all-reduce | flops 786432 | bytes 4718592 | tf_op jit(solution)/shard_map/psum | solution.py:307
  (474 shorter events, 616.4 us)
Async XLA Ops:
  7.2 5.2 copy-start
  7.2 5.2 copy-start.24
  7.2 32.1 %all-gather.5.cloned.1.call-start = ((), (), s32[]{:S(2)}) async-start(), calls=%async_computation.9 | async-start | bytes 1769472 | tf_op jit(solution)/shard_map/all_gather | solution.py:153
  9.7 57.4 %all-gather.3.cloned.1.call-start = ((), (), s32[]{:S(2)}) async-start(), calls=%async_computation.8 | async-start | bytes 1769472 | tf_op jit(solution)/shard_map/all_gather | solution.py:152
  12.3 1677.5 %reduce-scatter.27.cloned.1.call-start = ((), (), s32[]{:S(2)}) async-start(), calls=%async_computation.14 | async-start | bytes 1769472
  21.5 5.1 copy-start.73
  312.2 4.0 copy-start.8
  546.8 4.0 copy-start.8
  554.6 8.0 slice-start
  556.5 13.3 copy-start.11
  556.5 13.3 copy-start.58
  556.7 13.1 copy-start.60
  556.7 5.9 slice-start.1
  571.3 5.0 copy-start.13
  576.4 69.2 %copy-start.4 = (bf16[512,12,64]{0,2,1:T(8,128)(2,1)}, bf16[512,12,64]{0,2,1:T(8,128)(2,1)S(1)}, u32[]{:S(2)}) copy-start(bf16[512,12,64]{0,2,1:T(8,128)(2,1)S(1)} %get-tuple-element.1183) | copy-start | bytes 2359300 | tf_op jit(solution)/shard_map/while
  586.7 217.0 %copy-start.2 = (bf16[1,512,768]{1,2,0:T(8,128)(2,1)}, bf16[1,512,768]{1,2,0:T(8,128)(2,1)S(1)}, u32[]{:S(2)}) copy-start(bf16[1,512,768]{1,2,0:T(8,128)(2,1)S(1)} %get-tuple-element.1063) | copy-start | bytes 2359300 | tf_op jit(solution)/shard_map/while
  803.8 4.1 copy-start.6
  816.1 6.9 copy-start.14
  949.0 32.3 %copy-start.52 = (pred[639]{0:T(1024)(128)(4,1)S(1)}, pred[639]{0:T(1024)(128)(4,1)}, u32[]{:S(2)}) copy-start(pred[639]{0:T(1024)(128)(4,1)} %get-tuple-element.1071) | copy-start | bytes 1921 | tf_op jit(solution)/shard_map/while
  949.0 32.3 %copy-start.53 = (pred[639]{0:T(1024)(128)(4,1)S(1)}, pred[639]{0:T(1024)(128)(4,1)}, u32[]{:S(2)}) copy-start(pred[639]{0:T(1024)(128)(4,1)} %get-tuple-element.1072) | copy-start | bytes 1921 | tf_op jit(solution)/shard_map/while
  1009.2 17.2 copy-start.49
  1045.9 17.7 copy-start.75
  1063.6 8.5 copy-start.1
  1080.1 6.1 copy-start.3
  1086.1 6.4 copy-start.40
  1092.6 7.8 copy-start.5
  1092.6 7.8 copy-start.15
  1100.6 69.2 %copy-start.4 = (bf16[512,12,64]{0,2,1:T(8,128)(2,1)}, bf16[512,12,64]{0,2,1:T(8,128)(2,1)S(1)}, u32[]{:S(2)}) copy-start(bf16[512,12,64]{0,2,1:T(8,128)(2,1)S(1)} %get-tuple-element.1183) | copy-start | bytes 2359300 | tf_op jit(solution)/shard_map/while
  1110.9 219.4 %copy-start.2 = (bf16[1,512,768]{1,2,0:T(8,128)(2,1)}, bf16[1,512,768]{1,2,0:T(8,128)(2,1)S(1)}, u32[]{:S(2)}) copy-start(bf16[1,512,768]{1,2,0:T(8,128)(2,1)S(1)} %get-tuple-element.1063) | copy-start | bytes 2359300 | tf_op jit(solution)/shard_map/while
  1330.3 4.1 copy-start.6
  1342.6 6.9 copy-start.14
  1476.5 32.3 %copy-start.52 = (pred[639]{0:T(1024)(128)(4,1)S(1)}, pred[639]{0:T(1024)(128)(4,1)}, u32[]{:S(2)}) copy-start(pred[639]{0:T(1024)(128)(4,1)} %get-tuple-element.1071) | copy-start | bytes 1921 | tf_op jit(solution)/shard_map/while
  1476.5 32.4 %copy-start.53 = (pred[639]{0:T(1024)(128)(4,1)S(1)}, pred[639]{0:T(1024)(128)(4,1)}, u32[]{:S(2)}) copy-start(pred[639]{0:T(1024)(128)(4,1)} %get-tuple-element.1072) | copy-start | bytes 1921 | tf_op jit(solution)/shard_map/while
  1536.8 17.2 copy-start.49
  1575.1 17.7 copy-start.75
  1592.9 8.5 copy-start.1
  1609.3 6.0 copy-start.3
  1615.3 6.4 copy-start.40
  1621.8 7.8 copy-start.5
  1621.8 7.8 copy-start.15
  1636.5 54.7 %copy-start.16 = (f32[128,12,64]{0,2,1:T(8,128)}, f32[128,12,64]{0,2,1:T(8,128)S(1)}, u32[]{:S(2)}) copy-start(f32[128,12,64]{0,2,1:T(8,128)S(1)} %get-tuple-element.411) | copy-start | bytes 1179652
  1636.6 53.3 %copy-start.25 = (bf16[1,128,768]{2,1,0:T(8,128)(2,1)S(1)}, bf16[1,128,768]{2,1,0:T(8,128)(2,1)}, u32[]{:S(2)}) copy-start(bf16[1,128,768]{2,1,0:T(8,128)(2,1)} %param.22) | copy-start | bytes 589828
  1636.6 94.9 %reduce-scatter.25.cloned.1.call-start = ((), (), s32[]{:S(2)}) async-start(), calls=%async_computation.13 | async-start | bytes 1769472
  1637.2 55.6 %copy-start.28 = (f32[128,768]{1,0:T(8,128)S(1)}, f32[128,768]{1,0:T(8,128)}, u32[]{:S(2)}) copy-start(f32[128,768]{1,0:T(8,128)} %copy-done.27) | copy-start | bytes 1179652
  1637.2 55.6 %copy-start.39 = (bf16[128,12,64]{0,2,1:T(8,128)(2,1)S(1)}, bf16[128,12,64]{0,2,1:T(8,128)(2,1)}, u32[]{:S(2)}) copy-start(bf16[128,12,64]{0,2,1:T(8,128)(2,1)} %copy-done.38) | copy-start | bytes 589828
  1637.2 125.6 %reduce-scatter.33.cloned.1.call-start = ((), (), s32[]{:S(2)}) async-start(), calls=%async_computation.17 | async-start | bytes 1474560
  1692.8 100.1 %reduce-scatter.19.cloned.1.call-start = ((), (), s32[]{:S(2)}) async-start(), calls=%async_computation.10 | async-start | bytes 1474560 | tf_op jit(solution)/shard_map/reduce_scatter | solution.py:329
  1694.3 129.4 %reduce-scatter.29.cloned.1.call-start = ((), (), s32[]{:S(2)}) async-start(), calls=%async_computation.15 | async-start | bytes 1474560 | tf_op jit(solution)/shard_map/reduce_scatter | solution.py:320
  1703.7 6.7 copy-start.17
  1715.2 21.2 copy-start.23
  1715.2 21.2 copy-start.35
  1715.2 21.2 copy-start.57
  1715.2 21.2 copy-start.66
  1715.2 21.2 copy-start.68
  1715.2 21.2 copy-start.70
  1715.2 138.7 %reduce-scatter.31.cloned.1.call-start = ((), (), s32[]{:S(2)}) async-start(), calls=%async_computation.16 | async-start | bytes 1474560 | tf_op jit(solution)/shard_map/reduce_scatter | solution.py:323
  1736.3 204.0 %reduce-scatter.23.cloned.1.call-start = ((), (), s32[]{:S(2)}) async-start(), calls=%async_computation.12 | async-start | bytes 5898240 | tf_op jit(solution)/shard_map/reduce_scatter | solution.py:335
  1741.3 286.9 %reduce-scatter.21.cloned.1.call-start = ((), (), s32[]{:S(2)}) async-start(), calls=%async_computation.11 | async-start | bytes 5898240 | tf_op jit(solution)/shard_map/reduce_scatter | solution.py:332
  1747.1 400.1 %all-reduce.19.cloned.1.call-start = ((), (), s32[]{:S(2)}) async-start(), calls=%async_computation.18 | async-start | bytes 7274496 | tf_op jit(solution)/shard_map/psum | solution.py:352
  1753.3 275.0 %copy-start.29 = (f32[128,768]{1,0:T(8,128)S(1)}, f32[128,768]{1,0:T(8,128)}, u32[]{:S(2)}) copy-start(f32[128,768]{1,0:T(8,128)} %copy-done.27) | copy-start | bytes 1179652
  1753.3 275.0 %copy-start.37 = (bf16[128,12,64]{0,2,1:T(8,128)(2,1)S(1)}, bf16[128,12,64]{0,2,1:T(8,128)(2,1)}, u32[]{:S(2)}) copy-start(bf16[128,12,64]{0,2,1:T(8,128)(2,1)} %copy-done.36) | copy-start | bytes 589828
  2028.2 27.5 %copy-start.26 = (f32[12,64,512]{2,1,0:T(8,128)S(1)}, f32[12,64,512]{2,1,0:T(8,128)}, u32[]{:S(2)}) copy-start(f32[12,64,512]{2,1,0:T(8,128)} %convolution_add_fusion.1) | copy-start | bytes 4718596
  2147.2 5.1 copy-start.48
  2149.7 5.5 copy-start.44
  (44 other events, 93.3 us)
Sparse Core Ops, SparseCore 0:
  10.5 28.3 all-gather.4
  41.4 25.6 all-gather.2
  1636.7 53.0 reduce-scatter.26
  1693.0 38.4 reduce-scatter.24
  1733.6 29.1 reduce-scatter.32
  1765.0 27.8 reduce-scatter.18
  1795.8 27.8 reduce-scatter.28
  1826.0 27.8 reduce-scatter.30
  1856.3 83.9 reduce-scatter.22
  1942.4 85.7 reduce-scatter.20
  2032.9 85.5 all-reduce.18
where the time goes:
time: 2200 us; the launch traced here: 2170 us
  local copies, waits for them, and re-layouts  1280 us (58%)
  waiting for transfers between devices  368 us (17%)
  other arithmetic  175 us (8%)
  matrix products  173 us (8%)
  blocking collectives  119 us (5%)
  loops' own time  37.3 us (2%)
    rev x8, local copies, waits for them, and re-layouts, pick_band(): return jnp.flip(skewed, axis=2)  200 us
    reshape x8, local copies, waits for them, and re-layouts, spread_band(): wide = flat.reshape(heads, lines, diag)  131 us
    reshape x8, local copies, waits for them, and re-layouts, pick_band(): flat = wide.reshape(heads, lines * diag)  125 us
    gather x8, local copies, waits for them, and re-layouts, pick_band(): wide = jnp.take(table, column_ids, axis=2)  124 us
    select_n x8, local copies, waits for them, and re-layouts, pick_band(): wide = jnp.take(table, column_ids, axis=2)  111 us
    while x92, local copies, waits for them, and re-layouts  105 us
    select_n x16, other arithmetic, pick_band(): wide = jnp.take(table, column_ids, axis=2)  92.1 us
    reduce_scatter x1, waiting for transfers between devices, on_device(): lax.psum_scatter(grad_up.astype(jnp.bfloat16), 'row', scatter_dimension=0...  88 us
  transfers between devices with their start and end apart: 11, of which 9 were waited for; matrix products, arithmetic and copies ran while one was open for 4% of the time, Pallas kernels for 0%

commit v1 on v0

v1 whole, which is shorter than its diff:
```python
import functools, math
import jax, jax.numpy as jnp
from jax import lax
from jax.experimental import pallas as pl
from jax.experimental.pallas import tpu as pltpu
from jax.sharding import PartitionSpec as P

BLK = 128
PAIR = 128
NT = (((1,), (1,)), ((), ()))
NN = (((1,), (0,)), ((), ()))
TN = (((0,), (0,)), ((), ()))
bf16 = jnp.bfloat16
f32 = jnp.float32


def dot(a, b, form):
    return lax.dot_general(a, b, form, preferred_element_type=f32)


def half_masks(x):
    lane = lax.broadcasted_iota(jnp.int32, x.shape, 1)
    low = lane < PAIR // 2
    zero = jnp.zeros_like(x)
    return jnp.where(low, x, zero), jnp.where(low, zero, x)


def join_heads(stacked, rows):
    lane = lax.broadcasted_iota(jnp.int32, (rows, PAIR), 1)
    return jnp.where(lane < PAIR // 2, stacked[:rows], stacked[rows:])


def fill_scores(own_ref, all_ref, near_ref, far_ref, s_ref, length):
    wide = length + BLK
    own = jnp.concatenate(half_masks(own_ref[...]), axis=0)
    ext = dot(own, near_ref[...], NT)
    for h in range(2):
        moved = pltpu.roll(ext[h * BLK:(h + 1) * BLK], wide - (BLK - 1), 1, stride=1, stride_axis=0)
        s_ref[h] = moved[:, :length]
    for c in range(length // BLK):
        cols = slice(c * BLK, (c + 1) * BLK)
        blk = all_ref[cols, :]
        both = jnp.concatenate(half_masks(blk), axis=0)
        start = length - BLK - BLK * c
        win = far_ref[start:start + 2 * BLK, :]
        back = dot(both, win, NT)
        direct = dot(own, blk, NT)
        for h in range(2):
            rows = slice(h * BLK, (h + 1) * BLK)
            moved = pltpu.roll(back[rows], BLK + 1, 1, stride=1, stride_axis=0)[:, :BLK]
            s_ref[h, :, cols] += direct[rows] + moved.T


def forward_kernel(scale, length, q_ref, k_ref, v_ref, near_ref, far_ref, segq_ref, segk_ref,
                   p_ref, ctx_ref, lse_ref, s_ref):
    fill_scores(q_ref, k_ref, near_ref, far_ref, s_ref, length)
    allowed = segq_ref[...] == segk_ref[...]
    stats = []
    for h in range(2):
        logits = jnp.where(allowed, s_ref[h] * scale, -1e30)
        best = jnp.max(logits, axis=1, keepdims=True)
        weights = jnp.exp(logits - best)
        total = jnp.sum(weights, axis=1, keepdims=True)
        p_ref[h] = (weights * (1.0 / total)).astype(bf16)
        stats.append(best + jnp.log(total))
    stacked = jnp.concatenate([p_ref[0], p_ref[1]], axis=0)
    ctx_ref[...] = join_heads(dot(stacked, v_ref[...], NN), BLK)
    lane = lax.broadcasted_iota(jnp.int32, (BLK, BLK), 1)
    tile = jnp.where(lane == 0, stats[0], stats[1])
    lse_ref[0] = tile.T[:8]


def other_probs_kernel(scale, length, k_ref, q_ref, near_ref, far_ref, segk_ref, segq_ref, lse_ref, p_ref, s_ref):
    fill_scores(k_ref, q_ref, near_ref, far_ref, s_ref, length)
    allowed = segk_ref[...] == segq_ref[...]
    for h in range(2):
        logits = s_ref[h] * scale - lse_ref[0, h:h + 1, :]
        p_ref[h] = jnp.where(allowed, jnp.exp(logits), 0.0).astype(bf16)


def flip_matrix():
    r = lax.broadcasted_iota(jnp.int32, (BLK, BLK), 0)
    c = lax.broadcasted_iota(jnp.int32, (BLK, BLK), 1)
    return jnp.where(r + c == BLK - 1, 1.0, 0.0).astype(bf16)


def grads_tail(scale, length, ds_refs, own_ref, all_ref, near_ref, wide_ref, down_ref):
    wide = length + BLK
    flip = flip_matrix()
    for h in range(2):
        back = dot(flip, ds_refs[h], NN)
        down_ref[h * BLK:(h + 1) * BLK, :] = back.astype(bf16)
        padded = jnp.concatenate([back, jnp.zeros((BLK, BLK), f32)], axis=1)
        wide_ref[h * BLK:(h + 1) * BLK, :] = pltpu.roll(padded, 0, 1, stride=1, stride_axis=0).astype(bf16)
    own_grad = dot(down_ref[...], all_ref[...], NN) + dot(wide_ref[...], near_ref[...], NN)
    own_grad = (join_heads(own_grad, BLK) * scale).astype(bf16)
    own_grad = dot(flip, own_grad, NN).astype(bf16)
    own = dot(flip, own_ref[...], NN).astype(bf16)
    own = jnp.concatenate(half_masks(own), axis=0)
    near_grad = dot(own, wide_ref[...], TN) * scale
    return own_grad, near_grad


def query_grad_kernel(scale, length, p_ref, dctx_ref, ctx_ref, v_ref, q_ref, k_ref, near_ref,
                      dq_ref, dnear_ref, ds_ref, wide_ref, down_ref):
    dctx = jnp.concatenate(half_masks(dctx_ref[...]), axis=0)
    dprob = dot(dctx, v_ref[...], NT)
    ctx = ctx_ref[...]
    for h in range(2):
        rows = slice(h * BLK, (h + 1) * BLK)
        row_dot = jnp.sum(dctx[rows].astype(f32) * ctx, axis=1, keepdims=True)
        ds_ref[h] = (p_ref[h].astype(f32) * (dprob[rows] - row_dot)).astype(bf16)
    dq, dnear = grads_tail(scale, length, ds_ref, q_ref, k_ref, near_ref, wide_ref, down_ref)
    dq_ref[...] = dq
    dnear_ref[...] = dnear.astype(dnear_ref.dtype)


def key_grad_kernel(scale, length, p_ref, v_ref, dctx_ref, rdot_ref, k_ref, q_ref, near_ref,
                    dk_ref, dv_ref, dnear_ref, ds_ref, wide_ref, down_ref):
    vals = jnp.concatenate(half_masks(v_ref[...]), axis=0)
    dctx = dctx_ref[...]
    dprob = dot(vals, dctx, NT)
    for h in range(2):
        rows = slice(h * BLK, (h + 1) * BLK)
        ds_ref[h] = (p_ref[h].astype(f32) * (dprob[rows] - rdot_ref[0, h:h + 1, :])).astype(bf16)
    stacked = jnp.concatenate([p_ref[0], p_ref[1]], axis=0)
    dv_ref[...] = join_heads(dot(stacked, dctx, NN), BLK).astype(bf16)
    dk, dnear = grads_tail(scale, length, ds_ref, k_ref, q_ref, near_ref, wide_ref, down_ref)
    dk_ref[...] = dk
    dnear_ref[...] = dnear.astype(dnear_ref.dtype)


def col(rows):
    return pl.BlockSpec((rows, PAIR), lambda p: (0, p))


def full(shape):
    return pl.BlockSpec(shape, lambda p: (0,) * len(shape))


def params():
    return pltpu.CompilerParams(vmem_limit_bytes=56 * 1024 * 1024)


def forward_attention(q, k, v, near, far, seg_q, seg_k, scale):
    length, width = k.shape
    pairs = width // PAIR
    wide = length + BLK
    return pl.pallas_call(
        functools.partial(forward_kernel, scale, length),
        grid=(pairs,),
        in_specs=[col(BLK), col(length), col(length), col(wide), col(wide), full((BLK, 1)), full((1, length))],
        out_specs=[
            pl.BlockSpec((2, BLK, length), lambda p: (p, 0, 0)),
            col(BLK),
            pl.BlockSpec((1, 8, BLK), lambda p: (p, 0, 0)),
        ],
        out_shape=[
            jax.ShapeDtypeStruct((2 * pairs, BLK, length), bf16),
            jax.ShapeDtypeStruct((BLK, width), f32),
            jax.ShapeDtypeStruct((pairs, 8, BLK), f32),
        ],
        scratch_shapes=[pltpu.VMEM((2, BLK, length), f32)],
        compiler_params=params(),
        name="attend",
    )(q, k, v, near, far, seg_q, seg_k)


def other_probs(k, q, near, far, seg_k, seg_q, lse, scale):
    length, width = q.shape
    pairs = width // PAIR
    wide = length + BLK
    return pl.pallas_call(
        functools.partial(other_probs_kernel, scale, length),
        grid=(pairs,),
        in_specs=[col(BLK), col(length), col(wide), col(wide), full((BLK, 1)), full((1, length)),
                  pl.BlockSpec((1, 8, length), lambda p: (p, 0, 0))],
        out_specs=pl.BlockSpec((2, BLK, length), lambda p: (p, 0, 0)),
        out_shape=jax.ShapeDtypeStruct((2 * pairs, BLK, length), bf16),
        scratch_shapes=[pltpu.VMEM((2, BLK, length), f32)],
        compiler_params=params(),
        name="key_probs",
    )(k, q, near, far, seg_k, seg_q, lse)


def grad_scratch(length):
    return [pltpu.VMEM((2, BLK, length), bf16), pltpu.VMEM((2 * BLK, length + BLK), bf16),
            pltpu.VMEM((2 * BLK, length), bf16)]


def query_grads(p, dctx, ctx, v, q, k, near, scale):
    length, width = k.shape
    pairs = width // PAIR
    wide = length + BLK
    return pl.pallas_call(
        functools.partial(query_grad_kernel, scale, length),
        grid=(pairs,),
        in_specs=[pl.BlockSpec((2, BLK, length), lambda p: (p, 0, 0)), col(BLK), col(BLK), col(length),
                  col(BLK), col(length), col(wide)],
        out_specs=[col(BLK), pl.BlockSpec((PAIR, wide), lambda p: (p, 0))],
        out_shape=[jax.ShapeDtypeStruct((BLK, width), bf16), jax.ShapeDtypeStruct((width, wide), bf16)],
        scratch_shapes=grad_scratch(length),
        compiler_params=params(),
        name="query_grads",
    )(p, dctx, ctx, v, q, k, near)


def key_grads(p, v, dctx, rdot, k, q, near, scale):
    length, width = q.shape
    pairs = width // PAIR
    wide = length + BLK
    return pl.pallas_call(
        functools.partial(key_grad_kernel, scale, length),
        grid=(pairs,),
        in_specs=[pl.BlockSpec((2, BLK, length), lambda p: (p, 0, 0)), col(BLK), col(length),
                  pl.BlockSpec((1, 8, length), lambda p: (p, 0, 0)), col(BLK), col(length), col(wide)],
        out_specs=[col(BLK), col(BLK), pl.BlockSpec((PAIR, wide), lambda p: (p, 0))],
        out_shape=[jax.ShapeDtypeStruct((BLK, width), bf16), jax.ShapeDtypeStruct((BLK, width), bf16),
                   jax.ShapeDtypeStruct((width, wide), bf16)],
        scratch_shapes=grad_scratch(length),
        compiler_params=params(),
        name="key_grads",
    )(p, v, dctx, rdot, k, q, near)


HEADS = 12
EPSILON = 1e-07


def norm_forward(value, gain, shift):
    center = value - jnp.mean(value, axis=-1, keepdims=True)
    scaled = lax.rsqrt(jnp.mean(center * center, axis=-1, keepdims=True) + EPSILON)
    normed = center * scaled
    return (normed * gain + shift, normed, scaled)


def norm_backward(grad_out, normed, scaled, gain):
    grad_normed = grad_out * gain
    inner = grad_normed - jnp.mean(grad_normed, axis=-1, keepdims=True)
    inner = inner - normed * jnp.mean(grad_normed * normed, axis=-1, keepdims=True)
    return (scaled * inner, jnp.sum(grad_out * normed, axis=0), jnp.sum(grad_out, axis=0))


def gelu_exact(value):
    return jax.nn.gelu(value, approximate=False)


def relative_tables(flipped, length, first):
    span = flipped.shape[0] // 2
    side = length - span
    shape = (side, flipped.shape[1])
    padded = jnp.concatenate(
        [jnp.broadcast_to(flipped[:1], shape), flipped, jnp.broadcast_to(flipped[-1:], shape)], axis=0
    )
    near = lax.dynamic_slice_in_dim(padded, length - BLK - first, length + BLK, 0)
    far = lax.dynamic_slice_in_dim(padded, first, length + BLK, 0)
    return near, far


def on_device(
    hidden, segments, rel_embed, query_weight, key_weight, value_weight, output_weight, up_weight, down_weight,
    norm1_gain, norm1_bias, norm2_gain, norm2_bias, cotangent,
):
    tokens, width = hidden.shape[1:]
    span = rel_embed.shape[0] // 2
    scale = 1.0 / math.sqrt(3.0 * (width // HEADS))
    inputs = hidden[0]
    length = lax.axis_size("seq") * tokens
    first = lax.axis_index("seq") * tokens

    def mul(a, b, form=NN):
        return lax.dot_general(a, b, form, preferred_element_type=f32)

    def gather(a, axis):
        return lax.all_gather(a, "seq", axis=axis, tiled=True)

    row_in = gather(inputs, 0)
    row_segs = gather(segments, 1)
    own_segs = segments.reshape(tokens, 1)
    q_all = mul(row_in, query_weight).astype(bf16)
    k_all = mul(row_in, key_weight).astype(bf16)
    v_all = mul(row_in, value_weight).astype(bf16)
    q = mul(inputs, query_weight).astype(bf16)
    k = mul(inputs, key_weight).astype(bf16)
    v = mul(inputs, value_weight).astype(bf16)
    rel_flip = jnp.flip(rel_embed, axis=0)
    qr_near, qr_far = relative_tables(mul(rel_flip, query_weight).astype(bf16), length, first)
    kr_near, kr_far = relative_tables(mul(rel_flip, key_weight).astype(bf16), length, first)

    probs, ctx, lse = forward_attention(q, k_all, v_all, kr_near, qr_far, own_segs, row_segs, scale)
    lse_all = gather(lse, 2)
    probs_t = other_probs(k, q_all, qr_near, kr_far, own_segs, row_segs, lse_all, scale)

    ctx_low = ctx.astype(bf16)
    h1 = inputs.astype(f32) + mul(ctx_low, output_weight)
    normed1, unit1, scaled1 = norm_forward(h1, norm1_gain, norm1_bias)
    normed1_low = normed1.astype(bf16)
    inner = mul(normed1_low, up_weight)
    active, gelu_back = jax.vjp(gelu_exact, inner)
    active_low = active.astype(bf16)
    result, unit2, scaled2 = norm_forward(normed1 + mul(active_low, down_weight), norm2_gain, norm2_bias)
    output = result.astype(bf16)[None]
    cot = cotangent[0].astype(f32)
    d_h2, g_gain2, g_bias2 = norm_backward(cot, unit2, scaled2, norm2_gain)
    d_branch = d_h2.astype(bf16)
    g_down = mul(active_low, d_branch, TN)
    d_inner = gelu_back(mul(d_branch, down_weight, NT))[0].astype(bf16)
    g_up = mul(normed1_low, d_inner, TN)
    d_normed1 = d_h2 + mul(d_inner, up_weight, NT)
    d_h1, g_gain1, g_bias1 = norm_backward(d_normed1, unit1, scaled1, norm1_gain)
    d_attn = d_h1.astype(bf16)
    g_output = mul(ctx_low, d_attn, TN)
    d_ctx = mul(d_attn, output_weight, NT).astype(bf16)

    row_dot = jnp.sum((d_ctx.astype(f32) * ctx).reshape(tokens, HEADS, width // HEADS), axis=2)
    row_dot = jnp.pad(row_dot.T.reshape(HEADS // 2, 2, tokens), ((0, 0), (0, 6), (0, 0)))
    rdot_all = gather(row_dot, 2)
    dctx_all = gather(d_ctx, 0)
    dq, d_kr = query_grads(probs, d_ctx, ctx, v_all, q, k_all, kr_near, scale)
    dk, dv, d_qr = key_grads(probs_t, v, dctx_all, rdot_all, k, q_all, qr_near, scale)

    places = lax.broadcasted_iota(jnp.int32, (length + BLK, 2 * span), 0)
    spots = lax.broadcasted_iota(jnp.int32, (length + BLK, 2 * span), 1)
    select = (jnp.clip(places - first + BLK, 0, 2 * span - 1) == spots).astype(bf16)
    d_qr = mul(d_qr, select).astype(bf16)
    d_kr = mul(d_kr, select).astype(bf16)
    g_query = mul(inputs, dq, TN) + mul(rel_flip, d_qr, (((0,), (1,)), ((), ())))
    g_key = mul(inputs, dk, TN) + mul(rel_flip, d_kr, (((0,), (1,)), ((), ())))
    g_value = mul(inputs, dv, TN)
    both = (((0,), (1,)), ((), ()))
    g_rel = mul(d_qr, query_weight, both) + mul(d_kr, key_weight, both)
    g_rel = jnp.flip(lax.psum(g_rel.astype(bf16), ("seq", "row")).astype(f32), axis=0)

    grad_in = d_h1 + mul(dq, query_weight, NT) + mul(dk, key_weight, NT) + mul(dv, value_weight, NT)

    grads = [g_query, g_key, g_value, g_output, g_up, g_down, g_gain1, g_bias1, g_gain2, g_bias2]
    shares = []
    for g in grads:
        part = lax.psum_scatter(g.astype(bf16), "row", scatter_dimension=0, tiled=True)
        shares.append(lax.psum(part, "seq").astype(f32))
    return (output, grad_in.astype(bf16)[None], *shares, g_rel)


def solution(mesh):
    split = P("row", "seq", None)
    return jax.shard_map(
        on_device,
        mesh=mesh,
        in_specs=(split, P("row", "seq")) + (P(),) * 11 + (split,),
        out_specs=(split, split) + (P("row", None),) * 6 + (P("row"),) * 4 + (P(),),
        check_vma=False,
    )
```

time: 2200 us -> 682 us (0.31); the launches traced: 2170 us -> 679 us
  local copies, waits for them, and re-layouts: 1280 us -> 49.9 us
  other arithmetic: 175 us -> 10.2 us
  matrix products: 173 us -> 60.1 us
  waiting for transfers between devices: 368 us -> 439 us
  blocking collectives: 119 us -> 54.6 us
  Pallas kernels: 0 us -> 49 us
  loops' own time: 37.3 us -> 0 us
    reshape x16 -> x2, local copies, waits for them, and re-layouts: 256 us -> 0.74 us  [the longest x1 0.73 us: on_device(): own_segs = segments.reshape(tokens, 1)]
    rev x10 -> x2, local copies, waits for them, and re-layouts: 252 us -> 21.5 us  [the longest x1 12.1 us: on_device(): jnp.flip(lax.psum(g_rel.astype(bf16), ('seq', 'row')).astype(f32), axis=0)]
    gather x14 -> x0, local copies, waits for them, and re-layouts: 211 us -> none  [the longest x8 124 us: pick_band(): wide = jnp.take(table, column_ids, axis=2)]
    psum x1 -> x2, waiting for transfers between devices: 0.01 us -> 175 us  [the longest x1 104 us: on_device(): lax.psum(g_rel.astype(bf16), ('seq', 'row')).astype(f32)]
    dot_general x55 -> x29, matrix products: 173 us -> 60.1 us  [mul(): return lax.dot_general(a, b, form, preferred_element_type=f32)]
    select_n x8 -> x0, local copies, waits for them, and re-layouts: 111 us -> none  [pick_band(): wide = jnp.take(table, column_ids, axis=2)]
    while x92 -> x0, local copies, waits for them, and re-layouts: 105 us -> none
    pad x16 -> x1, local copies, waits for them, and re-layouts: 99.5 us -> 0.01 us  [on_device(): jnp.pad(row_dot.T.reshape(HEADS // 2, 2, tokens), ((0, 0), (0, 6), (0, 0)))]
  transfers between devices with their start and end apart: 11 -> 10, of which waited for: 9 -> 9; matrix products, arithmetic and copies ran while one was open for 4% -> 11% of each run, Pallas kernels for 0% -> 3%
where the time goes in v1:
time: 682 us; the launch traced here: 679 us
  waiting for transfers between devices  439 us (64%)
  matrix products  60.1 us (9%)
  blocking collectives  54.6 us (8%)
  local copies, waits for them, and re-layouts  49.9 us (7%)
  Pallas kernels  49 us (7%)
  between operations  15.6 us (2%)
  other arithmetic  10.2 us (1%)
    reduce_scatter x3, waiting for transfers between devices, on_device(): lax.psum_scatter(g.astype(bf16), 'row', scatter_dimension=0, tiled=True)  203 us
    psum x1, waiting for transfers between devices, on_device(): lax.psum(g_rel.astype(bf16), ('seq', 'row')).astype(f32)  104 us
    psum x1, waiting for transfers between devices, on_device(): shares.append(lax.psum(part, 'seq').astype(f32))  70.6 us
    dot_general x29, matrix products, mul(): return lax.dot_general(a, b, form, preferred_element_type=f32)  60.1 us
    unnamed x13, waiting for transfers between devices  59.5 us
    all_gather x3, blocking collectives, gather(): return lax.all_gather(a, 'seq', axis=axis, tiled=True)  31.6 us
    unnamed x118, local copies, waits for them, and re-layouts  22.2 us
    pallas_call x1, Pallas kernels, forward_attention(): pl.pallas_call(functools.partial(forward_kernel, scale, length), grid=(pa...  15.3 us
  transfers between devices with their start and end apart: 10, of which 9 were waited for; matrix products, arithmetic and copies ran while one was open for 11% of the time, Pallas kernels for 3%

profile of v1, /device:TPU:0, one launch (start us, length us, event | category | flops | bytes accessed | tf_op | source)
XLA Modules:
  0.0 678.8 jit_solution(12912015886073919444)
XLA Ops:
  8.0 9.5 %rev.8 = bf16[512,768]{1,0:T(8,128)(2,1)S(1)} reverse(bf16[512,768]{1,0:T(8,128)(2,1)} %param.16), dimensions={0} | reverse | bytes 1572864 | tf_op jit(solution)/shard_map/jit(_flip)/rev | solution.py:286
  18.2 10.9 %all_gather.16.segk_ref.segq_ref = s32[1,1024]{1,0:T(1,128)} all-gather(s32[1,128]{1,0:T(1,128)S(1)} %copy-done.41), channel_id=1, replica_groups=mesh['seq'=8,'row'=4] {'seq'}, dimensions={1}, use_global_device_ids=true | all-gather | bytes 4608 | tf_op jit(solution)/shard_map/all_gather | solution.py:275
  29.1 2.0 convolution_convert_fusion.8
  31.2 0.8 convolution_convert_fusion.7
  32.1 1.0 convolution_convert_fusion.12.q_ref
  34.2 3.1 constant_dynamic-slice_fusion
  37.3 1.1 all-gather.6.cloned.1.call-done
  38.4 4.4 convolution_convert_fusion.4.k_ref
  42.8 2.6 convolution_convert_fusion.3.v_ref
  45.4 15.3 %attend.1 = (bf16[12,128,1024]{2,1,0:T(8,128)(2,1)}, f32[128,768]{1,0:T(8,128)}, f32[6,8,128]{2,1,0:T(8,128)}) custom-call(bf16[128,768]{1,0:T(8,128)(2,1)} %convolution_convert_fusion.12.q_ref, bf16[1024,768]{1,0:T(8,128)(2,1)} %convolution_convert_fusion.4.k_ref, bf16[1024,768]{1,0:T(8,128)(2,1)} %convolution_convert_fusion.3.v_ref, ...), custom_call_target="tpu_custom_call" | custom-call | tf_op jit(solution)/shard_map/attend/pallas_call | solution.py:149
  60.8 1.6 fusion.50
  62.6 6.0 multiply_convert_fusion
  68.7 0.9 fusion.51
  69.9 1.5 fusion.26
  71.3 1.9 add_convert_fusion.3
  73.3 2.4 multiply_reduce_fusion
  75.9 1.4 convert_multiply_fusion.2
  77.4 2.4 convolution_convert_fusion.10.k_ref
  79.8 1.0 convolution_convert_fusion.9.v_ref
  80.8 10.6 %query_grads.1 = (bf16[128,768]{1,0:T(8,128)(2,1)}, bf16[768,1152]{1,0:T(8,128)(2,1)}) custom-call(bf16[12,128,1024]{2,1,0:T(8,128)(2,1)} %get-tuple-element.22.p_ref, bf16[128,768]{1,0:T(8,128)(2,1)} %get-tuple-element.107.dctx_ref, f32[128,768]{1,0:T(8,128)} %get-tuple-element.21.ctx_ref, bf16[1024,768]{1,0:T(8,128)(2,1)} %convolution_convert_fusion.3.v_ref, ...), custom_call_target="tpu_custom_call" | custom-call | tf_op jit(solution)/shard_map/query_grads/pallas_call | solution.py:195
  91.4 1.9 copy.40
  93.3 1.0 reduce_sum.128
  94.4 11.0 %all_gather.17.lse_ref = f32[6,8,1024]{2,1,0:T(8,128)} all-gather(f32[6,8,128]{2,1,0:T(8,128)S(1)} %copy-done.30), channel_id=1, replica_groups=mesh['seq'=8,'row'=4] {'seq'}, dimensions={2}, use_global_device_ids=true | all-gather | bytes 221184 | tf_op jit(solution)/shard_map/all_gather | solution.py:275
  105.4 3.9 convolution_convert_fusion.2.q_ref
  109.3 11.9 %key_probs.1.p_ref = bf16[12,128,1024]{2,1,0:T(8,128)(2,1)} custom-call(bf16[128,768]{1,0:T(8,128)(2,1)} %convolution_convert_fusion.10.k_ref, bf16[1024,768]{1,0:T(8,128)(2,1)} %convolution_convert_fusion.2.q_ref, bf16[1152,768]{1,0:T(8,128)(2,1)} %get-tuple-element.109.near_ref, bf16[1152,768]{1,0:T(8,128)(2,1)} %get-tuple-element.95.far_ref, ...), custom_call_target="tpu_custom_call" | custom-call | tf_op jit(solution)/shard_map/key_probs/pallas_call | solution.py:173
  121.3 9.7 %all_gather.19.rdot_ref = f32[6,8,1024]{2,1,0:T(8,128)} all-gather(f32[6,8,128]{2,1,0:T(8,128)S(1)} %pad.4), channel_id=1, replica_groups=mesh['seq'=8,'row'=4] {'seq'}, dimensions={2}, use_global_device_ids=true | all-gather | bytes 221184 | tf_op jit(solution)/shard_map/all_gather | solution.py:275
  131.0 11.2 %key_grads.1 = (bf16[128,768]{1,0:T(8,128)(2,1)}, bf16[128,768]{1,0:T(8,128)(2,1)}, bf16[768,1152]{1,0:T(8,128)(2,1)}) custom-call(bf16[12,128,1024]{2,1,0:T(8,128)(2,1)} %key_probs.1.p_ref, bf16[128,768]{1,0:T(8,128)(2,1)} %convolution_convert_fusion.9.v_ref, bf16[1024,768]{1,0:T(8,128)(2,1)} %all-gather.4.cloned.1.call-done.dctx_ref, ...), custom_call_target="tpu_custom_call" | custom-call | tf_op jit(solution)/shard_map/key_grads/pallas_call | solution.py:212
  142.2 2.8 fusion.11
  145.0 0.8 fusion.52
  146.1 1.5 fusion.14
  147.6 2.4 copy.44
  150.1 2.8 fusion.12
  152.9 0.8 fusion.53
  154.0 1.5 fusion.15
  155.5 2.5 copy.46
  158.1 1.5 fusion.13
  159.6 2.4 copy.48
  162.2 1.5 convolution_convert_fusion.5
  163.8 4.9 convolution_convert_fusion.1
  168.7 1.0 copy-done.7
  169.8 3.6 convolution_convert_fusion
  173.5 2.1 fusion.54
  175.6 1.7 add_convert_fusion.2
  177.7 1.7 reduce-scatter.19.cloned.1.call-done
  179.4 1.9 copy.45
  181.3 28.8 %reduce-scatter.21.cloned.1.call-done = bf16[192,768]{1,0:T(8,128)(2,1)} async-done(((bf16[768,768]{1,0:T(8,128)(2,1)}), bf16[192,768]{1,0:T(8,128)(2,1)}) %reduce-scatter.21.cloned.1.call-update) | async-done | bytes 294928
  210.1 1.9 copy.47
  212.0 28.2 %reduce-scatter.23.cloned.1.call-done = bf16[192,768]{1,0:T(8,128)(2,1)} async-done(((bf16[768,768]{1,0:T(8,128)(2,1)}), bf16[192,768]{1,0:T(8,128)(2,1)}) %reduce-scatter.23.cloned.1.call-update) | async-done | bytes 294928
  240.2 1.9 copy.49
  242.0 28.8 %reduce-scatter.13.cloned.1.call-done = bf16[192,768]{1,0:T(8,128)(2,1)} async-done(((bf16[768,768]{1,0:T(8,128)(2,1)}), bf16[192,768]{1,0:T(8,128)(2,1)}) %reduce-scatter.13.cloned.1.call-update) | async-done | bytes 294928 | tf_op jit(solution)/shard_map/reduce_scatter | solution.py:339
  270.8 86.3 %reduce-scatter.15.cloned.1.call-done = bf16[192,3072]{1,0:T(8,128)(2,1)} async-done(((bf16[768,3072]{1,0:T(8,128)(2,1)}), bf16[192,3072]{1,0:T(8,128)(2,1)}) %reduce-scatter.15.cloned.1.call-update) | async-done | bytes 1179664 | tf_op jit(solution)/shard_map/reduce_scatter | solution.py:339
  357.1 88.1 %reduce-scatter.17.cloned.1.call-done = bf16[768,768]{1,0:T(8,128)(2,1)} async-done(((bf16[3072,768]{1,0:T(8,128)(2,1)}), bf16[768,768]{1,0:T(8,128)(2,1)}) %reduce-scatter.17.cloned.1.call-update) | async-done | bytes 1179664 | tf_op jit(solution)/shard_map/reduce_scatter | solution.py:339
  447.2 11.1 %all-reduce.7 = (bf16[768]{0:T(1024)(128)(2,1)S(1)}, bf16[768]{0:T(1024)(128)(2,1)S(1)}, bf16[768]{0:T(1024)(128)(2,1)S(1)}, bf16[768]{0:T(1024)(128)(2,1)S(1)}) all-reduce(bf16[768]{0:T(1024)(128)(2,1)S(1)} %copy-done.34, bf16[768]{0:T(1024)(128)(2,1)S(1)} %copy-done.35, ...), channel_id=9, replica_groups=mesh['seq'=8,'row'=4] {'row'}, use_global_device_ids=true, to_apply=%region_22.23.clone | all-reduce | flops 3072 | bytes 12288
  458.6 11.9 %all-reduce.5 = (bf16[192]{0:T(256)(128)(2,1)S(1)}, bf16[192]{0:T(256)(128)(2,1)S(1)}, bf16[192]{0:T(256)(128)(2,1)S(1)}, bf16[192]{0:T(256)(128)(2,1)S(1)}) all-reduce(bf16[192]{0:T(256)(128)(2,1)S(1)} %dynamic-slice.1, bf16[192]{0:T(256)(128)(2,1)S(1)} %dynamic-slice.3, ...), channel_id=1, replica_groups=mesh['seq'=8,'row'=4] {'seq'}, use_global_device_ids=true, to_apply=%region_23.24 | all-reduce | flops 768 | bytes 3072 | tf_op jit(solution)/shard_map/psum | solution.py:340
  474.5 1.2 fusion.19
  475.8 104.3 %all-reduce.11.cloned.1.call-done = bf16[512,768]{1,0:T(8,128)(2,1)} async-done(((bf16[512,768]{1,0:T(8,128)(2,1)}), bf16[512,768]{1,0:T(8,128)(2,1)}) %all-reduce.11.cloned.1.call-update) | async-done | bytes 786448 | tf_op jit(solution)/shard_map/psum | solution.py:332
  580.0 12.1 %rev.9 = f32[512,768]{1,0:T(8,128)} reverse(bf16[512,768]{1,0:T(8,128)(2,1)} %all-reduce.11.cloned.1.call-done), dimensions={0} | reverse | bytes 2359296 | tf_op jit(solution)/shard_map/jit(_flip)/rev | solution.py:332
  592.1 70.6 %all-reduce.13.cloned.1.call-done = (bf16[192,768]{0,1:T(8,128)(2,1)}, bf16[192,768]{0,1:T(8,128)(2,1)}, bf16[192,768]{0,1:T(8,128)(2,1)}, bf16[192,768]{1,0:T(8...) async-done(((bf16[192,768]{0,1:T(8,128)(2,1)}, bf16[192,768]{0,1:T(8,128)(2,1)}, bf16[192,768]{0,1:T(8,128)(2,1)}, bf16[192,768]{1,0:T(8,128)(2,1)}, ...) | async-done | bytes 3538960 | tf_op jit(solution)/shard_map/psum | solution.py:340
  662.7 2.0 copy.41
  664.8 2.1 copy.42
  666.8 1.0 copy.43
  667.8 0.9 convert_element_type.178
  668.7 1.7 convert_element_type.180
  670.3 1.6 convert_element_type.182
  (161 shorter events, 10.5 us)
Async XLA Ops:
  7.2 24.0 %copy-start = (bf16[768,768]{1,0:T(8,128)(2,1)S(1)}, bf16[768,768]{1,0:T(8,128)(2,1)}, u32[]{:S(2)}) copy-start(bf16[768,768]{1,0:T(8,128)(2,1)} %param.17) | copy-start | bytes 3538948
  7.2 10.3 %copy-start.41 = (s32[1,128]{1,0:T(1,128)S(1)}, s32[1,128]{1,0:T(1,128)}, u32[]{:S(2)}) copy-start(s32[1,128]{1,0:T(1,128)} %param.15) | copy-start | bytes 1540
  7.2 31.1 %all-gather.6.cloned.1.call-start = ((), (), s32[]{:S(2)}) async-start(), calls=%async_computation.11 | async-start | bytes 1769472 | tf_op jit(solution)/shard_map/all_gather | solution.py:275
  7.9 123.1 %all-gather.4.cloned.1.call-start = ((), (), s32[]{:S(2)}) async-start(), calls=%async_computation.6 | async-start | bytes 1769472 | tf_op jit(solution)/shard_map/all_gather | solution.py:275
  31.2 0.9 copy-start.1
  38.4 4.4 copy-start.10
  38.4 4.4 copy-start.46
  45.4 15.3 %copy-start.8 = (bf16[768,768]{1,0:T(8,128)(2,1)S(1)}, bf16[768,768]{1,0:T(8,128)(2,1)}, u32[]{:S(2)}) copy-start(bf16[768,768]{1,0:T(8,128)(2,1)} %param.20) | copy-start | bytes 3538948
  60.7 1.8 copy-start.27
  60.7 1.8 copy-start.28
  60.7 7.9 %slice-start = ((s8[4718592]{0:T(1024)(128)(4,1)}), s8[4194304]{0:T(1024)(128)(4,1)S(1)}, s32[]{:S(2)}) async-start(s8[4718592]{0:T(1024)(128)(4,1)} %bitcast.91), calls=%async_computation.16 | async-start | bytes 8388608
  62.6 13.2 %copy-start.31 = (f32[128]{0:T(128)}, f32[128]{0:T(128)S(1)}, u32[]{:S(2)}) copy-start(f32[128]{0:T(128)S(1)} %add_rsqrt_fusion.1) | copy-start | bytes 1540
  62.6 6.1 slice-start.1
  68.6 1.0 copy-start.6
  68.6 1.2 copy-start.14
  68.7 1.2 copy-start.29
  68.7 1.2 copy-start.40
  68.7 4.6 slice-start.2
  69.6 3.6 copy-start.36
  69.9 3.4 copy-start.38
  71.3 1.9 copy-start.42
  71.3 1.9 copy-start.44
  71.3 1.9 slice-start.3
  73.3 2.5 copy-start.13
  73.3 2.6 copy-start.2
  75.9 1.4 copy-start.4
  77.3 102.1 %reduce-scatter.19.cloned.1.call-start = ((), (), s32[]{:S(2)}) async-start(), calls=%async_computation.12 | async-start | bytes 1474560
  77.4 2.4 copy-start.11
  80.8 13.6 %copy-start.30 = (f32[6,8,128]{2,1,0:T(8,128)S(1)}, f32[6,8,128]{2,1,0:T(8,128)}, u32[]{:S(2)}) copy-start(f32[6,8,128]{2,1,0:T(8,128)} %get-tuple-element.24) | copy-start | bytes 73732
  145.0 0.9 copy-start.17
  145.0 1.1 copy-start.20
  150.0 60.0 %reduce-scatter.21.cloned.1.call-start = ((), (), s32[]{:S(2)}) async-start(), calls=%async_computation.13 | async-start | bytes 1474560
  152.9 0.9 copy-start.18
  152.9 1.1 copy-start.23
  155.5 2.6 copy-start.21
  158.0 82.1 %reduce-scatter.23.cloned.1.call-start = ((), (), s32[]{:S(2)}) async-start(), calls=%async_computation.14 | async-start | bytes 1474560
  159.6 2.5 copy-start.3
  159.6 2.5 copy-start.5
  162.1 1.7 copy-start.32
  162.1 108.7 %reduce-scatter.13.cloned.1.call-start = ((), (), s32[]{:S(2)}) async-start(), calls=%async_computation.7 | async-start | bytes 1474560 | tf_op jit(solution)/shard_map/reduce_scatter | solution.py:339
  163.7 193.4 %reduce-scatter.15.cloned.1.call-start = ((), (), s32[]{:S(2)}) async-start(), calls=%async_computation.8 | async-start | bytes 5898240 | tf_op jit(solution)/shard_map/reduce_scatter | solution.py:339
  168.6 1.1 copy-start.7
  168.6 1.1 copy-start.37
  168.6 1.1 copy-start.39
  168.6 1.1 copy-start.43
  168.6 1.1 copy-start.45
  168.7 276.6 %reduce-scatter.17.cloned.1.call-start = ((), (), s32[]{:S(2)}) async-start(), calls=%async_computation.9 | async-start | bytes 5898240 | tf_op jit(solution)/shard_map/reduce_scatter | solution.py:339
  173.4 2.2 copy-start.9
  173.5 406.6 %all-reduce.11.cloned.1.call-start = ((), (), s32[]{:S(2)}) async-start(), calls=%async_computation.10 | async-start | bytes 1572864 | tf_op jit(solution)/shard_map/psum | solution.py:332
  173.5 2.1 copy-start.19
  177.4 485.4 %all-reduce.13.cloned.1.call-start = ((), (), s32[]{:S(2)}) async-start(), calls=%async_computation.15 | async-start | bytes 7667712 | tf_op jit(solution)/shard_map/psum | solution.py:340
  445.2 0.7 copy-start.47
  445.2 1.9 copy-start.33
  445.2 1.9 copy-start.34
  445.2 1.9 copy-start.35
  445.3 28.0 %copy-start.24 = (bf16[128,768]{1,0:T(8,128)(2,1)S(1)}, bf16[128,768]{1,0:T(8,128)(2,1)}, u32[]{:S(2)}) copy-start(bf16[128,768]{1,0:T(8,128)(2,1)} %get-tuple-element.25) | copy-start | bytes 589828
  473.2 1.3 copy-start.12
  473.3 1.3 copy-start.22
  662.7 4.1 copy-start.25
  662.7 5.1 copy-start.26
  664.8 3.9 copy-start.16
  668.7 1.7 copy-start.15
Sparse Core Ops, SparseCore 0:
  9.9 28.3 all-gather.5
  77.5 26.2 all-gather.3
  150.2 29.1 reduce-scatter.18
  182.1 27.8 reduce-scatter.20
  212.2 27.8 reduce-scatter.22
  242.9 27.8 reduce-scatter.12
  273.1 83.9 reduce-scatter.14
  359.4 85.7 reduce-scatter.16
  450.4 129.5 all-reduce.10
  585.1 77.5 all-reduce.12

commit v2 on v1

v2 whole, which is shorter than its diff:
```python
import functools, math
import jax, jax.numpy as jnp
from jax import lax
from jax.experimental import pallas as pl
from jax.experimental.pallas import tpu as pltpu
from jax.sharding import PartitionSpec as P

BLK = 128
PAIR = 128
NT = (((1,), (1,)), ((), ()))
NN = (((1,), (0,)), ((), ()))
TN = (((0,), (0,)), ((), ()))
bf16 = jnp.bfloat16
f32 = jnp.float32


def dot(a, b, form):
    return lax.dot_general(a, b, form, preferred_element_type=f32)


def half_masks(x):
    lane = lax.broadcasted_iota(jnp.int32, x.shape, 1)
    low = lane < PAIR // 2
    zero = jnp.zeros_like(x)
    return jnp.where(low, x, zero), jnp.where(low, zero, x)


def join_heads(stacked, rows):
    lane = lax.broadcasted_iota(jnp.int32, (rows, PAIR), 1)
    return jnp.where(lane < PAIR // 2, stacked[:rows], stacked[rows:])


def slot_order(count):
    return list(range(0, count, 2)) + list(range(1, count, 2))


def block_start(me, slot):
    return pl.multiple_of((me ^ slot) * BLK, BLK)


def fill_scores(me, own_ref, all_ref, near_ref, far_ref, s_ref, n_ref, length):
    wide = length + BLK
    own = jnp.concatenate(half_masks(own_ref[...]), axis=0)
    ext = dot(own, near_ref[...], NT)
    for h in range(2):
        moved = pltpu.roll(ext[h * BLK:(h + 1) * BLK], wide - (BLK - 1), 1, stride=1, stride_axis=0)
        n_ref[h] = moved[:, :length]
    for c, slot in enumerate(slot_order(length // BLK)):
        cols = slice(c * BLK, (c + 1) * BLK)
        blk = all_ref[cols, :]
        both = jnp.concatenate(half_masks(blk), axis=0)
        start = block_start(me, slot)
        win = far_ref[pl.ds(pl.multiple_of(length - BLK - start, BLK), 2 * BLK), :]
        back = dot(both, win, NT)
        direct = dot(own, blk, NT)
        for h in range(2):
            rows = slice(h * BLK, (h + 1) * BLK)
            moved = pltpu.roll(back[rows], BLK + 1, 1, stride=1, stride_axis=0)[:, :BLK]
            s_ref[h, :, cols] = direct[rows] + moved.T + n_ref[h, :, pl.ds(start, BLK)]


def by_slot(me, row):
    length = row.shape[1]
    return jnp.concatenate([row[:, pl.ds(block_start(me, k), BLK)] for k in slot_order(length // BLK)], axis=1)


def forward_kernel(scale, length, me_ref, q_ref, k_ref, v_ref, near_ref, far_ref, segq_ref, segk_ref,
                   p_ref, ctx_ref, lse_ref, s_ref, n_ref):
    me = me_ref[0]
    fill_scores(me, q_ref, k_ref, near_ref, far_ref, s_ref, n_ref, length)
    allowed = segq_ref[...] == by_slot(me, segk_ref)
    stats = []
    for h in range(2):
        logits = jnp.where(allowed, s_ref[h] * scale, -1e30)
        best = jnp.max(logits, axis=1, keepdims=True)
        weights = jnp.exp(logits - best)
        total = jnp.sum(weights, axis=1, keepdims=True)
        p_ref[h] = (weights * (1.0 / total)).astype(bf16)
        stats.append(best + jnp.log(total))
    stacked = jnp.concatenate([p_ref[0], p_ref[1]], axis=0)
    ctx_ref[...] = join_heads(dot(stacked, v_ref[...], NN), BLK)
    lane = lax.broadcasted_iota(jnp.int32, (BLK, BLK), 1)
    tile = jnp.where(lane == 0, stats[0], stats[1])
    lse_ref[0] = tile.T[:8]


def other_probs_kernel(scale, length, me_ref, k_ref, q_ref, near_ref, far_ref, segk_ref, segq_ref, lse_ref, p_ref,
                       s_ref, n_ref):
    me = me_ref[0]
    fill_scores(me, k_ref, q_ref, near_ref, far_ref, s_ref, n_ref, length)
    allowed = segk_ref[...] == by_slot(me, segq_ref)
    for h in range(2):
        logits = s_ref[h] * scale - by_slot(me, lse_ref.at[0, h:h + 1])
        p_ref[h] = jnp.where(allowed, jnp.exp(logits), 0.0).astype(bf16)


def flip_matrix():
    r = lax.broadcasted_iota(jnp.int32, (BLK, BLK), 0)
    c = lax.broadcasted_iota(jnp.int32, (BLK, BLK), 1)
    return jnp.where(r + c == BLK - 1, 1.0, 0.0).astype(bf16)


def fold_table(grad, first, places, fold_ref):
    wide = grad.shape[1]
    place = lax.broadcasted_iota(jnp.int32, grad.shape, 1)
    low = jnp.sum(jnp.where(place < first - BLK, grad, 0.0), axis=1, keepdims=True)
    high = jnp.sum(jnp.where(place >= first + places - BLK, grad, 0.0), axis=1, keepdims=True)
    edge = jnp.zeros((PAIR, BLK), f32)
    fold_ref[:, :BLK] = edge
    fold_ref[:, BLK:BLK + wide] = grad
    fold_ref[:, BLK + wide:] = jnp.zeros((PAIR, places - 3 * BLK), f32)
    table = fold_ref[:, pl.ds(pl.multiple_of(first, BLK), places)]
    spot = lax.broadcasted_iota(jnp.int32, table.shape, 1)
    return table + jnp.where(spot == 0, low, 0.0) + jnp.where(spot == places - 1, high, 0.0)


def grads_tail(scale, length, me, ds_refs, own_ref, all_ref, near_ref, table_ref, wide_ref, down_ref, fold_ref, n_ref):
    flip = flip_matrix()
    for h in range(2):
        back = dot(flip, ds_refs[h], NN)
        down_ref[h * BLK:(h + 1) * BLK, :] = back.astype(bf16)
        for c, slot in enumerate(slot_order(length // BLK)):
            n_ref[:, pl.ds(block_start(me, slot), BLK)] = back[:, c * BLK:(c + 1) * BLK]
        padded = jnp.concatenate([n_ref[...], jnp.zeros((BLK, BLK), f32)], axis=1)
        wide_ref[h * BLK:(h + 1) * BLK, :] = pltpu.roll(padded, 0, 1, stride=1, stride_axis=0).astype(bf16)
    own_grad = dot(down_ref[...], all_ref[...], NN) + dot(wide_ref[...], near_ref[...], NN)
    own_grad = (join_heads(own_grad, BLK) * scale).astype(bf16)
    turned = dot(own_grad, flip, TN).astype(bf16)
    own_grad = dot(flip, own_grad, NN).astype(bf16)
    own = dot(flip, own_ref[...], NN).astype(bf16)
    own = jnp.concatenate(half_masks(own), axis=0)
    near_grad = dot(own, wide_ref[...], TN) * scale
    places = fold_ref.shape[1] - length + BLK
    table_ref[:, :places] = fold_table(near_grad, me * BLK, places, fold_ref).astype(bf16)
    table_ref[:, places:places + BLK] = turned
    return own_grad


def query_grad_kernel(scale, length, me_ref, p_ref, dctx_ref, ctx_ref, v_ref, q_ref, k_ref, near_ref,
                      dq_ref, table_ref, ds_ref, *scratch):
    dctx = jnp.concatenate(half_masks(dctx_ref[...]), axis=0)
    dprob = dot(dctx, v_ref[...], NT)
    ctx = ctx_ref[...]
    for h in range(2):
        rows = slice(h * BLK, (h + 1) * BLK)
        row_dot = jnp.sum(dctx[rows].astype(f32) * ctx, axis=1, keepdims=True)
        ds_ref[h] = (p_ref[h].astype(f32) * (dprob[rows] - row_dot)).astype(bf16)
    dq_ref[...] = grads_tail(scale, length, me_ref[0], ds_ref, q_ref, k_ref, near_ref, table_ref, *scratch)


def key_grad_kernel(scale, length, me_ref, p_ref, v_ref, dctx_ref, rdot_ref, k_ref, q_ref, near_ref,
                    dk_ref, dv_ref, table_ref, ds_ref, *scratch):
    me = me_ref[0]
    vals = jnp.concatenate(half_masks(v_ref[...]), axis=0)
    dctx = dctx_ref[...]
    dprob = dot(vals, dctx, NT)
    for h in range(2):
        rows = slice(h * BLK, (h + 1) * BLK)
        ds_ref[h] = (p_ref[h].astype(f32) * (dprob[rows] - by_slot(me, rdot_ref.at[0, h:h + 1]))).astype(bf16)
    stacked = jnp.concatenate([p_ref[0], p_ref[1]], axis=0)
    dv = join_heads(dot(stacked, dctx, NN), BLK)
    dv_ref[...] = dv.astype(bf16)
    table_ref[:, table_ref.shape[1] - BLK:] = dv.T.astype(bf16)
    dk_ref[...] = grads_tail(scale, length, me, ds_ref, k_ref, q_ref, near_ref, table_ref, *scratch)


def col(rows):
    return pl.BlockSpec((rows, PAIR), lambda p: (0, p))


def full(shape):
    return pl.BlockSpec(shape, lambda p: (0,) * len(shape))


def params():
    return pltpu.CompilerParams(vmem_limit_bytes=56 * 1024 * 1024)


def forward_attention(me, q, k, v, near, far, seg_q, seg_k, scale):
    length, width = k.shape
    pairs = width // PAIR
    wide = length + BLK
    return pl.pallas_call(
        functools.partial(forward_kernel, scale, length),
        grid=(pairs,),
        in_specs=[scalar(), col(BLK), col(length), col(length), col(wide), col(wide), full((BLK, 1)), full((1, length))],
        out_specs=[
            pl.BlockSpec((2, BLK, length), lambda p: (p, 0, 0)),
            col(BLK),
            pl.BlockSpec((1, 8, BLK), lambda p: (p, 0, 0)),
        ],
        out_shape=[
            jax.ShapeDtypeStruct((2 * pairs, BLK, length), bf16),
            jax.ShapeDtypeStruct((BLK, width), f32),
            jax.ShapeDtypeStruct((pairs, 8, BLK), f32),
        ],
        scratch_shapes=[pltpu.VMEM((2, BLK, length), f32), pltpu.VMEM((2, BLK, length), f32)],
        compiler_params=params(),
        name="attend",
    )(me, q, k, v, near, far, seg_q, seg_k)


def other_probs(me, k, q, near, far, seg_k, seg_q, lse, scale):
    length, width = q.shape
    pairs = width // PAIR
    wide = length + BLK
    return pl.pallas_call(
        functools.partial(other_probs_kernel, scale, length),
        grid=(pairs,),
        in_specs=[scalar(), col(BLK), col(length), col(wide), col(wide), full((BLK, 1)), full((1, length)),
                  pl.BlockSpec((1, 8, length), lambda p: (p, 0, 0))],
        out_specs=pl.BlockSpec((2, BLK, length), lambda p: (p, 0, 0)),
        out_shape=jax.ShapeDtypeStruct((2 * pairs, BLK, length), bf16),
        scratch_shapes=[pltpu.VMEM((2, BLK, length), f32), pltpu.VMEM((2, BLK, length), f32)],
        compiler_params=params(),
        name="key_probs",
    )(me, k, q, near, far, seg_k, seg_q, lse)


def grad_scratch(length, places):
    return [
        pltpu.VMEM((2, BLK, length), bf16),
        pltpu.VMEM((2 * BLK, length + BLK), bf16),
        pltpu.VMEM((2 * BLK, length), bf16),
        pltpu.VMEM((PAIR, length + places - BLK), f32),
        pltpu.VMEM((BLK, length), f32),
    ]


def scalar():
    return pl.BlockSpec(memory_space=pltpu.SMEM)


def query_grads(me, p, dctx, ctx, v, q, k, near, places, scale):
    length, width = k.shape
    pairs = width // PAIR
    wide = length + BLK
    return pl.pallas_call(
        functools.partial(query_grad_kernel, scale, length),
        grid=(pairs,),
        in_specs=[scalar(), pl.BlockSpec((2, BLK, length), lambda p: (p, 0, 0)), col(BLK), col(BLK), col(length),
                  col(BLK), col(length), col(wide)],
        out_specs=[col(BLK), pl.BlockSpec((PAIR, places + BLK), lambda p: (p, 0))],
        out_shape=[jax.ShapeDtypeStruct((BLK, width), bf16), jax.ShapeDtypeStruct((width, places + BLK), bf16)],
        scratch_shapes=grad_scratch(length, places),
        compiler_params=params(),
        name="query_grads",
    )(me, p, dctx, ctx, v, q, k, near)


def key_grads(me, p, v, dctx, rdot, k, q, near, places, scale):
    length, width = q.shape
    pairs = width // PAIR
    wide = length + BLK
    return pl.pallas_call(
        functools.partial(key_grad_kernel, scale, length),
        grid=(pairs,),
        in_specs=[scalar(), pl.BlockSpec((2, BLK, length), lambda p: (p, 0, 0)), col(BLK), col(length),
                  pl.BlockSpec((1, 8, length), lambda p: (p, 0, 0)), col(BLK), col(length), col(wide)],
        out_specs=[col(BLK), col(BLK), pl.BlockSpec((PAIR, places + 2 * BLK), lambda p: (p, 0))],
        out_shape=[jax.ShapeDtypeStruct((BLK, width), bf16), jax.ShapeDtypeStruct((BLK, width), bf16),
                   jax.ShapeDtypeStruct((width, places + 2 * BLK), bf16)],
        scratch_shapes=grad_scratch(length, places),
        compiler_params=params(),
        name="key_grads",
    )(me, p, v, dctx, rdot, k, q, near)


def project_kernel(even_ref, odd_ref, wq_ref, wk_ref, wv_ref, q_ref, k_ref, v_ref):
    half = even_ref.shape[0]
    weights = jnp.concatenate([wq_ref[...], wk_ref[...], wv_ref[...]], axis=1)
    for i, ref in enumerate((even_ref, odd_ref)):
        out = dot(ref[...], weights, NN).astype(bf16)
        rows = slice(i * half, (i + 1) * half)
        q_ref[rows] = out[:, :PAIR]
        k_ref[rows] = out[:, PAIR:2 * PAIR]
        v_ref[rows] = out[:, 2 * PAIR:]


def project_rows(even, odd, wq, wk, wv):
    half, width = even.shape
    shape = jax.ShapeDtypeStruct((2 * half, width), bf16)
    return pl.pallas_call(
        project_kernel,
        grid=(width // PAIR,),
        in_specs=[full((half, width)), full((half, width))] + [col(width)] * 3,
        out_specs=[col(2 * half)] * 3,
        out_shape=[shape] * 3,
        compiler_params=params(),
        name="project",
    )(even, odd, wq, wk, wv)


def pack_kernel(cols, rows, me_ref, act_ref, din_ref, ctx_ref, out_ref, turn_ref):
    me = me_ref[0]
    units, width = act_ref.shape[1], ctx_ref.shape[1]

    def turn(ref, count):
        for i in range(count // BLK):
            turn_ref[i * BLK:(i + 1) * BLK, :] = ref[:, i * BLK:(i + 1) * BLK].astype(f32).T

    def pick(count, c):
        size = count // (rows * cols)
        starts = [r * (count // rows) + c * size for r in range(rows)]
        return jnp.concatenate([turn_ref[a:a + size, :] for a in starts], axis=0).astype(bf16)

    chunk = units // cols
    turn(act_ref, units)
    for c in range(cols):
        out_ref[me ^ c, :chunk] = pick(units, c)
    turn(din_ref, units)
    for c in range(cols):
        out_ref[me ^ c, chunk:2 * chunk] = turn_ref[c * chunk:(c + 1) * chunk, :].astype(bf16)
    turn(ctx_ref, width)
    for c in range(cols):
        out_ref[me ^ c, 2 * chunk:] = pick(width, c)


def pack(me, act, din, ctx, cols, rows):
    tokens, units = act.shape
    width = ctx.shape[1]
    return pl.pallas_call(
        functools.partial(pack_kernel, cols, rows),
        in_specs=[scalar()] + [pl.BlockSpec(memory_space=pltpu.VMEM)] * 3,
        out_specs=pl.BlockSpec(memory_space=pltpu.VMEM),
        out_shape=jax.ShapeDtypeStruct((cols, (2 * units + width) // cols, tokens), bf16),
        scratch_shapes=[pltpu.VMEM((units, tokens), f32)],
        compiler_params=params(),
        name="pack",
    )(me, act, din, ctx)


def lanes(parts):
    return jnp.concatenate(parts, axis=1)


def layer_sums_kernel(rows, chunk, me_ref, even_ref, odd_ref, attn_even_ref, attn_odd_ref, *refs):
    *part_refs, out_ref = refs
    me = me_ref[0]
    width = attn_even_ref.shape[2]
    features = part_refs[0].shape[0] - 2 * chunk
    half = width // 2
    down = up = out = 0.0
    for i in range(len(part_refs) // 2):
        part = lanes([part_refs[2 * i][...], part_refs[2 * i + 1][...]])
        normed = jnp.concatenate([even_ref[i, :, :width], odd_ref[i, :, :width]], axis=0)
        branch = jnp.concatenate([even_ref[i, :, width:], odd_ref[i, :, width:]], axis=0)
        attn = jnp.concatenate([attn_even_ref[i], attn_odd_ref[i]], axis=0)
        down = down + dot(part[:chunk], branch, NN)
        up = up + dot(part[chunk:2 * chunk], normed, NN)
        out = out + dot(part[2 * chunk:], attn, NN)
    up = up.T
    share, size, few = width // rows, chunk // rows, features // rows
    for r in range(rows):
        pieces = [
            down[r * size:(r + 1) * size, :half], down[r * size:(r + 1) * size, half:],
            up[r * share:(r + 1) * share],
            out[r * few:(r + 1) * few, :half], out[r * few:(r + 1) * few, half:],
        ]
        out_ref[me ^ r] = jnp.concatenate(pieces, axis=0).astype(bf16)


def layer_sums(row, even, odd, attn_even, attn_odd, parts, rows, chunk):
    width = attn_even.shape[2]
    features = parts[0].shape[0] - 2 * chunk
    height = (2 * chunk + 2 * features) // rows + width // rows
    return pl.pallas_call(
        functools.partial(layer_sums_kernel, rows, chunk),
        in_specs=[scalar()] + [pl.BlockSpec(memory_space=pltpu.VMEM)] * (4 + len(parts)),
        out_specs=pl.BlockSpec(memory_space=pltpu.VMEM),
        out_shape=jax.ShapeDtypeStruct((rows, height, chunk), bf16),
        compiler_params=params(),
        name="layer_sums",
    )(row, even, odd, attn_even, attn_odd, *parts)


def layer_unpack_kernel(cols, me_ref, even_ref, odd_ref, down_ref, up_ref, out_ref):
    me = me_ref[0]
    half = down_ref.shape[1] // 2
    size, share, few = down_ref.shape[0] // cols, up_ref.shape[0], out_ref.shape[0] // cols
    chunk = up_ref.shape[1] // cols
    for ref, odd in ((even_ref, 0), (odd_ref, 1)):
        for i in range(cols // 2):
            spot = me ^ (2 * i + odd)
            part = ref[i].astype(f32)
            down_rows = pl.ds(pl.multiple_of(spot * size, 8), size)
            down_ref[down_rows, :half] = part[:size]
            down_ref[down_rows, half:] = part[size:2 * size]
            at = 2 * size + share
            up_ref[:, pl.ds(pl.multiple_of(spot * chunk, BLK), chunk)] = part[2 * size:at]
            out_rows = pl.ds(pl.multiple_of(spot * few, 8), few)
            out_ref[out_rows, :half] = part[at:at + few]
            out_ref[out_rows, half:] = part[at + few:]


def layer_unpack(me, even, odd, rows, width, units):
    cols = 2 * even.shape[0]
    shapes = [(units // rows, width), (width // rows, units), (width // rows, width)]
    return pl.pallas_call(
        functools.partial(layer_unpack_kernel, cols),
        in_specs=[scalar()] + [pl.BlockSpec(memory_space=pltpu.VMEM)] * 2,
        out_specs=[pl.BlockSpec(memory_space=pltpu.VMEM)] * 3,
        out_shape=[jax.ShapeDtypeStruct(x, f32) for x in shapes],
        compiler_params=params(),
        name="layer_unpack",
    )(me, even, odd)


def attn_sums_kernel(rows, row_ref, even_ref, odd_ref, rel_ref, *refs):
    *refs, out_ref = refs
    count = len(refs) // 2
    me = row_ref[0]
    size = refs[0].shape[0]
    width, places = even_ref.shape[2], rel_ref.shape[0]
    table = {"q": 0.0, "k": 0.0}
    total = {"q": 0.0, "k": 0.0, "v": 0.0}
    for i in range(count // 2):
        rows_in = jnp.concatenate([even_ref[i], odd_ref[i]], axis=0)
        qa, qb, ka, kb = refs[2 * i], refs[2 * i + 1], refs[count + 2 * i], refs[count + 2 * i + 1]
        cut = lambda ref, j: ref[:, places + j * BLK:places + (j + 1) * BLK]
        total["q"] = total["q"] + dot(lanes([cut(qa, 0), cut(qb, 0)]), rows_in, NN)
        total["k"] = total["k"] + dot(lanes([cut(ka, 0), cut(kb, 0)]), rows_in, NN)
        total["v"] = total["v"] + dot(lanes([cut(ka, 1), cut(kb, 1)]), rows_in, NN)
        table["k"] = table["k"] + qa[:, :places].astype(f32) + qb[:, :places].astype(f32)
        table["q"] = table["q"] + ka[:, :places].astype(f32) + kb[:, :places].astype(f32)
    pieces = []
    for name in ("q", "k"):
        pieces.append(total[name] + dot(table[name].astype(bf16), rel_ref[...], NN))
    pieces.append(total["v"])
    fill = -3 * size % BLK
    if fill:
        pieces.append(jnp.zeros((fill, width), f32))
    full_sum = jnp.concatenate(pieces, axis=0).T
    share, spots = width // rows, places // rows
    wide = full_sum.shape[1]
    both = jnp.concatenate([table["q"], table["k"]], axis=0)
    lines = 2 * size * spots // wide
    for r in range(rows):
        cut = both[:, r * spots:(r + 1) * spots]
        cut = lanes([cut[j * lines:(j + 1) * lines] for j in range(wide // spots)])
        out_ref[me ^ r] = jnp.concatenate([full_sum[r * share:(r + 1) * share], cut], axis=0).astype(bf16)


def attn_sums(row, even, odd, rel, q_parts, k_parts, rows):
    size = q_parts[0].shape[0]
    width, places = even.shape[2], rel.shape[0]
    wide = 3 * size + (-3 * size % BLK)
    height = width // rows + 2 * size * (places // rows) // wide
    return pl.pallas_call(
        functools.partial(attn_sums_kernel, rows),
        in_specs=[scalar()] + [pl.BlockSpec(memory_space=pltpu.VMEM)] * (3 + len(q_parts) + len(k_parts)),
        out_specs=pl.BlockSpec(memory_space=pltpu.VMEM),
        out_shape=jax.ShapeDtypeStruct((rows, height, wide), bf16),
        compiler_params=params(),
        name="attn_sums",
    )(row, even, odd, rel, *q_parts, *k_parts)


def attn_unpack_kernel(cols, spots, me_ref, even_ref, odd_ref, wq_ref, wk_ref, q_ref, k_ref, v_ref, rel_ref, all_ref, tq_ref, tk_ref):
    me = me_ref[0]
    share, width = q_ref.shape
    size = width // cols
    for ref, odd in ((even_ref, 0), (odd_ref, 1)):
        for i in range(cols // 2):
            all_ref[me ^ (2 * i + odd)] = ref[i].astype(f32)
    wide = all_ref.shape[2]
    lines = all_ref.shape[1] - share
    for c in range(cols):
        spot = slice(c * size, (c + 1) * size)
        q_ref[:, spot] = all_ref[c, :share, :size]
        k_ref[:, spot] = all_ref[c, :share, size:2 * size]
        v_ref[:, spot] = all_ref[c, :share, 2 * size:3 * size]
        tail = all_ref[c, share:, :]
        tail = jnp.concatenate([tail[:, j * spots:(j + 1) * spots] for j in range(wide // spots)], axis=0)
        tq_ref[spot, :] = tail[:size].astype(bf16)
        tk_ref[spot, :] = tail[size:].astype(bf16)
    flip = flip_matrix()
    turned_q = dot(tq_ref[...], flip, NN).astype(bf16)
    turned_k = dot(tk_ref[...], flip, NN).astype(bf16)
    across = (((0,), (1,)), ((), ()))
    rel_ref[...] = (dot(turned_q, wq_ref[...], across) + dot(turned_k, wk_ref[...], across)).astype(bf16)


def attn_unpack(me, even, odd, wq, wk, rows, places):
    cols = 2 * even.shape[0]
    width = wq.shape[0]
    share, spots = width // rows, places // rows
    shape = jax.ShapeDtypeStruct((share, width), f32)
    return pl.pallas_call(
        functools.partial(attn_unpack_kernel, cols, spots),
        in_specs=[scalar()] + [pl.BlockSpec(memory_space=pltpu.VMEM)] * 4,
        out_specs=[pl.BlockSpec(memory_space=pltpu.VMEM)] * 4,
        out_shape=[shape] * 3 + [jax.ShapeDtypeStruct((spots, width), bf16)],
        scratch_shapes=[pltpu.VMEM((cols,) + even.shape[1:], f32), pltpu.VMEM((width, spots), bf16),
                        pltpu.VMEM((width, spots), bf16)],
        compiler_params=params(),
        name="attn_unpack",
    )(me, even, odd, wq, wk)


HEADS = 12
EPSILON = 1e-07


def norm_forward(value, gain, shift):
    center = value - jnp.mean(value, axis=-1, keepdims=True)
    scaled = lax.rsqrt(jnp.mean(center * center, axis=-1, keepdims=True) + EPSILON)
    normed = center * scaled
    return (normed * gain + shift, normed, scaled)


def norm_backward(grad_out, normed, scaled, gain):
    grad_normed = grad_out * gain
    inner = grad_normed - jnp.mean(grad_normed, axis=-1, keepdims=True)
    inner = inner - normed * jnp.mean(grad_normed * normed, axis=-1, keepdims=True)
    return (scaled * inner, jnp.sum(grad_out * normed, axis=0), jnp.sum(grad_out, axis=0))


def gelu_exact(value):
    return jax.nn.gelu(value, approximate=False)


def mul(a, b, form=NN):
    return lax.dot_general(a, b, form, preferred_element_type=f32)


def swap(x, axis, k):
    return lax.ppermute(x, axis, [(i, i ^ k) for i in range(lax.axis_size(axis))])


def gather(x):
    even = jnp.stack([x] + [swap(x, "seq", k) for k in range(2, lax.axis_size("seq"), 2)])
    return even, swap(even, "seq", 1)


def gather_small(x, axis):
    count = lax.axis_size(axis)
    out = jnp.zeros((count,) + x.shape, x.dtype)
    out = lax.dynamic_update_slice_in_dim(out, x[None], lax.axis_index(axis), 0)
    k = 1
    while k < count:
        out = out + swap(out, axis, k)
        k *= 2
    return out


def deal(x, axis):
    return [x[0]] + [swap(x[k], axis, k) for k in range(1, lax.axis_size(axis))]


def sum_small(x):
    for axis in ("seq", "row"):
        k = 1
        while k < lax.axis_size(axis):
            x = x + swap(x, axis, k)
            k *= 2
    return x


def relative_tables(flipped, length, first):
    span = flipped.shape[0] // 2
    side = length - span
    shape = (side, flipped.shape[1])
    padded = jnp.concatenate(
        [jnp.broadcast_to(flipped[:1], shape), flipped, jnp.broadcast_to(flipped[-1:], shape)], axis=0
    )
    near = lax.dynamic_slice_in_dim(padded, length - BLK - first, length + BLK, 0)
    far = lax.dynamic_slice_in_dim(padded, first, length + BLK, 0)
    return near, far


def flip_rows(count):
    r = lax.broadcasted_iota(jnp.int32, (count, count), 0)
    c = lax.broadcasted_iota(jnp.int32, (count, count), 1)
    return (r + c == count - 1).astype(bf16)


def reduced(g):
    part = lax.psum_scatter(g.astype(bf16), "row", scatter_dimension=0, tiled=True)
    return lax.psum(part, "seq").astype(f32)


def on_device(
    hidden, segments, rel_embed, query_weight, key_weight, value_weight, output_weight, up_weight, down_weight,
    norm1_gain, norm1_bias, norm2_gain, norm2_bias, cotangent,
):
    tokens, width = hidden.shape[1:]
    places = rel_embed.shape[0]
    units = up_weight.shape[1]
    heads = HEADS
    pairs = width // PAIR
    scale = 1.0 / math.sqrt(3.0 * (width // heads))
    inputs = hidden[0]
    cols, rows = lax.axis_size("seq"), lax.axis_size("row")
    length = cols * tokens
    place = lax.axis_index("seq")
    first = place * tokens
    me = place.reshape(1).astype(jnp.int32)
    row = lax.axis_index("row").reshape(1).astype(jnp.int32)
    share = width // rows
    dealt = (units // (rows * cols)) % 16 == 0 and places // rows == BLK

    in_even, in_odd = gather(inputs)
    row_segs = gather_small(segments, "seq").reshape(1, length)
    own_segs = segments.reshape(tokens, 1)
    rel_flip = mul(flip_rows(places), rel_embed).astype(bf16)
    qr_near, qr_far = relative_tables(mul(rel_flip, query_weight).astype(bf16), length, first)
    kr_near, kr_far = relative_tables(mul(rel_flip, key_weight).astype(bf16), length, first)
    half = (length // 2, width)
    q, k, v = project_rows(in_even.reshape(half), in_odd.reshape(half), query_weight, key_weight, value_weight)

    probs, ctx, lse = forward_attention(me, q, k, v, kr_near, qr_far, own_segs, row_segs, scale)

    ctx_low = ctx.astype(bf16)
    h1 = inputs.astype(f32) + mul(ctx_low, output_weight)
    normed1, unit1, scaled1 = norm_forward(h1, norm1_gain, norm1_bias)
    normed1_low = normed1.astype(bf16)
    inner = mul(normed1_low, up_weight)
    active, gelu_back = jax.vjp(gelu_exact, inner)
    active_low = active.astype(bf16)
    result, unit2, scaled2 = norm_forward(normed1 + mul(active_low, down_weight), norm2_gain, norm2_bias)
    output = result.astype(bf16)[None]
    cot = cotangent[0].astype(f32)
    d_h2, g_gain2, g_bias2 = norm_backward(cot, unit2, scaled2, norm2_gain)
    d_branch = d_h2.astype(bf16)
    d_inner = gelu_back(mul(d_branch, down_weight, NT))[0].astype(bf16)
    d_normed1 = d_h2 + mul(d_inner, up_weight, NT)
    d_h1, g_gain1, g_bias1 = norm_backward(d_normed1, unit1, scaled1, norm1_gain)
    d_attn = d_h1.astype(bf16)
    d_ctx = mul(d_attn, output_weight, NT).astype(bf16)
    row_dot = jnp.sum((d_ctx.astype(f32) * ctx).reshape(tokens, heads, width // heads), axis=2)

    stats = jnp.concatenate([lse[:, :2].reshape(heads, tokens), row_dot.T], axis=0)
    stats = gather_small(stats, "seq").reshape(cols, 2, pairs, 2, tokens).transpose(1, 2, 3, 0, 4)
    lse_all, rdot_all = jnp.pad(stats.reshape(2, pairs, 2, length), ((0, 0), (0, 0), (0, 6), (0, 0)))
    probs_t = other_probs(me, k, q, qr_near, kr_far, own_segs, row_segs, lse_all, scale)
    attn_even, attn_odd = gather(d_attn)
    dctx_all = jnp.concatenate([attn_even.reshape(half), attn_odd.reshape(half)], axis=0)
    dctx_all = mul(dctx_all, output_weight, NT).astype(bf16)
    dq, q_table = query_grads(me, probs, d_ctx, ctx, v, q, k, kr_near, places, scale)
    dk, dv, k_table = key_grads(me, probs_t, v, dctx_all, rdot_all, k, q, qr_near, places, scale)
    grad_in = d_h1 + mul(dq, query_weight, NT) + mul(dk, key_weight, NT) + mul(dv, value_weight, NT)

    if dealt:
        chunk = units // cols
        branch_even, branch_odd = gather(jnp.concatenate([normed1_low, d_branch], axis=1))
        parts = deal(pack(me, active_low, d_inner, ctx, cols, rows), "seq")
        sums = layer_sums(row, branch_even, branch_odd, attn_even, attn_odd, parts, rows, chunk)
        sums = sum(x.astype(f32) for x in deal(sums, "row")).astype(bf16)
        g_down, g_up, g_output = layer_unpack(me, *gather(sums), rows, width, units)
        q_parts = deal_dynamic(q_table, cols)
        k_parts = deal_dynamic(k_table, cols)
        sums = attn_sums(row, in_even, in_odd, rel_flip, q_parts, k_parts, rows)
        sums = sum(x.astype(f32) for x in deal(sums, "row")).astype(bf16)
        g_query, g_key, g_value, g_rel = attn_unpack(me, *gather(sums), query_weight, key_weight, rows, places)
        blocks = [g_rel] + [swap(g_rel, "row", k) for k in range(1, rows)]
        out = jnp.zeros((rows,) + g_rel.shape, bf16)
        for k, block in enumerate(blocks):
            out = lax.dynamic_update_slice_in_dim(out, block[None], rows - 1 - (row[0] ^ k), 0)
        g_rel = out.reshape(places, width).astype(f32)
    else:
        g_down = reduced(mul(active_low, d_branch, TN))
        g_up = reduced(mul(normed1_low, d_inner, TN))
        g_output = reduced(mul(ctx_low, d_attn, TN))
        across = (((0,), (1,)), ((), ()))
        d_kr, d_qr = q_table[:, :places], k_table[:, :places]
        g_query = reduced(mul(inputs, dq, TN) + mul(rel_flip, d_qr, across))
        g_key = reduced(mul(inputs, dk, TN) + mul(rel_flip, d_kr, across))
        g_value = reduced(mul(inputs, dv, TN))
        g_rel = mul(d_qr, query_weight, across) + mul(d_kr, key_weight, across)
        g_rel = lax.psum(mul(flip_rows(places), g_rel.astype(bf16)).astype(bf16), ("seq", "row")).astype(f32)

    small = sum_small(jnp.stack([g_gain1, g_bias1, g_gain2, g_bias2]))
    small = lax.dynamic_slice_in_dim(small, lax.axis_index("row") * share, share, 1)
    return (
        output, grad_in.astype(bf16)[None], g_query, g_key, g_value, g_output, g_up, g_down,
        small[0], small[1], small[2], small[3], g_rel,
    )


def deal_dynamic(x, cols):
    size = x.shape[0] // cols
    me = lax.axis_index("seq")
    parts = [lax.dynamic_slice_in_dim(x, (me ^ k) * size, size, 0) for k in range(cols)]
    return [parts[0]] + [swap(parts[k], "seq", k) for k in range(1, cols)]


def solution(mesh):
    split = P("row", "seq", None)
    return jax.shard_map(
        on_device,
        mesh=mesh,
        in_specs=(split, P("row", "seq")) + (P(),) * 11 + (split,),
        out_specs=(split, split) + (P("row", None),) * 6 + (P("row"),) * 4 + (P(),),
        check_vma=False,
    )
```

time: 682 us -> 317 us (0.46)
  waiting for transfers between devices: 439 us -> 99.8 us
  starting transfers between devices: 0.67 us -> 63.6 us
  blocking collectives: 54.6 us -> 0 us
  matrix products: 60.1 us -> 21.3 us
  Pallas kernels: 49 us -> 82.2 us
  local copies, waits for them, and re-layouts: 49.9 us -> 29.7 us
  between operations: 15.6 us -> 1.65 us
    reduce_scatter x3 -> x0, waiting for transfers between devices: 203 us -> none  [on_device(): lax.psum_scatter(g.astype(bf16), 'row', scatter_dimension=0, tiled=True)]
    psum x2 -> x0, waiting for transfers between devices: 175 us -> none  [the longest x1 104 us: on_device(): lax.psum(g_rel.astype(bf16), ('seq', 'row')).astype(f32)]
    ppermute x0 -> x61, waiting for transfers between devices: none -> 99.8 us  [swap(): lax.ppermute(x, axis, [(i, i ^ k) for i in range(lax.axis_size(axis))])]
    ppermute x0 -> x61, starting transfers between devices: none -> 63.6 us  [swap(): lax.ppermute(x, axis, [(i, i ^ k) for i in range(lax.axis_size(axis))])]
    unnamed x13 -> x0, waiting for transfers between devices: 59.5 us -> none
    dot_general x29 -> x13, matrix products: 60.1 us -> 21.3 us  [mul(): return lax.dot_general(a, b, form, preferred_element_type=f32)]
    pallas_call x0 -> x6, Pallas kernels: none -> 32.1 us  [the longest x1 9.65 us: project_rows(): pl.pallas_call(project_kernel, grid=(width // PAIR,), in_specs=[full((hal...]
    all_gather x3 -> x0, blocking collectives: 31.6 us -> none  [gather(): return lax.all_gather(a, 'seq', axis=axis, tiled=True)]
  transfers between devices with their start and end apart: 10 -> 61, of which waited for: 9 -> 19; matrix products, arithmetic and copies ran while one was open for 11% -> 14% of each run, Pallas kernels for 3% -> 17%
where the time goes in v2:
time: 317 us; the launch traced here: 314 us
  waiting for transfers between devices  99.8 us (31%)
  Pallas kernels  82.2 us (26%)
  starting transfers between devices  63.6 us (20%)
  local copies, waits for them, and re-layouts  29.7 us (9%)
  matrix products  21.3 us (7%)
  other arithmetic  16.2 us (5%)
    ppermute x61, waiting for transfers between devices, swap(): lax.ppermute(x, axis, [(i, i ^ k) for i in range(lax.axis_size(axis))])  99.8 us
    ppermute x61, starting transfers between devices, swap(): lax.ppermute(x, axis, [(i, i ^ k) for i in range(lax.axis_size(axis))])  63.6 us
    dot_general x13, matrix products, mul(): return lax.dot_general(a, b, form, preferred_element_type=f32)  21.3 us
    pallas_call x1, Pallas kernels, forward_attention(): pl.pallas_call(functools.partial(forward_kernel, scale, length), grid=(pa...  15.2 us
    pallas_call x1, Pallas kernels, other_probs(): pl.pallas_call(functools.partial(other_probs_kernel, scale, length), grid...  12 us
    pallas_call x1, Pallas kernels, key_grads(): pl.pallas_call(functools.partial(key_grad_kernel, scale, length), grid=(p...  11.6 us
    pallas_call x1, Pallas kernels, query_grads(): pl.pallas_call(functools.partial(query_grad_kernel, scale, length), grid=...  11.3 us
    pallas_call x1, Pallas kernels, project_rows(): pl.pallas_call(project_kernel, grid=(width // PAIR,), in_specs=[full((hal...  9.65 us
  transfers between devices with their start and end apart: 61, of which 19 were waited for; matrix products, arithmetic and copies ran while one was open for 14% of the time, Pallas kernels for 17%

profile of v2, /device:TPU:0, one launch (start us, length us, event | category | flops | bytes accessed | tf_op | source)
XLA Modules:
  0.0 314.4 jit_solution(11375638427505425080)
XLA Ops:
  0.7 4.0 %collective-permute-start.2 = (bf16[128,768]{1,0:T(8,128)(2,1)}, bf16[128,768]{1,0:T(8,128)(2,1)S(1)}, u32[]{:S(2)}, u32[]{:S(2)}) collective-permute-start(bf16[128,768]{1,0:T(8,128)(2,1)} %bitcast.165), channel_id=1, source_target_pairs={{0,24},{4,28},{8,16},{12,20},{16,8},{20,12},{24,0},{28,4},{1,25},{... | collective-permute-start | bytes 589832 | tf_op jit(solution)/shard_map/ppermute | solution.py:528
  5.9 1.7 convolution_convert_fusion.3.rel_ref
  10.2 2.1 pad_maximum_fusion
  12.5 1.9 pad_maximum_fusion.1
  14.4 1.9 collective-permute-start.5
  18.4 6.2 %constant_dynamic-slice_fusion.18 = (bf16[1152,768]{1,0:T(8,128)(2,1)}, bf16[1152,768]{1,0:T(8,128)(2,1)}, bf16[1152,768]{1,0:T(8,128)(2,1)}, bf16[1152,768]{1,0:T(8,128)(2,1)}) fusion(bf16[2048,768]{1,0:T(8,128)(2,1)} %pad_maximum_fusion, s32[]{:T(128)S(6)} %select_n.60, s32[]{:T(128)S(6)} %select_n.59, bf16[2048,768]{1,0:T(8,128)(2,1)} %pad_maximum_fusion.1), kind=kLoop, calls=%fused_computation.123 | loop fusion | bytes 14155784 | tf_op jit(solution)/shard_map/dynamic_slice | solution.py:568
  24.6 1.7 collective-permute-start.6
  29.8 9.7 %project.1 = (bf16[1024,768]{1,0:T(8,128)(2,1)}, bf16[1024,768]{1,0:T(8,128)(2,1)}, bf16[1024,768]{1,0:T(8,128)(2,1)}) custom-call(bf16[512,768]{1,0:T(8,128)(2,1)} %bitcast.155, bf16[512,768]{1,0:T(8,128)(2,1)} %bitcast.161, bf16[768,768]{1,0:T(8,128)(2,1)} %wq_ref.3, bf16[768,768]{1,0:T(8,128)(2,1)} %wk_ref.3, bf16[768,768]{1,0:T(8,128)(2,1)} %wv_ref.1), custom_call_target="tpu_custom_call" | custom-call | tf_op jit(solution)/shard_map/project/pallas_call | solution.py:283
  39.5 15.2 %attend.1 = (bf16[12,128,1024]{2,1,0:T(8,128)(2,1)}, f32[128,768]{1,0:T(8,128)}, f32[6,8,128]{2,1,0:T(8,128)}) custom-call(s32[1]{0:T(128)} %bitcast.1.me_ref, bf16[1024,768]{1,0:T(8,128)(2,1)} %get-tuple-element.31.q_ref, bf16[1024,768]{1,0:T(8,128)(2,1)} %get-tuple-element.32.k_ref, bf16[1024,768]{1,0:T(8,128)(2,1)} %get-tuple-element.33.v_ref, ...), custom_call_target="tpu_custom_call" | custom-call | tf_op jit(solution)/shard_map/attend/pallas_call | solution.py:183
  56.5 4.3 %multiply_convert_fusion = (bf16[128,3072]{1,0:T(8,128)(2,1)S(1)}, f32[128,3072]{1,0:T(8,128)S(1)}, f32[128,3072]{1,0:T(8,128)S(1)}) fusion(bf16[128,768]{1,0:T(8,128)(2,1)S(1)} %fusion.27, bf16[768,3072]{1,0:T(8,128)(2,1)S(1)} %bitcast.157), kind=kOutput, calls=%fused_computation.10 | convolution fusion | flops 629538816 | bytes 8847360 | tf_op jit(solution)/shard_map/dot_general | solution.py:524
  63.2 1.8 add_convert_fusion.din_ref
  65.0 1.9 multiply_reduce_fusion
  69.2 1.5 collective-permute-start.12
  71.1 1.6 collective-permute-start.10
  74.7 1.6 collective-permute-start.37
  76.3 11.3 %query_grads.1 = (bf16[128,768]{1,0:T(8,128)(2,1)}, bf16[768,640]{1,0:T(8,128)(2,1)}) custom-call(s32[1]{0:T(128)} %bitcast.1.me_ref, bf16[12,128,1024]{2,1,0:T(8,128)(2,1)} %get-tuple-element.35.p_ref, bf16[128,768]{1,0:T(8,128)(2,1)} %get-tuple-element.115.dctx_ref, f32[128,768]{1,0:T(8,128)} %get-tuple-element.34.ctx_ref, ...), custom_call_target="tpu_custom_call" | custom-call | tf_op jit(solution)/shard_map/query_grads/pallas_call | solution.py:238
  88.1 1.7 collective-permute-start.35
  92.3 9.1 %collective-permute-done.8 = f32[8,24,128]{2,1,0:T(8,128)S(1)} collective-permute-done((f32[8,24,128]{2,1,0:T(8,128)S(1)}, f32[8,24,128]{2,1,0:T(8,128)S(1)}, u32[]{:S(2)}, u32[]{:S(2)}) %collective-permute-start.8) | collective-permute-done | bytes 98336 | tf_op jit(solution)/shard_map/ppermute | solution.py:528
  101.4 1.5 collective-permute-start.54
  105.1 1.6 collective-permute-start.9
  106.8 3.0 collective-permute-done.9
  110.6 12.0 %key_probs.1.p_ref = bf16[12,128,1024]{2,1,0:T(8,128)(2,1)} custom-call(s32[1]{0:T(128)} %bitcast.1.me_ref, bf16[1024,768]{1,0:T(8,128)(2,1)} %get-tuple-element.32.k_ref, bf16[1024,768]{1,0:T(8,128)(2,1)} %get-tuple-element.31.q_ref, bf16[1152,768]{1,0:T(8,128)(2,1)} %get-tuple-element.117.near_ref, bf16[1152,768]{1,0:T(8,128)(2,1)} %get-tuple-element.64.far_ref, ...), custom_call_target="tpu_custom_call" | custom-call | tf_op jit(solution)/shard_map/key_probs/pallas_call | solution.py:207
  122.7 1.6 collective-permute-start.15
  124.6 1.6 collective-permute-start.55
  127.8 4.1 %convolution_convert_fusion.dctx_ref = bf16[1024,768]{1,0:T(8,128)(2,1)} fusion(bf16[768,768]{1,0:T(8,128)(2,1)S(1)} %copy-done, bf16[512,768]{1,0:T(8,128)(2,1)} %bitcast.23, bf16[512,768]{1,0:T(8,128)(2,1)S(1)} %bitcast.160), kind=kOutput, calls=%fused_computation.3 | convolution fusion | flops 1211891712 | bytes 4325376 | tf_op jit(solution)/shard_map/dot_general | solution.py:524
  131.9 11.6 %key_grads.1 = (bf16[128,768]{1,0:T(8,128)(2,1)}, bf16[128,768]{1,0:T(8,128)(2,1)}, bf16[768,768]{1,0:T(8,128)(2,1)}) custom-call(s32[1]{0:T(128)} %bitcast.1.me_ref, bf16[12,128,1024]{2,1,0:T(8,128)(2,1)} %key_probs.1.p_ref, bf16[1024,768]{1,0:T(8,128)(2,1)} %get-tuple-element.33.v_ref, bf16[1024,768]{1,0:T(8,128)(2,1)} %convolution_convert_fusion.dctx_ref, ...), custom_call_target="tpu_custom_call" | custom-call | tf_op jit(solution)/shard_map/key_grads/pallas_call | solution.py:255
  145.0 1.8 collective-permute-start.19
  146.9 2.3 constant_dynamic-slice_fusion.1
  149.4 3.1 collective-permute-done.17.refs_4_
  153.1 1.6 collective-permute-start.22
  156.7 3.2 %pack.1 = bf16[8,864,128]{2,1,0:T(8,128)(2,1)} custom-call(s32[1]{0:T(128)} %bitcast.1.me_ref, bf16[128,3072]{1,0:T(8,128)(2,1)} %copy-done.15, bf16[128,3072]{1,0:T(8,128)(2,1)} %copy-done.14, f32[128,768]{1,0:T(8,128)} %get-tuple-element.34.ctx_ref), custom_call_target="tpu_custom_call" | custom-call | tf_op jit(solution)/shard_map/pack/pallas_call | solution.py:322
  159.9 3.5 %collective-permute-done.20.refs_7_ = bf16[96,640]{1,0:T(8,128)(2,1)} collective-permute-done((bf16[96,640]{1,0:T(8,128)(2,1)}, bf16[96,640]{1,0:T(8,128)(2,1)}, u32[]{:S(2)}, u32[]{:S(2)}) %collective-permute-start.20) | collective-permute-done | bytes 122912 | tf_op jit(solution)/shard_map/ppermute | solution.py:528
  163.4 2.2 collective-permute-start.24
  165.7 2.2 collective-permute-start.26
  168.8 2.4 slice_bitcast_fusion.4
  171.2 5.6 %collective-permute-done.24.refs_12_ = bf16[96,768]{1,0:T(8,128)(2,1)S(1)} collective-permute-done((bf16[96,768]{1,0:T(8,128)(2,1)}, bf16[96,768]{1,0:T(8,128)(2,1)S(1)}, u32[]{:S(2)}, u32[]{:S(2)}) %collective-permute-start.24) | collective-permute-done | bytes 147488 | tf_op jit(solution)/shard_map/ppermute | solution.py:528
  176.8 1.8 collective-permute-done.25.refs_13_
  178.6 1.9 collective-permute-start.40
  180.5 1.7 collective-permute-start.56
  182.2 4.5 %attn_sums.1 = bf16[4,256,384]{2,1,0:T(8,128)(2,1)} custom-call(s32[1]{0:T(128)} %bitcast.26.row_ref.me_ref, bf16[4,128,768]{2,1,0:T(8,128)(2,1)} %copy-done.5, bf16[4,128,768]{2,1,0:T(8,128)(2,1)} %copy-done.13, bf16[512,768]{1,0:T(8,128)(2,1)} %copy-done.22, bf16[96,640]{1,0:T(8,128)(2,1)} %get-tuple-element.94.refs_0_, ...), custom_call_target="tpu_custom_call" | custom-call | tf_op jit(solution)/shard_map/attn_sums/pallas_call | solution.py:449
  186.7 1.9 slice_bitcast_fusion.14
  188.7 2.6 collective-permute-start.30
  193.8 2.0 collective-permute-start.42
  195.7 2.9 collective-permute-done.30
  198.6 10.5 %collective-permute-done.29 = bf16[256,384]{1,0:T(8,128)(2,1)} collective-permute-done((bf16[256,384]{1,0:T(8,128)(2,1)}, bf16[256,384]{1,0:T(8,128)(2,1)}, u32[]{:S(2)}, u32[]{:S(2)}) %collective-permute-start.29) | collective-permute-done | bytes 196640 | tf_op jit(solution)/shard_map/ppermute | solution.py:528
  209.1 3.3 %collective-permute-start.44 = (bf16[864,128]{1,0:T(8,128)(2,1)S(1)}, bf16[864,128]{1,0:T(8,128)(2,1)S(1)}, u32[]{:S(2)}, u32[]{:S(2)}) collective-permute-start(bf16[864,128]{1,0:T(8,128)(2,1)S(1)} %get-tuple-element.69), channel_id=1, source_target_pairs={{0,24},{4,28},{8,16},{12,20},{16,8},{20,12},{24,0},{28,4},{1,25},{... | collective-permute-start | bytes 663560 | tf_op jit(solution)/shard_map/ppermute | solution.py:528
  213.9 2.1 collective-permute-start.33
  216.0 2.7 collective-permute-done.44.refs_6_
  218.7 1.6 collective-permute-start.32
  220.3 2.7 collective-permute-done.45.refs_7_
  223.8 5.6 %layer_sums.1 = bf16[4,432,384]{2,1,0:T(8,128)(2,1)} custom-call(s32[1]{0:T(128)} %bitcast.26.row_ref.me_ref, bf16[4,128,1536]{2,1,0:T(8,128)(2,1)} %copy-done.7, bf16[4,128,1536]{2,1,0:T(8,128)(2,1)} %collective-permute-done.38.odd_ref, bf16[4,128,768]{2,1,0:T(8,128)(2,1)} %copy-done.11, bf16[4,128,768]{2,1,0:T(8,128)(2,1)} %collective-permute-done.13.attn_odd_ref, ...), custom_call_target="tpu_custom_call" | custom-call | tf_op jit(solution)/shard_map/layer_sums/pallas_call | solution.py:367
  230.8 2.7 collective-permute-start.48
  233.5 1.8 collective-permute-start.47
  236.6 6.9 %collective-permute-done.48 = bf16[432,384]{1,0:T(8,128)(2,1)S(1)} collective-permute-done((bf16[432,384]{1,0:T(8,128)(2,1)S(1)}, bf16[432,384]{1,0:T(8,128)(2,1)S(1)}, u32[]{:S(2)}, u32[]{:S(2)}) %collective-permute-start.48) | collective-permute-done | bytes 331808 | tf_op jit(solution)/shard_map/ppermute | solution.py:528
  243.5 20.6 %collective-permute-done.47 = bf16[432,384]{1,0:T(8,128)(2,1)S(1)} collective-permute-done((bf16[432,384]{1,0:T(8,128)(2,1)S(1)}, bf16[432,384]{1,0:T(8,128)(2,1)S(1)}, u32[]{:S(2)}, u32[]{:S(2)}) %collective-permute-start.47) | collective-permute-done | bytes 331808 | tf_op jit(solution)/shard_map/ppermute | solution.py:528
  265.2 1.8 collective-permute-start.51
  270.0 7.0 %collective-permute-done.51 = bf16[432,384]{1,0:T(8,128)(2,1)S(1)} collective-permute-done((bf16[432,384]{1,0:T(8,128)(2,1)S(1)}, bf16[432,384]{1,0:T(8,128)(2,1)S(1)}, u32[]{:S(2)}, u32[]{:S(2)}) %collective-permute-start.51) | collective-permute-done | bytes 331808 | tf_op jit(solution)/shard_map/ppermute | solution.py:528
  277.0 5.6 %collective-permute-done.50 = bf16[432,384]{1,0:T(8,128)(2,1)S(1)} collective-permute-done((bf16[432,384]{1,0:T(8,128)(2,1)S(1)}, bf16[432,384]{1,0:T(8,128)(2,1)S(1)}, u32[]{:S(2)}, u32[]{:S(2)}) %collective-permute-start.50) | collective-permute-done | bytes 331808 | tf_op jit(solution)/shard_map/ppermute | solution.py:528
  285.5 4.7 %attn_unpack.1 = (f32[192,768]{1,0:T(8,128)}, f32[192,768]{1,0:T(8,128)}, f32[192,768]{1,0:T(8,128)}, bf16[128,768]{1,0:T(8,128)(2,1)}) custom-call(s32[1]{0:T(128)} %bitcast.1.me_ref, bf16[4,256,384]{2,1,0:T(8,128)(2,1)} %copy-done.12, bf16[4,256,384]{2,1,0:T(8,128)(2,1)} %copy-done.21, bf16[768,768]{1,0:T(8,128)(2,1)} %wq_ref.3, bf16[768,768]{1,0:T(8,128)(2,1)} %wk_ref.3), custom_call_target="tpu_custom_call" | custom-call | tf_op jit(solution)/shard_map/attn_unpack/pallas_call | solution.py:489
  290.2 2.7 collective-permute-start.59
  292.8 1.7 collective-permute-start.60
  295.6 5.7 %collective-permute-done.58 = bf16[128,768]{1,0:T(8,128)(2,1)S(1)} collective-permute-done((bf16[128,768]{1,0:T(8,128)(2,1)}, bf16[128,768]{1,0:T(8,128)(2,1)S(1)}, u32[]{:S(2)}, u32[]{:S(2)}) %collective-permute-start.58) | collective-permute-done | bytes 196640 | tf_op jit(solution)/shard_map/ppermute | solution.py:528
  301.3 6.2 %collective-permute-done.59 = bf16[128,768]{1,0:T(8,128)(2,1)S(1)} collective-permute-done((bf16[128,768]{1,0:T(8,128)(2,1)}, bf16[128,768]{1,0:T(8,128)(2,1)S(1)}, u32[]{:S(2)}, u32[]{:S(2)}) %collective-permute-start.59) | collective-permute-done | bytes 196640 | tf_op jit(solution)/shard_map/ppermute | solution.py:528
  310.0 4.4 %layer_unpack.1 = (f32[768,768]{1,0:T(8,128)}, f32[192,3072]{1,0:T(8,128)}, f32[192,768]{1,0:T(8,128)}) custom-call(s32[1]{0:T(128)} %bitcast.1.me_ref, bf16[4,432,384]{2,1,0:T(8,128)(2,1)} %copy-done.8, bf16[4,432,384]{2,1,0:T(8,128)(2,1)} %copy-done.18), custom_call_target="tpu_custom_call" | custom-call | tf_op jit(solution)/shard_map/layer_unpack/pallas_call | solution.py:399
  (285 shorter events, 48.8 us)
Async XLA Ops:
  0.6 54.0 %copy-start = (bf16[768,768]{1,0:T(8,128)(2,1)S(1)}, bf16[768,768]{1,0:T(8,128)(2,1)}, u32[]{:S(2)}) copy-start(bf16[768,768]{1,0:T(8,128)(2,1)} %param.20) | copy-start | bytes 3538948
  0.7 15.7 %collective-permute-start.2 = (bf16[128,768]{1,0:T(8,128)(2,1)}, bf16[128,768]{1,0:T(8,128)(2,1)S(1)}, u32[]{:S(2)}, u32[]{:S(2)}) collective-permute-start(bf16[128,768]{1,0:T(8,128)(2,1)} %bitcast.165), channel_id=1, source_target_pairs={{0,24},{4,28},{8,16},{12,20},{16,8},{20,12},{24,0},{28,4},{1,25},{... | collective-permute-start | bytes 589832 | tf_op jit(solution)/shard_map/ppermute | solution.py:528
  4.6 11.7 %collective-permute-start.1 = (bf16[128,768]{1,0:T(8,128)(2,1)}, bf16[128,768]{1,0:T(8,128)(2,1)S(1)}, u32[]{:S(2)}, u32[]{:S(2)}) collective-permute-start(bf16[128,768]{1,0:T(8,128)(2,1)} %bitcast.166), channel_id=1, source_target_pairs={{0,16},{4,20},{8,24},{12,28},{16,0},{20,4},{24,8},{28,12},{1,17},{... | collective-permute-start | bytes 589832 | tf_op jit(solution)/shard_map/ppermute | solution.py:528
  5.1 11.2 %collective-permute-start = (bf16[128,768]{1,0:T(8,128)(2,1)}, bf16[128,768]{1,0:T(8,128)(2,1)S(1)}, u32[]{:S(2)}, u32[]{:S(2)}) collective-permute-start(bf16[128,768]{1,0:T(8,128)(2,1)} %bitcast.167), channel_id=1, source_target_pairs={{0,8},{4,12},{8,0},{12,4},{16,24},{20,28},{24,16},{28,20},{1,9},{5... | collective-permute-start | bytes 589832 | tf_op jit(solution)/shard_map/ppermute | solution.py:528
  5.9 8.5 %collective-permute-start.4 = (s32[8,1,128]{2,1,0:T(1,128)S(1)}, s32[8,1,128]{2,1,0:T(1,128)S(1)}, u32[]{:S(2)}, u32[]{:S(2)}) collective-permute-start(s32[8,1,128]{2,1,0:T(1,128)S(1)} %constant_dynamic-update-slice_fusion.2), channel_id=1, source_target_pairs={{0,4},{4,0},{8,12},{12,8},{16,20},{20,16},{24,28},{28,24},{1,5},{5... | collective-permute-start | bytes 12296 | tf_op jit(solution)/shard_map/ppermute | solution.py:528
  14.4 10.2 %collective-permute-start.5 = (s32[8,1,128]{2,1,0:T(1,128)S(1)}, s32[8,1,128]{2,1,0:T(1,128)S(1)}, u32[]{:S(2)}, u32[]{:S(2)}) collective-permute-start(s32[8,1,128]{2,1,0:T(1,128)S(1)} %constant_dynamic-update-slice_fusion.1), channel_id=1, source_target_pairs={{0,8},{4,12},{8,0},{12,4},{16,24},{20,28},{24,16},{28,20},{1,9},{5... | collective-permute-start | bytes 12296 | tf_op jit(solution)/shard_map/ppermute | solution.py:528
  18.1 10.8 %collective-permute-start.3 = (bf16[4,128,768]{2,1,0:T(8,128)(2,1)S(1)}, bf16[4,128,768]{2,1,0:T(8,128)(2,1)S(1)}, u32[]{:S(2)}, u32[]{:S(2)}) collective-permute-start(bf16[4,128,768]{2,1,0:T(8,128)(2,1)S(1)} %pad_maximum_fusion.4.even_ref), channel_id=1, source_target_pairs={{0,4},{4,0},{8,12},{12,8},{16,20},{20,16},{24,28},{28,24},{1,5},{5... | collective-permute-start | bytes 2359304 | tf_op jit(solution)/shard_map/ppermute | solution.py:528
  24.6 3.7 %collective-permute-start.6 = (s32[8,1,128]{2,1,0:T(1,128)S(1)}, s32[8,1,128]{2,1,0:T(1,128)S(1)}, u32[]{:S(2)}, u32[]{:S(2)}) collective-permute-start(s32[8,1,128]{2,1,0:T(1,128)S(1)} %add.177), channel_id=1, source_target_pairs={{0,16},{4,20},{8,24},{12,28},{16,0},{20,4},{24,8},{28,12},{1,17},{... | collective-permute-start | bytes 12296 | tf_op jit(solution)/shard_map/ppermute | solution.py:528
  69.2 18.9 %collective-permute-start.12 = (bf16[128,768]{1,0:T(8,128)(2,1)S(1)}, bf16[128,768]{1,0:T(8,128)(2,1)S(1)}, u32[]{:S(2)}, u32[]{:S(2)}) collective-permute-start(bf16[128,768]{1,0:T(8,128)(2,1)S(1)} %get-tuple-element.60), channel_id=1, source_target_pairs={{0,24},{4,28},{8,16},{12,20},{16,8},{20,12},{24,0},{28,4},{1,25},{... | collective-permute-start | bytes 589832 | tf_op jit(solution)/shard_map/ppermute | solution.py:528
  70.7 19.1 %collective-permute-start.11 = (bf16[128,768]{1,0:T(8,128)(2,1)S(1)}, bf16[128,768]{1,0:T(8,128)(2,1)S(1)}, u32[]{:S(2)}, u32[]{:S(2)}) collective-permute-start(bf16[128,768]{1,0:T(8,128)(2,1)S(1)} %get-tuple-element.60), channel_id=1, source_target_pairs={{0,16},{4,20},{8,24},{12,28},{16,0},{20,4},{24,8},{28,12},{1,17},{... | collective-permute-start | bytes 589832 | tf_op jit(solution)/shard_map/ppermute | solution.py:528
  71.1 18.7 %collective-permute-start.10 = (bf16[128,768]{1,0:T(8,128)(2,1)S(1)}, bf16[128,768]{1,0:T(8,128)(2,1)S(1)}, u32[]{:S(2)}, u32[]{:S(2)}) collective-permute-start(bf16[128,768]{1,0:T(8,128)(2,1)S(1)} %get-tuple-element.60), channel_id=1, source_target_pairs={{0,8},{4,12},{8,0},{12,4},{16,24},{20,28},{24,16},{28,20},{1,9},{5... | collective-permute-start | bytes 589832 | tf_op jit(solution)/shard_map/ppermute | solution.py:528
  74.6 13.0 %collective-permute-start.7 = (f32[8,24,128]{2,1,0:T(8,128)S(1)}, f32[8,24,128]{2,1,0:T(8,128)S(1)}, u32[]{:S(2)}, u32[]{:S(2)}) collective-permute-start(f32[8,24,128]{2,1,0:T(8,128)S(1)} %constant_dynamic-update-slice_fusion), channel_id=1, source_target_pairs={{0,4},{4,0},{8,12},{12,8},{16,20},{20,16},{24,28},{28,24},{1,5},{5... | collective-permute-start | bytes 294920 | tf_op jit(solution)/shard_map/ppermute | solution.py:528
  74.7 48.0 %collective-permute-start.37 = (bf16[128,1536]{1,0:T(8,128)(2,1)}, bf16[128,1536]{1,0:T(8,128)(2,1)S(1)}, u32[]{:S(2)}, u32[]{:S(2)}) collective-permute-start(bf16[128,1536]{1,0:T(8,128)(2,1)} %get-tuple-element.101), channel_id=1, source_target_pairs={{0,24},{4,28},{8,16},{12,20},{16,8},{20,12},{24,0},{28,4},{1,25},{... | collective-permute-start | bytes 1179656 | tf_op jit(solution)/shard_map/ppermute | solution.py:528
  87.6 36.7 %collective-permute-start.36 = (bf16[128,1536]{1,0:T(8,128)(2,1)}, bf16[128,1536]{1,0:T(8,128)(2,1)}, u32[]{:S(2)}, u32[]{:S(2)}) collective-permute-start(bf16[128,1536]{1,0:T(8,128)(2,1)} %get-tuple-element.101), channel_id=1, source_target_pairs={{0,16},{4,20},{8,24},{12,28},{16,0},{20,4},{24,8},{28,12},{1,17},{... | collective-permute-start | bytes 1179656 | tf_op jit(solution)/shard_map/ppermute | solution.py:528
  88.1 36.5 %collective-permute-start.35 = (bf16[128,1536]{1,0:T(8,128)(2,1)}, bf16[128,1536]{1,0:T(8,128)(2,1)}, u32[]{:S(2)}, u32[]{:S(2)}) collective-permute-start(bf16[128,1536]{1,0:T(8,128)(2,1)} %get-tuple-element.101), channel_id=1, source_target_pairs={{0,8},{4,12},{8,0},{12,4},{16,24},{20,28},{24,16},{28,20},{1,9},{5... | collective-permute-start | bytes 1179656 | tf_op jit(solution)/shard_map/ppermute | solution.py:528
  89.8 2.0 collective-permute-start.53
  89.8 11.6 %collective-permute-start.8 = (f32[8,24,128]{2,1,0:T(8,128)S(1)}, f32[8,24,128]{2,1,0:T(8,128)S(1)}, u32[]{:S(2)}, u32[]{:S(2)}) collective-permute-start(f32[8,24,128]{2,1,0:T(8,128)S(1)} %add_dynamic-update-slice_fusion), channel_id=1, source_target_pairs={{0,8},{4,12},{8,0},{12,4},{16,24},{20,28},{24,16},{28,20},{1,9},{5... | collective-permute-start | bytes 294920 | tf_op jit(solution)/shard_map/ppermute | solution.py:528
  91.8 36.0 %copy-start.11 = (bf16[4,128,768]{2,1,0:T(8,128)(2,1)}, bf16[4,128,768]{2,1,0:T(8,128)(2,1)S(1)}, u32[]{:S(2)}) copy-start(bf16[4,128,768]{2,1,0:T(8,128)(2,1)S(1)} %pad_maximum_fusion.5.attn_even_ref) | copy-start | bytes 2359300
  91.8 35.9 %collective-permute-start.13 = (bf16[4,128,768]{2,1,0:T(8,128)(2,1)S(1)}, bf16[4,128,768]{2,1,0:T(8,128)(2,1)}, u32[]{:S(2)}, u32[]{:S(2)}) collective-permute-start(bf16[4,128,768]{2,1,0:T(8,128)(2,1)S(1)} %pad_maximum_fusion.5.attn_even_ref), channel_id=1, source_target_pairs={{0,4},{4,0},{8,12},{12,8},{16,20},{20,16},{24,28},{28,24},{1,5},{5... | collective-permute-start | bytes 2359304 | tf_op jit(solution)/shard_map/ppermute | solution.py:528
  101.4 3.7 %collective-permute-start.54 = (f32[4,768]{1,0:T(4,128)S(1)}, f32[4,768]{1,0:T(4,128)S(1)}, u32[]{:S(2)}, u32[]{:S(2)}) collective-permute-start(f32[4,768]{1,0:T(4,128)S(1)} %fusion.36), channel_id=1, source_target_pairs={{0,8},{4,12},{8,0},{12,4},{16,24},{20,28},{24,16},{28,20},{1,9},{5... | collective-permute-start | bytes 36872 | tf_op jit(solution)/shard_map/ppermute | solution.py:528
  105.1 4.6 %collective-permute-start.9 = (f32[8,24,128]{2,1,0:T(8,128)S(1)}, f32[8,24,128]{2,1,0:T(8,128)S(1)}, u32[]{:S(2)}, u32[]{:S(2)}) collective-permute-start(f32[8,24,128]{2,1,0:T(8,128)S(1)} %add.190), channel_id=1, source_target_pairs={{0,16},{4,20},{8,24},{12,28},{16,0},{20,4},{24,8},{28,12},{1,17},{... | collective-permute-start | bytes 294920 | tf_op jit(solution)/shard_map/ppermute | solution.py:528
  109.7 34.3 %collective-permute-start.14 = (bf16[96,640]{1,0:T(8,128)(2,1)}, bf16[96,640]{1,0:T(8,128)(2,1)}, u32[]{:S(2)}, u32[]{:S(2)}) collective-permute-start(bf16[96,640]{1,0:T(8,128)(2,1)} %get-tuple-element.93), channel_id=1, source_target_pairs={{0,4},{4,0},{8,12},{12,8},{16,20},{20,16},{24,28},{28,24},{1,5},{5... | collective-permute-start | bytes 368648 | tf_op jit(solution)/shard_map/ppermute | solution.py:528
  122.7 22.3 %collective-permute-start.15 = (bf16[96,640]{1,0:T(8,128)(2,1)S(1)}, bf16[96,640]{1,0:T(8,128)(2,1)S(1)}, u32[]{:S(2)}, u32[]{:S(2)}) collective-permute-start(bf16[96,640]{1,0:T(8,128)(2,1)S(1)} %copy-done.53), channel_id=1, source_target_pairs={{0,8},{4,12},{8,0},{12,4},{16,24},{20,28},{24,16},{28,20},{1,9},{5... | collective-permute-start | bytes 368648 | tf_op jit(solution)/shard_map/ppermute | solution.py:528
  124.3 24.8 %collective-permute-start.16 = (bf16[96,640]{1,0:T(8,128)(2,1)S(1)}, bf16[96,640]{1,0:T(8,128)(2,1)S(1)}, u32[]{:S(2)}, u32[]{:S(2)}) collective-permute-start(bf16[96,640]{1,0:T(8,128)(2,1)S(1)} %copy-done.52), channel_id=1, source_target_pairs={{0,12},{4,8},{8,4},{12,0},{16,28},{20,24},{24,20},{28,16},{1,13},{... | collective-permute-start | bytes 368648 | tf_op jit(solution)/shard_map/ppermute | solution.py:528
  124.6 19.0 %collective-permute-start.55 = (f32[4,768]{1,0:T(4,128)S(1)}, f32[4,768]{1,0:T(4,128)S(1)}, u32[]{:S(2)}, u32[]{:S(2)}) collective-permute-start(f32[4,768]{1,0:T(4,128)S(1)} %fusion.67), channel_id=1, source_target_pairs={{0,16},{4,20},{8,24},{12,28},{16,0},{20,4},{24,8},{28,12},{1,17},{... | collective-permute-start | bytes 36872 | tf_op jit(solution)/shard_map/ppermute | solution.py:528
  127.7 95.5 %collective-permute-start.38 = (bf16[4,128,1536]{2,1,0:T(8,128)(2,1)S(1)}, bf16[4,128,1536]{2,1,0:T(8,128)(2,1)}, u32[]{:S(2)}, u32[]{:S(2)}) collective-permute-start(bf16[4,128,1536]{2,1,0:T(8,128)(2,1)S(1)} %pad_maximum_fusion.2.even_ref), channel_id=1, source_target_pairs={{0,4},{4,0},{8,12},{12,8},{16,20},{20,16},{24,28},{28,24},{1,5},{5... | collective-permute-start | bytes 4718600 | tf_op jit(solution)/shard_map/ppermute | solution.py:528
  143.6 8.9 %collective-permute-start.17 = (bf16[96,640]{1,0:T(8,128)(2,1)S(1)}, bf16[96,640]{1,0:T(8,128)(2,1)S(1)}, u32[]{:S(2)}, u32[]{:S(2)}) collective-permute-start(bf16[96,640]{1,0:T(8,128)(2,1)S(1)} %copy-done.51), channel_id=1, source_target_pairs={{0,16},{4,20},{8,24},{12,28},{16,0},{20,4},{24,8},{28,12},{1,17},{... | collective-permute-start | bytes 368648 | tf_op jit(solution)/shard_map/ppermute | solution.py:528
  144.1 10.7 %collective-permute-start.18 = (bf16[96,640]{1,0:T(8,128)(2,1)S(1)}, bf16[96,640]{1,0:T(8,128)(2,1)S(1)}, u32[]{:S(2)}, u32[]{:S(2)}) collective-permute-start(bf16[96,640]{1,0:T(8,128)(2,1)S(1)} %copy-done.50), channel_id=1, source_target_pairs={{0,20},{4,16},{8,28},{12,24},{16,4},{20,0},{24,12},{28,8},{1,21},{... | collective-permute-start | bytes 368648 | tf_op jit(solution)/shard_map/ppermute | solution.py:528
  145.0 10.8 %collective-permute-start.19 = (bf16[96,640]{1,0:T(8,128)(2,1)S(1)}, bf16[96,640]{1,0:T(8,128)(2,1)S(1)}, u32[]{:S(2)}, u32[]{:S(2)}) collective-permute-start(bf16[96,640]{1,0:T(8,128)(2,1)S(1)} %copy-done.49), channel_id=1, source_target_pairs={{0,24},{4,28},{8,16},{12,20},{16,8},{20,12},{24,0},{28,4},{1,25},{... | collective-permute-start | bytes 368648 | tf_op jit(solution)/shard_map/ppermute | solution.py:528
  149.1 16.5 %collective-permute-start.21 = (bf16[96,768]{1,0:T(8,128)(2,1)}, bf16[96,768]{1,0:T(8,128)(2,1)S(1)}, u32[]{:S(2)}, u32[]{:S(2)}) collective-permute-start(bf16[96,768]{1,0:T(8,128)(2,1)} %get-tuple-element.85), channel_id=1, source_target_pairs={{0,4},{4,0},{8,12},{12,8},{16,20},{20,16},{24,28},{28,24},{1,5},{5... | collective-permute-start | bytes 442376 | tf_op jit(solution)/shard_map/ppermute | solution.py:528
  153.1 12.5 %collective-permute-start.22 = (bf16[96,768]{1,0:T(8,128)(2,1)S(1)}, bf16[96,768]{1,0:T(8,128)(2,1)S(1)}, u32[]{:S(2)}, u32[]{:S(2)}) collective-permute-start(bf16[96,768]{1,0:T(8,128)(2,1)S(1)} %get-tuple-element.84), channel_id=1, source_target_pairs={{0,8},{4,12},{8,0},{12,4},{16,24},{20,28},{24,16},{28,20},{1,9},{5... | collective-permute-start | bytes 442376 | tf_op jit(solution)/shard_map/ppermute | solution.py:528
  155.4 12.5 %collective-permute-start.23 = (bf16[96,768]{1,0:T(8,128)(2,1)S(1)}, bf16[96,768]{1,0:T(8,128)(2,1)S(1)}, u32[]{:S(2)}, u32[]{:S(2)}) collective-permute-start(bf16[96,768]{1,0:T(8,128)(2,1)S(1)} %get-tuple-element.83), channel_id=1, source_target_pairs={{0,12},{4,8},{8,4},{12,0},{16,28},{20,24},{24,20},{28,16},{1,13},{... | collective-permute-start | bytes 442376 | tf_op jit(solution)/shard_map/ppermute | solution.py:528
  156.5 6.9 %collective-permute-start.20 = (bf16[96,640]{1,0:T(8,128)(2,1)}, bf16[96,640]{1,0:T(8,128)(2,1)}, u32[]{:S(2)}, u32[]{:S(2)}) collective-permute-start(bf16[96,640]{1,0:T(8,128)(2,1)} %get-tuple-element.87), channel_id=1, source_target_pairs={{0,28},{4,24},{8,20},{12,16},{16,12},{20,8},{24,4},{28,0},{1,29},{... | collective-permute-start | bytes 368648 | tf_op jit(solution)/shard_map/ppermute | solution.py:528
  163.4 13.4 %collective-permute-start.24 = (bf16[96,768]{1,0:T(8,128)(2,1)}, bf16[96,768]{1,0:T(8,128)(2,1)S(1)}, u32[]{:S(2)}, u32[]{:S(2)}) collective-permute-start(bf16[96,768]{1,0:T(8,128)(2,1)} %get-tuple-element.82), channel_id=1, source_target_pairs={{0,16},{4,20},{8,24},{12,28},{16,0},{20,4},{24,8},{28,12},{1,17},{... | collective-permute-start | bytes 442376 | tf_op jit(solution)/shard_map/ppermute | solution.py:528
  165.6 13.0 %collective-permute-start.25 = (bf16[96,768]{1,0:T(8,128)(2,1)}, bf16[96,768]{1,0:T(8,128)(2,1)S(1)}, u32[]{:S(2)}, u32[]{:S(2)}) collective-permute-start(bf16[96,768]{1,0:T(8,128)(2,1)} %get-tuple-element.81), channel_id=1, source_target_pairs={{0,20},{4,16},{8,28},{12,24},{16,4},{20,0},{24,12},{28,8},{1,21},{... | collective-permute-start | bytes 442376 | tf_op jit(solution)/shard_map/ppermute | solution.py:528
  165.7 14.8 %collective-permute-start.26 = (bf16[96,768]{1,0:T(8,128)(2,1)}, bf16[96,768]{1,0:T(8,128)(2,1)S(1)}, u32[]{:S(2)}, u32[]{:S(2)}) collective-permute-start(bf16[96,768]{1,0:T(8,128)(2,1)} %get-tuple-element.80), channel_id=1, source_target_pairs={{0,24},{4,28},{8,16},{12,20},{16,8},{20,12},{24,0},{28,4},{1,25},{... | collective-permute-start | bytes 442376 | tf_op jit(solution)/shard_map/ppermute | solution.py:528
  168.6 11.9 %collective-permute-start.27 = (bf16[96,768]{1,0:T(8,128)(2,1)}, bf16[96,768]{1,0:T(8,128)(2,1)S(1)}, u32[]{:S(2)}, u32[]{:S(2)}) collective-permute-start(bf16[96,768]{1,0:T(8,128)(2,1)} %get-tuple-element.79), channel_id=1, source_target_pairs={{0,28},{4,24},{8,20},{12,16},{16,12},{20,8},{24,4},{28,0},{1,29},{... | collective-permute-start | bytes 442376 | tf_op jit(solution)/shard_map/ppermute | solution.py:528
  176.8 14.4 %collective-permute-start.39 = (bf16[864,128]{1,0:T(8,128)(2,1)S(1)}, bf16[864,128]{1,0:T(8,128)(2,1)S(1)}, u32[]{:S(2)}, u32[]{:S(2)}) collective-permute-start(bf16[864,128]{1,0:T(8,128)(2,1)S(1)} %get-tuple-element.74), channel_id=1, source_target_pairs={{0,4},{4,0},{8,12},{12,8},{16,20},{20,16},{24,28},{28,24},{1,5},{5... | collective-permute-start | bytes 663560 | tf_op jit(solution)/shard_map/ppermute | solution.py:528
  178.6 12.7 %collective-permute-start.40 = (bf16[864,128]{1,0:T(8,128)(2,1)S(1)}, bf16[864,128]{1,0:T(8,128)(2,1)S(1)}, u32[]{:S(2)}, u32[]{:S(2)}) collective-permute-start(bf16[864,128]{1,0:T(8,128)(2,1)S(1)} %get-tuple-element.73), channel_id=1, source_target_pairs={{0,8},{4,12},{8,0},{12,4},{16,24},{20,28},{24,16},{28,20},{1,9},{5... | collective-permute-start | bytes 663560 | tf_op jit(solution)/shard_map/ppermute | solution.py:528
  180.5 13.3 %collective-permute-start.41 = (bf16[864,128]{1,0:T(8,128)(2,1)}, bf16[864,128]{1,0:T(8,128)(2,1)}, u32[]{:S(2)}, u32[]{:S(2)}) collective-permute-start(bf16[864,128]{1,0:T(8,128)(2,1)} %get-tuple-element.72), channel_id=1, source_target_pairs={{0,12},{4,8},{8,4},{12,0},{16,28},{20,24},{24,20},{28,16},{1,13},{... | collective-permute-start | bytes 663560 | tf_op jit(solution)/shard_map/ppermute | solution.py:528
  180.5 8.2 %collective-permute-start.56 = (f32[4,768]{1,0:T(4,128)S(1)}, f32[4,768]{1,0:T(4,128)S(1)}, u32[]{:S(2)}, u32[]{:S(2)}) collective-permute-start(f32[4,768]{1,0:T(4,128)S(1)} %add.210), channel_id=1, source_target_pairs={{0,1},{1,0},{2,3},{3,2},{4,5},{5,4},{6,7},{7,6},{8,9},{9,8},{10,11... | collective-permute-start | bytes 36872 | tf_op jit(solution)/shard_map/ppermute | solution.py:528
  188.7 10.0 %collective-permute-start.30 = (bf16[256,384]{1,0:T(8,128)(2,1)}, bf16[256,384]{1,0:T(8,128)(2,1)}, u32[]{:S(2)}, u32[]{:S(2)}) collective-permute-start(bf16[256,384]{1,0:T(8,128)(2,1)} %get-tuple-element.96), channel_id=1, source_target_pairs={{0,3},{1,2},{2,1},{3,0},{4,7},{5,6},{6,5},{7,4},{8,11},{9,10},{10,... | collective-permute-start | bytes 589832 | tf_op jit(solution)/shard_map/ppermute | solution.py:528
  191.3 17.9 %collective-permute-start.29 = (bf16[256,384]{1,0:T(8,128)(2,1)}, bf16[256,384]{1,0:T(8,128)(2,1)}, u32[]{:S(2)}, u32[]{:S(2)}) collective-permute-start(bf16[256,384]{1,0:T(8,128)(2,1)} %get-tuple-element.97), channel_id=1, source_target_pairs={{0,2},{1,3},{2,0},{3,1},{4,6},{5,7},{6,4},{7,5},{8,10},{9,11},{10,... | collective-permute-start | bytes 589832 | tf_op jit(solution)/shard_map/ppermute | solution.py:528
  192.6 19.8 %collective-permute-start.28 = (bf16[256,384]{1,0:T(8,128)(2,1)}, bf16[256,384]{1,0:T(8,128)(2,1)}, u32[]{:S(2)}, u32[]{:S(2)}) collective-permute-start(bf16[256,384]{1,0:T(8,128)(2,1)} %get-tuple-element.95), channel_id=1, source_target_pairs={{0,1},{1,0},{2,3},{3,2},{4,5},{5,4},{6,7},{7,6},{8,9},{9,8},{10,11... | collective-permute-start | bytes 589832 | tf_op jit(solution)/shard_map/ppermute | solution.py:528
  193.8 20.0 %collective-permute-start.42 = (bf16[864,128]{1,0:T(8,128)(2,1)}, bf16[864,128]{1,0:T(8,128)(2,1)S(1)}, u32[]{:S(2)}, u32[]{:S(2)}) collective-permute-start(bf16[864,128]{1,0:T(8,128)(2,1)} %get-tuple-element.71), channel_id=1, source_target_pairs={{0,16},{4,20},{8,24},{12,28},{16,0},{20,4},{24,8},{28,12},{1,17},{... | collective-permute-start | bytes 663560 | tf_op jit(solution)/shard_map/ppermute | solution.py:528
  198.6 15.2 %collective-permute-start.43 = (bf16[864,128]{1,0:T(8,128)(2,1)S(1)}, bf16[864,128]{1,0:T(8,128)(2,1)S(1)}, u32[]{:S(2)}, u32[]{:S(2)}) collective-permute-start(bf16[864,128]{1,0:T(8,128)(2,1)S(1)} %get-tuple-element.70), channel_id=1, source_target_pairs={{0,20},{4,16},{8,28},{12,24},{16,4},{20,0},{24,12},{28,8},{1,21},{... | collective-permute-start | bytes 663560 | tf_op jit(solution)/shard_map/ppermute | solution.py:528
  209.1 9.5 %collective-permute-start.44 = (bf16[864,128]{1,0:T(8,128)(2,1)S(1)}, bf16[864,128]{1,0:T(8,128)(2,1)S(1)}, u32[]{:S(2)}, u32[]{:S(2)}) collective-permute-start(bf16[864,128]{1,0:T(8,128)(2,1)S(1)} %get-tuple-element.69), channel_id=1, source_target_pairs={{0,24},{4,28},{8,16},{12,20},{16,8},{20,12},{24,0},{28,4},{1,25},{... | collective-permute-start | bytes 663560 | tf_op jit(solution)/shard_map/ppermute | solution.py:528
  212.4 10.6 %collective-permute-start.45 = (bf16[864,128]{1,0:T(8,128)(2,1)S(1)}, bf16[864,128]{1,0:T(8,128)(2,1)S(1)}, u32[]{:S(2)}, u32[]{:S(2)}) collective-permute-start(bf16[864,128]{1,0:T(8,128)(2,1)S(1)} %get-tuple-element.68), channel_id=1, source_target_pairs={{0,28},{4,24},{8,20},{12,16},{16,12},{20,8},{24,4},{28,0},{1,29},{... | collective-permute-start | bytes 663560 | tf_op jit(solution)/shard_map/ppermute | solution.py:528
  213.8 19.7 %collective-permute-start.57 = (f32[4,768]{1,0:T(4,128)S(1)}, f32[4,768]{1,0:T(4,128)S(1)}, u32[]{:S(2)}, u32[]{:S(2)}) collective-permute-start(f32[4,768]{1,0:T(4,128)S(1)} %add.211), channel_id=1, source_target_pairs={{0,2},{1,3},{2,0},{3,1},{4,6},{5,7},{6,4},{7,5},{8,10},{9,11},{10,... | collective-permute-start | bytes 36872 | tf_op jit(solution)/shard_map/ppermute | solution.py:528
  213.9 21.5 %collective-permute-start.33 = (bf16[256,384]{1,0:T(8,128)(2,1)S(1)}, bf16[256,384]{1,0:T(8,128)(2,1)S(1)}, u32[]{:S(2)}, u32[]{:S(2)}) collective-permute-start(bf16[256,384]{1,0:T(8,128)(2,1)S(1)} %fusion.26), channel_id=1, source_target_pairs={{0,24},{4,28},{8,16},{12,20},{16,8},{20,12},{24,0},{28,4},{1,25},{... | collective-permute-start | bytes 589832 | tf_op jit(solution)/shard_map/ppermute | solution.py:528
  218.7 17.6 %collective-permute-start.32 = (bf16[256,384]{1,0:T(8,128)(2,1)S(1)}, bf16[256,384]{1,0:T(8,128)(2,1)S(1)}, u32[]{:S(2)}, u32[]{:S(2)}) collective-permute-start(bf16[256,384]{1,0:T(8,128)(2,1)S(1)} %fusion.26), channel_id=1, source_target_pairs={{0,16},{4,20},{8,24},{12,28},{16,0},{20,4},{24,8},{28,12},{1,17},{... | collective-permute-start | bytes 589832 | tf_op jit(solution)/shard_map/ppermute | solution.py:528
  223.1 13.3 %collective-permute-start.31 = (bf16[256,384]{1,0:T(8,128)(2,1)S(1)}, bf16[256,384]{1,0:T(8,128)(2,1)S(1)}, u32[]{:S(2)}, u32[]{:S(2)}) collective-permute-start(bf16[256,384]{1,0:T(8,128)(2,1)S(1)} %fusion.26), channel_id=1, source_target_pairs={{0,8},{4,12},{8,0},{12,4},{16,24},{20,28},{24,16},{28,20},{1,9},{5... | collective-permute-start | bytes 589832 | tf_op jit(solution)/shard_map/ppermute | solution.py:528
  230.8 12.7 %collective-permute-start.48 = (bf16[432,384]{1,0:T(8,128)(2,1)S(1)}, bf16[432,384]{1,0:T(8,128)(2,1)S(1)}, u32[]{:S(2)}, u32[]{:S(2)}) collective-permute-start(bf16[432,384]{1,0:T(8,128)(2,1)S(1)} %get-tuple-element.77), channel_id=1, source_target_pairs={{0,3},{1,2},{2,1},{3,0},{4,7},{5,6},{6,5},{7,4},{8,11},{9,10},{10,... | collective-permute-start | bytes 995336 | tf_op jit(solution)/shard_map/ppermute | solution.py:528
  233.5 30.6 %collective-permute-start.47 = (bf16[432,384]{1,0:T(8,128)(2,1)S(1)}, bf16[432,384]{1,0:T(8,128)(2,1)S(1)}, u32[]{:S(2)}, u32[]{:S(2)}) collective-permute-start(bf16[432,384]{1,0:T(8,128)(2,1)S(1)} %get-tuple-element.78), channel_id=1, source_target_pairs={{0,2},{1,3},{2,0},{3,1},{4,6},{5,7},{6,4},{7,5},{8,10},{9,11},{10,... | collective-permute-start | bytes 995336 | tf_op jit(solution)/shard_map/ppermute | solution.py:528
  235.4 28.7 %collective-permute-start.46 = (bf16[432,384]{1,0:T(8,128)(2,1)S(1)}, bf16[432,384]{1,0:T(8,128)(2,1)S(1)}, u32[]{:S(2)}, u32[]{:S(2)}) collective-permute-start(bf16[432,384]{1,0:T(8,128)(2,1)S(1)} %get-tuple-element.76), channel_id=1, source_target_pairs={{0,1},{1,0},{2,3},{3,2},{4,5},{5,4},{6,7},{7,6},{8,9},{9,8},{10,11... | collective-permute-start | bytes 995336 | tf_op jit(solution)/shard_map/ppermute | solution.py:528
  236.5 33.4 %copy-start.12 = (bf16[4,256,384]{2,1,0:T(8,128)(2,1)}, bf16[4,256,384]{2,1,0:T(8,128)(2,1)S(1)}, u32[]{:S(2)}) copy-start(bf16[4,256,384]{2,1,0:T(8,128)(2,1)S(1)} %pad_maximum_fusion.6.even_ref) | copy-start | bytes 2359300
  236.5 48.1 %collective-permute-start.34 = (bf16[4,256,384]{2,1,0:T(8,128)(2,1)S(1)}, bf16[4,256,384]{2,1,0:T(8,128)(2,1)S(1)}, u32[]{:S(2)}, u32[]{:S(2)}) collective-permute-start(bf16[4,256,384]{2,1,0:T(8,128)(2,1)S(1)} %pad_maximum_fusion.6.even_ref), channel_id=1, source_target_pairs={{0,4},{4,0},{8,12},{12,8},{16,20},{20,16},{24,28},{28,24},{1,5},{5... | collective-permute-start | bytes 2359304 | tf_op jit(solution)/shard_map/ppermute | solution.py:528
  265.2 11.7 %collective-permute-start.51 = (bf16[432,384]{1,0:T(8,128)(2,1)S(1)}, bf16[432,384]{1,0:T(8,128)(2,1)S(1)}, u32[]{:S(2)}, u32[]{:S(2)}) collective-permute-start(bf16[432,384]{1,0:T(8,128)(2,1)S(1)} %fusion.13), channel_id=1, source_target_pairs={{0,24},{4,28},{8,16},{12,20},{16,8},{20,12},{24,0},{28,4},{1,25},{... | collective-permute-start | bytes 995336 | tf_op jit(solution)/shard_map/ppermute | solution.py:528
  267.0 15.5 %collective-permute-start.50 = (bf16[432,384]{1,0:T(8,128)(2,1)S(1)}, bf16[432,384]{1,0:T(8,128)(2,1)S(1)}, u32[]{:S(2)}, u32[]{:S(2)}) collective-permute-start(bf16[432,384]{1,0:T(8,128)(2,1)S(1)} %fusion.13), channel_id=1, source_target_pairs={{0,16},{4,20},{8,24},{12,28},{16,0},{20,4},{24,8},{28,12},{1,17},{... | collective-permute-start | bytes 995336 | tf_op jit(solution)/shard_map/ppermute | solution.py:528
  267.9 15.2 %collective-permute-start.49 = (bf16[432,384]{1,0:T(8,128)(2,1)S(1)}, bf16[432,384]{1,0:T(8,128)(2,1)S(1)}, u32[]{:S(2)}, u32[]{:S(2)}) collective-permute-start(bf16[432,384]{1,0:T(8,128)(2,1)S(1)} %fusion.13), channel_id=1, source_target_pairs={{0,8},{4,12},{8,0},{12,4},{16,24},{20,28},{24,16},{28,20},{1,9},{5... | collective-permute-start | bytes 995336 | tf_op jit(solution)/shard_map/ppermute | solution.py:528
  283.3 25.6 %collective-permute-start.52 = (bf16[4,432,384]{2,1,0:T(8,128)(2,1)S(1)}, bf16[4,432,384]{2,1,0:T(8,128)(2,1)S(1)}, u32[]{:S(2)}, u32[]{:S(2)}) collective-permute-start(bf16[4,432,384]{2,1,0:T(8,128)(2,1)S(1)} %pad_maximum_fusion.3.even_ref), channel_id=1, source_target_pairs={{0,4},{4,0},{8,12},{12,8},{16,20},{20,16},{24,28},{28,24},{1,5},{5... | collective-permute-start | bytes 3981320 | tf_op jit(solution)/shard_map/ppermute | solution.py:528
  290.2 11.2 %collective-permute-start.58 = (bf16[128,768]{1,0:T(8,128)(2,1)}, bf16[128,768]{1,0:T(8,128)(2,1)S(1)}, u32[]{:S(2)}, u32[]{:S(2)}) collective-permute-start(bf16[128,768]{1,0:T(8,128)(2,1)} %get-tuple-element.48), channel_id=1, source_target_pairs={{0,1},{1,0},{2,3},{3,2},{4,5},{5,4},{6,7},{7,6},{8,9},{9,8},{10,11... | collective-permute-start | bytes 589832 | tf_op jit(solution)/shard_map/ppermute | solution.py:528
  290.2 17.4 %collective-permute-start.59 = (bf16[128,768]{1,0:T(8,128)(2,1)}, bf16[128,768]{1,0:T(8,128)(2,1)S(1)}, u32[]{:S(2)}, u32[]{:S(2)}) collective-permute-start(bf16[128,768]{1,0:T(8,128)(2,1)} %get-tuple-element.48), channel_id=1, source_target_pairs={{0,2},{1,3},{2,0},{3,1},{4,6},{5,7},{6,4},{7,5},{8,10},{9,11},{10,... | collective-permute-start | bytes 589832 | tf_op jit(solution)/shard_map/ppermute | solution.py:528
  292.8 14.7 %collective-permute-start.60 = (bf16[128,768]{1,0:T(8,128)(2,1)}, bf16[128,768]{1,0:T(8,128)(2,1)S(1)}, u32[]{:S(2)}, u32[]{:S(2)}) collective-permute-start(bf16[128,768]{1,0:T(8,128)(2,1)} %get-tuple-element.48), channel_id=1, source_target_pairs={{0,3},{1,2},{2,1},{3,0},{4,7},{5,6},{6,5},{7,4},{8,11},{9,10},{10,... | collective-permute-start | bytes 589832 | tf_op jit(solution)/shard_map/ppermute | solution.py:528
  (62 other events, 398.2 us)

commit v3 on v1

v3 whole, which is shorter than its diff:
```python
import functools, math
import jax, jax.numpy as jnp
from jax import lax
from jax.experimental import pallas as pl
from jax.experimental.pallas import tpu as pltpu
from jax.sharding import PartitionSpec as P

BLK = 256
TOK = 128
PAIR = 128
EXTRA = 16
COST = 3e8
NT = (((1,), (1,)), ((), ()))
NN = (((1,), (0,)), ((), ()))
TN = (((0,), (0,)), ((), ()))
bf16 = jnp.bfloat16
f32 = jnp.float32


def dot(a, b, form):
    return lax.dot_general(a, b, form, preferred_element_type=f32)


def lanes(parts):
    return jnp.concatenate(parts, axis=1)


def half_masks(x):
    lane = lax.broadcasted_iota(jnp.int32, x.shape, 1)
    low = lane < PAIR // 2
    zero = jnp.zeros_like(x)
    return jnp.where(low, x, zero), jnp.where(low, zero, x)


def join_heads(stacked, rows):
    lane = lax.broadcasted_iota(jnp.int32, (rows, PAIR), 1)
    return jnp.where(lane < PAIR // 2, stacked[:rows], stacked[rows:])


def block_start(chip, slot):
    return pl.multiple_of((chip ^ slot) * BLK, BLK)


def fill_table(out_ref, flip_ref, start):
    places = flip_ref.shape[0]
    low = jnp.broadcast_to(flip_ref[0:1, :], (BLK, PAIR))
    high = jnp.broadcast_to(flip_ref[places - 1:places, :], (BLK, PAIR))
    for b in range(out_ref.shape[0] // BLK):
        out_ref[b * BLK:(b + 1) * BLK, :] = jnp.where(b * BLK < start, low, high)
    out_ref[pl.ds(pl.multiple_of(start, BLK), places), :] = flip_ref[...]


def fill_scores(chip, own_ref, all_ref, near_ref, far_ref, s_ref, n_ref, length):
    wide = length + BLK
    own = jnp.concatenate(half_masks(own_ref[...]), axis=0)
    ext = dot(own, near_ref[...], NT)
    for h in range(2):
        moved = pltpu.roll(ext[h * BLK:(h + 1) * BLK], wide - (BLK - 1), 1, stride=1, stride_axis=0)
        n_ref[h] = moved[:, :length]
    for slot in range(length // BLK):
        cols = slice(slot * BLK, (slot + 1) * BLK)
        blk = all_ref[cols, :]
        both = jnp.concatenate(half_masks(blk), axis=0)
        start = block_start(chip, slot)
        win = far_ref[pl.ds(pl.multiple_of(length - BLK - start, BLK), 2 * BLK), :]
        back = dot(both, win, NT)
        direct = dot(own, blk, NT)
        for h in range(2):
            rows = slice(h * BLK, (h + 1) * BLK)
            moved = pltpu.roll(back[rows], BLK + 1, 1, stride=1, stride_axis=0)[:, :BLK]
            s_ref[h, :, cols] = direct[rows] + moved.T + n_ref[h, :, pl.ds(start, BLK)]


def far_start(chip, length):
    return length - BLK - chip * BLK


def forward_kernel(scale, length, place_ref, q_ref, k_ref, v_ref, near_ref, far_ref, segq_ref, segk_ref,
                   p_ref, out_ref, s_ref, n_ref, near_tab, far_tab):
    chip = place_ref[0]
    fill_table(near_tab, near_ref, chip * BLK)
    fill_table(far_tab, far_ref, far_start(chip, length))
    fill_scores(chip, q_ref, k_ref, near_tab, far_tab, s_ref, n_ref, length)
    allowed = segq_ref[...] == segk_ref[...]
    stats = []
    for h in range(2):
        logits = jnp.where(allowed, s_ref[h] * scale, -1e30)
        best = jnp.max(logits, axis=1, keepdims=True)
        weights = jnp.exp(logits - best)
        total = jnp.sum(weights, axis=1, keepdims=True)
        p_ref[h] = (weights * (1.0 / total)).astype(bf16)
        stats.append(best + jnp.log(total))
    stacked = jnp.concatenate([p_ref[0], p_ref[1]], axis=0)
    ctx = join_heads(dot(stacked, v_ref[...], NN), BLK)
    lane = lax.broadcasted_iota(jnp.int32, (TOK, PAIR), 1)
    for c in range(2):
        rows = slice(c * TOK, (c + 1) * TOK)
        out_ref[c, :TOK, :] = ctx[rows]
        out_ref[c, TOK:, :] = jnp.where(lane == 0, stats[0][rows], stats[1][rows]).T[:8]


def flip_matrix(count):
    r = lax.broadcasted_iota(jnp.int32, (count, count), 0)
    c = lax.broadcasted_iota(jnp.int32, (count, count), 1)
    return jnp.where(r + c == count - 1, 1.0, 0.0).astype(bf16)


def fold_table(grad, start, places, fold_ref):
    place = lax.broadcasted_iota(jnp.int32, grad.shape, 1)
    low = jnp.sum(jnp.where(place < start, grad, 0.0), axis=1, keepdims=True)
    high = jnp.sum(jnp.where(place >= start + places, grad, 0.0), axis=1, keepdims=True)
    fold_ref[...] = grad
    table = fold_ref[:, pl.ds(pl.multiple_of(start, BLK), places)]
    spot = lax.broadcasted_iota(jnp.int32, table.shape, 1)
    return table + jnp.where(spot == 0, low, 0.0) + jnp.where(spot == places - 1, high, 0.0)


def grads_tail(scale, length, places, chip, ds_ref, own_ref, all_ref, near_ref, table_ref, wide_ref, down_ref, fold_ref, n_ref):
    flip = flip_matrix(BLK)
    rows = pair_rows()
    for h in range(2):
        back = dot(flip, ds_ref[h], NN)
        down_ref[h * BLK:(h + 1) * BLK, :] = back.astype(bf16)
        for slot in range(length // BLK):
            n_ref[h, :, pl.ds(block_start(chip, slot), BLK)] = back[:, slot * BLK:(slot + 1) * BLK]
        padded = lanes([n_ref[h], jnp.zeros((BLK, BLK), f32)])
        wide_ref[h * BLK:(h + 1) * BLK, :] = pltpu.roll(padded, 0, 1, stride=1, stride_axis=0).astype(bf16)
    own_grad = dot(down_ref[...], all_ref[...], NN) + dot(wide_ref[...], near_ref[...], NN)
    own_grad = (join_heads(own_grad, BLK) * scale).astype(bf16)
    table_ref[rows, places:places + BLK] = dot(own_grad, flip, TN).astype(bf16)
    own_grad = dot(flip, own_grad, NN).astype(bf16)
    own = dot(flip, own_ref[...], NN).astype(bf16)
    own = jnp.concatenate(half_masks(own), axis=0)
    near_grad = dot(own, wide_ref[...], TN) * scale
    table_ref[rows, :places] = fold_table(near_grad, chip * BLK, places, fold_ref).astype(bf16)
    return own_grad


def pair_rows():
    return pl.ds(pl.multiple_of(pl.program_id(0) * PAIR, PAIR), PAIR)


def deal_table(chip, table_ref, out_refs):
    @pl.when(pl.program_id(0) == pl.num_programs(0) - 1)
    def _():
        for k, ref in enumerate(out_refs):
            size = ref.shape[0]
            ref[...] = table_ref[pl.ds(pl.multiple_of((chip ^ k) * size, EXTRA), size), :]


def split_tokens(out_ref, value):
    for c in range(2):
        out_ref[c] = value[c * TOK:(c + 1) * TOK]


def query_grad_kernel(scale, length, chips, place_ref, p_ref, mine_ref, twin_ref, out_weight_ref, ctx_ref, v_ref, q_ref, k_ref,
                      near_ref, earlier_ref, dq_ref, *refs):
    out_refs, (near_tab, dctx_ref, table_ref, ds_ref, *scratch) = refs[:chips], refs[chips:]
    chip, core = place_ref[0], place_ref[1]
    places = near_ref.shape[0]
    fill_table(near_tab, near_ref, chip * BLK)
    for ref, at in ((mine_ref, core), (twin_ref, 1 - core)):
        rows = pl.ds(pl.multiple_of(at * TOK, TOK), TOK)
        dctx_ref[rows, :] = dot(ref[:TOK, :], out_weight_ref[...], NT).astype(bf16)
    dctx = jnp.concatenate(half_masks(dctx_ref[...]), axis=0)
    dprob = dot(dctx, v_ref[...], NT)
    ctx = jnp.concatenate([ctx_ref[0, :TOK, :], ctx_ref[1, :TOK, :]], axis=0)
    for h in range(2):
        rows = slice(h * BLK, (h + 1) * BLK)
        row_dot = jnp.sum(dctx[rows].astype(f32) * ctx, axis=1, keepdims=True)
        ds_ref[h] = (p_ref[h].astype(f32) * (dprob[rows] - row_dot)).astype(bf16)
    dq = grads_tail(scale, length, places, chip, ds_ref, q_ref, k_ref, near_tab, table_ref, *scratch)
    split_tokens(dq_ref, dq)
    deal_table(chip, table_ref, out_refs)


def key_grad_kernel(scale, length, pairs, chips, place_ref, k_ref, v_ref, q_ref, near_ref, far_ref, segk_ref, segq_ref,
                    mine_ref, twin_ref, even_ref, odd_ref, out_weight_ref, earlier_ref, dk_ref, dv_ref, *refs):
    out_refs, refs = refs[:chips], refs[chips:]
    s_ref, near_tab, far_tab, dctx_ref, p_ref, stat_ref, table_ref, ds_ref, *scratch = refs
    chip, core = place_ref[0], place_ref[1]
    places = near_ref.shape[0]
    fill_table(near_tab, near_ref, chip * BLK)
    fill_table(far_tab, far_ref, far_start(chip, length))
    fill_scores(chip, k_ref, q_ref, near_tab, far_tab, s_ref, scratch[-1], length)
    stat_cols = pl.ds(pl.multiple_of((core * pairs + pl.program_id(0)) * PAIR, PAIR), PAIR)
    for slot in range(length // BLK):
        for odd in range(2):
            at = pl.ds(pl.multiple_of(slot * BLK + (core ^ odd) * TOK, TOK), TOK)
            if slot == 0:
                ref = twin_ref if odd else mine_ref
            else:
                ref = (odd_ref if odd else even_ref).at[slot - 1]
            dctx_ref[at, :] = dot(ref[:TOK, :], out_weight_ref[...], NT).astype(bf16)
            stat_ref[:, at] = ref[TOK:, stat_cols].astype(f32)
    merged = [stat_ref[3 * j:3 * j + 1] + stat_ref[3 * j + 1:3 * j + 2] + stat_ref[3 * j + 2:3 * j + 3] for j in range(4)]
    allowed = segk_ref[...] == segq_ref[...]
    dctx = dctx_ref[...]
    vals = jnp.concatenate(half_masks(v_ref[...]), axis=0)
    dprob = dot(vals, dctx, NT)
    for h in range(2):
        rows = slice(h * BLK, (h + 1) * BLK)
        probs = jnp.where(allowed, jnp.exp(s_ref[h] * scale - merged[h]), 0.0)
        p_ref[rows, :] = probs.astype(bf16)
        ds_ref[h] = (probs * (dprob[rows] - merged[2 + h])).astype(bf16)
    dv = join_heads(dot(p_ref[...], dctx, NN), BLK)
    split_tokens(dv_ref, dv.astype(bf16))
    table_ref[pair_rows(), places + BLK:] = dv.T.astype(bf16)
    dk = grads_tail(scale, length, places, chip, ds_ref, k_ref, q_ref, near_tab, table_ref, *scratch)
    split_tokens(dk_ref, dk)
    deal_table(chip, table_ref, out_refs)


def col(rows):
    return pl.BlockSpec((rows, PAIR), lambda p: (0, p))


def full(shape):
    return pl.BlockSpec(shape, lambda p: (0,) * len(shape))


def whole():
    return pl.BlockSpec(memory_space=pltpu.VMEM)


def scalar():
    return pl.BlockSpec(memory_space=pltpu.SMEM)


def unread():
    return pl.BlockSpec(memory_space=pl.ANY)


def params():
    return pltpu.CompilerParams(vmem_limit_bytes=56 * 1024 * 1024)


def cost(microseconds):
    return pl.CostEstimate(flops=int(microseconds * COST), bytes_accessed=0, transcendentals=0)


def after(x, *earlier):
    def kernel(*refs):
        pass

    return pl.pallas_call(
        kernel,
        in_specs=[unread()] * (1 + len(earlier)),
        out_specs=unread(),
        out_shape=jax.ShapeDtypeStruct(x.shape, x.dtype),
        input_output_aliases={0: 0},
        cost_estimate=cost(0.1),
        name="after",
    )(x, *earlier)


def stack_kernel(count, *refs):
    for i in range(count):
        refs[-1][i] = refs[i][...]


def stack(arrays, *earlier):
    count = len(arrays)
    return pl.pallas_call(
        functools.partial(stack_kernel, count),
        in_specs=[whole()] * count + [unread()] * len(earlier),
        out_specs=whole(),
        out_shape=jax.ShapeDtypeStruct((count,) + arrays[0].shape, arrays[0].dtype),
        compiler_params=params(),
        cost_estimate=cost(1),
        name="stack",
    )(*arrays, *earlier)


def table_scratch(length):
    return pltpu.VMEM((length + BLK, PAIR), bf16)


def probs_block(length):
    return pl.BlockSpec((2, BLK, length), lambda p: (p, 0, 0))


def token_block():
    return pl.BlockSpec((2, TOK, PAIR), lambda p: (0, 0, p))


def forward_attention(place, q, k, v, near, far, seg_q, seg_k, scale):
    length, width = k.shape
    places = near.shape[0]
    pairs = width // PAIR
    return pl.pallas_call(
        functools.partial(forward_kernel, scale, length),
        grid=(pairs,),
        in_specs=[scalar(), col(BLK), col(length), col(length), col(places), col(places), full((BLK, 1)), full((1, length))],
        out_specs=[probs_block(length), pl.BlockSpec((2, TOK + 8, PAIR), lambda p: (0, 0, p))],
        out_shape=[
            jax.ShapeDtypeStruct((2 * pairs, BLK, length), bf16),
            jax.ShapeDtypeStruct((2, TOK + 8, width), f32),
        ],
        scratch_shapes=[pltpu.VMEM((2, BLK, length), f32)] * 2 + [table_scratch(length)] * 2,
        compiler_params=params(),
        cost_estimate=cost(14),
        name="attend",
    )(place, q, k, v, near, far, seg_q, seg_k)


def grad_scratch(length):
    return [
        pltpu.VMEM((2, BLK, length), bf16),
        pltpu.VMEM((2 * BLK, length + BLK), bf16),
        pltpu.VMEM((2 * BLK, length), bf16),
        pltpu.VMEM((PAIR, length + BLK), f32),
        pltpu.VMEM((2, BLK, length), f32),
    ]


def query_grads(place, p, mine, twin, out_weight, ctx, v, q, k, near, earlier, scale):
    length, width = k.shape
    places = near.shape[0]
    chips = length // BLK
    table = jax.ShapeDtypeStruct((width // chips, places + BLK), bf16)
    return pl.pallas_call(
        functools.partial(query_grad_kernel, scale, length, chips),
        grid=(width // PAIR,),
        in_specs=[scalar(), probs_block(length), full(mine.shape), full(twin.shape),
                  pl.BlockSpec((PAIR, out_weight.shape[1]), lambda p: (p, 0)),
                  pl.BlockSpec((2, TOK + 8, PAIR), lambda p: (0, 0, p)), col(length), col(BLK), col(length), col(places),
                  unread()],
        out_specs=[token_block()] + [full(table.shape)] * chips,
        out_shape=[jax.ShapeDtypeStruct((2, TOK, width), bf16)] + [table] * chips,
        scratch_shapes=[table_scratch(length), pltpu.VMEM((BLK, PAIR), bf16), pltpu.VMEM((width, places + BLK), bf16)]
        + grad_scratch(length),
        compiler_params=params(),
        cost_estimate=cost(1),
        name="query_grads",
    )(place, p, mine, twin, out_weight, ctx, v, q, k, near, earlier)


def key_grads(place, k, v, q, near, far, seg_k, seg_q, attn, out_weight, earlier, scale):
    length, width = q.shape
    places = near.shape[0]
    pairs = width // PAIR
    chips = length // BLK
    table = jax.ShapeDtypeStruct((width // chips, places + 2 * BLK), bf16)
    return pl.pallas_call(
        functools.partial(key_grad_kernel, scale, length, pairs, chips),
        grid=(pairs,),
        in_specs=[scalar(), col(BLK), col(BLK), col(length), col(places), col(places), full((BLK, 1)), full((1, length))]
        + [full(x.shape) for x in attn]
        + [pl.BlockSpec((PAIR, out_weight.shape[1]), lambda p: (p, 0)), unread()],
        out_specs=[token_block(), token_block()] + [full(table.shape)] * chips,
        out_shape=[jax.ShapeDtypeStruct((2, TOK, width), bf16)] * 2 + [table] * chips,
        scratch_shapes=[pltpu.VMEM((2, BLK, length), f32), table_scratch(length), table_scratch(length),
                        pltpu.VMEM((length, PAIR), bf16), pltpu.VMEM((2 * BLK, length), bf16),
                        pltpu.VMEM((EXTRA, length), f32), pltpu.VMEM((width, places + 2 * BLK), bf16)]
        + grad_scratch(length),
        compiler_params=params(),
        cost_estimate=cost(1),
        name="key_grads",
    )(place, k, v, q, near, far, seg_k, seg_q, *attn, out_weight, earlier)


def attn_out_kernel(dattn_ref, weight_ref, ctx_ref, vec_ref, pay_ref):
    tokens, width = dattn_ref.shape
    dattn = dattn_ref[...]
    pay_ref[:tokens, :] = dattn
    half = PAIR // 2
    for p in range(width // PAIR):
        cols = slice(p * PAIR, (p + 1) * PAIR)
        dctx = dot(dattn, weight_ref[cols, :], NT).astype(bf16)
        turned = (dctx.astype(f32) * ctx_ref[:tokens, cols]).T
        rows = [ctx_ref[tokens:tokens + 1, cols], ctx_ref[tokens + 1:tokens + 2, cols],
                jnp.sum(turned[:half], axis=0, keepdims=True), jnp.sum(turned[half:], axis=0, keepdims=True)]
        pieces = []
        for value in rows:
            for _ in range(3):
                piece = value.astype(bf16).astype(f32)
                pieces.append(piece)
                value = value - piece
        pieces.append(vec_ref[:, cols])
        pay_ref[tokens:, cols] = jnp.concatenate(pieces, axis=0).astype(bf16)


def attn_out(dattn, weight, ctx, vectors):
    tokens, width = dattn.shape
    return pl.pallas_call(
        attn_out_kernel,
        in_specs=[whole()] * 4,
        out_specs=whole(),
        out_shape=jax.ShapeDtypeStruct((tokens + EXTRA, width), bf16),
        compiler_params=params(),
        cost_estimate=cost(2),
        name="attn_out",
    )(dattn, weight, ctx, vectors)


def project_kernel(place_ref, mine_ref, twin_ref, even_ref, odd_ref, wq_ref, wk_ref, wv_ref, q_ref, k_ref, v_ref, seg_ref,
                   rows_ref):
    core = place_ref[1]
    count = even_ref.shape[0] + 1

    @pl.when(pl.program_id(0) == 0)
    def _():
        for slot in range(count):
            for odd in range(2):
                at = pl.ds(pl.multiple_of(slot * BLK + (core ^ odd) * TOK, TOK), TOK)
                if slot == 0:
                    ref = twin_ref if odd else mine_ref
                else:
                    ref = (odd_ref if odd else even_ref).at[slot - 1]
                rows_ref[at, :] = ref[:TOK, :]
                seg_ref[:, at] = ref[TOK:, :TOK].astype(f32)[:1]

    weights = lanes([wq_ref[...], wk_ref[...], wv_ref[...]])
    out = dot(rows_ref[...], weights, NN).astype(bf16)
    q_ref[...] = out[:, :PAIR]
    k_ref[...] = out[:, PAIR:2 * PAIR]
    v_ref[...] = out[:, 2 * PAIR:]


def project_rows(place, parts, wq, wk, wv):
    width, part = wq.shape
    length = BLK * (parts[2].shape[0] + 1)
    shape = jax.ShapeDtypeStruct((length, part), bf16)
    return pl.pallas_call(
        project_kernel,
        grid=(part // PAIR,),
        in_specs=[scalar()] + [full(x.shape) for x in parts] + [col(width)] * 3,
        out_specs=[col(length)] * 3 + [full((1, length)), full((length, width))],
        out_shape=[shape] * 3 + [jax.ShapeDtypeStruct((1, length), f32), jax.ShapeDtypeStruct((length, width), bf16)],
        compiler_params=params(),
        cost_estimate=cost(5),
        name="project",
    )(place, *parts, wq, wk, wv)


def pack_kernel(cols, kinds, *refs):
    *in_refs, out_ref, turn_ref = refs
    top = 0
    for ref, shares in zip(in_refs, kinds):
        tokens, count = out_ref.shape[2], ref.shape[1]
        for i in range(count // PAIR):
            turn_ref[i * PAIR:(i + 1) * PAIR, :] = ref[:tokens, i * PAIR:(i + 1) * PAIR].astype(f32).T
        size = count // (shares * cols)
        for c in range(cols):
            starts = [r * (count // shares) + c * size for r in range(shares)]
            rows = jnp.concatenate([turn_ref[a:a + size, :] for a in starts], axis=0)
            out_ref[c, top:top + shares * size, :] = rows.astype(bf16)
        top += shares * size


def pack(arrays, kinds, cols):
    tokens = arrays[0].shape[0]
    total = sum(x.shape[1] for x in arrays)
    return pl.pallas_call(
        functools.partial(pack_kernel, cols, kinds),
        in_specs=[whole()] * len(arrays),
        out_specs=whole(),
        out_shape=jax.ShapeDtypeStruct((cols, total // cols, tokens), bf16),
        scratch_shapes=[pltpu.VMEM((max(x.shape[1] for x in arrays), tokens), f32)],
        compiler_params=params(),
        cost_estimate=cost(3),
        name="pack",
    )(*arrays)


def layer_sums_kernel(rows, chunk, place_ref, pair_even_ref, pair_odd_ref, mine_ref, twin_ref, even_ref, odd_ref, part_ref,
                      earlier_ref, *out_refs):
    *out_refs, out_ref = out_refs
    me = 2 * place_ref[0] + place_ref[1]
    width = mine_ref.shape[1]
    features = part_ref.shape[1] - 2 * chunk
    half = width // 2
    down = up = out = small = 0.0
    for i in range(part_ref.shape[0] // 2):
        part = lanes([part_ref[me ^ (2 * i)], part_ref[me ^ (2 * i + 1)]])
        normed = jnp.concatenate([pair_even_ref[i, :, :width], pair_odd_ref[i, :, :width]], axis=0)
        branch = jnp.concatenate([pair_even_ref[i, :, width:], pair_odd_ref[i, :, width:]], axis=0)
        first, second = (even_ref.at[i - 1], odd_ref.at[i - 1]) if i else (mine_ref, twin_ref)
        attn = jnp.concatenate([first[:TOK, :], second[:TOK, :]], axis=0)
        down = down + dot(part[:chunk], branch, NN)
        out = out + dot(part[chunk:chunk + features], attn, NN)
        up = up + dot(part[chunk + features:], normed, NN)
        small = small + first[TOK:, :].astype(f32) + second[TOK:, :].astype(f32)
    up = up.T
    small = small[EXTRA - 4:]
    share, size, few = width // rows, chunk // rows, features // rows
    for r in range(rows):
        vectors = lanes([small[:, r * share:(r + 1) * share], jnp.zeros((4, chunk - share), f32)])
        pieces = [
            down[r * size:(r + 1) * size, :half], down[r * size:(r + 1) * size, half:],
            up[r * share:(r + 1) * share],
            out[r * few:(r + 1) * few, :half], out[r * few:(r + 1) * few, half:],
            vectors, jnp.zeros((EXTRA - 4, chunk), f32),
        ]
        out_ref[r] = jnp.concatenate(pieces, axis=0).astype(bf16)
    for k, ref in enumerate(out_refs):
        ref[...] = out_ref[place_ref[2] ^ k]


def layer_sums(place, pair, attn, parts, earlier, rows, chunk):
    width = attn[0].shape[1]
    features = parts.shape[1] - 2 * chunk
    height = (2 * chunk + 2 * features) // rows + width // rows + EXTRA
    return pl.pallas_call(
        functools.partial(layer_sums_kernel, rows, chunk),
        in_specs=[scalar()] + [whole()] * 7 + [unread()],
        out_specs=[whole()] * rows,
        out_shape=[jax.ShapeDtypeStruct((height, chunk), bf16)] * rows,
        scratch_shapes=[pltpu.VMEM((rows, height, chunk), bf16)],
        compiler_params=params(),
        cost_estimate=cost(6),
        name="layer_sums",
    )(place, *pair, *attn, parts, earlier)


def layer_unpack_kernel(cols, place_ref, even_ref, odd_ref, down_ref, up_ref, out_ref, small_ref):
    me = 2 * place_ref[0] + place_ref[1]
    half = down_ref.shape[1] // 2
    size, share, few = down_ref.shape[0] // cols, up_ref.shape[0], out_ref.shape[0] // cols
    chunk = up_ref.shape[1] // cols
    for ref, odd in ((even_ref, 0), (odd_ref, 1)):
        for i in range(cols // 2):
            spot = me ^ (2 * i + odd)
            part = ref[i].astype(f32)
            down_rows = pl.ds(pl.multiple_of(spot * size, 8), size)
            down_ref[down_rows, :half] = part[:size]
            down_ref[down_rows, half:] = part[size:2 * size]
            at = 2 * size + share
            up_ref[:, pl.ds(pl.multiple_of(spot * chunk, PAIR), chunk)] = part[2 * size:at]
            out_rows = pl.ds(pl.multiple_of(spot * few, 8), few)
            out_ref[out_rows, :half] = part[at:at + few]
            out_ref[out_rows, half:] = part[at + few:at + 2 * few]
            if i == 0 and not odd:
                small_ref[...] = part[at + 2 * few:at + 2 * few + 8, :share]


def layer_unpack(place, even, odd, rows, width, units):
    cols = 2 * even.shape[0]
    share = width // rows
    shapes = [(units // rows, width), (share, units), (share, width), (8, share)]
    return pl.pallas_call(
        functools.partial(layer_unpack_kernel, cols),
        in_specs=[scalar()] + [whole()] * 2,
        out_specs=[whole()] * 4,
        out_shape=[jax.ShapeDtypeStruct(x, f32) for x in shapes],
        compiler_params=params(),
        cost_estimate=cost(4),
        name="layer_unpack",
    )(place, even, odd)


def attn_sums_kernel(rows, place_ref, rows_ref, rel_ref, *refs):
    *out_refs, out_ref = refs[-rows - 1:]
    refs = refs[:-rows - 2]
    count = len(refs) // 2
    size = refs[0].shape[0]
    width, places = rows_ref.shape[1], rel_ref.shape[0]
    table_q = table_k = query = key = value = 0.0
    for j in range(count):
        rows_in = rows_ref[j * BLK:(j + 1) * BLK, :]
        q_ref, k_ref = refs[j], refs[count + j]
        query = query + dot(q_ref[:, places:], rows_in, NN)
        key = key + dot(k_ref[:, places:places + BLK], rows_in, NN)
        value = value + dot(k_ref[:, places + BLK:], rows_in, NN)
        table_k = table_k + q_ref[:, :places].astype(f32)
        table_q = table_q + k_ref[:, :places].astype(f32)
    query = query + dot(table_q.astype(bf16), rel_ref[...], NN)
    key = key + dot(table_k.astype(bf16), rel_ref[...], NN)
    pieces = [query, key, value]
    fill = -3 * size % PAIR
    if fill:
        pieces.append(jnp.zeros((fill, width), f32))
    full_sum = jnp.concatenate(pieces, axis=0).T
    share, spots = width // rows, places // rows
    wide = full_sum.shape[1]
    both = jnp.concatenate([table_q, table_k], axis=0)
    lines = 2 * size * spots // wide
    for r in range(rows):
        cut = both[:, r * spots:(r + 1) * spots]
        cut = lanes([cut[j * lines:(j + 1) * lines] for j in range(wide // spots)])
        out_ref[r] = jnp.concatenate([full_sum[r * share:(r + 1) * share], cut], axis=0).astype(bf16)
    for k, ref in enumerate(out_refs):
        ref[...] = out_ref[place_ref[2] ^ k]


def attn_sums(place, rows_in, rel, q_parts, k_parts, earlier, rows):
    size = q_parts[0].shape[0]
    width, places = rows_in.shape[1], rel.shape[0]
    wide = 3 * size + (-3 * size % PAIR)
    height = width // rows + 2 * size * (places // rows) // wide
    return pl.pallas_call(
        functools.partial(attn_sums_kernel, rows),
        in_specs=[scalar()] + [whole()] * (2 + len(q_parts) + len(k_parts)) + [unread()],
        out_specs=[whole()] * rows,
        out_shape=[jax.ShapeDtypeStruct((height, wide), bf16)] * rows,
        scratch_shapes=[pltpu.VMEM((rows, height, wide), bf16)],
        compiler_params=params(),
        cost_estimate=cost(5),
        name="attn_sums",
    )(place, rows_in, rel, *q_parts, *k_parts, earlier)


def attn_unpack_kernel(cols, spots, place_ref, even_ref, odd_ref, wq_ref, wk_ref, q_ref, k_ref, v_ref, rel_ref, all_ref,
                       tq_ref, tk_ref):
    me = 2 * place_ref[0] + place_ref[1]
    share, width = q_ref.shape
    size = width // cols
    for ref, odd in ((even_ref, 0), (odd_ref, 1)):
        for i in range(cols // 2):
            all_ref[me ^ (2 * i + odd)] = ref[i].astype(f32)
    wide = all_ref.shape[2]
    for c in range(cols):
        tail = all_ref[c, share:, :]
        tail = jnp.concatenate([tail[:, j * spots:(j + 1) * spots] for j in range(wide // spots)], axis=0)
        start = (c % 2) * width // 2 + (c // 2) * size
        spot = slice(start, start + size)
        for i, ref in enumerate((q_ref, k_ref, v_ref)):
            ref[:, spot] = all_ref[c, :share, i * size:(i + 1) * size]
        for i, ref in enumerate((tq_ref, tk_ref)):
            ref[spot, :] = tail[i * size:(i + 1) * size].astype(bf16)
    flip = flip_matrix(spots)
    turned_q = dot(tq_ref[...], flip, NN).astype(bf16)
    turned_k = dot(tk_ref[...], flip, NN).astype(bf16)
    across = (((0,), (1,)), ((), ()))
    rel_ref[...] = (dot(turned_q, wq_ref[...], across) + dot(turned_k, wk_ref[...], across)).astype(bf16)


def attn_unpack(place, even, odd, wq, wk, rows, places):
    cols = 2 * even.shape[0]
    width = wq.shape[0]
    share, spots = width // rows, places // rows
    shape = jax.ShapeDtypeStruct((share, width), f32)
    return pl.pallas_call(
        functools.partial(attn_unpack_kernel, cols, spots),
        in_specs=[scalar()] + [whole()] * 4,
        out_specs=[whole()] * 4,
        out_shape=[shape] * 3 + [jax.ShapeDtypeStruct((spots, width), bf16)],
        scratch_shapes=[pltpu.VMEM((cols,) + even.shape[1:], f32), pltpu.VMEM((width, spots), bf16),
                        pltpu.VMEM((width, spots), bf16)],
        compiler_params=params(),
        cost_estimate=cost(5),
        name="attn_unpack",
    )(place, even, odd, wq, wk)


HEADS = 12
EPSILON = 1e-07


def norm_forward(value, gain, shift):
    center = value - jnp.mean(value, axis=-1, keepdims=True)
    scaled = lax.rsqrt(jnp.mean(center * center, axis=-1, keepdims=True) + EPSILON)
    normed = center * scaled
    return (normed * gain + shift, normed, scaled)


def norm_backward(grad_out, normed, scaled, gain):
    grad_normed = grad_out * gain
    inner = grad_normed - jnp.mean(grad_normed, axis=-1, keepdims=True)
    inner = inner - normed * jnp.mean(grad_normed * normed, axis=-1, keepdims=True)
    return (scaled * inner, jnp.sum(grad_out * normed, axis=0), jnp.sum(grad_out, axis=0))


def gelu_exact(value):
    return jax.nn.gelu(value, approximate=False)


def mul(a, b, form=NN):
    return lax.dot_general(a, b, form, preferred_element_type=f32)


def swap(x, axis, k):
    return lax.ppermute(x, axis, [(i, i ^ k) for i in range(lax.axis_size(axis))])


def gather(x, *earlier):
    even = stack([x] + [swap(x, "seq", k) for k in range(2, lax.axis_size("seq"), 2)], *earlier)
    return even, swap(even, "seq", 1)


def gather_parts(x, *earlier):
    twin = swap(x, "seq", 1)
    even = stack([swap(x, "seq", k) for k in range(2, lax.axis_size("seq"), 2)], *earlier)
    return x, twin, even, swap(even, "seq", 1)


def deal_rows(parts):
    total = 0.0
    for k, part in enumerate(parts):
        total = total + (swap(part, "row", k) if k else part).astype(f32)
    return total.astype(bf16)


def deal_chips(parts):
    return [parts[0]] + [swap(part, "seq", 2 * k) for k, part in enumerate(parts) if k]


def in_order(parts, chip):
    out = jnp.zeros((len(parts),) + parts[0].shape, parts[0].dtype)
    for k, part in enumerate(parts):
        out = lax.dynamic_update_slice_in_dim(out, part[None], chip ^ k, 0)
    return out.reshape((-1,) + parts[0].shape[1:])


def reduced(g):
    part = lax.psum_scatter(g.astype(bf16), "row", scatter_dimension=0, tiled=True)
    return lax.psum(part, "seq").astype(f32)


def on_device(
    hidden, segments, rel_embed, query_weight, key_weight, value_weight, output_weight, up_weight, down_weight,
    norm1_gain, norm1_bias, norm2_gain, norm2_bias, cotangent,
):
    tokens, width = hidden.shape[1:]
    places = rel_embed.shape[0]
    units = up_weight.shape[1]
    part = width // 2
    scale = 1.0 / math.sqrt(3.0 * (width // HEADS))
    inputs = hidden[0]
    cols, rows = lax.axis_size("seq"), lax.axis_size("row")
    chip, core = lax.axis_index("seq") // 2, lax.axis_index("seq") % 2
    row = lax.axis_index("row")
    place = jnp.stack([chip, core, row]).astype(jnp.int32)
    share = width // rows
    chunk = units // cols
    dealt = (units // (rows * cols)) % 16 == 0 and places // rows == TOK

    def core_cols(w):
        return lax.dynamic_slice_in_dim(w, core * part, part, 1)

    def meet(x):
        mine = lax.dynamic_index_in_dim(x, core, 0, keepdims=False)
        other = swap(lax.dynamic_index_in_dim(x, 1 - core, 0, keepdims=False), "seq", 1)
        return jnp.where(core == 0, jnp.concatenate([mine, other], axis=-1), jnp.concatenate([other, mine], axis=-1))

    half_q, half_k, half_v = core_cols(query_weight), core_cols(key_weight), core_cols(value_weight)
    half_out = lax.dynamic_slice_in_dim(output_weight, core * part, part, 0)
    rel_flip = mul(flip_matrix(places), rel_embed).astype(bf16)
    qr = mul(rel_flip, half_q).astype(bf16)
    kr = mul(rel_flip, half_k).astype(bf16)
    seg_rows = jnp.pad(segments.astype(bf16), ((0, EXTRA - 1), (0, width - tokens)))
    in_parts = gather_parts(jnp.concatenate([inputs, seg_rows], axis=0), qr, kr)
    q, k, v, row_segs, row_in = project_rows(place, in_parts, half_q, half_k, half_v)
    own_segs = row_segs[0, :BLK].reshape(BLK, 1)

    probs, ctx_half = forward_attention(place, q, k, v, kr, qr, own_segs, row_segs, scale)
    ctx = meet(ctx_half)

    ctx_low = ctx[:tokens].astype(bf16)
    h1 = inputs.astype(f32) + mul(ctx_low, output_weight)
    normed1, unit1, scaled1 = norm_forward(h1, norm1_gain, norm1_bias)
    normed1_low = normed1.astype(bf16)
    inner = mul(normed1_low, up_weight)
    active, gelu_back = jax.vjp(gelu_exact, inner)
    active_low = active.astype(bf16)
    result, unit2, scaled2 = norm_forward(normed1 + mul(active_low, down_weight), norm2_gain, norm2_bias)
    output = result.astype(bf16)[None]
    cot = cotangent[0].astype(f32)
    d_h2, g_gain2, g_bias2 = norm_backward(cot, unit2, scaled2, norm2_gain)
    d_branch = d_h2.astype(bf16)
    d_inner = gelu_back(mul(d_branch, down_weight, NT))[0].astype(bf16)
    d_normed1 = d_h2 + mul(d_inner, up_weight, NT)
    d_h1, g_gain1, g_bias1 = norm_backward(d_normed1, unit1, scaled1, norm1_gain)
    d_attn = d_h1.astype(bf16)
    vectors = jnp.stack([g_gain1, g_bias1, g_gain2, g_bias2])
    attn_pay = attn_out(d_attn, output_weight, ctx, vectors)
    parts = pack([active_low, ctx, d_inner], [rows, rows, 1], cols) if dealt else attn_pay
    twin = swap(attn_pay, "seq", 1)
    dq_half, *q_table = query_grads(place, probs, attn_pay, twin, half_out, ctx_half, v, q, k, kr, parts, scale)
    even = stack([swap(attn_pay, "seq", i) for i in range(2, cols, 2)], dq_half)
    attn = attn_pay, twin, even, swap(even, "seq", 1)
    dk_half, dv_half, *k_table = key_grads(
        place, k, v, q, qr, kr, own_segs, row_segs, attn, half_out, dq_half, scale
    )
    d_own = meet(jnp.concatenate([dq_half, dk_half, dv_half], axis=1))
    dq, dk, dv = (d_own[i * tokens:(i + 1) * tokens] for i in range(3))
    grad_in = d_h1 + mul(dq, query_weight, NT) + mul(dk, key_weight, NT) + mul(dv, value_weight, NT)

    if dealt:
        q_parts = deal_chips(q_table)
        pair = gather(after(jnp.concatenate([normed1_low, d_branch], axis=1), dq_half), dk_half)
        parts = lax.all_to_all(parts, "seq", 0, 0, tiled=True)
        k_parts = deal_chips([after(x, parts, pair[0]) if i == 1 else x for i, x in enumerate(k_table)])
        layer_part = layer_sums(place, pair, attn, parts, dk_half, rows, chunk)
        layer = deal_rows(layer_part)
        g_down, g_up, g_output, small = layer_unpack(place, *gather(layer), rows, width, units)
        attn_part = attn_sums(place, row_in, rel_flip, q_parts, k_parts, layer_part[0], rows)
        sums = deal_rows(attn_part)
        g_query, g_key, g_value, g_rel = attn_unpack(place, *gather(sums), query_weight, key_weight, rows, places)
        blocks = [g_rel] + [swap(g_rel, "row", k) for k in range(1, rows)]
        out = jnp.zeros((rows,) + g_rel.shape, bf16)
        for k, block in enumerate(blocks):
            out = lax.dynamic_update_slice_in_dim(out, block[None], rows - 1 - (row ^ k), 0)
        g_rel = out.reshape(places, width).astype(f32)
    else:
        small = jnp.stack([reduced(x) for x in (g_gain1, g_bias1, g_gain2, g_bias2)])
        g_down = reduced(mul(active_low, d_branch, TN))
        g_up = reduced(mul(normed1_low, d_inner, TN))
        g_output = reduced(mul(ctx_low, d_attn, TN))
        across = (((0,), (1,)), ((), ()))
        d_kr, d_qr = (in_order(x, chip)[:, :places] for x in (q_table, k_table))
        placed = lambda g: lax.dynamic_update_slice_in_dim(jnp.zeros((width, width), f32), g, core * part, 1)
        g_query = reduced(mul(inputs, dq, TN) + placed(mul(rel_flip, d_qr, across)))
        g_key = reduced(mul(inputs, dk, TN) + placed(mul(rel_flip, d_kr, across)))
        g_value = reduced(mul(inputs, dv, TN))
        g_rel = mul(d_qr, half_q, across) + mul(d_kr, half_k, across)
        g_rel = lax.psum(mul(flip_matrix(places), g_rel.astype(bf16)).astype(bf16), ("seq", "row")).astype(f32)

    return (
        output, grad_in.astype(bf16)[None], g_query, g_key, g_value, g_output, g_up, g_down,
        small[0], small[1], small[2], small[3], g_rel,
    )


def solution(mesh):
    split = P("row", "seq", None)
    return jax.shard_map(
        on_device,
        mesh=mesh,
        in_specs=(split, P("row", "seq")) + (P(),) * 11 + (split,),
        out_specs=(split, split) + (P("row", None),) * 6 + (P("row"),) * 4 + (P(),),
        check_vma=False,
    )
```

time: 682 us -> 257 us (0.38)
  waiting for transfers between devices: 439 us -> 73.5 us
  blocking collectives: 54.6 us -> 0 us
  starting transfers between devices: 0.67 us -> 43.6 us
  matrix products: 60.1 us -> 18.7 us
  Pallas kernels: 49 us -> 90.4 us
  local copies, waits for them, and re-layouts: 49.9 us -> 18.1 us
  between operations: 15.6 us -> 1.33 us
    reduce_scatter x3 -> x0, waiting for transfers between devices: 203 us -> none  [on_device(): lax.psum_scatter(g.astype(bf16), 'row', scatter_dimension=0, tiled=True)]
    psum x2 -> x0, waiting for transfers between devices: 175 us -> none  [the longest x1 104 us: on_device(): lax.psum(g_rel.astype(bf16), ('seq', 'row')).astype(f32)]
    ppermute x0 -> x39, waiting for transfers between devices: none -> 68.6 us  [swap(): lax.ppermute(x, axis, [(i, i ^ k) for i in range(lax.axis_size(axis))])]
    unnamed x13 -> x0, waiting for transfers between devices: 59.5 us -> none
    pallas_call x3 -> x16, Pallas kernels: 33.7 us -> 76.7 us  [the longest x1 20.6 us: key_grads(): pl.pallas_call(functools.partial(key_grad_kernel, scale, length, pairs, c...]
    dot_general x29 -> x11, matrix products: 60.1 us -> 18.7 us  [mul(): return lax.dot_general(a, b, form, preferred_element_type=f32)]
    ppermute x0 -> x39, starting transfers between devices: none -> 40 us  [swap(): lax.ppermute(x, axis, [(i, i ^ k) for i in range(lax.axis_size(axis))])]
    all_gather x3 -> x0, blocking collectives: 31.6 us -> none  [gather(): return lax.all_gather(a, 'seq', axis=axis, tiled=True)]
  transfers between devices with their start and end apart: 10 -> 40, of which waited for: 9 -> 14; matrix products, arithmetic and copies ran while one was open for 11% -> 6% of each run, Pallas kernels for 3% -> 22%
where the time goes in v3:
time: 257 us; the launch traced here: 255 us
  Pallas kernels  90.4 us (35%)
  waiting for transfers between devices  73.5 us (29%)
  starting transfers between devices  43.6 us (17%)
  matrix products  18.7 us (7%)
  local copies, waits for them, and re-layouts  18.1 us (7%)
  other arithmetic  8.97 us (3%)
    ppermute x39, waiting for transfers between devices, swap(): lax.ppermute(x, axis, [(i, i ^ k) for i in range(lax.axis_size(axis))])  68.6 us
    ppermute x39, starting transfers between devices, swap(): lax.ppermute(x, axis, [(i, i ^ k) for i in range(lax.axis_size(axis))])  40 us
    pallas_call x1, Pallas kernels, key_grads(): pl.pallas_call(functools.partial(key_grad_kernel, scale, length, pairs, c...  20.6 us
    dot_general x11, matrix products, mul(): return lax.dot_general(a, b, form, preferred_element_type=f32)  18.7 us
    pallas_call x1, Pallas kernels, forward_attention(): pl.pallas_call(functools.partial(forward_kernel, scale, length), grid=(pa...  13.8 us
    pallas_call x1, Pallas kernels, query_grads(): pl.pallas_call(functools.partial(query_grad_kernel, scale, length, chips)...  13.4 us
    pallas_call x5, Pallas kernels, stack(): pl.pallas_call(functools.partial(stack_kernel, count), in_specs=[whole()]...  11.4 us
    unnamed x102, local copies, waits for them, and re-layouts  11 us
  transfers between devices with their start and end apart: 40, of which 14 were waited for; matrix products, arithmetic and copies ran while one was open for 6% of the time, Pallas kernels for 22%

profile of v3, /device:TPU:0, one launch (start us, length us, event | category | flops | bytes accessed | tf_op | source)
XLA Modules:
  0.0 254.6 jit_solution(17620431971755344727)
XLA Ops:
  1.4 1.8 fusion.22.mine_ref
  3.2 2.9 %collective-permute-start.1 = (bf16[144,768]{1,0:T(8,128)(2,1)}, bf16[144,768]{1,0:T(8,128)(2,1)}, u32[]{:S(2)}, u32[]{:S(2)}) collective-permute-start(bf16[144,768]{1,0:T(8,128)(2,1)} %fusion.22.mine_ref), channel_id=1, source_target_pairs={{0,8},{4,12},{8,0},{12,4},{16,24},{20,28},{24,16},{28,20},{1,9},{5... | collective-permute-start | bytes 663560 | tf_op jit(solution)/shard_map/ppermute | solution.py:674
  6.1 1.5 collective-permute-start.2
  7.7 2.6 %convolution_convert_fusion.rel_ref = bf16[512,768]{1,0:T(8,128)(2,1)} fusion(bf16[512,768]{1,0:T(8,128)(2,1)} %param.16), kind=kOutput, calls=%fused_computation.17 | convolution fusion | flops 404094976 | bytes 1572864 | tf_op jit(solution)/shard_map/dot_general | solution.py:670
  10.4 1.2 copy-done.45
  11.6 1.3 convolution_convert_fusion.2.refs_3_.far_ref.near_ref
  12.9 1.3 convolution_convert_fusion.1.refs_4_.near_ref.far_ref
  14.3 3.8 %collective-permute-done.2.refs_1_ = bf16[144,768]{1,0:T(8,128)(2,1)} collective-permute-done((bf16[144,768]{1,0:T(8,128)(2,1)}, bf16[144,768]{1,0:T(8,128)(2,1)}, u32[]{:S(2)}, u32[]{:S(2)}) %collective-permute-start.2) | collective-permute-done | bytes 221216 | tf_op jit(solution)/shard_map/ppermute | solution.py:674
  18.1 2.0 stack.41.even_ref
  24.3 6.2 %project.1 = (bf16[1024,384]{1,0:T(8,128)(2,1)}, bf16[1024,384]{1,0:T(8,128)(2,1)}, bf16[1024,384]{1,0:T(8,128)(2,1)}, f32[1,1024]{1,0:T(1,128)}, bf16[1024,768]{1,0:T(8,128)(2,1)}) custom-call(s32[3]{0:T(128)} %pad_add_fusion.place_ref, bf16[144,768]{1,0:T(8,128)(2,1)} %fusion.22.mine_ref, bf16[144,768]{1,0:T(8,128)(2,1)} %copy-done.39, ...), custom_call_target="tpu_custom_call" | custom-call | flops 1500000000 | tf_op jit(solution)/shard_map/project/pallas_call | solution.py:425
  32.0 13.8 %attend.1 = (bf16[6,256,1024]{2,1,0:T(8,128)(2,1)}, f32[2,136,384]{2,1,0:T(8,128)}) custom-call(s32[3]{0:T(128)} %pad_add_fusion.place_ref, bf16[1024,384]{1,0:T(8,128)(2,1)} %get-tuple-element.47.q_ref, bf16[1024,384]{1,0:T(8,128)(2,1)} %get-tuple-element.48.k_ref, bf16[1024,384]{1,0:T(8,128)(2,1)} %get-tuple-element.49.v_ref, ...), custom_call_target="tpu_custom_call" | custom-call | flops 4200000000 | tf_op jit(solution)/shard_map/attend/pallas_call | solution.py:291
  45.8 1.2 dynamic-slice_bitcast_fusion.3
  47.2 1.3 collective-permute-done.5
  49.4 6.0 %multiply_convert_fusion = (bf16[128,3072]{1,0:T(8,128)(2,1)S(1)}, f32[128,3072]{1,0:T(8,128)S(1)}, f32[128,3072]{1,0:T(8,128)S(1)}) fusion(bf16[128,768]{1,0:T(8,128)(2,1)S(1)} %fusion.21, bf16[768,3072]{1,0:T(8,128)(2,1)} %param.21), kind=kOutput, calls=%fused_computation.3 | convolution fusion | flops 629538816 | bytes 8847360 | tf_op jit(solution)/shard_map/dot_general | solution.py:670
  57.8 1.9 add_convert_fusion.refs_2_
  59.7 1.9 multiply_reduce_fusion
  61.7 1.0 fusion.31
  63.3 2.7 %attn_out.1.mine_ref = bf16[144,768]{1,0:T(8,128)(2,1)} custom-call(bf16[128,768]{1,0:T(8,128)(2,1)} %get-tuple-element.88.dattn_ref, bf16[768,768]{1,0:T(8,128)(2,1)} %weight_ref.1, f32[136,768]{1,0:T(8,128)} %copy-done.2, f32[4,768]{1,0:T(4,128)} %pad_maximum_fusion.1.vec_ref), custom_call_target="tpu_custom_call" | custom-call | flops 600000000 | tf_op jit(solution)/shard_map/attn_out/pallas_call | solution.py:386
  66.1 1.3 collective-permute-start.7
  68.2 1.4 collective-permute-start.9
  70.5 3.2 %pack.1.earlier_ref = bf16[8,864,128]{2,1,0:T(8,128)(2,1)} custom-call(bf16[128,3072]{1,0:T(8,128)(2,1)} %copy-done.5, f32[136,768]{1,0:T(8,128)} %copy-done.2, bf16[128,3072]{1,0:T(8,128)(2,1)} %copy-done.3), custom_call_target="tpu_custom_call" | custom-call | flops 900000000 | tf_op jit(solution)/shard_map/pack/pallas_call | solution.py:455
  74.4 13.4 %query_grads.1 = (bf16[2,128,384]{2,1,0:T(8,128)(2,1)}, bf16[96,768]{1,0:T(8,128)(2,1)}, bf16[96,768]{1,0:T(8,128)(2,1)}, bf16[96,768]{1,0:T(8,128)(2,1)}, bf16[96,768]{1,0:T(8,128)(2,1)}) custom-call(s32[3]{0:T(128)} %pad_add_fusion.place_ref, bf16[6,256,1024]{2,1,0:T(8,128)(2,1)} %get-tuple-element.52.p_ref, bf16[144,768]{1,0:T(8,128)(2,1)} %attn_out.1.mine_ref, ...), custom_call_target="tpu_custom_call" | custom-call | flops 300000000 | tf_op jit(solution)/shard_map/query_grads/pallas_call | solution.py:322
  88.6 2.0 stack.42.even_ref
  91.5 1.3 collective-permute-start.15
  93.6 1.4 collective-permute-start.17
  94.9 3.6 %all-to-all-start = ((bf16[8,864,128]{2,1,0:T(8,128)(2,1)}), bf16[8,864,128]{2,1,0:T(8,128)(2,1)S(1)}, u32[]{:S(2)}, u32[]{:S(2)}) async-start(bf16[8,864,128]{2,1,0:T(8,128)(2,1)} %pack.1.earlier_ref), calls=%async_computation | async-start | bytes 3538944 | tf_op jit(solution)/shard_map/all_to_all | solution.py:783
  98.6 20.6 %key_grads.1 = (bf16[2,128,384]{2,1,0:T(8,128)(2,1)}, bf16[2,128,384]{2,1,0:T(8,128)(2,1)}, bf16[96,1024]{1,0:T(8,128)(2,1)}, bf16[96,1024]{1,0:T(8,128)(2,1)}, ...) custom-call(s32[3]{0:T(128)} %pad_add_fusion.place_ref, bf16[1024,384]{1,0:T(8,128)(2,1)} %get-tuple-element.48.k_ref, ...), custom_call_target="tpu_custom_call" | custom-call | flops 300000000 | tf_op jit(solution)/shard_map/key_grads/pallas_call | solution.py:345
  119.9 2.6 %stack.43.refs_2_.pair_even_ref = bf16[4,128,1536]{2,1,0:T(8,128)(2,1)} custom-call(bf16[128,1536]{1,0:T(8,128)(2,1)} %after.2.refs_0_, bf16[128,1536]{1,0:T(8,128)(2,1)} %copy-done.22, bf16[128,1536]{1,0:T(8,128)(2,1)} %collective-permute-done.16.refs_2_, bf16[128,1536]{1,0:T(8,128)(2,1)} %collective-permute-done.17.refs_3_, ...), custom_call_target="tpu_custom_call" | custom-call | flops 300000000 | tf_op jit(solution)/shard_map/stack/pallas_call | solution.py:264
  122.9 1.7 collective-permute-start.12
  125.4 1.5 collective-permute-start.19
  127.1 4.9 %all-to-all-done.refs_1_.part_ref = bf16[8,864,128]{2,1,0:T(8,128)(2,1)S(1)} async-done(((bf16[8,864,128]{2,1,0:T(8,128)(2,1)}), bf16[8,864,128]{2,1,0:T(8,128)(2,1)S(1)}, u32[]{:S(2)}, u32[]{:S(2)}) %all-to-all-start) | async-done | bytes 1769504 | tf_op jit(solution)/shard_map/all_to_all | solution.py:783
  132.1 1.2 copy-done.1
  133.3 1.0 collective-permute-start.18
  134.9 1.5 collective-permute-start.13
  136.5 1.0 collective-permute-start.14
  137.5 5.8 %layer_sums.1 = (bf16[448,384]{1,0:T(8,128)(2,1)}, bf16[448,384]{1,0:T(8,128)(2,1)}, bf16[448,384]{1,0:T(8,128)(2,1)}, bf16[448,384]{1,0:T(8,128)(2,1)}) custom-call(s32[3]{0:T(128)} %pad_add_fusion.place_ref, bf16[4,128,1536]{2,1,0:T(8,128)(2,1)} %stack.43.refs_2_.pair_even_ref, bf16[4,128,1536]{2,1,0:T(8,128)(2,1)} %collective-permute-done.21.pair_odd_ref, ...), custom_call_target="tpu_custom_call" | custom-call | flops 1800000000 | tf_op jit(solution)/shard_map/layer_sums/pallas_call | solution.py:505
  143.5 2.9 %collective-permute-done.14.refs_3_ = bf16[96,768]{1,0:T(8,128)(2,1)S(1)} collective-permute-done((bf16[96,768]{1,0:T(8,128)(2,1)}, bf16[96,768]{1,0:T(8,128)(2,1)S(1)}, u32[]{:S(2)}, u32[]{:S(2)}) %collective-permute-start.14) | collective-permute-done | bytes 147488 | tf_op jit(solution)/shard_map/ppermute | solution.py:674
  147.3 4.2 %attn_sums.1 = (bf16[256,384]{1,0:T(8,128)(2,1)}, bf16[256,384]{1,0:T(8,128)(2,1)}, bf16[256,384]{1,0:T(8,128)(2,1)}, bf16[256,384]{1,0:T(8,128)(2,1)}) custom-call(s32[3]{0:T(128)} %pad_add_fusion.place_ref, bf16[1024,768]{1,0:T(8,128)(2,1)} %get-tuple-element.56.rows_ref, bf16[512,768]{1,0:T(8,128)(2,1)} %convolution_convert_fusion.rel_ref, ...), custom_call_target="tpu_custom_call" | custom-call | flops 1500000000 | tf_op jit(solution)/shard_map/attn_sums/pallas_call | solution.py:592
  151.5 3.6 %collective-permute-start.24 = (bf16[256,384]{1,0:T(8,128)(2,1)}, bf16[256,384]{1,0:T(8,128)(2,1)S(1)}, u32[]{:S(2)}, u32[]{:S(2)}) collective-permute-start(bf16[256,384]{1,0:T(8,128)(2,1)} %get-tuple-element.69), channel_id=1, source_target_pairs={{0,3},{1,2},{2,1},{3,0},{4,7},{5,6},{6,5},{7,4},{8,11},{9,10},{10,... | collective-permute-start | bytes 589832 | tf_op jit(solution)/shard_map/ppermute | solution.py:674
  156.1 5.3 %collective-permute-done.24 = bf16[256,384]{1,0:T(8,128)(2,1)S(1)} collective-permute-done((bf16[256,384]{1,0:T(8,128)(2,1)}, bf16[256,384]{1,0:T(8,128)(2,1)S(1)}, u32[]{:S(2)}, u32[]{:S(2)}) %collective-permute-start.24) | collective-permute-done | bytes 196640 | tf_op jit(solution)/shard_map/ppermute | solution.py:674
  161.4 10.5 %collective-permute-done.23 = bf16[256,384]{1,0:T(8,128)(2,1)S(1)} collective-permute-done((bf16[256,384]{1,0:T(8,128)(2,1)}, bf16[256,384]{1,0:T(8,128)(2,1)S(1)}, u32[]{:S(2)}, u32[]{:S(2)}) %collective-permute-start.23) | collective-permute-done | bytes 196640 | tf_op jit(solution)/shard_map/ppermute | solution.py:674
  172.7 2.5 collective-permute-start.31
  175.1 1.9 collective-permute-start.29
  177.0 1.2 collective-permute-start.26
  178.3 1.7 collective-permute-start.27
  180.1 6.0 %collective-permute-done.26.refs_2_ = bf16[256,384]{1,0:T(8,128)(2,1)} collective-permute-done((bf16[256,384]{1,0:T(8,128)(2,1)S(1)}, bf16[256,384]{1,0:T(8,128)(2,1)}, u32[]{:S(2)}, u32[]{:S(2)}) %collective-permute-start.26) | collective-permute-done | bytes 196640 | tf_op jit(solution)/shard_map/ppermute | solution.py:674
  186.2 2.2 stack.44.even_ref
  188.4 14.3 %collective-permute-done.30 = bf16[448,384]{1,0:T(8,128)(2,1)S(1)} collective-permute-done((bf16[448,384]{1,0:T(8,128)(2,1)}, bf16[448,384]{1,0:T(8,128)(2,1)S(1)}, u32[]{:S(2)}, u32[]{:S(2)}) %collective-permute-start.30) | collective-permute-done | bytes 344096 | tf_op jit(solution)/shard_map/ppermute | solution.py:674
  202.8 1.6 collective-permute-start.32
  204.8 1.6 collective-permute-start.34
  207.5 6.4 %collective-permute-done.32.refs_1_ = bf16[448,384]{1,0:T(8,128)(2,1)S(1)} collective-permute-done((bf16[448,384]{1,0:T(8,128)(2,1)S(1)}, bf16[448,384]{1,0:T(8,128)(2,1)S(1)}, u32[]{:S(2)}, u32[]{:S(2)}) %collective-permute-start.32) | collective-permute-done | bytes 344096 | tf_op jit(solution)/shard_map/ppermute | solution.py:674
  213.9 5.2 %collective-permute-done.33.refs_2_ = bf16[448,384]{1,0:T(8,128)(2,1)S(1)} collective-permute-done((bf16[448,384]{1,0:T(8,128)(2,1)S(1)}, bf16[448,384]{1,0:T(8,128)(2,1)S(1)}, u32[]{:S(2)}, u32[]{:S(2)}) %collective-permute-start.33) | collective-permute-done | bytes 344096 | tf_op jit(solution)/shard_map/ppermute | solution.py:674
  220.6 2.5 stack.45.even_ref
  223.1 1.2 fusion.7
  224.3 4.7 %attn_unpack.1 = (f32[192,768]{1,0:T(8,128)}, f32[192,768]{1,0:T(8,128)}, f32[192,768]{1,0:T(8,128)}, bf16[128,768]{1,0:T(8,128)(2,1)}) custom-call(s32[3]{0:T(128)} %pad_add_fusion.place_ref, bf16[4,256,384]{2,1,0:T(8,128)(2,1)} %stack.44.even_ref, bf16[4,256,384]{2,1,0:T(8,128)(2,1)} %collective-permute-done.28.odd_ref, bf16[768,768]{1,0:T(8,128)(2,1)} %wq_ref.1, ...), custom_call_target="tpu_custom_call" | custom-call | flops 1500000000 | tf_op jit(solution)/shard_map/attn_unpack/pallas_call | solution.py:634
  229.0 2.5 collective-permute-start.37
  231.5 1.9 collective-permute-start.38
  233.5 1.0 bitcast_dynamic-update-slice_fusion.3
  234.4 5.7 %collective-permute-done.36 = bf16[128,768]{1,0:T(8,128)(2,1)S(1)} collective-permute-done((bf16[128,768]{1,0:T(8,128)(2,1)}, bf16[128,768]{1,0:T(8,128)(2,1)S(1)}, u32[]{:S(2)}, u32[]{:S(2)}) %collective-permute-start.36) | collective-permute-done | bytes 196640 | tf_op jit(solution)/shard_map/ppermute | solution.py:674
  240.1 6.2 %collective-permute-done.37 = bf16[128,768]{1,0:T(8,128)(2,1)S(1)} collective-permute-done((bf16[128,768]{1,0:T(8,128)(2,1)}, bf16[128,768]{1,0:T(8,128)(2,1)S(1)}, u32[]{:S(2)}, u32[]{:S(2)}) %collective-permute-start.37) | collective-permute-done | bytes 196640 | tf_op jit(solution)/shard_map/ppermute | solution.py:674
  246.4 1.3 bitcast_convert_fusion
  247.7 1.1 copy-done.37
  248.8 4.5 %layer_unpack.1 = (f32[768,768]{1,0:T(8,128)}, f32[192,3072]{1,0:T(8,128)}, f32[192,768]{1,0:T(8,128)}, f32[8,192]{1,0:T(8,128)}) custom-call(s32[3]{0:T(128)} %pad_add_fusion.place_ref, bf16[4,448,384]{2,1,0:T(8,128)(2,1)} %stack.45.even_ref, bf16[4,448,384]{2,1,0:T(8,128)(2,1)} %copy-done.37), custom_call_target="tpu_custom_call" | custom-call | flops 1200000000 | tf_op jit(solution)/shard_map/layer_unpack/pallas_call | solution.py:542
  253.2 1.4 fusion.33
  (191 shorter events, 24.3 us)
Async XLA Ops:
  0.6 20.6 %copy-start = (bf16[768,768]{1,0:T(8,128)(2,1)S(1)}, bf16[768,768]{1,0:T(8,128)(2,1)}, u32[]{:S(2)}) copy-start(bf16[768,768]{1,0:T(8,128)(2,1)} %param.19) | copy-start | bytes 3538948
  1.4 8.9 %copy-start.7 = (bf16[768,768]{1,0:T(8,128)(2,1)S(1)}, bf16[768,768]{1,0:T(8,128)(2,1)}, u32[]{:S(2)}) copy-start(bf16[768,768]{1,0:T(8,128)(2,1)} %wk_ref.1) | copy-start | bytes 3538948
  1.4 8.9 %copy-start.9 = (bf16[768,768]{1,0:T(8,128)(2,1)S(1)}, bf16[768,768]{1,0:T(8,128)(2,1)}, u32[]{:S(2)}) copy-start(bf16[768,768]{1,0:T(8,128)(2,1)} %wq_ref.1) | copy-start | bytes 3538948
  3.2 11.1 %collective-permute-start.1 = (bf16[144,768]{1,0:T(8,128)(2,1)}, bf16[144,768]{1,0:T(8,128)(2,1)}, u32[]{:S(2)}, u32[]{:S(2)}) collective-permute-start(bf16[144,768]{1,0:T(8,128)(2,1)} %fusion.22.mine_ref), channel_id=1, source_target_pairs={{0,8},{4,12},{8,0},{12,4},{16,24},{20,28},{24,16},{28,20},{1,9},{5... | collective-permute-start | bytes 663560 | tf_op jit(solution)/shard_map/ppermute | solution.py:674
  6.1 11.9 %collective-permute-start.2 = (bf16[144,768]{1,0:T(8,128)(2,1)}, bf16[144,768]{1,0:T(8,128)(2,1)}, u32[]{:S(2)}, u32[]{:S(2)}) collective-permute-start(bf16[144,768]{1,0:T(8,128)(2,1)} %fusion.22.mine_ref), channel_id=1, source_target_pairs={{0,16},{4,20},{8,24},{12,28},{16,0},{20,4},{24,8},{28,12},{1,17},{... | collective-permute-start | bytes 663560 | tf_op jit(solution)/shard_map/ppermute | solution.py:674
  7.7 10.4 %collective-permute-start.3 = (bf16[144,768]{1,0:T(8,128)(2,1)}, bf16[144,768]{1,0:T(8,128)(2,1)}, u32[]{:S(2)}, u32[]{:S(2)}) collective-permute-start(bf16[144,768]{1,0:T(8,128)(2,1)} %fusion.22.mine_ref), channel_id=1, source_target_pairs={{0,24},{4,28},{8,16},{12,20},{16,8},{20,12},{24,0},{28,4},{1,25},{... | collective-permute-start | bytes 663560 | tf_op jit(solution)/shard_map/ppermute | solution.py:674
  10.4 3.9 %copy-start.20 = (bf16[768,384]{1,0:T(8,128)(2,1)}, bf16[768,384]{1,0:T(8,128)(2,1)S(1)}, u32[]{:S(2)}) copy-start(bf16[768,384]{1,0:T(8,128)(2,1)S(1)} %get-tuple-element.108.wk_ref) | copy-start | bytes 1769476
  10.4 3.9 %copy-start.21 = (bf16[768,384]{1,0:T(8,128)(2,1)}, bf16[768,384]{1,0:T(8,128)(2,1)S(1)}, u32[]{:S(2)}) copy-start(bf16[768,384]{1,0:T(8,128)(2,1)S(1)} %get-tuple-element.109.wq_ref) | copy-start | bytes 1769476
  20.1 2.6 %collective-permute-start.4 = (bf16[3,144,768]{2,1,0:T(8,128)(2,1)}, bf16[3,144,768]{2,1,0:T(8,128)(2,1)S(1)}, u32[]{:S(2)}, u32[]{:S(2)}) collective-permute-start(bf16[3,144,768]{2,1,0:T(8,128)(2,1)} %stack.41.even_ref), channel_id=1, source_target_pairs={{0,4},{4,0},{8,12},{12,8},{16,20},{20,16},{24,28},{28,24},{1,5},{5... | collective-permute-start | bytes 1990664 | tf_op jit(solution)/shard_map/ppermute | solution.py:674
  20.1 2.6 %collective-permute-start = (bf16[144,768]{1,0:T(8,128)(2,1)}, bf16[144,768]{1,0:T(8,128)(2,1)S(1)}, u32[]{:S(2)}, u32[]{:S(2)}) collective-permute-start(bf16[144,768]{1,0:T(8,128)(2,1)} %fusion.22.mine_ref), channel_id=1, source_target_pairs={{0,4},{4,0},{8,12},{12,8},{16,20},{20,16},{24,28},{28,24},{1,5},{5... | collective-permute-start | bytes 663560 | tf_op jit(solution)/shard_map/ppermute | solution.py:674
  32.0 15.2 %copy-start.4 = (bf16[1,128,768]{2,1,0:T(8,128)(2,1)S(1)}, bf16[1,128,768]{2,1,0:T(8,128)(2,1)}, u32[]{:S(2)}) copy-start(bf16[1,128,768]{2,1,0:T(8,128)(2,1)} %param.27) | copy-start | bytes 589828
  46.9 1.5 collective-permute-start.5
  49.0 6.4 %slice-start.2 = ((s8[4718592]{0:T(1024)(128)(4,1)}), s8[4194304]{0:T(1024)(128)(4,1)S(1)}, s32[]{:S(2)}) async-start(s8[4718592]{0:T(1024)(128)(4,1)} %bitcast.77), calls=%async_computation.3 | async-start | bytes 8388608
  49.4 6.0 %slice-start.3 = ((s8[4718592]{0:T(1024)(128)(4,1)}), s8[524288]{0:T(1024)(128)(4,1)S(1)}, s32[]{:S(2)}) async-start(s8[4718592]{0:T(1024)(128)(4,1)} %bitcast.77), calls=%async_computation.4 | async-start | bytes 1048576
  56.9 2.8 %slice-start = ((s8[4718592]{0:T(1024)(128)(4,1)}), s8[4194304]{0:T(1024)(128)(4,1)S(1)}, s32[]{:S(2)}) async-start(s8[4718592]{0:T(1024)(128)(4,1)} %bitcast.75), calls=%async_computation.1 | async-start | bytes 8388608
  61.7 7.9 %copy-start.12 = (bf16[768,768]{1,0:T(8,128)(2,1)S(1)}, bf16[768,768]{1,0:T(8,128)(2,1)}, u32[]{:S(2)}) copy-start(bf16[768,768]{1,0:T(8,128)(2,1)} %weight_ref.1) | copy-start | bytes 3538948
  66.0 7.8 %collective-permute-start.6 = (bf16[144,768]{1,0:T(8,128)(2,1)}, bf16[144,768]{1,0:T(8,128)(2,1)S(1)}, u32[]{:S(2)}, u32[]{:S(2)}) collective-permute-start(bf16[144,768]{1,0:T(8,128)(2,1)} %attn_out.1.mine_ref), channel_id=1, source_target_pairs={{0,4},{4,0},{8,12},{12,8},{16,20},{20,16},{24,28},{28,24},{1,5},{5... | collective-permute-start | bytes 663560 | tf_op jit(solution)/shard_map/ppermute | solution.py:674
  66.1 21.7 %collective-permute-start.7 = (bf16[144,768]{1,0:T(8,128)(2,1)}, bf16[144,768]{1,0:T(8,128)(2,1)S(1)}, u32[]{:S(2)}, u32[]{:S(2)}) collective-permute-start(bf16[144,768]{1,0:T(8,128)(2,1)} %attn_out.1.mine_ref), channel_id=1, source_target_pairs={{0,8},{4,12},{8,0},{12,4},{16,24},{20,28},{24,16},{28,20},{1,9},{5... | collective-permute-start | bytes 663560 | tf_op jit(solution)/shard_map/ppermute | solution.py:674
  67.4 20.4 %collective-permute-start.8 = (bf16[144,768]{1,0:T(8,128)(2,1)}, bf16[144,768]{1,0:T(8,128)(2,1)S(1)}, u32[]{:S(2)}, u32[]{:S(2)}) collective-permute-start(bf16[144,768]{1,0:T(8,128)(2,1)} %attn_out.1.mine_ref), channel_id=1, source_target_pairs={{0,16},{4,20},{8,24},{12,28},{16,0},{20,4},{24,8},{28,12},{1,17},{... | collective-permute-start | bytes 663560 | tf_op jit(solution)/shard_map/ppermute | solution.py:674
  68.2 19.6 %collective-permute-start.9 = (bf16[144,768]{1,0:T(8,128)(2,1)}, bf16[144,768]{1,0:T(8,128)(2,1)S(1)}, u32[]{:S(2)}, u32[]{:S(2)}) collective-permute-start(bf16[144,768]{1,0:T(8,128)(2,1)} %attn_out.1.mine_ref), channel_id=1, source_target_pairs={{0,24},{4,28},{8,16},{12,20},{16,8},{20,12},{24,0},{28,4},{1,25},{... | collective-permute-start | bytes 663560 | tf_op jit(solution)/shard_map/ppermute | solution.py:674
  90.7 7.9 %collective-permute-start.10 = (bf16[3,144,768]{2,1,0:T(8,128)(2,1)}, bf16[3,144,768]{2,1,0:T(8,128)(2,1)}, u32[]{:S(2)}, u32[]{:S(2)}) collective-permute-start(bf16[3,144,768]{2,1,0:T(8,128)(2,1)} %stack.42.even_ref), channel_id=1, source_target_pairs={{0,4},{4,0},{8,12},{12,8},{16,20},{20,16},{24,28},{28,24},{1,5},{5... | collective-permute-start | bytes 1990664 | tf_op jit(solution)/shard_map/ppermute | solution.py:674
  91.5 27.7 %collective-permute-start.15 = (bf16[128,1536]{1,0:T(8,128)(2,1)}, bf16[128,1536]{1,0:T(8,128)(2,1)S(1)}, u32[]{:S(2)}, u32[]{:S(2)}) collective-permute-start(bf16[128,1536]{1,0:T(8,128)(2,1)} %after.2.refs_0_), channel_id=1, source_target_pairs={{0,8},{4,12},{8,0},{12,4},{16,24},{20,28},{24,16},{28,20},{1,9},{5... | collective-permute-start | bytes 1179656 | tf_op jit(solution)/shard_map/ppermute | solution.py:674
  92.7 26.5 %collective-permute-start.16 = (bf16[128,1536]{1,0:T(8,128)(2,1)}, bf16[128,1536]{1,0:T(8,128)(2,1)}, u32[]{:S(2)}, u32[]{:S(2)}) collective-permute-start(bf16[128,1536]{1,0:T(8,128)(2,1)} %after.2.refs_0_), channel_id=1, source_target_pairs={{0,16},{4,20},{8,24},{12,28},{16,0},{20,4},{24,8},{28,12},{1,17},{... | collective-permute-start | bytes 1179656 | tf_op jit(solution)/shard_map/ppermute | solution.py:674
  93.6 25.6 %collective-permute-start.17 = (bf16[128,1536]{1,0:T(8,128)(2,1)}, bf16[128,1536]{1,0:T(8,128)(2,1)}, u32[]{:S(2)}, u32[]{:S(2)}) collective-permute-start(bf16[128,1536]{1,0:T(8,128)(2,1)} %after.2.refs_0_), channel_id=1, source_target_pairs={{0,24},{4,28},{8,16},{12,20},{16,8},{20,12},{24,0},{28,4},{1,25},{... | collective-permute-start | bytes 1179656 | tf_op jit(solution)/shard_map/ppermute | solution.py:674
  94.9 37.1 %all-to-all-start = ((bf16[8,864,128]{2,1,0:T(8,128)(2,1)}), bf16[8,864,128]{2,1,0:T(8,128)(2,1)S(1)}, u32[]{:S(2)}, u32[]{:S(2)}) async-start(bf16[8,864,128]{2,1,0:T(8,128)(2,1)} %pack.1.earlier_ref), calls=%async_computation | async-start | bytes 3538944 | tf_op jit(solution)/shard_map/all_to_all | solution.py:783
  119.9 4.7 %copy-start.6 = (bf16[2,128,384]{2,1,0:T(8,128)(2,1)S(1)}, bf16[2,128,384]{2,1,0:T(8,128)(2,1)}, u32[]{:S(2)}) copy-start(bf16[2,128,384]{2,1,0:T(8,128)(2,1)} %get-tuple-element.53.refs_3_.earlier_ref.refs_1_) | copy-start | bytes 589828
  119.9 7.0 %copy-start.40 = (bf16[96,1024]{1,0:T(8,128)(2,1)S(1)}, bf16[96,1024]{1,0:T(8,128)(2,1)}, u32[]{:S(2)}) copy-start(bf16[96,1024]{1,0:T(8,128)(2,1)} %get-tuple-element.64) | copy-start | bytes 589828
  122.6 13.9 %collective-permute-start.21 = (bf16[4,128,1536]{2,1,0:T(8,128)(2,1)}, bf16[4,128,1536]{2,1,0:T(8,128)(2,1)}, u32[]{:S(2)}, u32[]{:S(2)}) collective-permute-start(bf16[4,128,1536]{2,1,0:T(8,128)(2,1)} %stack.43.refs_2_.pair_even_ref), channel_id=1, source_target_pairs={{0,4},{4,0},{8,12},{12,8},{16,20},{20,16},{24,28},{28,24},{1,5},{5... | collective-permute-start | bytes 4718600 | tf_op jit(solution)/shard_map/ppermute | solution.py:674
  122.9 12.0 %collective-permute-start.12 = (bf16[96,768]{1,0:T(8,128)(2,1)}, bf16[96,768]{1,0:T(8,128)(2,1)}, u32[]{:S(2)}, u32[]{:S(2)}) collective-permute-start(bf16[96,768]{1,0:T(8,128)(2,1)} %get-tuple-element.58), channel_id=1, source_target_pairs={{0,8},{4,12},{8,0},{12,4},{16,24},{20,28},{24,16},{28,20},{1,9},{5... | collective-permute-start | bytes 442376 | tf_op jit(solution)/shard_map/ppermute | solution.py:674
  125.4 21.1 %collective-permute-start.19 = (bf16[96,1024]{1,0:T(8,128)(2,1)}, bf16[96,1024]{1,0:T(8,128)(2,1)S(1)}, u32[]{:S(2)}, u32[]{:S(2)}) collective-permute-start(bf16[96,1024]{1,0:T(8,128)(2,1)} %get-tuple-element.63), channel_id=1, source_target_pairs={{0,16},{4,20},{8,24},{12,28},{16,0},{20,4},{24,8},{28,12},{1,17},{... | collective-permute-start | bytes 589832 | tf_op jit(solution)/shard_map/ppermute | solution.py:674
  126.9 19.6 %collective-permute-start.20 = (bf16[96,1024]{1,0:T(8,128)(2,1)S(1)}, bf16[96,1024]{1,0:T(8,128)(2,1)}, u32[]{:S(2)}, u32[]{:S(2)}) collective-permute-start(bf16[96,1024]{1,0:T(8,128)(2,1)S(1)} %copy-done.40), channel_id=1, source_target_pairs={{0,24},{4,28},{8,16},{12,20},{16,8},{20,12},{24,0},{28,4},{1,25},{... | collective-permute-start | bytes 589832 | tf_op jit(solution)/shard_map/ppermute | solution.py:674
  133.3 13.2 %collective-permute-start.18 = (bf16[96,1024]{1,0:T(8,128)(2,1)}, bf16[96,1024]{1,0:T(8,128)(2,1)S(1)}, u32[]{:S(2)}, u32[]{:S(2)}) collective-permute-start(bf16[96,1024]{1,0:T(8,128)(2,1)} %after.3), channel_id=1, source_target_pairs={{0,8},{4,12},{8,0},{12,4},{16,24},{20,28},{24,16},{28,20},{1,9},{5... | collective-permute-start | bytes 589832 | tf_op jit(solution)/shard_map/ppermute | solution.py:674
  134.9 8.6 %collective-permute-start.13 = (bf16[96,768]{1,0:T(8,128)(2,1)}, bf16[96,768]{1,0:T(8,128)(2,1)S(1)}, u32[]{:S(2)}, u32[]{:S(2)}) collective-permute-start(bf16[96,768]{1,0:T(8,128)(2,1)} %get-tuple-element.59), channel_id=1, source_target_pairs={{0,16},{4,20},{8,24},{12,28},{16,0},{20,4},{24,8},{28,12},{1,17},{... | collective-permute-start | bytes 442376 | tf_op jit(solution)/shard_map/ppermute | solution.py:674
  136.5 10.0 %collective-permute-start.14 = (bf16[96,768]{1,0:T(8,128)(2,1)}, bf16[96,768]{1,0:T(8,128)(2,1)S(1)}, u32[]{:S(2)}, u32[]{:S(2)}) collective-permute-start(bf16[96,768]{1,0:T(8,128)(2,1)} %get-tuple-element.60), channel_id=1, source_target_pairs={{0,24},{4,28},{8,16},{12,20},{16,8},{20,12},{24,0},{28,4},{1,25},{... | collective-permute-start | bytes 442376 | tf_op jit(solution)/shard_map/ppermute | solution.py:674
  143.5 3.0 %copy-start.43 = (bf16[96,768]{1,0:T(8,128)(2,1)}, bf16[96,768]{1,0:T(8,128)(2,1)S(1)}, u32[]{:S(2)}) copy-start(bf16[96,768]{1,0:T(8,128)(2,1)S(1)} %collective-permute-done.13.refs_2_) | copy-start | bytes 442372
  147.3 8.6 %copy-start.17 = (bf16[2,384,384]{2,1,0:T(8,128)(2,1)S(1)}, bf16[2,384,384]{2,1,0:T(8,128)(2,1)}, u32[]{:S(2)}) copy-start(bf16[2,384,384]{2,1,0:T(8,128)(2,1)} %constant_dynamic-update-slice_fusion.1) | copy-start | bytes 1769476
  147.3 8.6 %copy-start.31 = (bf16[2,128,384]{2,1,0:T(8,128)(2,1)S(1)}, bf16[2,128,384]{2,1,0:T(8,128)(2,1)}, u32[]{:S(2)}) copy-start(bf16[2,128,384]{2,1,0:T(8,128)(2,1)} %get-tuple-element.55) | copy-start | bytes 589828
  151.5 20.4 %copy-start.32 = (bf16[256,384]{1,0:T(8,128)(2,1)S(1)}, bf16[256,384]{1,0:T(8,128)(2,1)}, u32[]{:S(2)}) copy-start(bf16[256,384]{1,0:T(8,128)(2,1)} %get-tuple-element.66) | copy-start | bytes 589828
  151.5 9.9 %collective-permute-start.24 = (bf16[256,384]{1,0:T(8,128)(2,1)}, bf16[256,384]{1,0:T(8,128)(2,1)S(1)}, u32[]{:S(2)}, u32[]{:S(2)}) collective-permute-start(bf16[256,384]{1,0:T(8,128)(2,1)} %get-tuple-element.69), channel_id=1, source_target_pairs={{0,3},{1,2},{2,1},{3,0},{4,7},{5,6},{6,5},{7,4},{8,11},{9,10},{10,... | collective-permute-start | bytes 589832 | tf_op jit(solution)/shard_map/ppermute | solution.py:674
  155.1 16.8 %collective-permute-start.23 = (bf16[256,384]{1,0:T(8,128)(2,1)}, bf16[256,384]{1,0:T(8,128)(2,1)S(1)}, u32[]{:S(2)}, u32[]{:S(2)}) collective-permute-start(bf16[256,384]{1,0:T(8,128)(2,1)} %get-tuple-element.68), channel_id=1, source_target_pairs={{0,2},{1,3},{2,0},{3,1},{4,6},{5,7},{6,4},{7,5},{8,10},{9,11},{10,... | collective-permute-start | bytes 589832 | tf_op jit(solution)/shard_map/ppermute | solution.py:674
  155.1 16.8 %collective-permute-start.22 = (bf16[256,384]{1,0:T(8,128)(2,1)}, bf16[256,384]{1,0:T(8,128)(2,1)S(1)}, u32[]{:S(2)}, u32[]{:S(2)}) collective-permute-start(bf16[256,384]{1,0:T(8,128)(2,1)} %get-tuple-element.67), channel_id=1, source_target_pairs={{0,1},{1,0},{2,3},{3,2},{4,5},{5,4},{6,7},{7,6},{8,9},{9,8},{10,11... | collective-permute-start | bytes 589832 | tf_op jit(solution)/shard_map/ppermute | solution.py:674
  156.0 21.0 %collective-permute-start.11 = (bf16[384,384]{1,0:T(8,128)(2,1)S(1)}, bf16[384,384]{1,0:T(8,128)(2,1)S(1)}, u32[]{:S(2)}, u32[]{:S(2)}) collective-permute-start(bf16[384,384]{1,0:T(8,128)(2,1)S(1)} %get-tuple-element.93), channel_id=1, source_target_pairs={{0,4},{4,0},{8,12},{12,8},{16,20},{20,16},{24,28},{28,24},{1,5},{5... | collective-permute-start | bytes 884744 | tf_op jit(solution)/shard_map/ppermute | solution.py:674
  172.0 14.2 %copy-start.19 = (bf16[256,384]{1,0:T(8,128)(2,1)}, bf16[256,384]{1,0:T(8,128)(2,1)S(1)}, u32[]{:S(2)}) copy-start(bf16[256,384]{1,0:T(8,128)(2,1)S(1)} %add_convert_fusion.2.refs_0_) | copy-start | bytes 589828
  172.0 30.6 %copy-start.23 = (bf16[448,384]{1,0:T(8,128)(2,1)S(1)}, bf16[448,384]{1,0:T(8,128)(2,1)}, u32[]{:S(2)}) copy-start(bf16[448,384]{1,0:T(8,128)(2,1)} %get-tuple-element.65.refs_8_) | copy-start | bytes 1032196
  172.0 6.2 %collective-permute-start.25 = (bf16[256,384]{1,0:T(8,128)(2,1)S(1)}, bf16[256,384]{1,0:T(8,128)(2,1)S(1)}, u32[]{:S(2)}, u32[]{:S(2)}) collective-permute-start(bf16[256,384]{1,0:T(8,128)(2,1)S(1)} %add_convert_fusion.2.refs_0_), channel_id=1, source_target_pairs={{0,8},{4,12},{8,0},{12,4},{16,24},{20,28},{24,16},{28,20},{1,9},{5... | collective-permute-start | bytes 589832 | tf_op jit(solution)/shard_map/ppermute | solution.py:674
  172.7 15.7 %collective-permute-start.31 = (bf16[448,384]{1,0:T(8,128)(2,1)}, bf16[448,384]{1,0:T(8,128)(2,1)S(1)}, u32[]{:S(2)}, u32[]{:S(2)}) collective-permute-start(bf16[448,384]{1,0:T(8,128)(2,1)} %get-tuple-element.75), channel_id=1, source_target_pairs={{0,3},{1,2},{2,1},{3,0},{4,7},{5,6},{6,5},{7,4},{8,11},{9,10},{10,... | collective-permute-start | bytes 1032200 | tf_op jit(solution)/shard_map/ppermute | solution.py:674
  175.1 27.5 %collective-permute-start.30 = (bf16[448,384]{1,0:T(8,128)(2,1)}, bf16[448,384]{1,0:T(8,128)(2,1)S(1)}, u32[]{:S(2)}, u32[]{:S(2)}) collective-permute-start(bf16[448,384]{1,0:T(8,128)(2,1)} %get-tuple-element.74), channel_id=1, source_target_pairs={{0,2},{1,3},{2,0},{3,1},{4,6},{5,7},{6,4},{7,5},{8,10},{9,11},{10,... | collective-permute-start | bytes 1032200 | tf_op jit(solution)/shard_map/ppermute | solution.py:674
  175.1 27.5 %collective-permute-start.29 = (bf16[448,384]{1,0:T(8,128)(2,1)}, bf16[448,384]{1,0:T(8,128)(2,1)S(1)}, u32[]{:S(2)}, u32[]{:S(2)}) collective-permute-start(bf16[448,384]{1,0:T(8,128)(2,1)} %get-tuple-element.73), channel_id=1, source_target_pairs={{0,1},{1,0},{2,3},{3,2},{4,5},{5,4},{6,7},{7,6},{8,9},{9,8},{10,11... | collective-permute-start | bytes 1032200 | tf_op jit(solution)/shard_map/ppermute | solution.py:674
  177.0 9.1 %collective-permute-start.26 = (bf16[256,384]{1,0:T(8,128)(2,1)S(1)}, bf16[256,384]{1,0:T(8,128)(2,1)}, u32[]{:S(2)}, u32[]{:S(2)}) collective-permute-start(bf16[256,384]{1,0:T(8,128)(2,1)S(1)} %add_convert_fusion.2.refs_0_), channel_id=1, source_target_pairs={{0,16},{4,20},{8,24},{12,28},{16,0},{20,4},{24,8},{28,12},{1,17},{... | collective-permute-start | bytes 589832 | tf_op jit(solution)/shard_map/ppermute | solution.py:674
  178.3 7.9 %copy-start.30 = (bf16[256,384]{1,0:T(8,128)(2,1)}, bf16[256,384]{1,0:T(8,128)(2,1)S(1)}, u32[]{:S(2)}) copy-start(bf16[256,384]{1,0:T(8,128)(2,1)S(1)} %collective-permute-done.25.refs_1_) | copy-start | bytes 589828
  178.3 7.9 %collective-permute-start.27 = (bf16[256,384]{1,0:T(8,128)(2,1)S(1)}, bf16[256,384]{1,0:T(8,128)(2,1)}, u32[]{:S(2)}, u32[]{:S(2)}) collective-permute-start(bf16[256,384]{1,0:T(8,128)(2,1)S(1)} %add_convert_fusion.2.refs_0_), channel_id=1, source_target_pairs={{0,24},{4,28},{8,16},{12,20},{16,8},{20,12},{24,0},{28,4},{1,25},{... | collective-permute-start | bytes 589832 | tf_op jit(solution)/shard_map/ppermute | solution.py:674
  180.1 26.3 %copy-start.10 = (bf16[768,768]{1,0:T(8,128)(2,1)S(1)}, bf16[768,768]{1,0:T(8,128)(2,1)}, u32[]{:S(2)}) copy-start(bf16[768,768]{1,0:T(8,128)(2,1)} %wq_ref.1) | copy-start | bytes 3538948
  180.1 26.3 %copy-start.15 = (f32[128,768]{1,0:T(8,128)S(1)}, f32[128,768]{1,0:T(8,128)}, u32[]{:S(2)}) copy-start(f32[128,768]{1,0:T(8,128)} %get-tuple-element.89) | copy-start | bytes 1179652
  188.4 18.6 %copy-start.8 = (bf16[768,768]{1,0:T(8,128)(2,1)S(1)}, bf16[768,768]{1,0:T(8,128)(2,1)}, u32[]{:S(2)}) copy-start(bf16[768,768]{1,0:T(8,128)(2,1)} %wk_ref.1) | copy-start | bytes 3538948
  188.4 36.0 %collective-permute-start.28 = (bf16[4,256,384]{2,1,0:T(8,128)(2,1)}, bf16[4,256,384]{2,1,0:T(8,128)(2,1)}, u32[]{:S(2)}, u32[]{:S(2)}) collective-permute-start(bf16[4,256,384]{2,1,0:T(8,128)(2,1)} %stack.44.even_ref), channel_id=1, source_target_pairs={{0,4},{4,0},{8,12},{12,8},{16,20},{20,16},{24,28},{28,24},{1,5},{5... | collective-permute-start | bytes 2359304 | tf_op jit(solution)/shard_map/ppermute | solution.py:674
  202.8 4.7 %copy-start.16 = (bf16[448,384]{1,0:T(8,128)(2,1)}, bf16[448,384]{1,0:T(8,128)(2,1)S(1)}, u32[]{:S(2)}) copy-start(bf16[448,384]{1,0:T(8,128)(2,1)S(1)} %add_convert_fusion.1.refs_0_) | copy-start | bytes 1032196
  202.8 11.1 %collective-permute-start.32 = (bf16[448,384]{1,0:T(8,128)(2,1)S(1)}, bf16[448,384]{1,0:T(8,128)(2,1)S(1)}, u32[]{:S(2)}, u32[]{:S(2)}) collective-permute-start(bf16[448,384]{1,0:T(8,128)(2,1)S(1)} %add_convert_fusion.1.refs_0_), channel_id=1, source_target_pairs={{0,8},{4,12},{8,0},{12,4},{16,24},{20,28},{24,16},{28,20},{1,9},{5... | collective-permute-start | bytes 1032200 | tf_op jit(solution)/shard_map/ppermute | solution.py:674
  204.4 14.7 %collective-permute-start.33 = (bf16[448,384]{1,0:T(8,128)(2,1)S(1)}, bf16[448,384]{1,0:T(8,128)(2,1)S(1)}, u32[]{:S(2)}, u32[]{:S(2)}) collective-permute-start(bf16[448,384]{1,0:T(8,128)(2,1)S(1)} %add_convert_fusion.1.refs_0_), channel_id=1, source_target_pairs={{0,16},{4,20},{8,24},{12,28},{16,0},{20,4},{24,8},{28,12},{1,17},{... | collective-permute-start | bytes 1032200 | tf_op jit(solution)/shard_map/ppermute | solution.py:674
  204.8 14.3 %collective-permute-start.34 = (bf16[448,384]{1,0:T(8,128)(2,1)S(1)}, bf16[448,384]{1,0:T(8,128)(2,1)S(1)}, u32[]{:S(2)}, u32[]{:S(2)}) collective-permute-start(bf16[448,384]{1,0:T(8,128)(2,1)S(1)} %add_convert_fusion.1.refs_0_), channel_id=1, source_target_pairs={{0,24},{4,28},{8,16},{12,20},{16,8},{20,12},{24,0},{28,4},{1,25},{... | collective-permute-start | bytes 1032200 | tf_op jit(solution)/shard_map/ppermute | solution.py:674
  213.9 5.2 %copy-start.24 = (bf16[448,384]{1,0:T(8,128)(2,1)}, bf16[448,384]{1,0:T(8,128)(2,1)S(1)}, u32[]{:S(2)}) copy-start(bf16[448,384]{1,0:T(8,128)(2,1)S(1)} %collective-permute-done.32.refs_1_) | copy-start | bytes 1032196
  223.1 24.6 %collective-permute-start.35 = (bf16[4,448,384]{2,1,0:T(8,128)(2,1)}, bf16[4,448,384]{2,1,0:T(8,128)(2,1)S(1)}, u32[]{:S(2)}, u32[]{:S(2)}) collective-permute-start(bf16[4,448,384]{2,1,0:T(8,128)(2,1)} %stack.45.even_ref), channel_id=1, source_target_pairs={{0,4},{4,0},{8,12},{12,8},{16,20},{20,16},{24,28},{28,24},{1,5},{5... | collective-permute-start | bytes 4128776 | tf_op jit(solution)/shard_map/ppermute | solution.py:674
  229.0 11.1 %collective-permute-start.36 = (bf16[128,768]{1,0:T(8,128)(2,1)}, bf16[128,768]{1,0:T(8,128)(2,1)S(1)}, u32[]{:S(2)}, u32[]{:S(2)}) collective-permute-start(bf16[128,768]{1,0:T(8,128)(2,1)} %get-tuple-element.80), channel_id=1, source_target_pairs={{0,1},{1,0},{2,3},{3,2},{4,5},{5,4},{6,7},{7,6},{8,9},{9,8},{10,11... | collective-permute-start | bytes 589832 | tf_op jit(solution)/shard_map/ppermute | solution.py:674
  229.0 17.3 %collective-permute-start.37 = (bf16[128,768]{1,0:T(8,128)(2,1)}, bf16[128,768]{1,0:T(8,128)(2,1)S(1)}, u32[]{:S(2)}, u32[]{:S(2)}) collective-permute-start(bf16[128,768]{1,0:T(8,128)(2,1)} %get-tuple-element.80), channel_id=1, source_target_pairs={{0,2},{1,3},{2,0},{3,1},{4,6},{5,7},{6,4},{7,5},{8,10},{9,11},{10,... | collective-permute-start | bytes 589832 | tf_op jit(solution)/shard_map/ppermute | solution.py:674
  231.5 14.8 %collective-permute-start.38 = (bf16[128,768]{1,0:T(8,128)(2,1)}, bf16[128,768]{1,0:T(8,128)(2,1)S(1)}, u32[]{:S(2)}, u32[]{:S(2)}) collective-permute-start(bf16[128,768]{1,0:T(8,128)(2,1)} %get-tuple-element.80), channel_id=1, source_target_pairs={{0,3},{1,2},{2,1},{3,0},{4,7},{5,6},{6,5},{7,4},{8,11},{9,10},{10,... | collective-permute-start | bytes 589832 | tf_op jit(solution)/shard_map/ppermute | solution.py:674
  (26 other events, 28.7 us)

commit v4 on v3

--- a/solution.py
+++ b/solution.py
@@ -9,7 +9,8 @@
 TOK = 128
 PAIR = 128
 EXTRA = 16
-COST = 3e8
+COST = 1e6
+EPSILON = 1e-07
 NT = (((1,), (1,)), ((), ()))
 NN = (((1,), (0,)), ((), ()))
 TN = (((0,), (0,)), ((), ()))
@@ -272,6 +273,47 @@
     )(*arrays, *earlier)
 
 
+def sum_kernel(count, *refs):
+    total = 0.0
+    for ref in refs[:count]:
+        total = total + ref[...].astype(f32)
+    refs[-1][...] = total.astype(bf16)
+
+
+def sum_arrays(arrays, *earlier):
+    count = len(arrays)
+    return pl.pallas_call(
+        functools.partial(sum_kernel, count),
+        in_specs=[whole()] * count + [unread()] * len(earlier),
+        out_specs=whole(),
+        out_shape=jax.ShapeDtypeStruct(arrays[0].shape, bf16),
+        compiler_params=params(),
+        cost_estimate=cost(1),
+        name="sum_rows",
+    )(*arrays, *earlier)
+
+
+def join_kernel(place_ref, *refs):
+    *refs, _, _, out_ref = refs
+    size = refs[0].shape[0]
+    for k, ref in enumerate(refs):
+        spot = len(refs) - 1 - (place_ref[2] ^ k)
+        out_ref[pl.ds(pl.multiple_of(spot * size, size), size), :] = ref[...].astype(f32)
+
+
+def join_rows(place, blocks, *earlier):
+    size, width = blocks[0].shape
+    return pl.pallas_call(
+        join_kernel,
+        in_specs=[scalar()] + [whole()] * len(blocks) + [unread()] * 2,
+        out_specs=whole(),
+        out_shape=jax.ShapeDtypeStruct((len(blocks) * size, width), f32),
+        compiler_params=params(),
+        cost_estimate=cost(1),
+        name="join_rows",
+    )(place, *blocks, *earlier)
+
+
 def table_scratch(length):
     return pltpu.VMEM((length + BLK, PAIR), bf16)
 
@@ -360,40 +402,6 @@
     )(place, k, v, q, near, far, seg_k, seg_q, *attn, out_weight, earlier)
 
 
-def attn_out_kernel(dattn_ref, weight_ref, ctx_ref, vec_ref, pay_ref):
-    tokens, width = dattn_ref.shape
-    dattn = dattn_ref[...]
-    pay_ref[:tokens, :] = dattn
-    half = PAIR // 2
-    for p in range(width // PAIR):
-        cols = slice(p * PAIR, (p + 1) * PAIR)
-        dctx = dot(dattn, weight_ref[cols, :], NT).astype(bf16)
-        turned = (dctx.astype(f32) * ctx_ref[:tokens, cols]).T
-        rows = [ctx_ref[tokens:tokens + 1, cols], ctx_ref[tokens + 1:tokens + 2, cols],
-                jnp.sum(turned[:half], axis=0, keepdims=True), jnp.sum(turned[half:], axis=0, keepdims=True)]
-        pieces = []
-        for value in rows:
-            for _ in range(3):
-                piece = value.astype(bf16).astype(f32)
-                pieces.append(piece)
-                value = value - piece
-        pieces.append(vec_ref[:, cols])
-        pay_ref[tokens:, cols] = jnp.concatenate(pieces, axis=0).astype(bf16)
-
-
-def attn_out(dattn, weight, ctx, vectors):
-    tokens, width = dattn.shape
-    return pl.pallas_call(
-        attn_out_kernel,
-        in_specs=[whole()] * 4,
-        out_specs=whole(),
-        out_shape=jax.ShapeDtypeStruct((tokens + EXTRA, width), bf16),
-        compiler_params=params(),
-        cost_estimate=cost(2),
-        name="attn_out",
-    )(dattn, weight, ctx, vectors)
-
-
 def project_kernel(place_ref, mine_ref, twin_ref, even_ref, odd_ref, wq_ref, wk_ref, wv_ref, q_ref, k_ref, v_ref, seg_ref,
                    rows_ref):
     core = place_ref[1]
@@ -434,53 +442,205 @@
     )(place, *parts, wq, wk, wv)
 
 
-def pack_kernel(cols, kinds, *refs):
-    *in_refs, out_ref, turn_ref = refs
-    top = 0
-    for ref, shares in zip(in_refs, kinds):
-        tokens, count = out_ref.shape[2], ref.shape[1]
-        for i in range(count // PAIR):
-            turn_ref[i * PAIR:(i + 1) * PAIR, :] = ref[:tokens, i * PAIR:(i + 1) * PAIR].astype(f32).T
-        size = count // (shares * cols)
-        for c in range(cols):
-            starts = [r * (count // shares) + c * size for r in range(shares)]
-            rows = jnp.concatenate([turn_ref[a:a + size, :] for a in starts], axis=0)
-            out_ref[c, top:top + shares * size, :] = rows.astype(bf16)
-        top += shares * size
-
-
-def pack(arrays, kinds, cols):
-    tokens = arrays[0].shape[0]
-    total = sum(x.shape[1] for x in arrays)
-    return pl.pallas_call(
-        functools.partial(pack_kernel, cols, kinds),
-        in_specs=[whole()] * len(arrays),
-        out_specs=whole(),
-        out_shape=jax.ShapeDtypeStruct((cols, total // cols, tokens), bf16),
-        scratch_shapes=[pltpu.VMEM((max(x.shape[1] for x in arrays), tokens), f32)],
-        compiler_params=params(),
-        cost_estimate=cost(3),
-        name="pack",
-    )(*arrays)
-
-
-def layer_sums_kernel(rows, chunk, place_ref, pair_even_ref, pair_odd_ref, mine_ref, twin_ref, even_ref, odd_ref, part_ref,
-                      earlier_ref, *out_refs):
+def mean(x):
+    return jnp.mean(x, axis=-1, keepdims=True)
+
+
+def norm_forward(value):
+    center = value - mean(value)
+    scaled = lax.rsqrt(mean(center * center) + EPSILON)
+    return center * scaled, scaled
+
+
+def norm_backward(grad_out, normed, scaled, gain):
+    grad_normed = grad_out * gain
+    inner = grad_normed - mean(grad_normed) - normed * mean(grad_normed * normed)
+    return scaled * inner, jnp.sum(grad_out * normed, axis=0, keepdims=True), jnp.sum(grad_out, axis=0, keepdims=True)
+
+
+def turn(turn_ref, at, value):
+    for i in range(value.shape[1] // PAIR):
+        turn_ref[pl.ds(pl.multiple_of(at + i * PAIR, PAIR), PAIR), :] = value[:, i * PAIR:(i + 1) * PAIR].T
+
+
+def pack(out_ref, top, turn_ref, count, shares, cols):
+    size = count // (shares * cols)
+    for c in range(cols):
+        starts = [r * (count // shares) + c * size for r in range(shares)]
+        rows = jnp.concatenate([turn_ref[a:a + size, :] for a in starts], axis=0)
+        out_ref[c, top:top + shares * size, :] = rows.astype(bf16)
+
+
+def layer_forward_kernel(cols, rows, in_ref, ctx_ref, out_weight_ref, up_ref, down_ref, cot_ref, gain1_ref, bias1_ref,
+                         gain2_ref, bias2_ref, output_ref, pair_ref, active_ref, slope_ref, unit_ref, scaled_ref,
+                         d_h2_ref, vec_ref, part_ref, normed_ref, sum_ref, turn_ref):
+    step = pl.program_id(0)
+    tokens, width = in_ref.shape
+    chunk = up_ref.shape[1]
+
+    @pl.when(step == 0)
+    def _():
+        h1 = in_ref[...].astype(f32) + dot(ctx_ref[:tokens, :].astype(bf16), out_weight_ref[...], NN)
+        unit, scaled = norm_forward(h1)
+        unit_ref[...] = unit
+        scaled_ref[...] = jnp.broadcast_to(scaled, scaled_ref.shape)
+        normed = unit * gain1_ref[...] + bias1_ref[...]
+        normed_ref[...] = normed.astype(bf16)
+        pair_ref[:, :width] = normed.astype(bf16)
+        sum_ref[...] = normed
+
+    inner = dot(normed_ref[...], up_ref[...], NN)
+    upper = 0.5 * (1.0 + lax.erf(inner * math.sqrt(0.5)))
+    slope_ref[...] = upper + inner * jnp.exp(-0.5 * inner * inner) * (1.0 / math.sqrt(2.0 * math.pi))
+    active = (inner * upper).astype(bf16)
+    active_ref[...] = active
+    sum_ref[...] += dot(active, down_ref[...], NN)
+    if part_ref is not None:
+        turn(turn_ref, step * chunk, active.astype(f32))
+
+    @pl.when(step == pl.num_programs(0) - 1)
+    def _():
+        unit, scaled = norm_forward(sum_ref[...])
+        output_ref[...] = (unit * gain2_ref[...] + bias2_ref[...]).astype(bf16)
+        d_h2, g_gain, g_bias = norm_backward(cot_ref[...].astype(f32), unit, scaled, gain2_ref[...])
+        d_h2_ref[...] = d_h2
+        pair_ref[:, width:] = d_h2.astype(bf16)
+        vec_ref[...] = jnp.concatenate([g_gain, g_bias] * 4, axis=0)
+        if part_ref is not None:
+            units = turn_ref.shape[0]
+            pack(part_ref, 0, turn_ref, units, rows, cols)
+            turn(turn_ref, 0, ctx_ref[:tokens, :])
+            pack(part_ref, units // cols, turn_ref, width, rows, cols)
+
+
+def step_cols(rows, chunk):
+    return pl.BlockSpec((rows, chunk), lambda i: (0, i))
+
+
+def step_rows(chunk, cols):
+    return pl.BlockSpec((chunk, cols), lambda i: (i, 0))
+
+
+def layer_forward(inputs, ctx, out_weight, up, down, cot, vectors, cols, rows, dealt):
+    tokens, width = inputs.shape
+    units = up.shape[1]
+    chunk = width
+    square = (tokens, width)
+    shapes = [(square, bf16), ((tokens, 2 * width), bf16), ((tokens, units), bf16), ((tokens, units), f32), (square, f32),
+              ((tokens, PAIR), f32), (square, f32), ((8, width), f32)]
+    specs = [full(square), full((tokens, 2 * width)), step_cols(tokens, chunk), step_cols(tokens, chunk), full(square),
+             full((tokens, PAIR)), full(square), full((8, width))]
+    kernel = functools.partial(layer_forward_kernel, cols, rows)
+    if dealt:
+        shapes.append(((cols, (units + width) // cols, tokens), bf16))
+        specs.append(full(shapes[-1][0]))
+    else:
+        kernel = lambda *refs: layer_forward_kernel(cols, rows, *refs[:-3], None, *refs[-3:])
+    return pl.pallas_call(
+        kernel,
+        grid=(units // chunk,),
+        in_specs=[full(square), full(ctx.shape), full(out_weight.shape), step_cols(width, chunk), step_rows(chunk, width),
+                  full(square)] + [full((1, width))] * 4,
+        out_specs=specs,
+        out_shape=[jax.ShapeDtypeStruct(*x) for x in shapes],
+        scratch_shapes=[pltpu.VMEM(square, bf16), pltpu.VMEM(square, f32), pltpu.VMEM((units, tokens), f32)],
+        compiler_params=params(),
+        cost_estimate=cost(1),
+        name="layer_forward",
+    )(inputs, ctx, out_weight, up, down, cot, *(x.reshape(1, width) for x in vectors))
+
+
+def layer_backward_kernel(cols, pair_ref, slope_ref, down_ref, up_ref, d_h2_ref, unit_ref, scaled_ref, gain1_ref,
+                          out_weight_ref, ctx_ref, vec_ref, d_h1_ref, pay_ref, din_ref, part_ref, sum_ref, turn_ref):
+    step = pl.program_id(0)
+    tokens, width = d_h2_ref.shape
+    chunk = up_ref.shape[1]
+    d_inner = (dot(pair_ref[:, width:], down_ref[...], NT) * slope_ref[...]).astype(bf16)
+    din_ref[...] = d_inner
+    part = dot(d_inner, up_ref[...], NT)
+    if part_ref is not None:
+        turn(turn_ref, step * chunk, d_inner.astype(f32))
+
+    @pl.when(step == 0)
+    def _():
+        sum_ref[...] = d_h2_ref[...] + part
+
+    @pl.when(step > 0)
+    def _():
+        sum_ref[...] += part
+
+    @pl.when(step == pl.num_programs(0) - 1)
+    def _():
+        d_h1, g_gain, g_bias = norm_backward(sum_ref[...], unit_ref[...], scaled_ref[:, :1], gain1_ref[...])
+        d_h1_ref[...] = d_h1
+        d_attn = d_h1.astype(bf16)
+        pay_ref[:tokens, :] = d_attn
+        vectors = jnp.concatenate([g_gain, g_bias, vec_ref[:2]], axis=0)
+        half = PAIR // 2
+        for p in range(width // PAIR):
+            at = slice(p * PAIR, (p + 1) * PAIR)
+            d_ctx = dot(d_attn, out_weight_ref[at, :], NT).astype(bf16)
+            turned = (d_ctx.astype(f32) * ctx_ref[:tokens, at]).T
+            rows = [ctx_ref[tokens:tokens + 1, at], ctx_ref[tokens + 1:tokens + 2, at],
+                    jnp.sum(turned[:half], axis=0, keepdims=True), jnp.sum(turned[half:], axis=0, keepdims=True)]
+            pieces = []
+            for value in rows:
+                for _ in range(3):
+                    piece = value.astype(bf16).astype(f32)
+                    pieces.append(piece)
+                    value = value - piece
+            pieces.append(vectors[:, at])
+            pay_ref[tokens:, at] = jnp.concatenate(pieces, axis=0).astype(bf16)
+        if part_ref is not None:
+            pack(part_ref, 0, turn_ref, turn_ref.shape[0], 1, cols)
+
+
+def layer_backward(pair, slope, down, up, d_h2, unit, scaled, gain1, out_weight, ctx, vec, cols, dealt):
+    tokens, width = d_h2.shape
+    units = up.shape[1]
+    chunk = width
+    square = (tokens, width)
+    shapes = [(square, f32), ((tokens + EXTRA, width), bf16), ((tokens, units), bf16)]
+    specs = [full(square), full((tokens + EXTRA, width)), step_cols(tokens, chunk)]
+    kernel = functools.partial(layer_backward_kernel, cols)
+    if dealt:
+        shapes.append(((cols, units // cols, tokens), bf16))
+        specs.append(full(shapes[-1][0]))
+    else:
+        kernel = lambda *refs: layer_backward_kernel(cols, *refs[:-2], None, *refs[-2:])
+    return pl.pallas_call(
+        kernel,
+        grid=(units // chunk,),
+        in_specs=[full((tokens, 2 * width)), step_cols(tokens, chunk), step_rows(chunk, width), step_cols(width, chunk),
+                  full(square), full(square), full((tokens, PAIR)), full((1, width)), full(out_weight.shape), full(ctx.shape),
+                  full((8, width))],
+        out_specs=specs,
+        out_shape=[jax.ShapeDtypeStruct(*x) for x in shapes],
+        scratch_shapes=[pltpu.VMEM(square, f32), pltpu.VMEM((units, tokens), f32)],
+        compiler_params=params(),
+        cost_estimate=cost(1),
+        name="layer_backward",
+    )(pair, slope, down, up, d_h2, unit, scaled, gain1.reshape(1, width), out_weight, ctx, vec)
+
+
+def layer_sums_kernel(rows, chunk, place_ref, pair_even_ref, pair_odd_ref, mine_ref, twin_ref, even_ref, odd_ref, act_ref,
+                      din_ref, earlier_ref, *out_refs):
     *out_refs, out_ref = out_refs
     me = 2 * place_ref[0] + place_ref[1]
     width = mine_ref.shape[1]
-    features = part_ref.shape[1] - 2 * chunk
+    features = act_ref.shape[1] - chunk
     half = width // 2
     down = up = out = small = 0.0
-    for i in range(part_ref.shape[0] // 2):
-        part = lanes([part_ref[me ^ (2 * i)], part_ref[me ^ (2 * i + 1)]])
+    for i in range(act_ref.shape[0] // 2):
+        part = lanes([act_ref[me ^ (2 * i)], act_ref[me ^ (2 * i + 1)]])
+        din = lanes([din_ref[me ^ (2 * i)], din_ref[me ^ (2 * i + 1)]])
         normed = jnp.concatenate([pair_even_ref[i, :, :width], pair_odd_ref[i, :, :width]], axis=0)
         branch = jnp.concatenate([pair_even_ref[i, :, width:], pair_odd_ref[i, :, width:]], axis=0)
         first, second = (even_ref.at[i - 1], odd_ref.at[i - 1]) if i else (mine_ref, twin_ref)
         attn = jnp.concatenate([first[:TOK, :], second[:TOK, :]], axis=0)
         down = down + dot(part[:chunk], branch, NN)
-        out = out + dot(part[chunk:chunk + features], attn, NN)
-        up = up + dot(part[chunk + features:], normed, NN)
+        out = out + dot(part[chunk:], attn, NN)
+        up = up + dot(din, normed, NN)
         small = small + first[TOK:, :].astype(f32) + second[TOK:, :].astype(f32)
     up = up.T
     small = small[EXTRA - 4:]
@@ -498,20 +658,20 @@
         ref[...] = out_ref[place_ref[2] ^ k]
 
 
-def layer_sums(place, pair, attn, parts, earlier, rows, chunk):
+def layer_sums(place, pair, attn, act, din, earlier, rows, chunk):
     width = attn[0].shape[1]
-    features = parts.shape[1] - 2 * chunk
+    features = act.shape[1] - chunk
     height = (2 * chunk + 2 * features) // rows + width // rows + EXTRA
     return pl.pallas_call(
         functools.partial(layer_sums_kernel, rows, chunk),
-        in_specs=[scalar()] + [whole()] * 7 + [unread()],
+        in_specs=[scalar()] + [whole()] * 8 + [unread()],
         out_specs=[whole()] * rows,
         out_shape=[jax.ShapeDtypeStruct((height, chunk), bf16)] * rows,
         scratch_shapes=[pltpu.VMEM((rows, height, chunk), bf16)],
         compiler_params=params(),
         cost_estimate=cost(6),
         name="layer_sums",
-    )(place, *pair, *attn, parts, earlier)
+    )(place, *pair, *attn, act, din, earlier)
 
 
 def layer_unpack_kernel(cols, place_ref, even_ref, odd_ref, down_ref, up_ref, out_ref, small_ref):
@@ -601,69 +761,70 @@
     )(place, rows_in, rel, *q_parts, *k_parts, earlier)
 
 
-def attn_unpack_kernel(cols, spots, place_ref, even_ref, odd_ref, wq_ref, wk_ref, q_ref, k_ref, v_ref, rel_ref, all_ref,
-                       tq_ref, tk_ref):
+def rel_kernel(cols, share, spots, place_ref, even_ref, odd_ref, wq_ref, wk_ref, rel_ref, tq_ref, tk_ref):
+    me = 2 * place_ref[0] + place_ref[1]
+    width = wq_ref.shape[0]
+    size = width // cols
+    for ref, odd in ((even_ref, 0), (odd_ref, 1)):
+        for i in range(cols // 2):
+            spot = me ^ (2 * i + odd)
+            tail = ref[i, share:, :].astype(f32)
+            tail = jnp.concatenate([tail[:, j * spots:(j + 1) * spots] for j in range(tail.shape[1] // spots)], axis=0)
+            at = pl.ds(pl.multiple_of((spot % 2) * (width // 2) + (spot // 2) * size, EXTRA), size)
+            tq_ref[at, :] = tail[:size].astype(bf16)
+            tk_ref[at, :] = tail[size:].astype(bf16)
+    flip = flip_matrix(spots)
+    across = (((0,), (1,)), ((), ()))
+    turned_q = dot(tq_ref[...], flip, NN).astype(bf16)
+    turned_k = dot(tk_ref[...], flip, NN).astype(bf16)
+    rel_ref[...] = (dot(turned_q, wq_ref[...], across) + dot(turned_k, wk_ref[...], across)).astype(bf16)
+
+
+def rel_share(place, even, odd, wq, wk, rows, places):
+    cols = 2 * even.shape[0]
+    width = wq.shape[0]
+    spots = places // rows
+    return pl.pallas_call(
+        functools.partial(rel_kernel, cols, width // rows, spots),
+        in_specs=[scalar()] + [whole()] * 4,
+        out_specs=whole(),
+        out_shape=jax.ShapeDtypeStruct((spots, width), bf16),
+        scratch_shapes=[pltpu.VMEM((width, spots), bf16)] * 2,
+        compiler_params=params(),
+        cost_estimate=cost(2),
+        name="rel_share",
+    )(place, even, odd, wq, wk)
+
+
+def attn_unpack_kernel(cols, place_ref, even_ref, odd_ref, earlier_ref, q_ref, k_ref, v_ref, all_ref):
     me = 2 * place_ref[0] + place_ref[1]
     share, width = q_ref.shape
     size = width // cols
     for ref, odd in ((even_ref, 0), (odd_ref, 1)):
         for i in range(cols // 2):
-            all_ref[me ^ (2 * i + odd)] = ref[i].astype(f32)
-    wide = all_ref.shape[2]
+            all_ref[me ^ (2 * i + odd)] = ref[i, :share, :].astype(f32)
     for c in range(cols):
-        tail = all_ref[c, share:, :]
-        tail = jnp.concatenate([tail[:, j * spots:(j + 1) * spots] for j in range(wide // spots)], axis=0)
         start = (c % 2) * width // 2 + (c // 2) * size
-        spot = slice(start, start + size)
         for i, ref in enumerate((q_ref, k_ref, v_ref)):
-            ref[:, spot] = all_ref[c, :share, i * size:(i + 1) * size]
-        for i, ref in enumerate((tq_ref, tk_ref)):
-            ref[spot, :] = tail[i * size:(i + 1) * size].astype(bf16)
-    flip = flip_matrix(spots)
-    turned_q = dot(tq_ref[...], flip, NN).astype(bf16)
-    turned_k = dot(tk_ref[...], flip, NN).astype(bf16)
-    across = (((0,), (1,)), ((), ()))
-    rel_ref[...] = (dot(turned_q, wq_ref[...], across) + dot(turned_k, wk_ref[...], across)).astype(bf16)
-
-
-def attn_unpack(place, even, odd, wq, wk, rows, places):
-    cols = 2 * even.shape[0]
-    width = wq.shape[0]
-    share, spots = width // rows, places // rows
-    shape = jax.ShapeDtypeStruct((share, width), f32)
-    return pl.pallas_call(
-        functools.partial(attn_unpack_kernel, cols, spots),
-        in_specs=[scalar()] + [whole()] * 4,
-        out_specs=[whole()] * 4,
-        out_shape=[shape] * 3 + [jax.ShapeDtypeStruct((spots, width), bf16)],
-        scratch_shapes=[pltpu.VMEM((cols,) + even.shape[1:], f32), pltpu.VMEM((width, spots), bf16),
-                        pltpu.VMEM((width, spots), bf16)],
-        compiler_params=params(),
-        cost_estimate=cost(5),
+            ref[:, start:start + size] = all_ref[c, :, i * size:(i + 1) * size]
+
+
+def attn_unpack(place, even, odd, earlier, rows, width):
+    count, _, wide = even.shape
+    share = width // rows
+    return pl.pallas_call(
+        functools.partial(attn_unpack_kernel, 2 * count),
+        in_specs=[scalar()] + [whole()] * 2 + [unread()],
+        out_specs=[whole()] * 3,
+        out_shape=[jax.ShapeDtypeStruct((share, width), f32)] * 3,
+        scratch_shapes=[pltpu.VMEM((2 * count, share, wide), f32)],
+        compiler_params=params(),
+        cost_estimate=cost(4),
         name="attn_unpack",
-    )(place, even, odd, wq, wk)
+    )(place, even, odd, earlier)
 
 
 HEADS = 12
-EPSILON = 1e-07
-
-
-def norm_forward(value, gain, shift):
-    center = value - jnp.mean(value, axis=-1, keepdims=True)
-    scaled = lax.rsqrt(jnp.mean(center * center, axis=-1, keepdims=True) + EPSILON)
-    normed = center * scaled
-    return (normed * gain + shift, normed, scaled)
-
-
-def norm_backward(grad_out, normed, scaled, gain):
-    grad_normed = grad_out * gain
-    inner = grad_normed - jnp.mean(grad_normed, axis=-1, keepdims=True)
-    inner = inner - normed * jnp.mean(grad_normed * normed, axis=-1, keepdims=True)
-    return (scaled * inner, jnp.sum(grad_out * normed, axis=0), jnp.sum(grad_out, axis=0))
-
-
-def gelu_exact(value):
-    return jax.nn.gelu(value, approximate=False)
 
 
 def mul(a, b, form=NN):
@@ -685,11 +846,8 @@
     return x, twin, even, swap(even, "seq", 1)
 
 
-def deal_rows(parts):
-    total = 0.0
-    for k, part in enumerate(parts):
-        total = total + (swap(part, "row", k) if k else part).astype(f32)
-    return total.astype(bf16)
+def deal_rows(parts, *earlier):
+    return sum_arrays([swap(part, "row", k) if k else part for k, part in enumerate(parts)], *earlier)
 
 
 def deal_chips(parts):
@@ -747,57 +905,51 @@
     probs, ctx_half = forward_attention(place, q, k, v, kr, qr, own_segs, row_segs, scale)
     ctx = meet(ctx_half)
 
-    ctx_low = ctx[:tokens].astype(bf16)
-    h1 = inputs.astype(f32) + mul(ctx_low, output_weight)
-    normed1, unit1, scaled1 = norm_forward(h1, norm1_gain, norm1_bias)
-    normed1_low = normed1.astype(bf16)
-    inner = mul(normed1_low, up_weight)
-    active, gelu_back = jax.vjp(gelu_exact, inner)
-    active_low = active.astype(bf16)
-    result, unit2, scaled2 = norm_forward(normed1 + mul(active_low, down_weight), norm2_gain, norm2_bias)
-    output = result.astype(bf16)[None]
-    cot = cotangent[0].astype(f32)
-    d_h2, g_gain2, g_bias2 = norm_backward(cot, unit2, scaled2, norm2_gain)
-    d_branch = d_h2.astype(bf16)
-    d_inner = gelu_back(mul(d_branch, down_weight, NT))[0].astype(bf16)
-    d_normed1 = d_h2 + mul(d_inner, up_weight, NT)
-    d_h1, g_gain1, g_bias1 = norm_backward(d_normed1, unit1, scaled1, norm1_gain)
-    d_attn = d_h1.astype(bf16)
-    vectors = jnp.stack([g_gain1, g_bias1, g_gain2, g_bias2])
-    attn_pay = attn_out(d_attn, output_weight, ctx, vectors)
-    parts = pack([active_low, ctx, d_inner], [rows, rows, 1], cols) if dealt else attn_pay
+    norms = (norm1_gain, norm1_bias, norm2_gain, norm2_bias)
+    output, pair_low, active_low, slope, unit1, scaled1, d_h2, vec, *act = layer_forward(
+        inputs, ctx, output_weight, up_weight, down_weight, cotangent[0], norms, cols, rows, dealt
+    )
+    d_h1, attn_pay, d_inner, *parts = layer_backward(
+        pair_low, slope, down_weight, up_weight, d_h2, unit1, scaled1, norm1_gain, output_weight, ctx, vec, cols, dealt
+    )
+    if dealt:
+        act, = (lax.all_to_all(x, "seq", 0, 0, tiled=True) for x in act)
+
+        parts, = parts
+        pair = gather(pair_low, attn_pay)
+        parts = lax.all_to_all(after(parts, act), "seq", 0, 0, tiled=True)
+    else:
+        act = parts = attn_pay
     twin = swap(attn_pay, "seq", 1)
-    dq_half, *q_table = query_grads(place, probs, attn_pay, twin, half_out, ctx_half, v, q, k, kr, parts, scale)
+    dq_half, *q_table = query_grads(place, probs, attn_pay, twin, half_out, ctx_half, v, q, k, kr, attn_pay, scale)
     even = stack([swap(attn_pay, "seq", i) for i in range(2, cols, 2)], dq_half)
     attn = attn_pay, twin, even, swap(even, "seq", 1)
+    if dealt:
+        layer_part = layer_sums(place, pair, attn, act, parts, dq_half, rows, chunk)
     dk_half, dv_half, *k_table = key_grads(
-        place, k, v, q, qr, kr, own_segs, row_segs, attn, half_out, dq_half, scale
+        place, k, v, q, qr, kr, own_segs, row_segs, attn, half_out, layer_part[0] if dealt else act, scale
     )
     d_own = meet(jnp.concatenate([dq_half, dk_half, dv_half], axis=1))
     dq, dk, dv = (d_own[i * tokens:(i + 1) * tokens] for i in range(3))
     grad_in = d_h1 + mul(dq, query_weight, NT) + mul(dk, key_weight, NT) + mul(dv, value_weight, NT)
+    grad_in = grad_in.astype(bf16)
 
     if dealt:
+        k_parts = deal_chips(k_table)
+        layer = deal_rows(layer_part, dk_half)
         q_parts = deal_chips(q_table)
-        pair = gather(after(jnp.concatenate([normed1_low, d_branch], axis=1), dq_half), dk_half)
-        parts = lax.all_to_all(parts, "seq", 0, 0, tiled=True)
-        k_parts = deal_chips([after(x, parts, pair[0]) if i == 1 else x for i, x in enumerate(k_table)])
-        layer_part = layer_sums(place, pair, attn, parts, dk_half, rows, chunk)
-        layer = deal_rows(layer_part)
-        g_down, g_up, g_output, small = layer_unpack(place, *gather(layer), rows, width, units)
-        attn_part = attn_sums(place, row_in, rel_flip, q_parts, k_parts, layer_part[0], rows)
-        sums = deal_rows(attn_part)
-        g_query, g_key, g_value, g_rel = attn_unpack(place, *gather(sums), query_weight, key_weight, rows, places)
-        blocks = [g_rel] + [swap(g_rel, "row", k) for k in range(1, rows)]
-        out = jnp.zeros((rows,) + g_rel.shape, bf16)
-        for k, block in enumerate(blocks):
-            out = lax.dynamic_update_slice_in_dim(out, block[None], rows - 1 - (row ^ k), 0)
-        g_rel = out.reshape(places, width).astype(f32)
+        attn_part = attn_sums(place, row_in, rel_flip, q_parts, k_parts, layer, rows)
+        attn_sum = deal_rows(attn_part)
+        g_down, g_up, g_output, small = layer_unpack(place, *gather(after(layer, attn_part[0]), attn_sum), rows, width, units)
+        sums = gather(attn_sum)
+        g_rel = rel_share(place, *sums, query_weight, key_weight, rows, places)
+        g_query, g_key, g_value = attn_unpack(place, *sums, g_rel, rows, width)
+        g_rel = join_rows(place, [g_rel] + [swap(g_rel, "row", k) for k in range(1, rows)], small, grad_in)
     else:
-        small = jnp.stack([reduced(x) for x in (g_gain1, g_bias1, g_gain2, g_bias2)])
-        g_down = reduced(mul(active_low, d_branch, TN))
-        g_up = reduced(mul(normed1_low, d_inner, TN))
-        g_output = reduced(mul(ctx_low, d_attn, TN))
+        small = jnp.stack([reduced(x) for x in attn_pay[tokens + EXTRA - 4:]])
+        g_down = reduced(mul(active_low, pair_low[:, width:], TN))
+        g_up = reduced(mul(pair_low[:, :width], d_inner, TN))
+        g_output = reduced(mul(ctx[:tokens].astype(bf16), attn_pay[:tokens], TN))
         across = (((0,), (1,)), ((), ()))
         d_kr, d_qr = (in_order(x, chip)[:, :places] for x in (q_table, k_table))
         placed = lambda g: lax.dynamic_update_slice_in_dim(jnp.zeros((width, width), f32), g, core * part, 1)
@@ -808,7 +960,7 @@
         g_rel = lax.psum(mul(flip_matrix(places), g_rel.astype(bf16)).astype(bf16), ("seq", "row")).astype(f32)
 
     return (
-        output, grad_in.astype(bf16)[None], g_query, g_key, g_value, g_output, g_up, g_down,
+        output[None], grad_in[None], g_query, g_key, g_value, g_output, g_up, g_down,
         small[0], small[1], small[2], small[3], g_rel,
     )
 

time: 257 us -> 247 us (0.961)
  waiting for transfers between devices: 73.5 us -> 44.6 us
  Pallas kernels: 90.4 us -> 113 us
  matrix products: 18.7 us -> 7.68 us
  starting transfers between devices: 43.6 us -> 53.4 us
  other arithmetic: 8.97 us -> 3.95 us
  local copies, waits for them, and re-layouts: 18.1 us -> 22.5 us
    ppermute x39, waiting for transfers between devices: 68.6 us -> 42.5 us  [swap(): lax.ppermute(x, axis, [(i, i ^ k) for i in range(lax.axis_size(axis))])]
    pallas_call x3 -> x7, Pallas kernels: 10.6 us -> 33.2 us  [the longest x1 9.98 us: layer_backward(): pl.pallas_call(kernel, grid=(units // chunk,), in_specs=[full((tokens, 2...]
    dot_general x11 -> x6, matrix products: 18.7 us -> 7.68 us  [mul(): return lax.dot_general(a, b, form, preferred_element_type=f32)]
    ppermute x39, starting transfers between devices: 40 us -> 45.4 us  [swap(): lax.ppermute(x, axis, [(i, i ^ k) for i in range(lax.axis_size(axis))])]
    all_to_all x1 -> x2, starting transfers between devices: 3.59 us -> 8.08 us  [the longest x1 4.53 us: on_device(): parts = lax.all_to_all(after(parts, act), 'seq', 0, 0, tiled=True)]
    convert_element_type x6 -> x0, other arithmetic: 3.58 us -> none  [the longest x1 1.3 us: on_device(): g_rel = out.reshape(places, width).astype(f32)]
    unnamed x102 -> x100, local copies, waits for them, and re-layouts: 11 us -> 14.2 us
    all_to_all x1 -> x2, waiting for transfers between devices: 4.93 us -> 2.14 us  [the longest x1 2.14 us: on_device(): act, = (lax.all_to_all(x, 'seq', 0, 0, tiled=True) for x in act)]
  transfers between devices with their start and end apart: 40 -> 41, of which waited for: 14 -> 10; matrix products, arithmetic and copies ran while one was open for 6% -> 6% of each run, Pallas kernels for 22% -> 27%
where the time goes in v4:
time: 247 us; the launch traced here: 246 us
  Pallas kernels  113 us (46%)
  starting transfers between devices  53.4 us (22%)
  waiting for transfers between devices  44.6 us (18%)
  local copies, waits for them, and re-layouts  22.5 us (9%)
  matrix products  7.68 us (3%)
  other arithmetic  3.95 us (2%)
    ppermute x39, starting transfers between devices, swap(): lax.ppermute(x, axis, [(i, i ^ k) for i in range(lax.axis_size(axis))])  45.4 us
    ppermute x39, waiting for transfers between devices, swap(): lax.ppermute(x, axis, [(i, i ^ k) for i in range(lax.axis_size(axis))])  42.5 us
    pallas_call x1, Pallas kernels, key_grads(): pl.pallas_call(functools.partial(key_grad_kernel, scale, length, pairs, c...  20.6 us
    unnamed x100, local copies, waits for them, and re-layouts  14.2 us
    pallas_call x1, Pallas kernels, forward_attention(): pl.pallas_call(functools.partial(forward_kernel, scale, length), grid=(pa...  13.8 us
    pallas_call x1, Pallas kernels, query_grads(): pl.pallas_call(functools.partial(query_grad_kernel, scale, length, chips)...  13.4 us
    pallas_call x5, Pallas kernels, stack(): pl.pallas_call(functools.partial(stack_kernel, count), in_specs=[whole()]...  11.3 us
    pallas_call x1, Pallas kernels, layer_backward(): pl.pallas_call(kernel, grid=(units // chunk,), in_specs=[full((tokens, 2...  9.98 us
  transfers between devices with their start and end apart: 41, of which 10 were waited for; matrix products, arithmetic and copies ran while one was open for 6% of the time, Pallas kernels for 27%

profile of v4, /device:TPU:0, one launch (start us, length us, event | category | flops | bytes accessed | tf_op | source)
XLA Modules:
  0.0 246.0 jit_solution(623350378353811747)
XLA Ops:
  1.4 1.6 fusion.5.mine_ref
  3.0 2.9 %collective-permute-start.1 = (bf16[144,768]{1,0:T(8,128)(2,1)}, bf16[144,768]{1,0:T(8,128)(2,1)}, u32[]{:S(2)}, u32[]{:S(2)}) collective-permute-start(bf16[144,768]{1,0:T(8,128)(2,1)} %fusion.5.mine_ref), channel_id=1, source_target_pairs={{0,8},{4,12},{8,0},{12,4},{16,24},{20,28},{24,16},{28,20},{1,9},{5... | collective-permute-start | bytes 663560 | tf_op jit(solution)/shard_map/ppermute | solution.py:835
  6.0 1.5 collective-permute-start.2
  7.5 2.7 %convolution_convert_fusion.rel_ref = bf16[512,768]{1,0:T(8,128)(2,1)} fusion(bf16[512,768]{1,0:T(8,128)(2,1)} %param.16), kind=kOutput, calls=%fused_computation | convolution fusion | flops 404094976 | bytes 1572864 | tf_op jit(solution)/shard_map/dot_general | solution.py:831
  10.4 1.2 copy-done.13
  11.6 1.3 convolution_convert_fusion.2.refs_3_.far_ref.near_ref
  12.9 1.3 convolution_convert_fusion.1.refs_4_.near_ref.far_ref
  14.3 3.7 %collective-permute-done.2.refs_1_ = bf16[144,768]{1,0:T(8,128)(2,1)} collective-permute-done((bf16[144,768]{1,0:T(8,128)(2,1)}, bf16[144,768]{1,0:T(8,128)(2,1)}, u32[]{:S(2)}, u32[]{:S(2)}) %collective-permute-start.2) | collective-permute-done | bytes 221216 | tf_op jit(solution)/shard_map/ppermute | solution.py:835
  17.9 2.0 stack.21.even_ref
  21.1 0.9 constant_dynamic-slice_fusion.1.wv_ref
  24.1 6.2 %project.1 = (bf16[1024,384]{1,0:T(8,128)(2,1)}, bf16[1024,384]{1,0:T(8,128)(2,1)}, bf16[1024,384]{1,0:T(8,128)(2,1)}, f32[1,1024]{1,0:T(1,128)}, bf16[1024,768]{1,0:T(8,128)(2,1)}) custom-call(s32[3]{0:T(128)} %pad_add_fusion.place_ref, bf16[144,768]{1,0:T(8,128)(2,1)} %fusion.5.mine_ref, bf16[144,768]{1,0:T(8,128)(2,1)} %copy-done.23, ...), custom_call_target="tpu_custom_call" | custom-call | flops 5000000 | tf_op jit(solution)/shard_map/project/pallas_call | solution.py:433
  31.8 13.8 %attend.1 = (bf16[6,256,1024]{2,1,0:T(8,128)(2,1)}, f32[2,136,384]{2,1,0:T(8,128)}) custom-call(s32[3]{0:T(128)} %pad_add_fusion.place_ref, bf16[1024,384]{1,0:T(8,128)(2,1)} %get-tuple-element.57.q_ref, bf16[1024,384]{1,0:T(8,128)(2,1)} %get-tuple-element.58.k_ref, bf16[1024,384]{1,0:T(8,128)(2,1)} %get-tuple-element.59.v_ref, ...), custom_call_target="tpu_custom_call" | custom-call | flops 14000000 | tf_op jit(solution)/shard_map/attend/pallas_call | solution.py:333
  45.6 1.1 dynamic-slice_bitcast_fusion.3
  50.0 9.2 %layer_forward.1 = (bf16[128,768]{1,0:T(8,128)(2,1)}, bf16[128,1536]{1,0:T(8,128)(2,1)}, bf16[128,3072]{1,0:T(8,128)(2,1)}, f32[128,3072]{1,0:T(8,128)}, f32[128...) custom-call(bf16[128,768]{1,0:T(8,128)(2,1)} %bitcast.31, ...), custom_call_target="tpu_custom_call" | custom-call | flops 1000000 | tf_op jit(solution)/shard_map/layer_forward/pallas_call | solution.py:539
  59.2 1.3 collective-permute-start.11
  61.4 1.4 collective-permute-start.13
  62.8 3.6 %all-to-all-start = ((bf16[8,480,128]{2,1,0:T(8,128)(2,1)}), bf16[8,480,128]{2,1,0:T(8,128)(2,1)S(1)}, u32[]{:S(2)}, u32[]{:S(2)}) async-start(bf16[8,480,128]{2,1,0:T(8,128)(2,1)} %get-tuple-element.73), calls=%async_computation | async-start | bytes 1966080 | tf_op jit(solution)/shard_map/all_to_all | solution.py:916
  66.4 10.0 %layer_backward.1 = (f32[128,768]{1,0:T(8,128)}, bf16[144,768]{1,0:T(8,128)(2,1)}, bf16[128,3072]{1,0:T(8,128)(2,1)}, bf16[8,384,128]{2,1,0:T(8,128)(2,1)}) custom-call(bf16[128,1536]{1,0:T(8,128)(2,1)} %get-tuple-element.63.pair_ref.refs_0_, f32[128,3072]{1,0:T(8,128)} %get-tuple-element.64.slope_ref, bf16[3072,768]{1,0:T(8,128)(2,1)} %down_ref.3, ...), custom_call_target="tpu_custom_call" | custom-call | flops 1000000 | tf_op jit(solution)/shard_map/layer_backward/pallas_call | solution.py:611
  76.4 4.9 %collective-permute-done.12.refs_2_ = bf16[128,1536]{1,0:T(8,128)(2,1)} collective-permute-done((bf16[128,1536]{1,0:T(8,128)(2,1)}, bf16[128,1536]{1,0:T(8,128)(2,1)}, u32[]{:S(2)}, u32[]{:S(2)}) %collective-permute-start.12) | collective-permute-done | bytes 393248 | tf_op jit(solution)/shard_map/ppermute | solution.py:835
  81.3 2.6 %stack.23.pair_even_ref = bf16[4,128,1536]{2,1,0:T(8,128)(2,1)} custom-call(bf16[128,1536]{1,0:T(8,128)(2,1)} %get-tuple-element.63.pair_ref.refs_0_, bf16[128,1536]{1,0:T(8,128)(2,1)} %collective-permute-done.11.refs_1_, bf16[128,1536]{1,0:T(8,128)(2,1)} %collective-permute-done.12.refs_2_, bf16[128,1536]{1,0:T(8,128)(2,1)} %collective-permute-done.13.refs_3_, ...), custom_call_target="tpu_custom_call" | custom-call | flops 1000000 | tf_op jit(solution)/shard_map/stack/pallas_call | solution.py:265
  84.4 3.4 %collective-permute-start.7 = (bf16[144,768]{1,0:T(8,128)(2,1)}, bf16[144,768]{1,0:T(8,128)(2,1)}, u32[]{:S(2)}, u32[]{:S(2)}) collective-permute-start(bf16[144,768]{1,0:T(8,128)(2,1)} %get-tuple-element.71.mine_ref.earlier_ref.refs_4_), channel_id=1, source_target_pairs={{0,8},{4,12},{8,0},{12,4},{16,24},{20,28},{24,16},{28,20},{1,9},{5... | collective-permute-start | bytes 663560 | tf_op jit(solution)/shard_map/ppermute | solution.py:835
  87.8 1.5 collective-permute-start.8
  89.3 2.1 all-to-all-done.refs_1_.act_ref
  91.5 0.9 copy-done.1
  92.4 4.5 %all-to-all-start.1 = ((bf16[8,384,128]{2,1,0:T(8,128)(2,1)}), bf16[8,384,128]{2,1,0:T(8,128)(2,1)}, u32[]{:S(2)}, u32[]{:S(2)}) async-start(bf16[8,384,128]{2,1,0:T(8,128)(2,1)} %after.2), calls=%async_computation.1 | async-start | bytes 1572864 | tf_op jit(solution)/shard_map/all_to_all | solution.py:920
  97.8 13.4 %query_grads.1 = (bf16[2,128,384]{2,1,0:T(8,128)(2,1)}, bf16[96,768]{1,0:T(8,128)(2,1)}, bf16[96,768]{1,0:T(8,128)(2,1)}, bf16[96,768]{1,0:T(8,128)(2,1)}, bf16[96,768]{1,0:T(8,128)(2,1)}) custom-call(s32[3]{0:T(128)} %pad_add_fusion.place_ref, bf16[6,256,1024]{2,1,0:T(8,128)(2,1)} %get-tuple-element.70.p_ref, ...), custom_call_target="tpu_custom_call" | custom-call | flops 1000000 | tf_op jit(solution)/shard_map/query_grads/pallas_call | solution.py:364
  111.2 2.1 stack.22.even_ref
  113.5 2.1 collective-permute-done.10.odd_ref
  115.6 0.9 copy-done.7
  116.5 5.7 %layer_sums.1 = (bf16[448,384]{1,0:T(8,128)(2,1)}, bf16[448,384]{1,0:T(8,128)(2,1)}, bf16[448,384]{1,0:T(8,128)(2,1)}, bf16[448,384]{1,0:T(8,128)(2,1)}) custom-call(s32[3]{0:T(128)} %pad_add_fusion.place_ref, bf16[4,128,1536]{2,1,0:T(8,128)(2,1)} %stack.23.pair_even_ref, bf16[4,128,1536]{2,1,0:T(8,128)(2,1)} %collective-permute-done.14.pair_odd_ref, ...), custom_call_target="tpu_custom_call" | custom-call | flops 6000000 | tf_op jit(solution)/shard_map/layer_sums/pallas_call | solution.py:665
  122.3 1.6 collective-permute-start.22
  123.8 2.6 %collective-permute-start.23 = (bf16[448,384]{1,0:T(8,128)(2,1)}, bf16[448,384]{1,0:T(8,128)(2,1)S(1)}, u32[]{:S(2)}, u32[]{:S(2)}) collective-permute-start(bf16[448,384]{1,0:T(8,128)(2,1)} %get-tuple-element.88), channel_id=1, source_target_pairs={{0,2},{1,3},{2,0},{3,1},{4,6},{5,7},{6,4},{7,5},{8,10},{9,11},{10,... | collective-permute-start | bytes 1032200 | tf_op jit(solution)/shard_map/ppermute | solution.py:835
  126.6 1.7 collective-permute-start.16
  128.4 20.6 %key_grads.1 = (bf16[2,128,384]{2,1,0:T(8,128)(2,1)}, bf16[2,128,384]{2,1,0:T(8,128)(2,1)}, bf16[96,1024]{1,0:T(8,128)(2,1)}, bf16[96,1024]{1,0:T(8,128)(2,1)}, ...) custom-call(s32[3]{0:T(128)} %pad_add_fusion.place_ref, bf16[1024,384]{1,0:T(8,128)(2,1)} %get-tuple-element.58.k_ref, ...), custom_call_target="tpu_custom_call" | custom-call | flops 1000000 | tf_op jit(solution)/shard_map/key_grads/pallas_call | solution.py:387
  149.4 1.7 collective-permute-start.20
  151.1 1.4 collective-permute-start.21
  152.5 1.6 collective-permute-start.17
  154.9 2.2 sum_rows.2.refs_8_.refs_0_
  157.1 8.7 %collective-permute-done.17.refs_2_ = bf16[96,768]{1,0:T(8,128)(2,1)S(1)} collective-permute-done((bf16[96,768]{1,0:T(8,128)(2,1)S(1)}, bf16[96,768]{1,0:T(8,128)(2,1)S(1)}, u32[]{:S(2)}, u32[]{:S(2)}) %collective-permute-start.17) | collective-permute-done | bytes 147488 | tf_op jit(solution)/shard_map/ppermute | solution.py:835
  166.7 4.2 %attn_sums.1 = (bf16[256,384]{1,0:T(8,128)(2,1)}, bf16[256,384]{1,0:T(8,128)(2,1)}, bf16[256,384]{1,0:T(8,128)(2,1)}, bf16[256,384]{1,0:T(8,128)(2,1)}) custom-call(s32[3]{0:T(128)} %pad_add_fusion.place_ref, bf16[1024,768]{1,0:T(8,128)(2,1)} %get-tuple-element.78.rows_ref, bf16[512,768]{1,0:T(8,128)(2,1)} %convolution_convert_fusion.rel_ref, ...), custom_call_target="tpu_custom_call" | custom-call | flops 5000000 | tf_op jit(solution)/shard_map/attn_sums/pallas_call | solution.py:752
  171.7 1.6 collective-permute-start.32
  173.3 1.5 collective-permute-start.33
  175.2 3.5 %collective-permute-start.26 = (bf16[256,384]{1,0:T(8,128)(2,1)S(1)}, bf16[256,384]{1,0:T(8,128)(2,1)S(1)}, u32[]{:S(2)}, u32[]{:S(2)}) collective-permute-start(bf16[256,384]{1,0:T(8,128)(2,1)S(1)} %copy-done.45), channel_id=1, source_target_pairs={{0,2},{1,3},{2,0},{3,1},{4,6},{5,7},{6,4},{7,5},{8,10},{9,11},{10,... | collective-permute-start | bytes 589832 | tf_op jit(solution)/shard_map/ppermute | solution.py:835
  178.8 2.9 %collective-permute-start.27 = (bf16[256,384]{1,0:T(8,128)(2,1)S(1)}, bf16[256,384]{1,0:T(8,128)(2,1)S(1)}, u32[]{:S(2)}, u32[]{:S(2)}) collective-permute-start(bf16[256,384]{1,0:T(8,128)(2,1)S(1)} %copy-done.44), channel_id=1, source_target_pairs={{0,3},{1,2},{2,1},{3,0},{4,7},{5,6},{6,5},{7,4},{8,11},{9,10},{10,... | collective-permute-start | bytes 589832 | tf_op jit(solution)/shard_map/ppermute | solution.py:835
  181.7 9.4 %collective-permute-done.26.refs_2_ = bf16[256,384]{1,0:T(8,128)(2,1)S(1)} collective-permute-done((bf16[256,384]{1,0:T(8,128)(2,1)S(1)}, bf16[256,384]{1,0:T(8,128)(2,1)S(1)}, u32[]{:S(2)}, u32[]{:S(2)}) %collective-permute-start.26) | collective-permute-done | bytes 196640 | tf_op jit(solution)/shard_map/ppermute | solution.py:835
  192.5 2.0 sum_rows.3.refs_0_.refs_4_
  196.1 2.5 %stack.25.even_ref = bf16[4,448,384]{2,1,0:T(8,128)(2,1)} custom-call(bf16[448,384]{1,0:T(8,128)(2,1)} %after.3.refs_0_, bf16[448,384]{1,0:T(8,128)(2,1)} %copy-done.20, bf16[448,384]{1,0:T(8,128)(2,1)} %copy-done.21, bf16[448,384]{1,0:T(8,128)(2,1)} %copy-done.22, bf16[256,384]{1,0:T(8,128)(2,1)} %sum_rows.3.refs_0_.refs_4_), custom_call_target="tpu_custom_call" | custom-call | flops 1000000 | tf_op jit(solution)/shard_map/stack/pallas_call | solution.py:265
  199.5 1.6 collective-permute-start.28
  201.1 1.5 collective-permute-start.29
  203.1 4.2 %collective-permute-done.28.refs_1_ = bf16[256,384]{1,0:T(8,128)(2,1)S(1)} collective-permute-done((bf16[256,384]{1,0:T(8,128)(2,1)S(1)}, bf16[256,384]{1,0:T(8,128)(2,1)S(1)}, u32[]{:S(2)}, u32[]{:S(2)}) %collective-permute-start.28) | collective-permute-done | bytes 196640 | tf_op jit(solution)/shard_map/ppermute | solution.py:835
  207.3 4.4 %collective-permute-done.29.refs_2_ = bf16[256,384]{1,0:T(8,128)(2,1)S(1)} collective-permute-done((bf16[256,384]{1,0:T(8,128)(2,1)S(1)}, bf16[256,384]{1,0:T(8,128)(2,1)S(1)}, u32[]{:S(2)}, u32[]{:S(2)}) %collective-permute-start.29) | collective-permute-done | bytes 196640 | tf_op jit(solution)/shard_map/ppermute | solution.py:835
  213.0 2.2 stack.24.even_ref
  216.7 1.2 fusion.refs_5_
  217.9 0.9 copy-done.6
  218.8 3.9 %rel_share.1.earlier_ref.refs_0_ = bf16[128,768]{1,0:T(8,128)(2,1)} custom-call(s32[3]{0:T(128)} %pad_add_fusion.place_ref, bf16[4,256,384]{2,1,0:T(8,128)(2,1)} %stack.24.even_ref, bf16[4,256,384]{2,1,0:T(8,128)(2,1)} %copy-done.6, bf16[768,768]{1,0:T(8,128)(2,1)} %wq_ref.1, bf16[768,768]{1,0:T(8,128)(2,1)} %wk_ref.1), custom_call_target="tpu_custom_call" | custom-call | flops 2000000 | tf_op jit(solution)/shard_map/rel_share/pallas_call | solution.py:787
  222.7 2.2 collective-permute-start.36
  224.9 1.0 collective-permute-start.37
  225.9 1.5 collective-permute-start.38
  227.4 3.5 %attn_unpack.1 = (f32[192,768]{1,0:T(8,128)}, f32[192,768]{1,0:T(8,128)}, f32[192,768]{1,0:T(8,128)}) custom-call(s32[3]{0:T(128)} %pad_add_fusion.place_ref, bf16[4,256,384]{2,1,0:T(8,128)(2,1)} %stack.24.even_ref, bf16[4,256,384]{2,1,0:T(8,128)(2,1)} %copy-done.6, bf16[128,768]{1,0:T(8,128)(2,1)} %rel_share.1.earlier_ref.refs_0_), custom_call_target="tpu_custom_call" | custom-call | flops 4000000 | tf_op jit(solution)/shard_map/attn_unpack/pallas_call | solution.py:815
  230.8 1.1 copy-done.12
  231.9 4.5 %layer_unpack.1 = (f32[768,768]{1,0:T(8,128)}, f32[192,3072]{1,0:T(8,128)}, f32[192,768]{1,0:T(8,128)}, f32[8,192]{1,0:T(8,128)}) custom-call(s32[3]{0:T(128)} %pad_add_fusion.place_ref, bf16[4,448,384]{2,1,0:T(8,128)(2,1)} %stack.25.even_ref, bf16[4,448,384]{2,1,0:T(8,128)(2,1)} %copy-done.12), custom_call_target="tpu_custom_call" | custom-call | flops 4000000 | tf_op jit(solution)/shard_map/layer_unpack/pallas_call | solution.py:702
  236.4 1.4 fusion.13
  237.8 4.4 %collective-permute-done.37.refs_2_ = bf16[128,768]{1,0:T(8,128)(2,1)S(1)} collective-permute-done((bf16[128,768]{1,0:T(8,128)(2,1)}, bf16[128,768]{1,0:T(8,128)(2,1)S(1)}, u32[]{:S(2)}, u32[]{:S(2)}) %collective-permute-start.37) | collective-permute-done | bytes 196640 | tf_op jit(solution)/shard_map/ppermute | solution.py:835
  243.5 2.5 %join_rows.1 = f32[512,768]{1,0:T(8,128)} custom-call(s32[3]{0:T(128)} %pad_add_fusion.place_ref, bf16[128,768]{1,0:T(8,128)(2,1)} %rel_share.1.earlier_ref.refs_0_, bf16[128,768]{1,0:T(8,128)(2,1)} %copy-done.27, bf16[128,768]{1,0:T(8,128)(2,1)} %copy-done.28, bf16[128,768]{1,0:T(8,128)(2,1)} %copy-done.29, f32[8,192]{1,0:T(8,128)} %get-tuple-element.100.refs_4_, ...), custom_call_target="tpu_custom_call" | custom-call | flops 1000000 | tf_op jit(solution)/shard_map/join_rows/pallas_call | solution.py:306
  (163 shorter events, 23.6 us)
Async XLA Ops:
  0.6 20.5 %copy-start = (bf16[768,768]{1,0:T(8,128)(2,1)S(1)}, bf16[768,768]{1,0:T(8,128)(2,1)}, u32[]{:S(2)}) copy-start(bf16[768,768]{1,0:T(8,128)(2,1)} %param.19) | copy-start | bytes 3538948
  3.0 11.2 %collective-permute-start.1 = (bf16[144,768]{1,0:T(8,128)(2,1)}, bf16[144,768]{1,0:T(8,128)(2,1)}, u32[]{:S(2)}, u32[]{:S(2)}) collective-permute-start(bf16[144,768]{1,0:T(8,128)(2,1)} %fusion.5.mine_ref), channel_id=1, source_target_pairs={{0,8},{4,12},{8,0},{12,4},{16,24},{20,28},{24,16},{28,20},{1,9},{5... | collective-permute-start | bytes 663560 | tf_op jit(solution)/shard_map/ppermute | solution.py:835
  6.0 11.9 %collective-permute-start.2 = (bf16[144,768]{1,0:T(8,128)(2,1)}, bf16[144,768]{1,0:T(8,128)(2,1)}, u32[]{:S(2)}, u32[]{:S(2)}) collective-permute-start(bf16[144,768]{1,0:T(8,128)(2,1)} %fusion.5.mine_ref), channel_id=1, source_target_pairs={{0,16},{4,20},{8,24},{12,28},{16,0},{20,4},{24,8},{28,12},{1,17},{... | collective-permute-start | bytes 663560 | tf_op jit(solution)/shard_map/ppermute | solution.py:835
  7.5 10.4 %collective-permute-start.3 = (bf16[144,768]{1,0:T(8,128)(2,1)}, bf16[144,768]{1,0:T(8,128)(2,1)}, u32[]{:S(2)}, u32[]{:S(2)}) collective-permute-start(bf16[144,768]{1,0:T(8,128)(2,1)} %fusion.5.mine_ref), channel_id=1, source_target_pairs={{0,24},{4,28},{8,16},{12,20},{16,8},{20,12},{24,0},{28,4},{1,25},{... | collective-permute-start | bytes 663560 | tf_op jit(solution)/shard_map/ppermute | solution.py:835
  7.5 2.7 %copy-start.4 = (bf16[768,768]{1,0:T(8,128)(2,1)S(1)}, bf16[768,768]{1,0:T(8,128)(2,1)}, u32[]{:S(2)}) copy-start(bf16[768,768]{1,0:T(8,128)(2,1)} %wq_ref.1) | copy-start | bytes 3538948
  10.4 3.9 %copy-start.8 = (bf16[768,384]{1,0:T(8,128)(2,1)}, bf16[768,384]{1,0:T(8,128)(2,1)S(1)}, u32[]{:S(2)}) copy-start(bf16[768,384]{1,0:T(8,128)(2,1)S(1)} %get-tuple-element.109.wk_ref) | copy-start | bytes 1769476
  10.4 3.9 %copy-start.9 = (bf16[768,384]{1,0:T(8,128)(2,1)}, bf16[768,384]{1,0:T(8,128)(2,1)S(1)}, u32[]{:S(2)}) copy-start(bf16[768,384]{1,0:T(8,128)(2,1)S(1)} %get-tuple-element.110.wq_ref) | copy-start | bytes 1769476
  20.0 2.6 %collective-permute-start.4 = (bf16[3,144,768]{2,1,0:T(8,128)(2,1)}, bf16[3,144,768]{2,1,0:T(8,128)(2,1)S(1)}, u32[]{:S(2)}, u32[]{:S(2)}) collective-permute-start(bf16[3,144,768]{2,1,0:T(8,128)(2,1)} %stack.21.even_ref), channel_id=1, source_target_pairs={{0,4},{4,0},{8,12},{12,8},{16,20},{20,16},{24,28},{28,24},{1,5},{5... | collective-permute-start | bytes 1990664 | tf_op jit(solution)/shard_map/ppermute | solution.py:835
  20.0 2.6 %collective-permute-start = (bf16[144,768]{1,0:T(8,128)(2,1)}, bf16[144,768]{1,0:T(8,128)(2,1)S(1)}, u32[]{:S(2)}, u32[]{:S(2)}) collective-permute-start(bf16[144,768]{1,0:T(8,128)(2,1)} %fusion.5.mine_ref), channel_id=1, source_target_pairs={{0,4},{4,0},{8,12},{12,8},{16,20},{20,16},{24,28},{28,24},{1,5},{5... | collective-permute-start | bytes 663560 | tf_op jit(solution)/shard_map/ppermute | solution.py:835
  31.8 15.0 %copy-start.40 = (f32[768]{0:T(1024)S(1)}, f32[768]{0:T(1024)}, u32[]{:S(2)}) copy-start(f32[768]{0:T(1024)} %param.23) | copy-start | bytes 9220
  31.8 15.6 %copy-start.41 = (f32[768]{0:T(1024)S(1)}, f32[768]{0:T(1024)}, u32[]{:S(2)}) copy-start(f32[768]{0:T(1024)} %param.24) | copy-start | bytes 9220
  31.8 16.2 %copy-start.42 = (f32[768]{0:T(1024)S(1)}, f32[768]{0:T(1024)}, u32[]{:S(2)}) copy-start(f32[768]{0:T(1024)} %param.25) | copy-start | bytes 9220
  31.8 16.8 %copy-start.43 = (f32[768]{0:T(1024)S(1)}, f32[768]{0:T(1024)}, u32[]{:S(2)}) copy-start(f32[768]{0:T(1024)} %param.26) | copy-start | bytes 9220
  46.7 2.6 %collective-permute-start.5 = (f32[136,384]{1,0:T(8,128)S(1)}, f32[136,384]{1,0:T(8,128)S(1)}, u32[]{:S(2)}, u32[]{:S(2)}) collective-permute-start(f32[136,384]{1,0:T(8,128)S(1)} %get-tuple-element.104), channel_id=1, source_target_pairs={{0,4},{4,0},{8,12},{12,8},{16,20},{20,16},{24,28},{28,24},{1,5},{5... | collective-permute-start | bytes 626696 | tf_op jit(solution)/shard_map/ppermute | solution.py:835
  59.2 17.1 %collective-permute-start.11 = (bf16[128,1536]{1,0:T(8,128)(2,1)}, bf16[128,1536]{1,0:T(8,128)(2,1)}, u32[]{:S(2)}, u32[]{:S(2)}) collective-permute-start(bf16[128,1536]{1,0:T(8,128)(2,1)} %get-tuple-element.63.pair_ref.refs_0_), channel_id=1, source_target_pairs={{0,8},{4,12},{8,0},{12,4},{16,24},{20,28},{24,16},{28,20},{1,9},{5... | collective-permute-start | bytes 1179656 | tf_op jit(solution)/shard_map/ppermute | solution.py:835
  60.6 20.7 %collective-permute-start.12 = (bf16[128,1536]{1,0:T(8,128)(2,1)}, bf16[128,1536]{1,0:T(8,128)(2,1)}, u32[]{:S(2)}, u32[]{:S(2)}) collective-permute-start(bf16[128,1536]{1,0:T(8,128)(2,1)} %get-tuple-element.63.pair_ref.refs_0_), channel_id=1, source_target_pairs={{0,16},{4,20},{8,24},{12,28},{16,0},{20,4},{24,8},{28,12},{1,17},{... | collective-permute-start | bytes 1179656 | tf_op jit(solution)/shard_map/ppermute | solution.py:835
  61.4 19.9 %collective-permute-start.13 = (bf16[128,1536]{1,0:T(8,128)(2,1)}, bf16[128,1536]{1,0:T(8,128)(2,1)}, u32[]{:S(2)}, u32[]{:S(2)}) collective-permute-start(bf16[128,1536]{1,0:T(8,128)(2,1)} %get-tuple-element.63.pair_ref.refs_0_), channel_id=1, source_target_pairs={{0,24},{4,28},{8,16},{12,20},{16,8},{20,12},{24,0},{28,4},{1,25},{... | collective-permute-start | bytes 1179656 | tf_op jit(solution)/shard_map/ppermute | solution.py:835
  62.8 28.7 %all-to-all-start = ((bf16[8,480,128]{2,1,0:T(8,128)(2,1)}), bf16[8,480,128]{2,1,0:T(8,128)(2,1)S(1)}, u32[]{:S(2)}, u32[]{:S(2)}) async-start(bf16[8,480,128]{2,1,0:T(8,128)(2,1)} %get-tuple-element.73), calls=%async_computation | async-start | bytes 1966080 | tf_op jit(solution)/shard_map/all_to_all | solution.py:916
  83.9 31.7 %collective-permute-start.14 = (bf16[4,128,1536]{2,1,0:T(8,128)(2,1)}, bf16[4,128,1536]{2,1,0:T(8,128)(2,1)}, u32[]{:S(2)}, u32[]{:S(2)}) collective-permute-start(bf16[4,128,1536]{2,1,0:T(8,128)(2,1)} %stack.23.pair_even_ref), channel_id=1, source_target_pairs={{0,4},{4,0},{8,12},{12,8},{16,20},{20,16},{24,28},{28,24},{1,5},{5... | collective-permute-start | bytes 4718600 | tf_op jit(solution)/shard_map/ppermute | solution.py:835
  83.9 13.9 %collective-permute-start.6 = (bf16[144,768]{1,0:T(8,128)(2,1)}, bf16[144,768]{1,0:T(8,128)(2,1)}, u32[]{:S(2)}, u32[]{:S(2)}) collective-permute-start(bf16[144,768]{1,0:T(8,128)(2,1)} %get-tuple-element.71.mine_ref.earlier_ref.refs_4_), channel_id=1, source_target_pairs={{0,4},{4,0},{8,12},{12,8},{16,20},{20,16},{24,28},{28,24},{1,5},{5... | collective-permute-start | bytes 663560 | tf_op jit(solution)/shard_map/ppermute | solution.py:835
  84.4 26.8 %collective-permute-start.7 = (bf16[144,768]{1,0:T(8,128)(2,1)}, bf16[144,768]{1,0:T(8,128)(2,1)}, u32[]{:S(2)}, u32[]{:S(2)}) collective-permute-start(bf16[144,768]{1,0:T(8,128)(2,1)} %get-tuple-element.71.mine_ref.earlier_ref.refs_4_), channel_id=1, source_target_pairs={{0,8},{4,12},{8,0},{12,4},{16,24},{20,28},{24,16},{28,20},{1,9},{5... | collective-permute-start | bytes 663560 | tf_op jit(solution)/shard_map/ppermute | solution.py:835
  87.8 23.4 %collective-permute-start.8 = (bf16[144,768]{1,0:T(8,128)(2,1)}, bf16[144,768]{1,0:T(8,128)(2,1)}, u32[]{:S(2)}, u32[]{:S(2)}) collective-permute-start(bf16[144,768]{1,0:T(8,128)(2,1)} %get-tuple-element.71.mine_ref.earlier_ref.refs_4_), channel_id=1, source_target_pairs={{0,16},{4,20},{8,24},{12,28},{16,0},{20,4},{24,8},{28,12},{1,17},{... | collective-permute-start | bytes 663560 | tf_op jit(solution)/shard_map/ppermute | solution.py:835
  89.3 21.9 %collective-permute-start.9 = (bf16[144,768]{1,0:T(8,128)(2,1)}, bf16[144,768]{1,0:T(8,128)(2,1)}, u32[]{:S(2)}, u32[]{:S(2)}) collective-permute-start(bf16[144,768]{1,0:T(8,128)(2,1)} %get-tuple-element.71.mine_ref.earlier_ref.refs_4_), channel_id=1, source_target_pairs={{0,24},{4,28},{8,16},{12,20},{16,8},{20,12},{24,0},{28,4},{1,25},{... | collective-permute-start | bytes 663560 | tf_op jit(solution)/shard_map/ppermute | solution.py:835
  92.4 4.5 %copy-start.2 = (bf16[768,768]{1,0:T(8,128)(2,1)S(1)}, bf16[768,768]{1,0:T(8,128)(2,1)}, u32[]{:S(2)}) copy-start(bf16[768,768]{1,0:T(8,128)(2,1)} %out_weight_ref.3) | copy-start | bytes 3538948
  92.4 23.2 %all-to-all-start.1 = ((bf16[8,384,128]{2,1,0:T(8,128)(2,1)}), bf16[8,384,128]{2,1,0:T(8,128)(2,1)}, u32[]{:S(2)}, u32[]{:S(2)}) async-start(bf16[8,384,128]{2,1,0:T(8,128)(2,1)} %after.2), calls=%async_computation.1 | async-start | bytes 1572864 | tf_op jit(solution)/shard_map/all_to_all | solution.py:920
  113.3 13.3 %copy-start.48 = (bf16[96,768]{1,0:T(8,128)(2,1)S(1)}, bf16[96,768]{1,0:T(8,128)(2,1)}, u32[]{:S(2)}) copy-start(bf16[96,768]{1,0:T(8,128)(2,1)} %get-tuple-element.80) | copy-start | bytes 442372
  113.3 2.3 collective-permute-start.10
  122.3 28.9 %collective-permute-start.22 = (bf16[448,384]{1,0:T(8,128)(2,1)}, bf16[448,384]{1,0:T(8,128)(2,1)S(1)}, u32[]{:S(2)}, u32[]{:S(2)}) collective-permute-start(bf16[448,384]{1,0:T(8,128)(2,1)} %get-tuple-element.87), channel_id=1, source_target_pairs={{0,1},{1,0},{2,3},{3,2},{4,5},{5,4},{6,7},{7,6},{8,9},{9,8},{10,11... | collective-permute-start | bytes 1032200 | tf_op jit(solution)/shard_map/ppermute | solution.py:835
  123.8 28.7 %collective-permute-start.23 = (bf16[448,384]{1,0:T(8,128)(2,1)}, bf16[448,384]{1,0:T(8,128)(2,1)S(1)}, u32[]{:S(2)}, u32[]{:S(2)}) collective-permute-start(bf16[448,384]{1,0:T(8,128)(2,1)} %get-tuple-element.88), channel_id=1, source_target_pairs={{0,2},{1,3},{2,0},{3,1},{4,6},{5,7},{6,4},{7,5},{8,10},{9,11},{10,... | collective-permute-start | bytes 1032200 | tf_op jit(solution)/shard_map/ppermute | solution.py:835
  126.4 27.7 %collective-permute-start.24 = (bf16[448,384]{1,0:T(8,128)(2,1)}, bf16[448,384]{1,0:T(8,128)(2,1)S(1)}, u32[]{:S(2)}, u32[]{:S(2)}) collective-permute-start(bf16[448,384]{1,0:T(8,128)(2,1)} %get-tuple-element.89), channel_id=1, source_target_pairs={{0,3},{1,2},{2,1},{3,0},{4,7},{5,6},{6,5},{7,4},{8,11},{9,10},{10,... | collective-permute-start | bytes 1032200 | tf_op jit(solution)/shard_map/ppermute | solution.py:835
  126.6 22.7 %collective-permute-start.16 = (bf16[96,768]{1,0:T(8,128)(2,1)S(1)}, bf16[96,768]{1,0:T(8,128)(2,1)S(1)}, u32[]{:S(2)}, u32[]{:S(2)}) collective-permute-start(bf16[96,768]{1,0:T(8,128)(2,1)S(1)} %copy-done.48), channel_id=1, source_target_pairs={{0,8},{4,12},{8,0},{12,4},{16,24},{20,28},{24,16},{28,20},{1,9},{5... | collective-permute-start | bytes 442376 | tf_op jit(solution)/shard_map/ppermute | solution.py:835
  128.4 24.2 %copy-start.47 = (bf16[96,768]{1,0:T(8,128)(2,1)S(1)}, bf16[96,768]{1,0:T(8,128)(2,1)}, u32[]{:S(2)}) copy-start(bf16[96,768]{1,0:T(8,128)(2,1)} %get-tuple-element.81) | copy-start | bytes 442372
  128.4 25.8 %copy-start.46 = (bf16[96,768]{1,0:T(8,128)(2,1)S(1)}, bf16[96,768]{1,0:T(8,128)(2,1)}, u32[]{:S(2)}) copy-start(bf16[96,768]{1,0:T(8,128)(2,1)} %get-tuple-element.82) | copy-start | bytes 442372
  149.0 16.9 %collective-permute-start.19 = (bf16[96,1024]{1,0:T(8,128)(2,1)}, bf16[96,1024]{1,0:T(8,128)(2,1)S(1)}, u32[]{:S(2)}, u32[]{:S(2)}) collective-permute-start(bf16[96,1024]{1,0:T(8,128)(2,1)} %get-tuple-element.84), channel_id=1, source_target_pairs={{0,8},{4,12},{8,0},{12,4},{16,24},{20,28},{24,16},{28,20},{1,9},{5... | collective-permute-start | bytes 589832 | tf_op jit(solution)/shard_map/ppermute | solution.py:835
  149.4 16.5 %copy-start.37 = (bf16[96,768]{1,0:T(8,128)(2,1)}, bf16[96,768]{1,0:T(8,128)(2,1)S(1)}, u32[]{:S(2)}) copy-start(bf16[96,768]{1,0:T(8,128)(2,1)S(1)} %collective-permute-done.16.refs_1_) | copy-start | bytes 442372
  149.4 16.5 %collective-permute-start.20 = (bf16[96,1024]{1,0:T(8,128)(2,1)}, bf16[96,1024]{1,0:T(8,128)(2,1)S(1)}, u32[]{:S(2)}, u32[]{:S(2)}) collective-permute-start(bf16[96,1024]{1,0:T(8,128)(2,1)} %get-tuple-element.85), channel_id=1, source_target_pairs={{0,16},{4,20},{8,24},{12,28},{16,0},{20,4},{24,8},{28,12},{1,17},{... | collective-permute-start | bytes 589832 | tf_op jit(solution)/shard_map/ppermute | solution.py:835
  151.1 3.4 %copy-start.17 = (bf16[448,384]{1,0:T(8,128)(2,1)}, bf16[448,384]{1,0:T(8,128)(2,1)S(1)}, u32[]{:S(2)}) copy-start(bf16[448,384]{1,0:T(8,128)(2,1)S(1)} %collective-permute-done.22.refs_1_) | copy-start | bytes 1032196
  151.1 14.7 %collective-permute-start.21 = (bf16[96,1024]{1,0:T(8,128)(2,1)}, bf16[96,1024]{1,0:T(8,128)(2,1)S(1)}, u32[]{:S(2)}, u32[]{:S(2)}) collective-permute-start(bf16[96,1024]{1,0:T(8,128)(2,1)} %get-tuple-element.86), channel_id=1, source_target_pairs={{0,24},{4,28},{8,16},{12,20},{16,8},{20,12},{24,0},{28,4},{1,25},{... | collective-permute-start | bytes 589832 | tf_op jit(solution)/shard_map/ppermute | solution.py:835
  152.5 13.3 %collective-permute-start.17 = (bf16[96,768]{1,0:T(8,128)(2,1)S(1)}, bf16[96,768]{1,0:T(8,128)(2,1)S(1)}, u32[]{:S(2)}, u32[]{:S(2)}) collective-permute-start(bf16[96,768]{1,0:T(8,128)(2,1)S(1)} %copy-done.47), channel_id=1, source_target_pairs={{0,16},{4,20},{8,24},{12,28},{16,0},{20,4},{24,8},{28,12},{1,17},{... | collective-permute-start | bytes 442376 | tf_op jit(solution)/shard_map/ppermute | solution.py:835
  154.1 11.7 %collective-permute-start.18 = (bf16[96,768]{1,0:T(8,128)(2,1)S(1)}, bf16[96,768]{1,0:T(8,128)(2,1)S(1)}, u32[]{:S(2)}, u32[]{:S(2)}) collective-permute-start(bf16[96,768]{1,0:T(8,128)(2,1)S(1)} %copy-done.46), channel_id=1, source_target_pairs={{0,24},{4,28},{8,16},{12,20},{16,8},{20,12},{24,0},{28,4},{1,25},{... | collective-permute-start | bytes 442376 | tf_op jit(solution)/shard_map/ppermute | solution.py:835
  166.7 8.5 %copy-start.10 = (bf16[2,128,384]{2,1,0:T(8,128)(2,1)S(1)}, bf16[2,128,384]{2,1,0:T(8,128)(2,1)}, u32[]{:S(2)}) copy-start(bf16[2,128,384]{2,1,0:T(8,128)(2,1)} %get-tuple-element.72.refs_3_.earlier_ref) | copy-start | bytes 589828
  170.9 4.3 %copy-start.45 = (bf16[256,384]{1,0:T(8,128)(2,1)S(1)}, bf16[256,384]{1,0:T(8,128)(2,1)}, u32[]{:S(2)}) copy-start(bf16[256,384]{1,0:T(8,128)(2,1)} %get-tuple-element.92) | copy-start | bytes 589828
  170.9 7.8 %copy-start.44 = (bf16[256,384]{1,0:T(8,128)(2,1)S(1)}, bf16[256,384]{1,0:T(8,128)(2,1)}, u32[]{:S(2)}) copy-start(bf16[256,384]{1,0:T(8,128)(2,1)} %get-tuple-element.93) | copy-start | bytes 589828
  170.9 10.7 %copy-start.14 = (bf16[2,128,384]{2,1,0:T(8,128)(2,1)S(1)}, bf16[2,128,384]{2,1,0:T(8,128)(2,1)}, u32[]{:S(2)}) copy-start(bf16[2,128,384]{2,1,0:T(8,128)(2,1)} %get-tuple-element.76.refs_4_) | copy-start | bytes 589828
  170.9 10.7 %copy-start.33 = (bf16[2,128,384]{2,1,0:T(8,128)(2,1)S(1)}, bf16[2,128,384]{2,1,0:T(8,128)(2,1)}, u32[]{:S(2)}) copy-start(bf16[2,128,384]{2,1,0:T(8,128)(2,1)} %get-tuple-element.77) | copy-start | bytes 589828
  170.9 7.8 %collective-permute-start.25 = (bf16[256,384]{1,0:T(8,128)(2,1)}, bf16[256,384]{1,0:T(8,128)(2,1)S(1)}, u32[]{:S(2)}, u32[]{:S(2)}) collective-permute-start(bf16[256,384]{1,0:T(8,128)(2,1)} %get-tuple-element.91), channel_id=1, source_target_pairs={{0,1},{1,0},{2,3},{3,2},{4,5},{5,4},{6,7},{7,6},{8,9},{9,8},{10,11... | collective-permute-start | bytes 589832 | tf_op jit(solution)/shard_map/ppermute | solution.py:835
  171.7 22.8 %collective-permute-start.32 = (bf16[448,384]{1,0:T(8,128)(2,1)}, bf16[448,384]{1,0:T(8,128)(2,1)S(1)}, u32[]{:S(2)}, u32[]{:S(2)}) collective-permute-start(bf16[448,384]{1,0:T(8,128)(2,1)} %after.3.refs_0_), channel_id=1, source_target_pairs={{0,8},{4,12},{8,0},{12,4},{16,24},{20,28},{24,16},{28,20},{1,9},{5... | collective-permute-start | bytes 1032200 | tf_op jit(solution)/shard_map/ppermute | solution.py:835
  173.3 21.2 %collective-permute-start.33 = (bf16[448,384]{1,0:T(8,128)(2,1)}, bf16[448,384]{1,0:T(8,128)(2,1)S(1)}, u32[]{:S(2)}, u32[]{:S(2)}) collective-permute-start(bf16[448,384]{1,0:T(8,128)(2,1)} %after.3.refs_0_), channel_id=1, source_target_pairs={{0,16},{4,20},{8,24},{12,28},{16,0},{20,4},{24,8},{28,12},{1,17},{... | collective-permute-start | bytes 1032200 | tf_op jit(solution)/shard_map/ppermute | solution.py:835
  174.8 19.8 %collective-permute-start.34 = (bf16[448,384]{1,0:T(8,128)(2,1)}, bf16[448,384]{1,0:T(8,128)(2,1)S(1)}, u32[]{:S(2)}, u32[]{:S(2)}) collective-permute-start(bf16[448,384]{1,0:T(8,128)(2,1)} %after.3.refs_0_), channel_id=1, source_target_pairs={{0,24},{4,28},{8,16},{12,20},{16,8},{20,12},{24,0},{28,4},{1,25},{... | collective-permute-start | bytes 1032200 | tf_op jit(solution)/shard_map/ppermute | solution.py:835
  175.2 15.9 %collective-permute-start.26 = (bf16[256,384]{1,0:T(8,128)(2,1)S(1)}, bf16[256,384]{1,0:T(8,128)(2,1)S(1)}, u32[]{:S(2)}, u32[]{:S(2)}) collective-permute-start(bf16[256,384]{1,0:T(8,128)(2,1)S(1)} %copy-done.45), channel_id=1, source_target_pairs={{0,2},{1,3},{2,0},{3,1},{4,6},{5,7},{6,4},{7,5},{8,10},{9,11},{10,... | collective-permute-start | bytes 589832 | tf_op jit(solution)/shard_map/ppermute | solution.py:835
  178.8 12.4 %copy-start.34 = (bf16[256,384]{1,0:T(8,128)(2,1)}, bf16[256,384]{1,0:T(8,128)(2,1)S(1)}, u32[]{:S(2)}) copy-start(bf16[256,384]{1,0:T(8,128)(2,1)S(1)} %collective-permute-done.25.refs_1_) | copy-start | bytes 589828
  178.8 12.4 %collective-permute-start.27 = (bf16[256,384]{1,0:T(8,128)(2,1)S(1)}, bf16[256,384]{1,0:T(8,128)(2,1)S(1)}, u32[]{:S(2)}, u32[]{:S(2)}) collective-permute-start(bf16[256,384]{1,0:T(8,128)(2,1)S(1)} %copy-done.44), channel_id=1, source_target_pairs={{0,3},{1,2},{2,1},{3,0},{4,7},{5,6},{6,5},{7,4},{8,11},{9,10},{10,... | collective-permute-start | bytes 589832 | tf_op jit(solution)/shard_map/ppermute | solution.py:835
  198.6 32.3 %collective-permute-start.35 = (bf16[4,448,384]{2,1,0:T(8,128)(2,1)}, bf16[4,448,384]{2,1,0:T(8,128)(2,1)S(1)}, u32[]{:S(2)}, u32[]{:S(2)}) collective-permute-start(bf16[4,448,384]{2,1,0:T(8,128)(2,1)} %stack.25.even_ref), channel_id=1, source_target_pairs={{0,4},{4,0},{8,12},{12,8},{16,20},{20,16},{24,28},{28,24},{1,5},{5... | collective-permute-start | bytes 4128776 | tf_op jit(solution)/shard_map/ppermute | solution.py:835
  198.6 4.4 %collective-permute-start.15 = (bf16[384,384]{1,0:T(8,128)(2,1)S(1)}, bf16[384,384]{1,0:T(8,128)(2,1)S(1)}, u32[]{:S(2)}, u32[]{:S(2)}) collective-permute-start(bf16[384,384]{1,0:T(8,128)(2,1)S(1)} %get-tuple-element.102), channel_id=1, source_target_pairs={{0,4},{4,0},{8,12},{12,8},{16,20},{20,16},{24,28},{28,24},{1,5},{5... | collective-permute-start | bytes 884744 | tf_op jit(solution)/shard_map/ppermute | solution.py:835
  199.5 7.8 %collective-permute-start.28 = (bf16[256,384]{1,0:T(8,128)(2,1)S(1)}, bf16[256,384]{1,0:T(8,128)(2,1)S(1)}, u32[]{:S(2)}, u32[]{:S(2)}) collective-permute-start(bf16[256,384]{1,0:T(8,128)(2,1)S(1)} %copy-done.11), channel_id=1, source_target_pairs={{0,8},{4,12},{8,0},{12,4},{16,24},{20,28},{24,16},{28,20},{1,9},{5... | collective-permute-start | bytes 589832 | tf_op jit(solution)/shard_map/ppermute | solution.py:835
  201.1 10.5 %collective-permute-start.29 = (bf16[256,384]{1,0:T(8,128)(2,1)S(1)}, bf16[256,384]{1,0:T(8,128)(2,1)S(1)}, u32[]{:S(2)}, u32[]{:S(2)}) collective-permute-start(bf16[256,384]{1,0:T(8,128)(2,1)S(1)} %copy-done.11), channel_id=1, source_target_pairs={{0,16},{4,20},{8,24},{12,28},{16,0},{20,4},{24,8},{28,12},{1,17},{... | collective-permute-start | bytes 589832 | tf_op jit(solution)/shard_map/ppermute | solution.py:835
  202.6 9.1 %collective-permute-start.30 = (bf16[256,384]{1,0:T(8,128)(2,1)S(1)}, bf16[256,384]{1,0:T(8,128)(2,1)S(1)}, u32[]{:S(2)}, u32[]{:S(2)}) collective-permute-start(bf16[256,384]{1,0:T(8,128)(2,1)S(1)} %copy-done.11), channel_id=1, source_target_pairs={{0,24},{4,28},{8,16},{12,20},{16,8},{20,12},{24,0},{28,4},{1,25},{... | collective-permute-start | bytes 589832 | tf_op jit(solution)/shard_map/ppermute | solution.py:835
  203.0 12.2 %copy-start.5 = (bf16[768,768]{1,0:T(8,128)(2,1)S(1)}, bf16[768,768]{1,0:T(8,128)(2,1)}, u32[]{:S(2)}) copy-start(bf16[768,768]{1,0:T(8,128)(2,1)} %wq_ref.1) | copy-start | bytes 3538948
  207.3 4.4 %copy-start.30 = (bf16[256,384]{1,0:T(8,128)(2,1)}, bf16[256,384]{1,0:T(8,128)(2,1)S(1)}, u32[]{:S(2)}) copy-start(bf16[256,384]{1,0:T(8,128)(2,1)S(1)} %collective-permute-done.28.refs_1_) | copy-start | bytes 589828
  215.2 2.8 %collective-permute-start.31 = (bf16[4,256,384]{2,1,0:T(8,128)(2,1)}, bf16[4,256,384]{2,1,0:T(8,128)(2,1)S(1)}, u32[]{:S(2)}, u32[]{:S(2)}) collective-permute-start(bf16[4,256,384]{2,1,0:T(8,128)(2,1)} %stack.24.even_ref), channel_id=1, source_target_pairs={{0,4},{4,0},{8,12},{12,8},{16,20},{20,16},{24,28},{28,24},{1,5},{5... | collective-permute-start | bytes 2359304 | tf_op jit(solution)/shard_map/ppermute | solution.py:835
  222.7 15.1 %collective-permute-start.36 = (bf16[128,768]{1,0:T(8,128)(2,1)}, bf16[128,768]{1,0:T(8,128)(2,1)S(1)}, u32[]{:S(2)}, u32[]{:S(2)}) collective-permute-start(bf16[128,768]{1,0:T(8,128)(2,1)} %rel_share.1.earlier_ref.refs_0_), channel_id=1, source_target_pairs={{0,1},{1,0},{2,3},{3,2},{4,5},{5,4},{6,7},{7,6},{8,9},{9,8},{10,11... | collective-permute-start | bytes 589832 | tf_op jit(solution)/shard_map/ppermute | solution.py:835
  224.9 17.3 %collective-permute-start.37 = (bf16[128,768]{1,0:T(8,128)(2,1)}, bf16[128,768]{1,0:T(8,128)(2,1)S(1)}, u32[]{:S(2)}, u32[]{:S(2)}) collective-permute-start(bf16[128,768]{1,0:T(8,128)(2,1)} %rel_share.1.earlier_ref.refs_0_), channel_id=1, source_target_pairs={{0,2},{1,3},{2,0},{3,1},{4,6},{5,7},{6,4},{7,5},{8,10},{9,11},{10,... | collective-permute-start | bytes 589832 | tf_op jit(solution)/shard_map/ppermute | solution.py:835
  225.9 16.3 %collective-permute-start.38 = (bf16[128,768]{1,0:T(8,128)(2,1)}, bf16[128,768]{1,0:T(8,128)(2,1)S(1)}, u32[]{:S(2)}, u32[]{:S(2)}) collective-permute-start(bf16[128,768]{1,0:T(8,128)(2,1)} %rel_share.1.earlier_ref.refs_0_), channel_id=1, source_target_pairs={{0,3},{1,2},{2,1},{3,0},{4,7},{5,6},{6,5},{7,4},{8,11},{9,10},{10,... | collective-permute-start | bytes 589832 | tf_op jit(solution)/shard_map/ppermute | solution.py:835
  237.8 4.4 %copy-start.27 = (bf16[128,768]{1,0:T(8,128)(2,1)}, bf16[128,768]{1,0:T(8,128)(2,1)S(1)}, u32[]{:S(2)}) copy-start(bf16[128,768]{1,0:T(8,128)(2,1)S(1)} %collective-permute-done.36.refs_1_) | copy-start | bytes 589828
  (26 other events, 24.2 us)

commit v5 on v4

--- a/solution.py
+++ b/solution.py
@@ -916,18 +916,19 @@
         act, = (lax.all_to_all(x, "seq", 0, 0, tiled=True) for x in act)
 
         parts, = parts
-        pair = gather(pair_low, attn_pay)
         parts = lax.all_to_all(after(parts, act), "seq", 0, 0, tiled=True)
     else:
         act = parts = attn_pay
     twin = swap(attn_pay, "seq", 1)
-    dq_half, *q_table = query_grads(place, probs, attn_pay, twin, half_out, ctx_half, v, q, k, kr, attn_pay, scale)
+    dq_half, *q_table = query_grads(place, probs, attn_pay, twin, half_out, ctx_half, v, q, k, kr, act, scale)
     even = stack([swap(attn_pay, "seq", i) for i in range(2, cols, 2)], dq_half)
     attn = attn_pay, twin, even, swap(even, "seq", 1)
     if dealt:
+        q_parts = deal_chips(q_table)
+        pair = gather(pair_low, dq_half)
         layer_part = layer_sums(place, pair, attn, act, parts, dq_half, rows, chunk)
     dk_half, dv_half, *k_table = key_grads(
-        place, k, v, q, qr, kr, own_segs, row_segs, attn, half_out, layer_part[0] if dealt else act, scale
+        place, k, v, q, qr, kr, own_segs, row_segs, attn, half_out, after(layer_part[0], *q_parts[1:]) if dealt else act, scale
     )
     d_own = meet(jnp.concatenate([dq_half, dk_half, dv_half], axis=1))
     dq, dk, dv = (d_own[i * tokens:(i + 1) * tokens] for i in range(3))
@@ -937,7 +938,6 @@
     if dealt:
         k_parts = deal_chips(k_table)
         layer = deal_rows(layer_part, dk_half)
-        q_parts = deal_chips(q_table)
         attn_part = attn_sums(place, row_in, rel_flip, q_parts, k_parts, layer, rows)
         attn_sum = deal_rows(attn_part)
         g_down, g_up, g_output, small = layer_unpack(place, *gather(after(layer, attn_part[0]), attn_sum), rows, width, units)

time: 247 us -> 246 us (level)
  starting transfers between devices: 53.4 us -> 49.9 us
    all_to_all x1, waiting for transfers between devices: 0.01 us -> 3.7 us  [on_device(): parts = lax.all_to_all(after(parts, act), 'seq', 0, 0, tiled=True)]
    ppermute x39, starting transfers between devices: 45.4 us -> 42.4 us  [swap(): lax.ppermute(x, axis, [(i, i ^ k) for i in range(lax.axis_size(axis))])]
    unnamed x100 -> x95, local copies, waits for them, and re-layouts: 14.2 us -> 15.5 us
  transfers between devices with their start and end apart: 41 -> 41, of which waited for: 10 -> 18; matrix products, arithmetic and copies ran while one was open for 6% -> 7% of each run, Pallas kernels for 27% -> 26%
where the time goes in v5:
time: 246 us; the launch traced here: 245 us
  Pallas kernels  113 us (46%)
  starting transfers between devices  49.9 us (20%)
  waiting for transfers between devices  45.5 us (18%)
  local copies, waits for them, and re-layouts  23.8 us (10%)
  matrix products  7.68 us (3%)
  other arithmetic  3.96 us (2%)
    ppermute x39, starting transfers between devices, swap(): lax.ppermute(x, axis, [(i, i ^ k) for i in range(lax.axis_size(axis))])  42.4 us
    ppermute x39, waiting for transfers between devices, swap(): lax.ppermute(x, axis, [(i, i ^ k) for i in range(lax.axis_size(axis))])  41.8 us
    pallas_call x1, Pallas kernels, key_grads(): pl.pallas_call(functools.partial(key_grad_kernel, scale, length, pairs, c...  20.6 us
    unnamed x95, local copies, waits for them, and re-layouts  15.5 us
    pallas_call x1, Pallas kernels, forward_attention(): pl.pallas_call(functools.partial(forward_kernel, scale, length), grid=(pa...  13.8 us
    pallas_call x1, Pallas kernels, query_grads(): pl.pallas_call(functools.partial(query_grad_kernel, scale, length, chips)...  13.4 us
    pallas_call x5, Pallas kernels, stack(): pl.pallas_call(functools.partial(stack_kernel, count), in_specs=[whole()]...  11.3 us
    pallas_call x1, Pallas kernels, layer_backward(): pl.pallas_call(kernel, grid=(units // chunk,), in_specs=[full((tokens, 2...  9.99 us
  transfers between devices with their start and end apart: 41, of which 18 were waited for; matrix products, arithmetic and copies ran while one was open for 7% of the time, Pallas kernels for 26%

profile of v5, /device:TPU:0, one launch (start us, length us, event | category | flops | bytes accessed | tf_op | source)
XLA Modules:
  0.0 244.6 jit_solution(4363293315747693149)
XLA Ops:
  1.4 1.6 fusion.5.mine_ref
  3.0 2.9 %collective-permute-start.1 = (bf16[144,768]{1,0:T(8,128)(2,1)}, bf16[144,768]{1,0:T(8,128)(2,1)}, u32[]{:S(2)}, u32[]{:S(2)}) collective-permute-start(bf16[144,768]{1,0:T(8,128)(2,1)} %fusion.5.mine_ref), channel_id=1, source_target_pairs={{0,8},{4,12},{8,0},{12,4},{16,24},{20,28},{24,16},{28,20},{1,9},{5... | collective-permute-start | bytes 663560 | tf_op jit(solution)/shard_map/ppermute | solution.py:835
  6.0 1.5 collective-permute-start.2
  7.5 2.7 %convolution_convert_fusion.rel_ref = bf16[512,768]{1,0:T(8,128)(2,1)} fusion(bf16[512,768]{1,0:T(8,128)(2,1)} %param.16), kind=kOutput, calls=%fused_computation | convolution fusion | flops 404094976 | bytes 1572864 | tf_op jit(solution)/shard_map/dot_general | solution.py:831
  10.4 1.2 copy-done.14
  11.6 1.3 convolution_convert_fusion.1.refs_4_.near_ref.far_ref
  12.9 1.3 convolution_convert_fusion.2.refs_3_.far_ref.near_ref
  14.3 3.7 %collective-permute-done.2.refs_1_ = bf16[144,768]{1,0:T(8,128)(2,1)} collective-permute-done((bf16[144,768]{1,0:T(8,128)(2,1)}, bf16[144,768]{1,0:T(8,128)(2,1)}, u32[]{:S(2)}, u32[]{:S(2)}) %collective-permute-start.2) | collective-permute-done | bytes 221216 | tf_op jit(solution)/shard_map/ppermute | solution.py:835
  17.9 2.0 stack.21.even_ref
  24.1 6.2 %project.1 = (bf16[1024,384]{1,0:T(8,128)(2,1)}, bf16[1024,384]{1,0:T(8,128)(2,1)}, bf16[1024,384]{1,0:T(8,128)(2,1)}, f32[1,1024]{1,0:T(1,128)}, bf16[1024,768]{1,0:T(8,128)(2,1)}) custom-call(s32[3]{0:T(128)} %pad_add_fusion.place_ref, bf16[144,768]{1,0:T(8,128)(2,1)} %fusion.5.mine_ref, bf16[144,768]{1,0:T(8,128)(2,1)} %copy-done.25, ...), custom_call_target="tpu_custom_call" | custom-call | flops 5000000 | tf_op jit(solution)/shard_map/project/pallas_call | solution.py:433
  31.8 13.8 %attend.1 = (bf16[6,256,1024]{2,1,0:T(8,128)(2,1)}, f32[2,136,384]{2,1,0:T(8,128)}) custom-call(s32[3]{0:T(128)} %pad_add_fusion.place_ref, bf16[1024,384]{1,0:T(8,128)(2,1)} %get-tuple-element.57.q_ref, bf16[1024,384]{1,0:T(8,128)(2,1)} %get-tuple-element.58.k_ref, bf16[1024,384]{1,0:T(8,128)(2,1)} %get-tuple-element.59.v_ref, ...), custom_call_target="tpu_custom_call" | custom-call | flops 14000000 | tf_op jit(solution)/shard_map/attend/pallas_call | solution.py:333
  50.0 9.2 %layer_forward.1 = (bf16[128,768]{1,0:T(8,128)(2,1)}, bf16[128,1536]{1,0:T(8,128)(2,1)}, bf16[128,3072]{1,0:T(8,128)(2,1)}, f32[128,3072]{1,0:T(8,128)}, f32[128...) custom-call(bf16[128,768]{1,0:T(8,128)(2,1)} %bitcast.31, ...), custom_call_target="tpu_custom_call" | custom-call | flops 1000000 | tf_op jit(solution)/shard_map/layer_forward/pallas_call | solution.py:539
  59.2 3.7 %all-to-all-start = ((bf16[8,480,128]{2,1,0:T(8,128)(2,1)}), bf16[8,480,128]{2,1,0:T(8,128)(2,1)S(1)}, u32[]{:S(2)}, u32[]{:S(2)}) async-start(bf16[8,480,128]{2,1,0:T(8,128)(2,1)} %get-tuple-element.72), calls=%async_computation | async-start | bytes 1966080 | tf_op jit(solution)/shard_map/all_to_all | solution.py:916
  63.0 1.7 collective-permute-start.11
  64.7 1.5 collective-permute-start.12
  66.5 10.0 %layer_backward.1 = (f32[128,768]{1,0:T(8,128)}, bf16[144,768]{1,0:T(8,128)(2,1)}, bf16[128,3072]{1,0:T(8,128)(2,1)}, bf16[8,384,128]{2,1,0:T(8,128)(2,1)}) custom-call(bf16[128,1536]{1,0:T(8,128)(2,1)} %get-tuple-element.63.pair_ref.refs_0_, f32[128,3072]{1,0:T(8,128)} %get-tuple-element.64.slope_ref, bf16[3072,768]{1,0:T(8,128)(2,1)} %down_ref.3, ...), custom_call_target="tpu_custom_call" | custom-call | flops 1000000 | tf_op jit(solution)/shard_map/layer_backward/pallas_call | solution.py:611
  79.4 13.4 %query_grads.1 = (bf16[2,128,384]{2,1,0:T(8,128)(2,1)}, bf16[96,768]{1,0:T(8,128)(2,1)}, bf16[96,768]{1,0:T(8,128)(2,1)}, bf16[96,768]{1,0:T(8,128)(2,1)}, bf16[96,768]{1,0:T(8,128)(2,1)}) custom-call(s32[3]{0:T(128)} %pad_add_fusion.place_ref, bf16[6,256,1024]{2,1,0:T(8,128)(2,1)} %get-tuple-element.70.p_ref, bf16[144,768]{1,0:T(8,128)(2,1)} %get-tuple-element.71.mine_ref, ...), custom_call_target="tpu_custom_call" | custom-call | flops 1000000 | tf_op jit(solution)/shard_map/query_grads/pallas_call | solution.py:364
  92.8 1.7 collective-permute-done.13.refs_3_
  94.4 2.6 %stack.23.pair_even_ref = bf16[4,128,1536]{2,1,0:T(8,128)(2,1)} custom-call(bf16[128,1536]{1,0:T(8,128)(2,1)} %get-tuple-element.63.pair_ref.refs_0_, bf16[128,1536]{1,0:T(8,128)(2,1)} %collective-permute-done.11.refs_1_, bf16[128,1536]{1,0:T(8,128)(2,1)} %collective-permute-done.12.refs_2_, bf16[128,1536]{1,0:T(8,128)(2,1)} %collective-permute-done.13.refs_3_, ...), custom_call_target="tpu_custom_call" | custom-call | flops 1000000 | tf_op jit(solution)/shard_map/stack/pallas_call | solution.py:265
  97.6 1.1 collective-permute-start.8
  98.8 1.8 collective-permute-start.9
  100.6 3.8 %all-to-all-start.1 = ((bf16[8,384,128]{2,1,0:T(8,128)(2,1)}), bf16[8,384,128]{2,1,0:T(8,128)(2,1)S(1)}, u32[]{:S(2)}, u32[]{:S(2)}) async-start(bf16[8,384,128]{2,1,0:T(8,128)(2,1)} %after.3), calls=%async_computation.1 | async-start | bytes 1572864 | tf_op jit(solution)/shard_map/all_to_all | solution.py:919
  105.4 4.7 %collective-permute-done.8.refs_1_ = bf16[144,768]{1,0:T(8,128)(2,1)} collective-permute-done((bf16[144,768]{1,0:T(8,128)(2,1)S(1)}, bf16[144,768]{1,0:T(8,128)(2,1)}, u32[]{:S(2)}, u32[]{:S(2)}) %collective-permute-start.8) | collective-permute-done | bytes 221216 | tf_op jit(solution)/shard_map/ppermute | solution.py:835
  110.2 2.0 stack.22.even_ref
  112.2 2.4 %collective-permute-done.10.odd_ref = bf16[3,144,768]{2,1,0:T(8,128)(2,1)} collective-permute-done((bf16[3,144,768]{2,1,0:T(8,128)(2,1)}, bf16[3,144,768]{2,1,0:T(8,128)(2,1)}, u32[]{:S(2)}, u32[]{:S(2)}) %collective-permute-start.10) | collective-permute-done | bytes 663584 | tf_op jit(solution)/shard_map/ppermute | solution.py:835
  114.7 3.7 %all-to-all-done.1.din_ref = bf16[8,384,128]{2,1,0:T(8,128)(2,1)S(1)} async-done(((bf16[8,384,128]{2,1,0:T(8,128)(2,1)}), bf16[8,384,128]{2,1,0:T(8,128)(2,1)S(1)}, u32[]{:S(2)}, u32[]{:S(2)}) %all-to-all-start.1) | async-done | bytes 786464 | tf_op jit(solution)/shard_map/all_to_all | solution.py:919
  119.3 5.7 %layer_sums.1 = (bf16[448,384]{1,0:T(8,128)(2,1)}, bf16[448,384]{1,0:T(8,128)(2,1)}, bf16[448,384]{1,0:T(8,128)(2,1)}, bf16[448,384]{1,0:T(8,128)(2,1)}) custom-call(s32[3]{0:T(128)} %pad_add_fusion.place_ref, bf16[4,128,1536]{2,1,0:T(8,128)(2,1)} %stack.23.pair_even_ref, bf16[4,128,1536]{2,1,0:T(8,128)(2,1)} %collective-permute-done.14.pair_odd_ref, ...), custom_call_target="tpu_custom_call" | custom-call | flops 6000000 | tf_op jit(solution)/shard_map/layer_sums/pallas_call | solution.py:665
  125.0 1.6 collective-permute-start.22
  126.6 1.5 collective-permute-start.15
  128.6 1.5 collective-permute-start.17
  130.1 2.6 %collective-permute-start.23 = (bf16[448,384]{1,0:T(8,128)(2,1)}, bf16[448,384]{1,0:T(8,128)(2,1)}, u32[]{:S(2)}, u32[]{:S(2)}) collective-permute-start(bf16[448,384]{1,0:T(8,128)(2,1)} %get-tuple-element.88), channel_id=1, source_target_pairs={{0,2},{1,3},{2,0},{3,1},{4,6},{5,7},{6,4},{7,5},{8,10},{9,11},{10,... | collective-permute-start | bytes 1032200 | tf_op jit(solution)/shard_map/ppermute | solution.py:835
  133.2 2.5 %collective-permute-start.24 = (bf16[448,384]{1,0:T(8,128)(2,1)}, bf16[448,384]{1,0:T(8,128)(2,1)}, u32[]{:S(2)}, u32[]{:S(2)}) collective-permute-start(bf16[448,384]{1,0:T(8,128)(2,1)} %get-tuple-element.89), channel_id=1, source_target_pairs={{0,3},{1,2},{2,1},{3,0},{4,7},{5,6},{6,5},{7,4},{8,11},{9,10},{10,... | collective-permute-start | bytes 1032200 | tf_op jit(solution)/shard_map/ppermute | solution.py:835
  135.6 1.7 copy.33.refs_0_
  138.7 20.6 %key_grads.1 = (bf16[2,128,384]{2,1,0:T(8,128)(2,1)}, bf16[2,128,384]{2,1,0:T(8,128)(2,1)}, bf16[96,1024]{1,0:T(8,128)(2,1)}, bf16[96,1024]{1,0:T(8,128)(2,1)}, ...) custom-call(s32[3]{0:T(128)} %pad_add_fusion.place_ref, bf16[1024,384]{1,0:T(8,128)(2,1)} %get-tuple-element.58.k_ref, ...), custom_call_target="tpu_custom_call" | custom-call | flops 1000000 | tf_op jit(solution)/shard_map/key_grads/pallas_call | solution.py:387
  159.3 1.7 collective-permute-start.19
  161.7 1.1 collective-permute-start.21
  162.8 2.2 sum_rows.2.refs_8_.refs_0_
  165.6 3.4 %collective-permute-done.20.refs_6_ = bf16[96,1024]{1,0:T(8,128)(2,1)S(1)} collective-permute-done((bf16[96,1024]{1,0:T(8,128)(2,1)}, bf16[96,1024]{1,0:T(8,128)(2,1)S(1)}, u32[]{:S(2)}, u32[]{:S(2)}) %collective-permute-start.20) | collective-permute-done | bytes 196640 | tf_op jit(solution)/shard_map/ppermute | solution.py:835
  169.7 4.2 %attn_sums.1 = (bf16[256,384]{1,0:T(8,128)(2,1)}, bf16[256,384]{1,0:T(8,128)(2,1)}, bf16[256,384]{1,0:T(8,128)(2,1)}, bf16[256,384]{1,0:T(8,128)(2,1)}) custom-call(s32[3]{0:T(128)} %pad_add_fusion.place_ref, bf16[1024,768]{1,0:T(8,128)(2,1)} %get-tuple-element.81.rows_ref, bf16[512,768]{1,0:T(8,128)(2,1)} %convolution_convert_fusion.rel_ref, ...), custom_call_target="tpu_custom_call" | custom-call | flops 5000000 | tf_op jit(solution)/shard_map/attn_sums/pallas_call | solution.py:752
  175.4 1.1 collective-permute-start.33
  176.5 1.7 collective-permute-start.34
  178.2 1.4 collective-permute-start.26
  179.6 3.7 %collective-permute-done.25.refs_1_ = bf16[256,384]{1,0:T(8,128)(2,1)S(1)} collective-permute-done((bf16[256,384]{1,0:T(8,128)(2,1)}, bf16[256,384]{1,0:T(8,128)(2,1)S(1)}, u32[]{:S(2)}, u32[]{:S(2)}) %collective-permute-start.25) | collective-permute-done | bytes 196640 | tf_op jit(solution)/shard_map/ppermute | solution.py:835
  183.3 2.2 collective-permute-start.27
  185.6 3.2 %collective-permute-done.26.refs_2_ = bf16[256,384]{1,0:T(8,128)(2,1)S(1)} collective-permute-done((bf16[256,384]{1,0:T(8,128)(2,1)S(1)}, bf16[256,384]{1,0:T(8,128)(2,1)S(1)}, u32[]{:S(2)}, u32[]{:S(2)}) %collective-permute-start.26) | collective-permute-done | bytes 196640 | tf_op jit(solution)/shard_map/ppermute | solution.py:835
  188.7 2.1 collective-permute-done.27.refs_3_
  191.6 2.0 sum_rows.3.refs_0_.refs_4_
  195.1 2.5 %stack.25.even_ref = bf16[4,448,384]{2,1,0:T(8,128)(2,1)} custom-call(bf16[448,384]{1,0:T(8,128)(2,1)} %after.5.refs_0_, bf16[448,384]{1,0:T(8,128)(2,1)} %copy-done.22, bf16[448,384]{1,0:T(8,128)(2,1)} %copy-done.23, bf16[448,384]{1,0:T(8,128)(2,1)} %copy-done.24, bf16[256,384]{1,0:T(8,128)(2,1)} %sum_rows.3.refs_0_.refs_4_), custom_call_target="tpu_custom_call" | custom-call | flops 1000000 | tf_op jit(solution)/shard_map/stack/pallas_call | solution.py:265
  198.6 1.9 collective-permute-start.28
  201.1 1.1 collective-permute-start.30
  202.4 4.0 %collective-permute-done.28.refs_1_ = bf16[256,384]{1,0:T(8,128)(2,1)S(1)} collective-permute-done((bf16[256,384]{1,0:T(8,128)(2,1)S(1)}, bf16[256,384]{1,0:T(8,128)(2,1)S(1)}, u32[]{:S(2)}, u32[]{:S(2)}) %collective-permute-start.28) | collective-permute-done | bytes 196640 | tf_op jit(solution)/shard_map/ppermute | solution.py:835
  206.3 2.9 %collective-permute-done.29.refs_2_ = bf16[256,384]{1,0:T(8,128)(2,1)S(1)} collective-permute-done((bf16[256,384]{1,0:T(8,128)(2,1)S(1)}, bf16[256,384]{1,0:T(8,128)(2,1)S(1)}, u32[]{:S(2)}, u32[]{:S(2)}) %collective-permute-start.29) | collective-permute-done | bytes 196640 | tf_op jit(solution)/shard_map/ppermute | solution.py:835
  209.2 1.8 collective-permute-done.30.refs_3_
  211.7 2.2 stack.24.even_ref
  215.4 1.2 fusion.refs_5_
  217.5 3.9 %rel_share.1.earlier_ref.refs_0_ = bf16[128,768]{1,0:T(8,128)(2,1)} custom-call(s32[3]{0:T(128)} %pad_add_fusion.place_ref, bf16[4,256,384]{2,1,0:T(8,128)(2,1)} %stack.24.even_ref, bf16[4,256,384]{2,1,0:T(8,128)(2,1)} %copy-done.7, bf16[768,768]{1,0:T(8,128)(2,1)} %wq_ref.1, bf16[768,768]{1,0:T(8,128)(2,1)} %wk_ref.1), custom_call_target="tpu_custom_call" | custom-call | flops 2000000 | tf_op jit(solution)/shard_map/rel_share/pallas_call | solution.py:787
  221.4 2.0 collective-permute-start.36
  224.2 1.5 collective-permute-start.38
  225.8 3.5 %attn_unpack.1 = (f32[192,768]{1,0:T(8,128)}, f32[192,768]{1,0:T(8,128)}, f32[192,768]{1,0:T(8,128)}) custom-call(s32[3]{0:T(128)} %pad_add_fusion.place_ref, bf16[4,256,384]{2,1,0:T(8,128)(2,1)} %stack.24.even_ref, bf16[4,256,384]{2,1,0:T(8,128)(2,1)} %copy-done.7, bf16[128,768]{1,0:T(8,128)(2,1)} %rel_share.1.earlier_ref.refs_0_), custom_call_target="tpu_custom_call" | custom-call | flops 4000000 | tf_op jit(solution)/shard_map/attn_unpack/pallas_call | solution.py:815
  229.2 1.1 copy-done.13
  230.3 4.5 %layer_unpack.1 = (f32[768,768]{1,0:T(8,128)}, f32[192,3072]{1,0:T(8,128)}, f32[192,768]{1,0:T(8,128)}, f32[8,192]{1,0:T(8,128)}) custom-call(s32[3]{0:T(128)} %pad_add_fusion.place_ref, bf16[4,448,384]{2,1,0:T(8,128)(2,1)} %stack.25.even_ref, bf16[4,448,384]{2,1,0:T(8,128)(2,1)} %copy-done.13), custom_call_target="tpu_custom_call" | custom-call | flops 4000000 | tf_op jit(solution)/shard_map/layer_unpack/pallas_call | solution.py:702
  234.8 1.4 fusion.13
  236.2 4.5 %collective-permute-done.37.refs_2_ = bf16[128,768]{1,0:T(8,128)(2,1)S(1)} collective-permute-done((bf16[128,768]{1,0:T(8,128)(2,1)}, bf16[128,768]{1,0:T(8,128)(2,1)S(1)}, u32[]{:S(2)}, u32[]{:S(2)}) %collective-permute-start.37) | collective-permute-done | bytes 196640 | tf_op jit(solution)/shard_map/ppermute | solution.py:835
  242.1 2.5 %join_rows.1 = f32[512,768]{1,0:T(8,128)} custom-call(s32[3]{0:T(128)} %pad_add_fusion.place_ref, bf16[128,768]{1,0:T(8,128)(2,1)} %rel_share.1.earlier_ref.refs_0_, bf16[128,768]{1,0:T(8,128)(2,1)} %copy-done.29, bf16[128,768]{1,0:T(8,128)(2,1)} %copy-done.30, bf16[128,768]{1,0:T(8,128)(2,1)} %copy-done.31, f32[8,192]{1,0:T(8,128)} %get-tuple-element.100.refs_4_, ...), custom_call_target="tpu_custom_call" | custom-call | flops 1000000 | tf_op jit(solution)/shard_map/join_rows/pallas_call | solution.py:306
  (159 shorter events, 31.9 us)
Async XLA Ops:
  0.6 20.5 %copy-start = (bf16[768,768]{1,0:T(8,128)(2,1)S(1)}, bf16[768,768]{1,0:T(8,128)(2,1)}, u32[]{:S(2)}) copy-start(bf16[768,768]{1,0:T(8,128)(2,1)} %param.19) | copy-start | bytes 3538948
  3.0 11.2 %collective-permute-start.1 = (bf16[144,768]{1,0:T(8,128)(2,1)}, bf16[144,768]{1,0:T(8,128)(2,1)}, u32[]{:S(2)}, u32[]{:S(2)}) collective-permute-start(bf16[144,768]{1,0:T(8,128)(2,1)} %fusion.5.mine_ref), channel_id=1, source_target_pairs={{0,8},{4,12},{8,0},{12,4},{16,24},{20,28},{24,16},{28,20},{1,9},{5... | collective-permute-start | bytes 663560 | tf_op jit(solution)/shard_map/ppermute | solution.py:835
  6.0 11.9 %collective-permute-start.2 = (bf16[144,768]{1,0:T(8,128)(2,1)}, bf16[144,768]{1,0:T(8,128)(2,1)}, u32[]{:S(2)}, u32[]{:S(2)}) collective-permute-start(bf16[144,768]{1,0:T(8,128)(2,1)} %fusion.5.mine_ref), channel_id=1, source_target_pairs={{0,16},{4,20},{8,24},{12,28},{16,0},{20,4},{24,8},{28,12},{1,17},{... | collective-permute-start | bytes 663560 | tf_op jit(solution)/shard_map/ppermute | solution.py:835
  7.5 10.4 %collective-permute-start.3 = (bf16[144,768]{1,0:T(8,128)(2,1)}, bf16[144,768]{1,0:T(8,128)(2,1)}, u32[]{:S(2)}, u32[]{:S(2)}) collective-permute-start(bf16[144,768]{1,0:T(8,128)(2,1)} %fusion.5.mine_ref), channel_id=1, source_target_pairs={{0,24},{4,28},{8,16},{12,20},{16,8},{20,12},{24,0},{28,4},{1,25},{... | collective-permute-start | bytes 663560 | tf_op jit(solution)/shard_map/ppermute | solution.py:835
  7.5 2.8 %copy-start.3 = (bf16[768,768]{1,0:T(8,128)(2,1)S(1)}, bf16[768,768]{1,0:T(8,128)(2,1)}, u32[]{:S(2)}) copy-start(bf16[768,768]{1,0:T(8,128)(2,1)} %wk_ref.1) | copy-start | bytes 3538948
  7.5 2.8 %copy-start.4 = (bf16[768,768]{1,0:T(8,128)(2,1)S(1)}, bf16[768,768]{1,0:T(8,128)(2,1)}, u32[]{:S(2)}) copy-start(bf16[768,768]{1,0:T(8,128)(2,1)} %wq_ref.1) | copy-start | bytes 3538948
  10.4 3.9 %copy-start.9 = (bf16[768,384]{1,0:T(8,128)(2,1)}, bf16[768,384]{1,0:T(8,128)(2,1)S(1)}, u32[]{:S(2)}) copy-start(bf16[768,384]{1,0:T(8,128)(2,1)S(1)} %get-tuple-element.109.wk_ref) | copy-start | bytes 1769476
  10.4 3.8 %copy-start.10 = (bf16[768,384]{1,0:T(8,128)(2,1)}, bf16[768,384]{1,0:T(8,128)(2,1)S(1)}, u32[]{:S(2)}) copy-start(bf16[768,384]{1,0:T(8,128)(2,1)S(1)} %get-tuple-element.110.wq_ref) | copy-start | bytes 1769476
  20.0 2.6 %collective-permute-start.4 = (bf16[3,144,768]{2,1,0:T(8,128)(2,1)}, bf16[3,144,768]{2,1,0:T(8,128)(2,1)S(1)}, u32[]{:S(2)}, u32[]{:S(2)}) collective-permute-start(bf16[3,144,768]{2,1,0:T(8,128)(2,1)} %stack.21.even_ref), channel_id=1, source_target_pairs={{0,4},{4,0},{8,12},{12,8},{16,20},{20,16},{24,28},{28,24},{1,5},{5... | collective-permute-start | bytes 1990664 | tf_op jit(solution)/shard_map/ppermute | solution.py:835
  20.0 2.6 %collective-permute-start = (bf16[144,768]{1,0:T(8,128)(2,1)}, bf16[144,768]{1,0:T(8,128)(2,1)S(1)}, u32[]{:S(2)}, u32[]{:S(2)}) collective-permute-start(bf16[144,768]{1,0:T(8,128)(2,1)} %fusion.5.mine_ref), channel_id=1, source_target_pairs={{0,4},{4,0},{8,12},{12,8},{16,20},{20,16},{24,28},{28,24},{1,5},{5... | collective-permute-start | bytes 663560 | tf_op jit(solution)/shard_map/ppermute | solution.py:835
  31.8 15.0 %copy-start.39 = (f32[768]{0:T(1024)S(1)}, f32[768]{0:T(1024)}, u32[]{:S(2)}) copy-start(f32[768]{0:T(1024)} %param.23) | copy-start | bytes 9220
  31.8 15.6 %copy-start.40 = (f32[768]{0:T(1024)S(1)}, f32[768]{0:T(1024)}, u32[]{:S(2)}) copy-start(f32[768]{0:T(1024)} %param.24) | copy-start | bytes 9220
  31.8 16.2 %copy-start.41 = (f32[768]{0:T(1024)S(1)}, f32[768]{0:T(1024)}, u32[]{:S(2)}) copy-start(f32[768]{0:T(1024)} %param.25) | copy-start | bytes 9220
  31.8 16.8 %copy-start.42 = (f32[768]{0:T(1024)S(1)}, f32[768]{0:T(1024)}, u32[]{:S(2)}) copy-start(f32[768]{0:T(1024)} %param.26) | copy-start | bytes 9220
  46.6 2.6 %collective-permute-start.5 = (f32[136,384]{1,0:T(8,128)S(1)}, f32[136,384]{1,0:T(8,128)S(1)}, u32[]{:S(2)}, u32[]{:S(2)}) collective-permute-start(f32[136,384]{1,0:T(8,128)S(1)} %get-tuple-element.104), channel_id=1, source_target_pairs={{0,4},{4,0},{8,12},{12,8},{16,20},{20,16},{24,28},{28,24},{1,5},{5... | collective-permute-start | bytes 626696 | tf_op jit(solution)/shard_map/ppermute | solution.py:835
  59.2 19.2 %all-to-all-start = ((bf16[8,480,128]{2,1,0:T(8,128)(2,1)}), bf16[8,480,128]{2,1,0:T(8,128)(2,1)S(1)}, u32[]{:S(2)}, u32[]{:S(2)}) async-start(bf16[8,480,128]{2,1,0:T(8,128)(2,1)} %get-tuple-element.72), calls=%async_computation | async-start | bytes 1966080 | tf_op jit(solution)/shard_map/all_to_all | solution.py:916
  63.0 29.8 %collective-permute-start.11 = (bf16[128,1536]{1,0:T(8,128)(2,1)}, bf16[128,1536]{1,0:T(8,128)(2,1)}, u32[]{:S(2)}, u32[]{:S(2)}) collective-permute-start(bf16[128,1536]{1,0:T(8,128)(2,1)} %get-tuple-element.63.pair_ref.refs_0_), channel_id=1, source_target_pairs={{0,8},{4,12},{8,0},{12,4},{16,24},{20,28},{24,16},{28,20},{1,9},{5... | collective-permute-start | bytes 1179656 | tf_op jit(solution)/shard_map/ppermute | solution.py:835
  64.7 28.0 %collective-permute-start.12 = (bf16[128,1536]{1,0:T(8,128)(2,1)}, bf16[128,1536]{1,0:T(8,128)(2,1)}, u32[]{:S(2)}, u32[]{:S(2)}) collective-permute-start(bf16[128,1536]{1,0:T(8,128)(2,1)} %get-tuple-element.63.pair_ref.refs_0_), channel_id=1, source_target_pairs={{0,16},{4,20},{8,24},{12,28},{16,0},{20,4},{24,8},{28,12},{1,17},{... | collective-permute-start | bytes 1179656 | tf_op jit(solution)/shard_map/ppermute | solution.py:835
  66.2 28.2 %collective-permute-start.13 = (bf16[128,1536]{1,0:T(8,128)(2,1)}, bf16[128,1536]{1,0:T(8,128)(2,1)}, u32[]{:S(2)}, u32[]{:S(2)}) collective-permute-start(bf16[128,1536]{1,0:T(8,128)(2,1)} %get-tuple-element.63.pair_ref.refs_0_), channel_id=1, source_target_pairs={{0,24},{4,28},{8,16},{12,20},{16,8},{20,12},{24,0},{28,4},{1,25},{... | collective-permute-start | bytes 1179656 | tf_op jit(solution)/shard_map/ppermute | solution.py:835
  66.5 10.1 %copy-start.2 = (bf16[768,768]{1,0:T(8,128)(2,1)S(1)}, bf16[768,768]{1,0:T(8,128)(2,1)}, u32[]{:S(2)}) copy-start(bf16[768,768]{1,0:T(8,128)(2,1)} %out_weight_ref.3) | copy-start | bytes 3538948
  76.5 1.9 collective-permute-start.6
  94.4 2.6 %copy-start.11 = (bf16[144,768]{1,0:T(8,128)(2,1)S(1)}, bf16[144,768]{1,0:T(8,128)(2,1)}, u32[]{:S(2)}) copy-start(bf16[144,768]{1,0:T(8,128)(2,1)} %get-tuple-element.71.mine_ref) | copy-start | bytes 663556
  97.1 21.3 %collective-permute-start.14 = (bf16[4,128,1536]{2,1,0:T(8,128)(2,1)}, bf16[4,128,1536]{2,1,0:T(8,128)(2,1)}, u32[]{:S(2)}, u32[]{:S(2)}) collective-permute-start(bf16[4,128,1536]{2,1,0:T(8,128)(2,1)} %stack.23.pair_even_ref), channel_id=1, source_target_pairs={{0,4},{4,0},{8,12},{12,8},{16,20},{20,16},{24,28},{28,24},{1,5},{5... | collective-permute-start | bytes 4718600 | tf_op jit(solution)/shard_map/ppermute | solution.py:835
  97.1 8.3 %collective-permute-start.7 = (bf16[144,768]{1,0:T(8,128)(2,1)S(1)}, bf16[144,768]{1,0:T(8,128)(2,1)}, u32[]{:S(2)}, u32[]{:S(2)}) collective-permute-start(bf16[144,768]{1,0:T(8,128)(2,1)S(1)} %copy-done.11), channel_id=1, source_target_pairs={{0,8},{4,12},{8,0},{12,4},{16,24},{20,28},{24,16},{28,20},{1,9},{5... | collective-permute-start | bytes 663560 | tf_op jit(solution)/shard_map/ppermute | solution.py:835
  97.6 12.5 %collective-permute-start.8 = (bf16[144,768]{1,0:T(8,128)(2,1)S(1)}, bf16[144,768]{1,0:T(8,128)(2,1)}, u32[]{:S(2)}, u32[]{:S(2)}) collective-permute-start(bf16[144,768]{1,0:T(8,128)(2,1)S(1)} %copy-done.11), channel_id=1, source_target_pairs={{0,16},{4,20},{8,24},{12,28},{16,0},{20,4},{24,8},{28,12},{1,17},{... | collective-permute-start | bytes 663560 | tf_op jit(solution)/shard_map/ppermute | solution.py:835
  98.8 11.4 %collective-permute-start.9 = (bf16[144,768]{1,0:T(8,128)(2,1)S(1)}, bf16[144,768]{1,0:T(8,128)(2,1)}, u32[]{:S(2)}, u32[]{:S(2)}) collective-permute-start(bf16[144,768]{1,0:T(8,128)(2,1)S(1)} %copy-done.11), channel_id=1, source_target_pairs={{0,24},{4,28},{8,16},{12,20},{16,8},{20,12},{24,0},{28,4},{1,25},{... | collective-permute-start | bytes 663560 | tf_op jit(solution)/shard_map/ppermute | solution.py:835
  100.6 17.8 %all-to-all-start.1 = ((bf16[8,384,128]{2,1,0:T(8,128)(2,1)}), bf16[8,384,128]{2,1,0:T(8,128)(2,1)S(1)}, u32[]{:S(2)}, u32[]{:S(2)}) async-start(bf16[8,384,128]{2,1,0:T(8,128)(2,1)} %after.3), calls=%async_computation.1 | async-start | bytes 1572864 | tf_op jit(solution)/shard_map/all_to_all | solution.py:919
  112.2 16.4 %copy-start.45 = (bf16[96,768]{1,0:T(8,128)(2,1)S(1)}, bf16[96,768]{1,0:T(8,128)(2,1)}, u32[]{:S(2)}) copy-start(bf16[96,768]{1,0:T(8,128)(2,1)} %get-tuple-element.78) | copy-start | bytes 442372
  112.2 2.5 %collective-permute-start.10 = (bf16[3,144,768]{2,1,0:T(8,128)(2,1)}, bf16[3,144,768]{2,1,0:T(8,128)(2,1)}, u32[]{:S(2)}, u32[]{:S(2)}) collective-permute-start(bf16[3,144,768]{2,1,0:T(8,128)(2,1)} %stack.22.even_ref), channel_id=1, source_target_pairs={{0,4},{4,0},{8,12},{12,8},{16,20},{20,16},{24,28},{28,24},{1,5},{5... | collective-permute-start | bytes 1990664 | tf_op jit(solution)/shard_map/ppermute | solution.py:835
  125.0 36.7 %collective-permute-start.22 = (bf16[448,384]{1,0:T(8,128)(2,1)}, bf16[448,384]{1,0:T(8,128)(2,1)S(1)}, u32[]{:S(2)}, u32[]{:S(2)}) collective-permute-start(bf16[448,384]{1,0:T(8,128)(2,1)} %get-tuple-element.87), channel_id=1, source_target_pairs={{0,1},{1,0},{2,3},{3,2},{4,5},{5,4},{6,7},{7,6},{8,9},{9,8},{10,11... | collective-permute-start | bytes 1032200 | tf_op jit(solution)/shard_map/ppermute | solution.py:835
  126.6 6.6 %collective-permute-start.15 = (bf16[96,768]{1,0:T(8,128)(2,1)}, bf16[96,768]{1,0:T(8,128)(2,1)S(1)}, u32[]{:S(2)}, u32[]{:S(2)}) collective-permute-start(bf16[96,768]{1,0:T(8,128)(2,1)} %get-tuple-element.76), channel_id=1, source_target_pairs={{0,8},{4,12},{8,0},{12,4},{16,24},{20,28},{24,16},{28,20},{1,9},{5... | collective-permute-start | bytes 442376 | tf_op jit(solution)/shard_map/ppermute | solution.py:835
  128.1 9.3 %collective-permute-start.16 = (bf16[96,768]{1,0:T(8,128)(2,1)}, bf16[96,768]{1,0:T(8,128)(2,1)S(1)}, u32[]{:S(2)}, u32[]{:S(2)}) collective-permute-start(bf16[96,768]{1,0:T(8,128)(2,1)} %get-tuple-element.77), channel_id=1, source_target_pairs={{0,16},{4,20},{8,24},{12,28},{16,0},{20,4},{24,8},{28,12},{1,17},{... | collective-permute-start | bytes 442376 | tf_op jit(solution)/shard_map/ppermute | solution.py:835
  128.6 8.8 %collective-permute-start.17 = (bf16[96,768]{1,0:T(8,128)(2,1)S(1)}, bf16[96,768]{1,0:T(8,128)(2,1)S(1)}, u32[]{:S(2)}, u32[]{:S(2)}) collective-permute-start(bf16[96,768]{1,0:T(8,128)(2,1)S(1)} %copy-done.45), channel_id=1, source_target_pairs={{0,24},{4,28},{8,16},{12,20},{16,8},{20,12},{24,0},{28,4},{1,25},{... | collective-permute-start | bytes 442376 | tf_op jit(solution)/shard_map/ppermute | solution.py:835
  130.1 32.8 %collective-permute-start.23 = (bf16[448,384]{1,0:T(8,128)(2,1)}, bf16[448,384]{1,0:T(8,128)(2,1)}, u32[]{:S(2)}, u32[]{:S(2)}) collective-permute-start(bf16[448,384]{1,0:T(8,128)(2,1)} %get-tuple-element.88), channel_id=1, source_target_pairs={{0,2},{1,3},{2,0},{3,1},{4,6},{5,7},{6,4},{7,5},{8,10},{9,11},{10,... | collective-permute-start | bytes 1032200 | tf_op jit(solution)/shard_map/ppermute | solution.py:835
  133.2 4.2 %copy-start.17 = (bf16[96,768]{1,0:T(8,128)(2,1)}, bf16[96,768]{1,0:T(8,128)(2,1)S(1)}, u32[]{:S(2)}) copy-start(bf16[96,768]{1,0:T(8,128)(2,1)S(1)} %collective-permute-done.15.refs_1_) | copy-start | bytes 442372
  133.2 29.7 %collective-permute-start.24 = (bf16[448,384]{1,0:T(8,128)(2,1)}, bf16[448,384]{1,0:T(8,128)(2,1)}, u32[]{:S(2)}, u32[]{:S(2)}) collective-permute-start(bf16[448,384]{1,0:T(8,128)(2,1)} %get-tuple-element.89), channel_id=1, source_target_pairs={{0,3},{1,2},{2,1},{3,0},{4,7},{5,6},{6,5},{7,4},{8,11},{9,10},{10,... | collective-permute-start | bytes 1032200 | tf_op jit(solution)/shard_map/ppermute | solution.py:835
  159.3 6.4 %collective-permute-start.19 = (bf16[96,1024]{1,0:T(8,128)(2,1)}, bf16[96,1024]{1,0:T(8,128)(2,1)S(1)}, u32[]{:S(2)}, u32[]{:S(2)}) collective-permute-start(bf16[96,1024]{1,0:T(8,128)(2,1)} %get-tuple-element.84), channel_id=1, source_target_pairs={{0,8},{4,12},{8,0},{12,4},{16,24},{20,28},{24,16},{28,20},{1,9},{5... | collective-permute-start | bytes 589832 | tf_op jit(solution)/shard_map/ppermute | solution.py:835
  161.0 8.0 %collective-permute-start.20 = (bf16[96,1024]{1,0:T(8,128)(2,1)}, bf16[96,1024]{1,0:T(8,128)(2,1)S(1)}, u32[]{:S(2)}, u32[]{:S(2)}) collective-permute-start(bf16[96,1024]{1,0:T(8,128)(2,1)} %get-tuple-element.85), channel_id=1, source_target_pairs={{0,16},{4,20},{8,24},{12,28},{16,0},{20,4},{24,8},{28,12},{1,17},{... | collective-permute-start | bytes 589832 | tf_op jit(solution)/shard_map/ppermute | solution.py:835
  161.7 7.3 %collective-permute-start.21 = (bf16[96,1024]{1,0:T(8,128)(2,1)}, bf16[96,1024]{1,0:T(8,128)(2,1)S(1)}, u32[]{:S(2)}, u32[]{:S(2)}) collective-permute-start(bf16[96,1024]{1,0:T(8,128)(2,1)} %get-tuple-element.86), channel_id=1, source_target_pairs={{0,24},{4,28},{8,16},{12,20},{16,8},{20,12},{24,0},{28,4},{1,25},{... | collective-permute-start | bytes 589832 | tf_op jit(solution)/shard_map/ppermute | solution.py:835
  165.6 3.4 %copy-start.26 = (bf16[96,1024]{1,0:T(8,128)(2,1)}, bf16[96,1024]{1,0:T(8,128)(2,1)S(1)}, u32[]{:S(2)}) copy-start(bf16[96,1024]{1,0:T(8,128)(2,1)S(1)} %collective-permute-done.19.refs_5_) | copy-start | bytes 589828
  169.7 8.5 %copy-start.6 = (bf16[2,128,384]{2,1,0:T(8,128)(2,1)S(1)}, bf16[2,128,384]{2,1,0:T(8,128)(2,1)}, u32[]{:S(2)}) copy-start(bf16[2,128,384]{2,1,0:T(8,128)(2,1)} %get-tuple-element.73.refs_3_.refs_4_.earlier_ref) | copy-start | bytes 589828
  173.9 4.3 %copy-start.44 = (bf16[256,384]{1,0:T(8,128)(2,1)S(1)}, bf16[256,384]{1,0:T(8,128)(2,1)}, u32[]{:S(2)}) copy-start(bf16[256,384]{1,0:T(8,128)(2,1)} %get-tuple-element.92) | copy-start | bytes 589828
  173.9 9.4 %copy-start.43 = (bf16[256,384]{1,0:T(8,128)(2,1)S(1)}, bf16[256,384]{1,0:T(8,128)(2,1)}, u32[]{:S(2)}) copy-start(bf16[256,384]{1,0:T(8,128)(2,1)} %get-tuple-element.93) | copy-start | bytes 589828
  173.9 11.6 %copy-start.15 = (bf16[2,128,384]{2,1,0:T(8,128)(2,1)S(1)}, bf16[2,128,384]{2,1,0:T(8,128)(2,1)}, u32[]{:S(2)}) copy-start(bf16[2,128,384]{2,1,0:T(8,128)(2,1)} %get-tuple-element.79.refs_4_) | copy-start | bytes 589828
  173.9 11.6 %copy-start.35 = (bf16[2,128,384]{2,1,0:T(8,128)(2,1)S(1)}, bf16[2,128,384]{2,1,0:T(8,128)(2,1)}, u32[]{:S(2)}) copy-start(bf16[2,128,384]{2,1,0:T(8,128)(2,1)} %get-tuple-element.80) | copy-start | bytes 589828
  173.9 9.4 %collective-permute-start.25 = (bf16[256,384]{1,0:T(8,128)(2,1)}, bf16[256,384]{1,0:T(8,128)(2,1)S(1)}, u32[]{:S(2)}, u32[]{:S(2)}) collective-permute-start(bf16[256,384]{1,0:T(8,128)(2,1)} %get-tuple-element.91), channel_id=1, source_target_pairs={{0,1},{1,0},{2,3},{3,2},{4,5},{5,4},{6,7},{7,6},{8,9},{9,8},{10,11... | collective-permute-start | bytes 589832 | tf_op jit(solution)/shard_map/ppermute | solution.py:835
  174.7 18.9 %collective-permute-start.32 = (bf16[448,384]{1,0:T(8,128)(2,1)}, bf16[448,384]{1,0:T(8,128)(2,1)S(1)}, u32[]{:S(2)}, u32[]{:S(2)}) collective-permute-start(bf16[448,384]{1,0:T(8,128)(2,1)} %after.5.refs_0_), channel_id=1, source_target_pairs={{0,8},{4,12},{8,0},{12,4},{16,24},{20,28},{24,16},{28,20},{1,9},{5... | collective-permute-start | bytes 1032200 | tf_op jit(solution)/shard_map/ppermute | solution.py:835
  175.4 18.2 %collective-permute-start.33 = (bf16[448,384]{1,0:T(8,128)(2,1)}, bf16[448,384]{1,0:T(8,128)(2,1)S(1)}, u32[]{:S(2)}, u32[]{:S(2)}) collective-permute-start(bf16[448,384]{1,0:T(8,128)(2,1)} %after.5.refs_0_), channel_id=1, source_target_pairs={{0,16},{4,20},{8,24},{12,28},{16,0},{20,4},{24,8},{28,12},{1,17},{... | collective-permute-start | bytes 1032200 | tf_op jit(solution)/shard_map/ppermute | solution.py:835
  176.5 17.1 %collective-permute-start.34 = (bf16[448,384]{1,0:T(8,128)(2,1)}, bf16[448,384]{1,0:T(8,128)(2,1)S(1)}, u32[]{:S(2)}, u32[]{:S(2)}) collective-permute-start(bf16[448,384]{1,0:T(8,128)(2,1)} %after.5.refs_0_), channel_id=1, source_target_pairs={{0,24},{4,28},{8,16},{12,20},{16,8},{20,12},{24,0},{28,4},{1,25},{... | collective-permute-start | bytes 1032200 | tf_op jit(solution)/shard_map/ppermute | solution.py:835
  178.2 10.5 %collective-permute-start.26 = (bf16[256,384]{1,0:T(8,128)(2,1)S(1)}, bf16[256,384]{1,0:T(8,128)(2,1)S(1)}, u32[]{:S(2)}, u32[]{:S(2)}) collective-permute-start(bf16[256,384]{1,0:T(8,128)(2,1)S(1)} %copy-done.44), channel_id=1, source_target_pairs={{0,2},{1,3},{2,0},{3,1},{4,6},{5,7},{6,4},{7,5},{8,10},{9,11},{10,... | collective-permute-start | bytes 589832 | tf_op jit(solution)/shard_map/ppermute | solution.py:835
  183.3 7.6 %copy-start.36 = (bf16[256,384]{1,0:T(8,128)(2,1)}, bf16[256,384]{1,0:T(8,128)(2,1)S(1)}, u32[]{:S(2)}) copy-start(bf16[256,384]{1,0:T(8,128)(2,1)S(1)} %collective-permute-done.25.refs_1_) | copy-start | bytes 589828
  183.3 7.6 %collective-permute-start.27 = (bf16[256,384]{1,0:T(8,128)(2,1)S(1)}, bf16[256,384]{1,0:T(8,128)(2,1)S(1)}, u32[]{:S(2)}, u32[]{:S(2)}) collective-permute-start(bf16[256,384]{1,0:T(8,128)(2,1)S(1)} %copy-done.43), channel_id=1, source_target_pairs={{0,3},{1,2},{2,1},{3,0},{4,7},{5,6},{6,5},{7,4},{8,11},{9,10},{10,... | collective-permute-start | bytes 589832 | tf_op jit(solution)/shard_map/ppermute | solution.py:835
  197.6 31.6 %collective-permute-start.35 = (bf16[4,448,384]{2,1,0:T(8,128)(2,1)}, bf16[4,448,384]{2,1,0:T(8,128)(2,1)S(1)}, u32[]{:S(2)}, u32[]{:S(2)}) collective-permute-start(bf16[4,448,384]{2,1,0:T(8,128)(2,1)} %stack.25.even_ref), channel_id=1, source_target_pairs={{0,4},{4,0},{8,12},{12,8},{16,20},{20,16},{24,28},{28,24},{1,5},{5... | collective-permute-start | bytes 4128776 | tf_op jit(solution)/shard_map/ppermute | solution.py:835
  197.7 4.5 %collective-permute-start.18 = (bf16[384,384]{1,0:T(8,128)(2,1)S(1)}, bf16[384,384]{1,0:T(8,128)(2,1)S(1)}, u32[]{:S(2)}, u32[]{:S(2)}) collective-permute-start(bf16[384,384]{1,0:T(8,128)(2,1)S(1)} %get-tuple-element.102), channel_id=1, source_target_pairs={{0,4},{4,0},{8,12},{12,8},{16,20},{20,16},{24,28},{28,24},{1,5},{5... | collective-permute-start | bytes 884744 | tf_op jit(solution)/shard_map/ppermute | solution.py:835
  198.6 7.8 %collective-permute-start.28 = (bf16[256,384]{1,0:T(8,128)(2,1)S(1)}, bf16[256,384]{1,0:T(8,128)(2,1)S(1)}, u32[]{:S(2)}, u32[]{:S(2)}) collective-permute-start(bf16[256,384]{1,0:T(8,128)(2,1)S(1)} %copy-done.12), channel_id=1, source_target_pairs={{0,8},{4,12},{8,0},{12,4},{16,24},{20,28},{24,16},{28,20},{1,9},{5... | collective-permute-start | bytes 589832 | tf_op jit(solution)/shard_map/ppermute | solution.py:835
  200.4 8.8 %collective-permute-start.29 = (bf16[256,384]{1,0:T(8,128)(2,1)S(1)}, bf16[256,384]{1,0:T(8,128)(2,1)S(1)}, u32[]{:S(2)}, u32[]{:S(2)}) collective-permute-start(bf16[256,384]{1,0:T(8,128)(2,1)S(1)} %copy-done.12), channel_id=1, source_target_pairs={{0,16},{4,20},{8,24},{12,28},{16,0},{20,4},{24,8},{28,12},{1,17},{... | collective-permute-start | bytes 589832 | tf_op jit(solution)/shard_map/ppermute | solution.py:835
  201.1 9.9 %collective-permute-start.30 = (bf16[256,384]{1,0:T(8,128)(2,1)S(1)}, bf16[256,384]{1,0:T(8,128)(2,1)S(1)}, u32[]{:S(2)}, u32[]{:S(2)}) collective-permute-start(bf16[256,384]{1,0:T(8,128)(2,1)S(1)} %copy-done.12), channel_id=1, source_target_pairs={{0,24},{4,28},{8,16},{12,20},{16,8},{20,12},{24,0},{28,4},{1,25},{... | collective-permute-start | bytes 589832 | tf_op jit(solution)/shard_map/ppermute | solution.py:835
  202.2 11.6 %copy-start.5 = (bf16[768,768]{1,0:T(8,128)(2,1)S(1)}, bf16[768,768]{1,0:T(8,128)(2,1)}, u32[]{:S(2)}) copy-start(bf16[768,768]{1,0:T(8,128)(2,1)} %wq_ref.1) | copy-start | bytes 3538948
  206.3 4.7 %copy-start.32 = (bf16[256,384]{1,0:T(8,128)(2,1)}, bf16[256,384]{1,0:T(8,128)(2,1)S(1)}, u32[]{:S(2)}) copy-start(bf16[256,384]{1,0:T(8,128)(2,1)S(1)} %collective-permute-done.28.refs_1_) | copy-start | bytes 589828
  213.9 2.8 %collective-permute-start.31 = (bf16[4,256,384]{2,1,0:T(8,128)(2,1)}, bf16[4,256,384]{2,1,0:T(8,128)(2,1)S(1)}, u32[]{:S(2)}, u32[]{:S(2)}) collective-permute-start(bf16[4,256,384]{2,1,0:T(8,128)(2,1)} %stack.24.even_ref), channel_id=1, source_target_pairs={{0,4},{4,0},{8,12},{12,8},{16,20},{20,16},{24,28},{28,24},{1,5},{5... | collective-permute-start | bytes 2359304 | tf_op jit(solution)/shard_map/ppermute | solution.py:835
  221.4 14.8 %collective-permute-start.36 = (bf16[128,768]{1,0:T(8,128)(2,1)}, bf16[128,768]{1,0:T(8,128)(2,1)S(1)}, u32[]{:S(2)}, u32[]{:S(2)}) collective-permute-start(bf16[128,768]{1,0:T(8,128)(2,1)} %rel_share.1.earlier_ref.refs_0_), channel_id=1, source_target_pairs={{0,1},{1,0},{2,3},{3,2},{4,5},{5,4},{6,7},{7,6},{8,9},{9,8},{10,11... | collective-permute-start | bytes 589832 | tf_op jit(solution)/shard_map/ppermute | solution.py:835
  223.4 17.3 %collective-permute-start.37 = (bf16[128,768]{1,0:T(8,128)(2,1)}, bf16[128,768]{1,0:T(8,128)(2,1)S(1)}, u32[]{:S(2)}, u32[]{:S(2)}) collective-permute-start(bf16[128,768]{1,0:T(8,128)(2,1)} %rel_share.1.earlier_ref.refs_0_), channel_id=1, source_target_pairs={{0,2},{1,3},{2,0},{3,1},{4,6},{5,7},{6,4},{7,5},{8,10},{9,11},{10,... | collective-permute-start | bytes 589832 | tf_op jit(solution)/shard_map/ppermute | solution.py:835
  224.2 16.5 %collective-permute-start.38 = (bf16[128,768]{1,0:T(8,128)(2,1)}, bf16[128,768]{1,0:T(8,128)(2,1)S(1)}, u32[]{:S(2)}, u32[]{:S(2)}) collective-permute-start(bf16[128,768]{1,0:T(8,128)(2,1)} %rel_share.1.earlier_ref.refs_0_), channel_id=1, source_target_pairs={{0,3},{1,2},{2,1},{3,0},{4,7},{5,6},{6,5},{7,4},{8,11},{9,10},{10,... | collective-permute-start | bytes 589832 | tf_op jit(solution)/shard_map/ppermute | solution.py:835
  236.2 4.5 %copy-start.29 = (bf16[128,768]{1,0:T(8,128)(2,1)}, bf16[128,768]{1,0:T(8,128)(2,1)S(1)}, u32[]{:S(2)}) copy-start(bf16[128,768]{1,0:T(8,128)(2,1)S(1)} %collective-permute-done.36.refs_1_) | copy-start | bytes 589828
  (23 other events, 21.5 us)
